TPU v7x, 512 devices: a whole 4x8x8 slice. The times are simulated.
512 devices in a mesh: sec: 2 (over x_lo), grp: 64 (over z, y), tp: 4 (over x_hi, core).
Axes of the slice: x: 4 (x_hi: 2, x_lo: 2; x = x_hi * 2 + x_lo), y: 8, z: 8, core: 2. Of those that a mesh axis runs over, the one named last changes fastest.
Arguments:
- latent_cache: bfloat16 [64, 2048, 576], P('grp', 'sec'), may hold values from -8 to 8
- new_latent: bfloat16 [3, 64, 576], P(None, 'grp'), may hold values from -6 to 6
- queries: bfloat16 [3, 64, 128, 576], P(None, 'grp', 'tp'), may hold values from -48 to 48
- lengths: int32 [64], P('grp'), may hold values from 1 to 2048, as said below
- token_rows: bfloat16 [3, 768, 3584], P(None, 'grp'), may hold values from -6 to 6
- routes: int32 [3, 768, 8], P(None, 'grp'), may hold values from 0 to 63, all different within a row; in each aligned block of 12 rows (0 to 11, 12 to 23, ..., all dimensions but the last counted through in order) at most 3 rows name the same one
- route_gates: float32 [3, 768, 8], P(None, 'grp'), may hold values from 0.1 to 1
- gate_proj: bfloat16 [64, 3584, 1024], P('grp', None, ('sec', 'tp')), may hold values from -0.09375 to 0.09375
- up_proj: bfloat16 [64, 3584, 1024], P('grp', None, ('sec', 'tp')), may hold values from -0.09375 to 0.09375
- down_proj: bfloat16 [64, 1024, 3584], P('grp', ('sec', 'tp')), may hold values from -0.1875 to 0.1875
Outputs:
- attention_out: bfloat16 [3, 64, 128, 512], P(None, 'grp', 'tp', 'sec')
- moe_out: bfloat16 [3, 768, 3584], P(None, 'grp', ('sec', 'tp'))
Inputs may be any that keep to these rules, and one draw needn't show every extreme that they name: Request r attends to its first lengths[r] cached positions; some request uses all 2048. `routes`: each token names 8 different experts; within the 12 tokens of one index of grp at one step no expert is named more than 3 times, a bound that some block reaches.
All inputs are finite; a program needn't handle non-finite values.
Results may differ from a plain program's by a relative error of at most 0.0065.
Values may be sent and summed in bfloat16 or wider, within the bound.
No kernel may reach another device: no remote copies, remote signals or barrier semaphores. Data moves between devices by JAX's collectives and lax.ppermute only.
A program may use at most 128 MiB of HBM per device.

v0:
```python
import jax
import jax.numpy as jnp
from jax import lax
from jax.sharding import PartitionSpec as P

EXPERTS = 64
TOPK = 8
CAP = 3
KL = 512


score_scale = 192.0 ** (-0.5)
neg_big = -1e30


def joined(part, axis, combine):
    gathered = jax.tree.map(lambda a: lax.all_gather(a, axis), part)

    def take(source):
        return jax.tree.map(lambda a: lax.dynamic_index_in_dim(a, source, 0, False), gathered)

    return lax.fori_loop(
        1, lax.axis_size(axis), lambda source, state: combine(state, take(source)), take(0)
    )


def partial_softmax(scores, usable):
    masked = jnp.where(usable, scores, neg_big)
    top_score = jnp.max(masked, axis=-1)
    weights = jnp.where(usable, jnp.exp(masked - top_score[..., None]), 0.0)
    return (weights, top_score, jnp.sum(weights, axis=-1))


def join_parts(earlier, later):
    output_one, top_one, sum_one = earlier
    output_two, top_two, sum_two = later
    top_score = jnp.maximum(top_one, top_two)
    factor_one = jnp.exp(top_one - top_score)
    factor_two = jnp.exp(top_two - top_score)
    return (
        output_one * factor_one[..., None] + output_two * factor_two[..., None],
        top_score,
        sum_one * factor_one + sum_two * factor_two,
    )


def attend_cache(queries, cache_rows, positions, lengths, value_cols):
    scores = (
        jnp.einsum("srhk,rck->rshc", queries, cache_rows, preferred_element_type=jnp.float32)
        * score_scale
    )
    usable = (positions[None, :] < lengths[:, None])[:, None, None, :]
    weights, top_score, weight_sum = partial_softmax(scores, usable)
    output = jnp.einsum(
        "rshc,rcv->rshv",
        weights.astype(jnp.bfloat16),
        value_cols,
        preferred_element_type=jnp.float32,
    )
    return (output, top_score, weight_sum)


def local(
    latent_cache,
    new_latent,
    queries,
    lengths,
    token_rows,
    routes,
    route_gates,
    gate_proj,
    up_proj,
    down_proj,
):
    section = lax.axis_index("sec")
    value_half = KL // lax.axis_size("sec")
    step_count = queries.shape[0]
    step_ids = jnp.arange(step_count)
    causal = (step_ids[:, None] >= step_ids[None, :])[None, :, None, :]
    new_scores = (
        jnp.einsum("srhk,trk->rsht", queries, new_latent, preferred_element_type=jnp.float32)
        * score_scale
    )
    new_weights, new_top, new_sum = partial_softmax(new_scores, causal)
    new_values = lax.dynamic_slice_in_dim(new_latent, section * value_half, value_half, 2)
    new_output = jnp.einsum(
        "rsht,trv->rshv",
        new_weights,
        new_values,
        precision=lax.Precision.HIGHEST,
        preferred_element_type=jnp.float32,
    )
    local_length = latent_cache.shape[1]
    positions = section * local_length + jnp.arange(local_length)
    partials = attend_cache(queries, latent_cache, positions, lengths, latent_cache[:, :, :KL])
    merged = joined(partials, "sec", join_parts)
    cached = (
        lax.dynamic_slice_in_dim(merged[0], section * value_half, value_half, 3),
        merged[1],
        merged[2],
    )
    output, top_score, weight_sum = join_parts(cached, (new_output, new_top, new_sum))
    attention_out = jnp.transpose(output / weight_sum[..., None], (1, 0, 2, 3)).astype(jnp.bfloat16)
    grp_size = lax.axis_size("grp")
    local_count = gate_proj.shape[0]
    slot_total = EXPERTS * CAP
    token_count = token_rows.shape[1]
    moe_steps = []
    for step in range(token_rows.shape[0]):
        flat_ids = routes[step].reshape(-1)
        onehot = (flat_ids[:, None] == jnp.arange(EXPERTS, dtype=jnp.int32)[None, :]).astype(
            jnp.int32
        )
        before = jnp.cumsum(onehot, axis=0) - onehot
        slot_ids = jnp.sum(onehot * before, axis=1)
        target = flat_ids * CAP + slot_ids
        target_hot = (target[:, None] == jnp.arange(slot_total, dtype=jnp.int32)[None, :]).astype(
            jnp.float32
        )
        token_hot = (
            (jnp.arange(flat_ids.shape[0]) // TOPK)[:, None] == jnp.arange(token_count)[None, :]
        ).astype(jnp.float32)
        placing = jnp.dot(target_hot.T, token_hot).astype(jnp.bfloat16)
        outgoing = jnp.dot(placing, token_rows[step], preferred_element_type=jnp.float32).astype(
            jnp.bfloat16
        )
        outgoing = outgoing.reshape(grp_size, local_count * CAP, outgoing.shape[1])
        weighting = jnp.dot(
            token_hot.T,
            target_hot * route_gates[step].reshape(-1)[:, None],
            precision=lax.Precision.HIGHEST,
        )
        received = lax.all_to_all(outgoing, "grp", split_axis=0, concat_axis=0, tiled=True)
        model_width = received.shape[2]
        arranged = received.reshape(grp_size, local_count, CAP, model_width).transpose(1, 0, 2, 3)
        arranged = arranged.reshape(local_count, grp_size * CAP, model_width)
        gate_pre = jnp.einsum(
            "erd,edf->erf", arranged, gate_proj, preferred_element_type=jnp.float32
        )
        up_pre = jnp.einsum("erd,edf->erf", arranged, up_proj, preferred_element_type=jnp.float32)
        hidden = (jax.nn.silu(gate_pre) * up_pre).astype(jnp.bfloat16)
        partial_value = jnp.einsum(
            "erf,efd->erd", hidden, down_proj, preferred_element_type=jnp.float32
        )
        return_rows = partial_value.reshape(local_count, grp_size, CAP, model_width).transpose(
            1, 0, 2, 3
        )
        return_rows = return_rows.reshape(grp_size, local_count * CAP, model_width)
        returned = lax.all_to_all(return_rows, "grp", split_axis=0, concat_axis=0, tiled=True)
        combined = jnp.dot(
            weighting, returned.reshape(slot_total, model_width), precision=lax.Precision.HIGHEST
        )
        reduced = lax.psum_scatter(combined, ("sec", "tp"), scatter_dimension=1, tiled=True)
        moe_steps.append(reduced.astype(jnp.bfloat16))
    return (attention_out, jnp.stack(moe_steps))


def solution(mesh):
    in_specs = (
        P("grp", "sec", None),
        P(None, "grp", None),
        P(None, "grp", "tp", None),
        P("grp"),
        P(None, "grp", None),
        P(None, "grp", None),
        P(None, "grp", None),
        P("grp", None, ("sec", "tp")),
        P("grp", None, ("sec", "tp")),
        P("grp", ("sec", "tp"), None),
    )
    out_specs = (P(None, "grp", "tp", "sec"), P(None, "grp", ("sec", "tp")))
    return jax.shard_map(local, mesh=mesh, in_specs=in_specs, out_specs=out_specs, check_vma=False)
```

profile of v0, /device:TPU:32, one launch (start us, length us, event | category | flops | bytes accessed | tf_op | source)
XLA Modules:
  0.0 584.3 jit_solution(16943223825959397368)
XLA Ops:
  12.4 16.4 %all-to-all-start.4 = ((bf16[64,3,3584]{2,1,0:T(4,128)(2,1)}), bf16[64,3,3584]{2,1,0:T(4,128)(2,1)S(1)}, u32[]{:S(2)}, u32[]{:S(2)}) async-start(bf16[64,3,3584]{2,1,0:T(4,128)(2,1)} %reshape.408), calls=%async_computation.4 | async-start | bytes 3670016 | tf_op jit(solution)/shard_map/all_to_all | solution.py:133
  31.3 3.9 reshape.405
  35.2 38.0 %all-to-all-done.4 = bf16[64,3,3584]{2,1,0:T(4,128)(2,1)S(1)} async-done(((bf16[64,3,3584]{2,1,0:T(4,128)(2,1)}), bf16[64,3,3584]{2,1,0:T(4,128)(2,1)S(1)}, u32[]{:S(2)}, u32[]{:S(2)}) %all-to-all-start.4) | async-done | bytes 1376288 | tf_op jit(solution)/shard_map/all_to_all | solution.py:133
  74.4 10.4 %all-to-all-start.2 = ((bf16[64,3,3584]{2,1,0:T(4,128)(2,1)}), bf16[64,3,3584]{2,1,0:T(4,128)(2,1)}, u32[]{:S(2)}, u32[]{:S(2)}) async-start(bf16[64,3,3584]{2,1,0:T(4,128)(2,1)} %reshape.405), calls=%async_computation.2 | async-start | bytes 3670016 | tf_op jit(solution)/shard_map/all_to_all | solution.py:133
  88.4 39.2 %all-to-all-done.2 = bf16[64,3,3584]{2,1,0:T(4,128)(2,1)} async-done(((bf16[64,3,3584]{2,1,0:T(4,128)(2,1)}), bf16[64,3,3584]{2,1,0:T(4,128)(2,1)}, u32[]{:S(2)}, u32[]{:S(2)}) %all-to-all-start.2) | async-done | bytes 1376288 | tf_op jit(solution)/shard_map/all_to_all | solution.py:133
  127.6 9.3 %all-to-all-start = ((bf16[64,3,3584]{2,1,0:T(4,128)(2,1)}), bf16[64,3,3584]{2,1,0:T(4,128)(2,1)}, u32[]{:S(2)}, u32[]{:S(2)}) async-start(bf16[64,3,3584]{2,1,0:T(4,128)(2,1)} %reshape.399), calls=%async_computation | async-start | bytes 3670016 | tf_op jit(solution)/shard_map/all_to_all | solution.py:133
  145.9 33.5 %all-to-all-done = bf16[64,3,3584]{2,1,0:T(4,128)(2,1)} async-done(((bf16[64,3,3584]{2,1,0:T(4,128)(2,1)}), bf16[64,3,3584]{2,1,0:T(4,128)(2,1)}, u32[]{:S(2)}, u32[]{:S(2)}) %all-to-all-start) | async-done | bytes 1376288 | tf_op jit(solution)/shard_map/all_to_all | solution.py:133
  179.4 9.6 %all-to-all-start.5 = ((f32[64,3,3584]{2,1,0:T(4,128)}), f32[64,3,3584]{2,1,0:T(4,128)}, u32[]{:S(2)}, u32[]{:S(2)}) async-start(f32[64,3,3584]{2,1,0:T(4,128)} %copy.49), calls=%async_computation.5 | async-start | bytes 7340032 | tf_op jit(solution)/shard_map/all_to_all | solution.py:149
  197.9 90.4 %all-to-all-done.5 = f32[64,3,3584]{2,1,0:T(4,128)} async-done(((f32[64,3,3584]{2,1,0:T(4,128)}), f32[64,3,3584]{2,1,0:T(4,128)}, u32[]{:S(2)}, u32[]{:S(2)}) %all-to-all-start.5) | async-done | bytes 2752544 | tf_op jit(solution)/shard_map/all_to_all | solution.py:149
  288.3 14.1 %all-to-all-start.3 = ((f32[64,3,3584]{2,1,0:T(4,128)}), f32[64,3,3584]{2,1,0:T(4,128)}, u32[]{:S(2)}, u32[]{:S(2)}) async-start(f32[64,3,3584]{2,1,0:T(4,128)} %copy.45), calls=%async_computation.3 | async-start | bytes 7340032 | tf_op jit(solution)/shard_map/all_to_all | solution.py:149
  311.3 78.7 %all-to-all-done.3 = f32[64,3,3584]{2,1,0:T(4,128)} async-done(((f32[64,3,3584]{2,1,0:T(4,128)}), f32[64,3,3584]{2,1,0:T(4,128)}, u32[]{:S(2)}, u32[]{:S(2)}) %all-to-all-start.3) | async-done | bytes 2752544 | tf_op jit(solution)/shard_map/all_to_all | solution.py:149
  390.0 13.4 %all-to-all-start.1 = ((f32[64,3,3584]{2,1,0:T(4,128)}), f32[64,3,3584]{2,1,0:T(4,128)}, u32[]{:S(2)}, u32[]{:S(2)}) async-start(f32[64,3,3584]{2,1,0:T(4,128)} %copy.41), calls=%async_computation.1 | async-start | bytes 7340032 | tf_op jit(solution)/shard_map/all_to_all | solution.py:149
  405.7 6.9 %all-gather = f32[6,32,512]{2,1,0:T(8,128)S(1)} all-gather(f32[3,32,512]{2,1,0:T(8,128)S(1)} %fusion.11), channel_id=2, replica_groups=mesh['sec'=2,'grp'=64,'tp'=4] {'sec'}, dimensions={0}, use_global_device_ids=true | all-gather | bytes 589824 | tf_op jit(solution)/shard_map/all_gather | solution.py:17
  413.7 4.8 reshape.410
  418.5 8.9 %convolution_bitcast_fusion = f32[3584,12]{1,0:T(8,128)} fusion(f32[12,192]{1,0:T(8,128)S(1)} %fusion.45, f32[192,3584]{1,0:T(8,128)} %reshape.410), kind=kOutput, calls=%fused_computation.3 | convolution fusion | flops 99090432 | bytes 2933760
  427.9 4.9 reshape.407
  432.8 9.0 %convolution_bitcast_fusion.1 = f32[3584,12]{1,0:T(8,128)} fusion(f32[12,192]{1,0:T(8,128)S(1)} %fusion.47, f32[192,3584]{1,0:T(8,128)} %reshape.407), kind=kOutput, calls=%fused_computation.4 | convolution fusion | flops 99090432 | bytes 2933760
  441.9 4.3 all-gather.4
  446.2 4.5 all-gather.3
  450.8 37.5 %all-to-all-done.1 = f32[64,3,3584]{2,1,0:T(4,128)} async-done(((f32[64,3,3584]{2,1,0:T(4,128)}), f32[64,3,3584]{2,1,0:T(4,128)}, u32[]{:S(2)}, u32[]{:S(2)}) %all-to-all-start.1) | async-done | bytes 2752544 | tf_op jit(solution)/shard_map/all_to_all | solution.py:149
  488.2 4.8 reshape.404
  493.1 9.0 %convolution_bitcast_fusion.2 = f32[3584,12]{1,0:T(8,128)} fusion(f32[12,192]{1,0:T(8,128)S(1)} %fusion.49, f32[192,3584]{1,0:T(8,128)} %reshape.404), kind=kOutput, calls=%fused_computation.5 | convolution fusion | flops 99090432 | bytes 2933760
  504.1 26.2 %reduce-scatter.12.cloned.1.call-done = f32[448,12]{1,0:T(8,128)} async-done(((f32[3584,12]{1,0:T(8,128)}), f32[448,12]{1,0:T(8,128)}) %reduce-scatter.12.cloned.1.call-update) | async-done | bytes 21520
  531.4 44.4 %reduce-scatter.10.cloned.1.call-done = f32[448,12]{1,0:T(8,128)} async-done(((f32[3584,12]{1,0:T(8,128)}), f32[448,12]{1,0:T(8,128)}) %reduce-scatter.10.cloned.1.call-update) | async-done | bytes 21520
  (97 shorter events, 47.1 us)
Async XLA Ops:
  7.2 134.6 %copy-start = (bf16[1,128,3584]{2,1,0:T(8,128)(2,1)S(1)}, bf16[1,128,3584]{2,1,0:T(8,128)(2,1)}, u32[]{:S(2)}) copy-start(bf16[1,128,3584]{2,1,0:T(8,128)(2,1)} %param.19) | copy-start | bytes 2752516
  12.4 17.0 %copy-start.5 = (bf16[3,12,3584]{2,1,0:T(8,128)(2,1)S(1)}, bf16[3,12,3584]{2,1,0:T(8,128)(2,1)}, u32[]{:S(2)}) copy-start(bf16[3,12,3584]{2,1,0:T(8,128)(2,1)} %param.14) | copy-start | bytes 774148
  12.4 60.8 %all-to-all-start.4 = ((bf16[64,3,3584]{2,1,0:T(4,128)(2,1)}), bf16[64,3,3584]{2,1,0:T(4,128)(2,1)S(1)}, u32[]{:S(2)}, u32[]{:S(2)}) async-start(bf16[64,3,3584]{2,1,0:T(4,128)(2,1)} %reshape.408), calls=%async_computation.4 | async-start | bytes 3670016 | tf_op jit(solution)/shard_map/all_to_all | solution.py:133
  73.2 1.2 copy-start.3
  74.4 53.2 %all-to-all-start.2 = ((bf16[64,3,3584]{2,1,0:T(4,128)(2,1)}), bf16[64,3,3584]{2,1,0:T(4,128)(2,1)}, u32[]{:S(2)}, u32[]{:S(2)}) async-start(bf16[64,3,3584]{2,1,0:T(4,128)(2,1)} %reshape.405), calls=%async_computation.2 | async-start | bytes 3670016 | tf_op jit(solution)/shard_map/all_to_all | solution.py:133
  127.6 51.8 %all-to-all-start = ((bf16[64,3,3584]{2,1,0:T(4,128)(2,1)}), bf16[64,3,3584]{2,1,0:T(4,128)(2,1)}, u32[]{:S(2)}, u32[]{:S(2)}) async-start(bf16[64,3,3584]{2,1,0:T(4,128)(2,1)} %reshape.399), calls=%async_computation | async-start | bytes 3670016 | tf_op jit(solution)/shard_map/all_to_all | solution.py:133
  136.9 3.1 copy-start.2
  140.0 1.2 copy-start.8
  179.4 108.9 %all-to-all-start.5 = ((f32[64,3,3584]{2,1,0:T(4,128)}), f32[64,3,3584]{2,1,0:T(4,128)}, u32[]{:S(2)}, u32[]{:S(2)}) async-start(f32[64,3,3584]{2,1,0:T(4,128)} %copy.49), calls=%async_computation.5 | async-start | bytes 7340032 | tf_op jit(solution)/shard_map/all_to_all | solution.py:149
  191.9 1.2 copy-start.9
  288.3 101.7 %all-to-all-start.3 = ((f32[64,3,3584]{2,1,0:T(4,128)}), f32[64,3,3584]{2,1,0:T(4,128)}, u32[]{:S(2)}, u32[]{:S(2)}) async-start(f32[64,3,3584]{2,1,0:T(4,128)} %copy.45), calls=%async_computation.3 | async-start | bytes 7340032 | tf_op jit(solution)/shard_map/all_to_all | solution.py:149
  305.4 1.2 copy-start.10
  311.3 92.2 %copy-start.7 = (f32[3,12,8]{1,2,0:T(8,128)S(1)}, f32[3,12,8]{1,2,0:T(8,128)}, u32[]{:S(2)}) copy-start(f32[3,12,8]{1,2,0:T(8,128)} %param.16) | copy-start | bytes 3460
  311.3 93.4 %copy-start.4 = (bf16[1,1024,576]{1,2,0:T(8,128)(2,1)S(1)}, bf16[1,1024,576]{1,2,0:T(8,128)(2,1)}, u32[]{:S(2)}) copy-start(bf16[1,1024,576]{1,2,0:T(8,128)(2,1)} %param.10) | copy-start | bytes 3538948
  311.3 93.4 %copy-start.6 = (bf16[3,1,32,576]{3,2,1,0:T(8,128)(2,1)S(1)}, bf16[3,1,32,576]{3,2,1,0:T(8,128)(2,1)}, u32[]{:S(2)}) copy-start(bf16[3,1,32,576]{3,2,1,0:T(8,128)(2,1)} %param.12) | copy-start | bytes 331780
  390.0 98.2 %all-to-all-start.1 = ((f32[64,3,3584]{2,1,0:T(4,128)}), f32[64,3,3584]{2,1,0:T(4,128)}, u32[]{:S(2)}, u32[]{:S(2)}) async-start(f32[64,3,3584]{2,1,0:T(4,128)} %copy.41), calls=%async_computation.1 | async-start | bytes 7340032 | tf_op jit(solution)/shard_map/all_to_all | solution.py:149
  403.5 99.6 %reduce-scatter.14.cloned.1.call-start = ((), (), s32[]{:S(2)}) async-start(), calls=%async_computation.11 | async-start | bytes 2064384
  405.2 8.2 %copy-start.11 = (bf16[3,1,576]{2,0,1:T(4,128)(2,1)S(1)}, bf16[3,1,576]{2,0,1:T(4,128)(2,1)}, u32[]{:S(2)}) copy-start(bf16[3,1,576]{2,0,1:T(4,128)(2,1)} %param.11) | copy-start | bytes 10372
  427.4 102.9 %reduce-scatter.12.cloned.1.call-start = ((), (), s32[]{:S(2)}) async-start(), calls=%async_computation.10 | async-start | bytes 2064384
  441.8 134.0 %reduce-scatter.10.cloned.1.call-start = ((), (), s32[]{:S(2)}) async-start(), calls=%async_computation.9 | async-start | bytes 2064384
  493.0 84.5 %copy-start.1 = (bf16[1,128,3584]{2,1,0:T(8,128)(2,1)S(1)}, bf16[1,128,3584]{2,1,0:T(8,128)(2,1)}, u32[]{:S(2)}) copy-start(bf16[1,128,3584]{2,1,0:T(8,128)(2,1)} %param.19) | copy-start | bytes 2752516
Sparse Core Ops, SparseCore 0:
  427.6 57.2 reduce-scatter.13
  487.7 42.5 reduce-scatter.11
  533.2 42.5 reduce-scatter.9
where the time goes:
time: 593 us; the launch traced here: 584 us
  waiting for transfers between devices  388 us (65%)
  starting transfers between devices  73.5 us (12%)
  local copies, waits for them, and re-layouts  51.1 us (9%)
  matrix products  38.8 us (7%)
  blocking collectives  15.7 us (3%)
  between operations  15 us (3%)
    all_to_all x3, waiting for transfers between devices, local(): lax.all_to_all(return_rows, 'grp', split_axis=0, concat_axis=0, tiled=True)  207 us
    all_to_all x3, waiting for transfers between devices, local(): lax.all_to_all(outgoing, 'grp', split_axis=0, concat_axis=0, tiled=True)  111 us
    unnamed x6, waiting for transfers between devices  70.7 us
    all_to_all x3, starting transfers between devices, local(): lax.all_to_all(return_rows, 'grp', split_axis=0, concat_axis=0, tiled=True)  37.1 us
    all_to_all x3, starting transfers between devices, local(): lax.all_to_all(outgoing, 'grp', split_axis=0, concat_axis=0, tiled=True)  36.1 us
    unnamed x3, matrix products  26.9 us
    all_gather x3, blocking collectives, joined(): gathered = jax.tree.map(lambda a: lax.all_gather(a, axis), part)  15.7 us
    reshape x3, local copies, waits for them, and re-layouts, local(): returned.reshape(slot_total, model_width)  14.5 us
  transfers between devices with their start and end apart: 9, of which 8 were waited for; matrix products, arithmetic and copies ran while one was open for 14% of the time, Pallas kernels for 0%

commit v1 on v0

v1 whole, which is shorter than its diff:
```python
import jax
import jax.numpy as jnp
from jax import lax
from jax.experimental import pallas as pl
from jax.experimental.pallas import tpu as pltpu
from jax.sharding import PartitionSpec as P

CAP = 3
KL = 512
ROWS = 8
HALF = 64

score_scale = 192.0 ** (-0.5)
neg_big = -1e30
BF = jnp.bfloat16
F32 = jnp.float32
LINE = ("sec", "tp")

SMEM = pl.BlockSpec(memory_space=pltpu.SMEM)
VMEM = pl.BlockSpec(memory_space=pltpu.VMEM)


def dot(a, b, dims=((1,), (0,))):
    return lax.dot_general(a, b, (dims, ((), ())), preferred_element_type=F32)


def iota(shape, axis):
    return lax.broadcasted_iota(jnp.int32, shape, axis)


def call(body, out_shape, in_specs, flops, moved, name):
    single = not isinstance(out_shape, (list, tuple))
    return pl.pallas_call(
        body,
        out_shape=out_shape,
        in_specs=in_specs,
        out_specs=VMEM if single else [VMEM] * len(out_shape),
        compiler_params=pltpu.CompilerParams(vmem_limit_bytes=40 * 1024 * 1024),
        cost_estimate=pl.CostEstimate(flops=flops, bytes_accessed=moved, transcendentals=0),
        name=name,
    )


def attend_body(info, q_ref, cache_ref, new_ref, send_ref, keep_ref):
    section, length = info[0], info[1]
    q = q_ref[...]
    rows, local_length = q.shape[0], cache_ref.shape[0]
    steps = new_ref.shape[0]
    heads = rows // steps
    scores = dot(q, cache_ref[...], ((1,), (1,))) * score_scale
    usable = iota((rows, local_length), 1) + section * local_length < length
    scores = jnp.where(usable, scores, neg_big)
    top = jnp.max(scores, axis=1, keepdims=True)
    new_rows = new_ref[...]
    fresh = dot(q, new_rows, ((1,), (1,))) * score_scale
    step_of = iota((rows, steps), 0) // heads
    causal = (iota((rows, steps), 1) <= step_of) & (section == 0)
    fresh = jnp.where(causal, fresh, neg_big)
    top = jnp.maximum(top, jnp.max(fresh, axis=1, keepdims=True))
    weights = jnp.where(usable, jnp.exp(scores - top), 0.0)
    new_weights = jnp.where(causal, jnp.exp(fresh - top), 0.0)
    total = jnp.sum(weights, axis=1, keepdims=True) + jnp.sum(new_weights, axis=1, keepdims=True)
    out = dot(weights.astype(BF), cache_ref[:, :KL])
    values = new_rows[:, :KL].astype(F32)
    for t in range(steps):
        out = out + new_weights[:, t : t + 1] * values[t : t + 1, :]
    mine = section == 0
    half = KL // 2
    keep_ref[:, :half] = jnp.where(mine, out[:, :half], out[:, half:])
    send_ref[:, :half] = jnp.where(mine, out[:, half:], out[:, :half])
    for ref in (keep_ref, send_ref):
        ref[:, half : half + 128] = jnp.broadcast_to(top, (rows, 128))
        ref[:, half + 128 : half + 256] = jnp.broadcast_to(total, (rows, 128))


def merge_body(one_ref, two_ref, out_ref):
    half = out_ref.shape[1]
    top_one, top_two = one_ref[:, half : half + 1], two_ref[:, half : half + 1]
    top = jnp.maximum(top_one, top_two)
    factor_one, factor_two = jnp.exp(top_one - top), jnp.exp(top_two - top)
    total = (
        one_ref[:, half + 128 : half + 129] * factor_one
        + two_ref[:, half + 128 : half + 129] * factor_two
    )
    out = one_ref[:, :half] * factor_one + two_ref[:, :half] * factor_two
    out_ref[...] = (out / total).astype(BF)


def named_slots(routes, experts):
    tokens, picks = routes.shape
    experts_of = iota((tokens, experts), 1)
    named = jnp.zeros((tokens, experts), F32)
    for k in range(picks):
        named = named + (routes[:, k : k + 1] == experts_of).astype(F32)
    earlier = (iota((tokens, tokens), 1) < iota((tokens, tokens), 0)).astype(BF)
    before = dot(earlier, named.astype(BF))
    return jnp.where(named > 0.5, before, -1.0)


def spread(values, experts):
    rows = experts * ROWS
    repeat = (iota((experts, rows), 1) // ROWS == iota((experts, rows), 0)).astype(BF)
    return dot(values.astype(BF), repeat)


def pack_body(where_ref, tokens_ref, routes_ref, out_ref):
    chip, core = where_ref[0], where_ref[1]
    rows = out_ref.shape[0]
    experts = rows // ROWS
    steps, tokens = routes_ref.shape[0], routes_ref.shape[1]
    part = tokens_ref.shape[2] // 8
    place = iota((tokens, rows), 1) % ROWS
    main = jnp.zeros((rows, part), F32)
    for step in range(steps):
        columns = tokens_ref[step, :, pl.ds(pl.multiple_of(chip * 2 * part, 128), 2 * part)]
        own = jnp.where(core == 0, columns[:, :part], columns[:, part:])
        slots = spread(named_slots(routes_ref[step], experts), experts)
        wanted = (place - CAP * step).astype(F32)
        chosen = ((slots == wanted) & (wanted >= 0)).astype(BF)
        main = main + dot(chosen, own, ((0,), (0,)))
        if step == steps - 1:
            last = dot((slots == CAP - 1.0).astype(BF), own, ((0,), (0,)))
    out_ref[:, :part] = main.astype(BF)
    row = iota((rows, HALF), 0) % ROWS
    tail = jnp.zeros((rows, HALF), F32)
    for i in range(part // HALF):
        tail = tail + jnp.where(row == i, last[:, i * HALF : (i + 1) * HALF], 0.0)
    out_ref[:, part:] = tail.astype(BF)


def gates_body(routes_ref, gates_ref, out_ref):
    steps, tokens, picks = routes_ref.shape
    rows = out_ref.shape[2]
    experts = rows // ROWS
    out_ref[...] = jnp.zeros(out_ref.shape, BF)
    place = iota((tokens, rows), 1) % ROWS
    experts_of = iota((tokens, experts), 1)
    for step in range(steps):
        routes = routes_ref[step]
        gates = gates_ref[step]
        slots = spread(named_slots(routes, experts), experts)
        gate = jnp.zeros((tokens, experts), F32)
        for k in range(picks):
            gate = gate + jnp.where(routes[:, k : k + 1] == experts_of, gates[:, k : k + 1], 0.0)
        high = gate.astype(BF)
        low = gate - high.astype(F32)
        wanted = (place - CAP * step).astype(F32)
        chosen = (slots == wanted) & (wanted >= 0)
        for n, part in enumerate((spread(high, experts), spread(low, experts))):
            out_ref[n, 16 * step : 16 * step + tokens, :] = jnp.where(chosen, part, 0.0).astype(BF)
            if step == steps - 1:
                for i in range(7):
                    start = 16 * (steps + i)
                    out_ref[n, start : start + tokens, :] = jnp.where(
                        (slots == CAP - 1.0) & (place == i), part, 0.0
                    ).astype(BF)


def hidden_body(info, *refs):
    pieces, (gate_ref, up_ref, out_ref) = refs[:8], refs[8:]
    rows = pieces[0].shape[0]
    experts = rows // ROWS
    part = gate_ref.shape[0] // 8
    me = info[0]

    def weights(k, start, size):
        offset = pl.multiple_of((me ^ k) * part + start, HALF)
        return jnp.concatenate(
            [gate_ref[pl.ds(offset, size), :], up_ref[pl.ds(offset, size), :]], axis=1
        )

    def finish(pre):
        wide = pre.shape[1] // 2
        gate, up = pre[:, :wide], pre[:, wide:]
        return (gate / (1.0 + jnp.exp(-gate)) * up).astype(BF)

    pre = jnp.zeros((rows, 2 * out_ref.shape[1]), F32)
    for k in range(8):
        pre = pre + dot(pieces[k][:, :part], weights(k, 0, part))
    out_ref[:rows, :] = finish(pre)
    tail = jnp.concatenate([pieces[k][:, part:] for k in range(8)], axis=1)
    count = part // HALF
    source = iota((count * experts, rows), 0)
    wanted = (source % experts) * ROWS + source // experts
    chosen = (iota((count * experts, rows), 1) == wanted).astype(BF)
    ninth = dot(chosen, tail).astype(BF)
    pre = jnp.zeros((experts, 2 * out_ref.shape[1]), F32)
    for i in range(count):
        part_weights = jnp.concatenate([weights(k, i * HALF, HALF) for k in range(8)], axis=0)
        pre = pre + dot(ninth[i * experts : (i + 1) * experts], part_weights)
    out_ref[rows:, :] = finish(pre)


def down_body(*refs):
    hidden, down, out_ref = refs[:8], refs[8:16], refs[16]
    rows, part = out_ref.shape[0], down[0].shape[1]
    experts = rows // ROWS
    total = jnp.zeros((hidden[0].shape[0], part), F32)
    for k in range(8):
        total = total + dot(hidden[k][...], down[k][...])
    total = total.astype(BF)
    out_ref[:, :part] = total[:rows]
    repeat = (iota((rows, experts), 0) // ROWS == iota((rows, experts), 1)).astype(BF)
    last = dot(repeat, total[rows:])
    row = iota((rows, HALF), 0) % ROWS
    tail = jnp.zeros((rows, HALF), F32)
    for i in range(part // HALF):
        tail = tail + jnp.where(row == i, last[:, i * HALF : (i + 1) * HALF], 0.0)
    out_ref[:, part:] = tail.astype(BF)


def slices_body(info, down_ref, *outs):
    me = info[0]
    part = outs[0].shape[1]
    for k in range(8):
        other = me ^ k
        columns = down_ref[:, pl.ds(pl.multiple_of((other // 2) * 2 * part, 128), 2 * part)]
        outs[k][...] = jnp.where(other % 2 == 0, columns[:, :part], columns[:, part:])


def combine_body(gates_ref, rows_ref, out_ref):
    steps, tokens, part = out_ref.shape
    values = rows_ref[...]
    total = dot(gates_ref[0], values) + dot(gates_ref[1], values)
    for step in range(steps):
        out = total[16 * step : 16 * step + tokens, :part]
        if step == steps - 1:
            more = [
                total[16 * (steps + i) : 16 * (steps + i) + tokens, part:]
                for i in range(part // HALF)
            ]
            out = out + jnp.concatenate(more, axis=1)
        out_ref[step] = out.astype(BF)


def swap(value, k):
    return lax.ppermute(value, LINE, [(d, d ^ k) for d in range(8)])


def gather_line(own):
    middle = own.shape[0] // 2 // 16 * 16
    pieces = [own] + [None] * 7
    pieces[4] = swap(own, 4)
    pieces[6] = swap(own, 6)
    pieces[1] = swap(own, 1)
    first = swap(pieces[4][:middle], 6)
    second = swap(pieces[6][middle:], 4)
    pieces[5] = swap(pieces[4], 1)
    pieces[7] = swap(pieces[6], 1)
    pieces[2] = jnp.concatenate([first, second], axis=0)
    pieces[3] = jnp.concatenate([swap(first, 1), swap(second, 1)], axis=0)
    return pieces


def local(
    latent_cache,
    new_latent,
    queries,
    lengths,
    token_rows,
    routes,
    route_gates,
    gate_proj,
    up_proj,
    down_proj,
):
    section = lax.axis_index("sec")
    me = lax.axis_index(LINE)
    experts = lax.axis_size("grp")
    rows = experts * ROWS
    steps, tokens, width = token_rows.shape
    part = width // 8
    units = gate_proj.shape[2]
    here = me.astype(jnp.int32).reshape(1)

    packed = call(
        pack_body, jax.ShapeDtypeStruct((rows, part + HALF), BF), [SMEM, VMEM, VMEM],
        10**8, 10**6, "pack",
    )(jnp.stack([me // 2, me % 2]).astype(jnp.int32), token_rows, routes)
    arrived = lax.all_to_all(
        packed.reshape(experts, ROWS, part + HALF), "grp", split_axis=0, concat_axis=0, tiled=True
    ).reshape(rows, part + HALF)

    down = call(
        slices_body, [jax.ShapeDtypeStruct((units, part), BF)] * 8, [SMEM, VMEM],
        10**6, 2 * 10**6, "slices",
    )(here, down_proj.reshape(units, width))
    down = [down[0]] + [swap(down[k], k) for k in range(1, 8)]

    gates = call(
        gates_body,
        jax.ShapeDtypeStruct((2, 16 * (steps + part // HALF), rows), BF),
        [VMEM, VMEM], 10**8, 10**6, "gates",
    )(routes, route_gates)

    heads = queries.shape[2]
    send, keep = call(
        attend_body, [jax.ShapeDtypeStruct((steps * heads, KL // 2 + 256), F32)] * 2,
        [SMEM, VMEM, VMEM, VMEM], 3 * 10**8, 2 * 10**6, "attend",
    )(
        jnp.stack([section.astype(jnp.int32), lengths[0]]),
        queries.reshape(steps * heads, queries.shape[3]),
        latent_cache.reshape(latent_cache.shape[1:]),
        new_latent.reshape(steps, new_latent.shape[2]),
    )
    other = swap(send, 4)
    attention = call(
        merge_body, jax.ShapeDtypeStruct((steps * heads, KL // 2), BF), [VMEM, VMEM],
        10**6, 10**6, "merge",
    )(keep, other)

    pieces = gather_line(arrived)
    hidden = call(
        hidden_body, jax.ShapeDtypeStruct((rows + experts, units), BF), [SMEM] + [VMEM] * 10,
        10**9, 6 * 10**6, "hidden",
    )(here, *pieces, gate_proj.reshape(width, units), up_proj.reshape(width, units))
    hidden = gather_line(hidden)
    outgoing = call(
        down_body, jax.ShapeDtypeStruct((rows, part + HALF), BF), [VMEM] * 16,
        10**9, 3 * 10**6, "down",
    )(*hidden, *down)
    returned = lax.all_to_all(
        outgoing.reshape(experts, ROWS, part + HALF), "grp", split_axis=0, concat_axis=0, tiled=True
    ).reshape(rows, part + HALF)
    moe = call(
        combine_body, jax.ShapeDtypeStruct((steps, tokens, part), BF), [VMEM, VMEM],
        10**8, 10**6, "combine",
    )(gates, returned)
    return attention.reshape(steps, 1, heads, KL // 2), moe


def solution(mesh):
    in_specs = (
        P("grp", "sec", None),
        P(None, "grp", None),
        P(None, "grp", "tp", None),
        P("grp"),
        P(None, "grp", None),
        P(None, "grp", None),
        P(None, "grp", None),
        P("grp", None, ("sec", "tp")),
        P("grp", None, ("sec", "tp")),
        P("grp", ("sec", "tp"), None),
    )
    out_specs = (P(None, "grp", "tp", "sec"), P(None, "grp", ("sec", "tp")))
    return jax.shard_map(local, mesh=mesh, in_specs=in_specs, out_specs=out_specs, check_vma=False)
```

time: 593 us -> 157 us (0.26)
  the two profiles are of different devices: /device:TPU:32 before, /device:TPU:6 now
where the time goes in v1:
time: 157 us; the launch traced here: 155 us
  starting transfers between devices  72.9 us (46%)
  blocking collectives  36.1 us (23%)
  waiting for transfers between devices  30.1 us (19%)
  Pallas kernels  11.3 us (7%)
  local copies, waits for them, and re-layouts  2.68 us (2%)
  between operations  1.87 us (1%)
    ppermute x26, starting transfers between devices, swap(): return lax.ppermute(value, LINE, [(d, d ^ k) for d in range(8)])  67.6 us
    all_to_all x1, blocking collectives, local(): lax.all_to_all(packed.reshape(experts, ROWS, part + HALF), 'grp', split_a...  36.1 us
    ppermute x26, waiting for transfers between devices, swap(): return lax.ppermute(value, LINE, [(d, d ^ k) for d in range(8)])  22.7 us
    all_to_all x1, waiting for transfers between devices, local(): lax.all_to_all(outgoing.reshape(experts, ROWS, part + HALF), 'grp', split...  7.42 us
    all_to_all x1, starting transfers between devices, local(): lax.all_to_all(outgoing.reshape(experts, ROWS, part + HALF), 'grp', split...  5.23 us
  transfers between devices with their start and end apart: 27, of which 7 were waited for; matrix products, arithmetic and copies ran while one was open for 1% of the time, Pallas kernels for 2%

profile of v1, /device:TPU:6, one launch (start us, length us, event | category | flops | bytes accessed | tf_op | source)
XLA Modules:
  0.0 155.2 jit_solution(9317759665454869723)
XLA Ops:
  2.5 2.3 %pack.1 = bf16[512,512]{1,0:T(8,128)(2,1)S(1)} custom-call(s32[2]{0:T(128)S(1)} %pad_add_fusion.1.where_ref, bf16[3,12,3584]{2,1,0:T(8,128)(2,1)S(1)} %copy-done.3, s32[3,12,8]{2,1,0:T(8,128)S(1)} %copy.13.routes_ref), custom_call_target="tpu_custom_call" | custom-call | flops 100000000 | bytes 1000000 | tf_op jit(solution)/shard_map/pack/pallas_call | solution.py:276
  4.8 36.1 %all_to_all.10 = bf16[64,8,512]{2,1,0:T(8,128)(2,1)S(1)} all-to-all(bf16[64,8,512]{2,1,0:T(8,128)(2,1)S(1)} %bitcast.23), channel_id=1, replica_groups=mesh['sec'=2,'grp'=64,'tp'=4] {'grp'}, dimensions={0} | all-to-all | bytes 1048576 | tf_op jit(solution)/shard_map/all_to_all | solution.py:280
  40.9 2.7 %collective-permute-start.2 = (bf16[512,512]{1,0:T(8,128)(2,1)S(1)}, bf16[512,512]{1,0:T(8,128)(2,1)S(1)}, u32[]{:S(2)}, u32[]{:S(2)}) collective-permute-start(bf16[512,512]{1,0:T(8,128)(2,1)S(1)} %bitcast.18), channel_id=1, source_target_pairs={{0,256},{1,257},{2,258},{3,259},{256,0},{257,1},{258,2},{259,3},{4... | collective-permute-start | bytes 1572872 | tf_op jit(solution)/shard_map/ppermute | solution.py:237
  43.7 3.0 %collective-permute-start.4 = (bf16[512,512]{1,0:T(8,128)(2,1)S(1)}, bf16[512,512]{1,0:T(8,128)(2,1)S(1)}, u32[]{:S(2)}, u32[]{:S(2)}) collective-permute-start(bf16[512,512]{1,0:T(8,128)(2,1)S(1)} %bitcast.19), channel_id=1, source_target_pairs={{0,258},{1,259},{2,256},{3,257},{256,2},{257,3},{258,0},{259,1},{4... | collective-permute-start | bytes 1572872 | tf_op jit(solution)/shard_map/ppermute | solution.py:237
  46.7 6.9 %collective-permute-done.2.refs_4_ = bf16[512,512]{1,0:T(8,128)(2,1)S(1)} collective-permute-done((bf16[512,512]{1,0:T(8,128)(2,1)S(1)}, bf16[512,512]{1,0:T(8,128)(2,1)S(1)}, u32[]{:S(2)}, u32[]{:S(2)}) %collective-permute-start.2) | collective-permute-done | bytes 524320 | tf_op jit(solution)/shard_map/ppermute | solution.py:237
  53.7 2.5 %collective-permute-start.3 = (bf16[256,512]{1,0:T(8,128)(2,1)S(1)}, bf16[256,512]{1,0:T(8,128)(2,1)S(1)}, u32[]{:S(2)}, u32[]{:S(2)}) collective-permute-start(bf16[256,512]{1,0:T(8,128)(2,1)S(1)} %slice.16), channel_id=1, source_target_pairs={{0,258},{1,259},{2,256},{3,257},{256,2},{257,3},{258,0},{259,1},{4... | collective-permute-start | bytes 786440 | tf_op jit(solution)/shard_map/ppermute | solution.py:237
  56.2 2.8 %collective-permute-done.4.refs_6_ = bf16[512,512]{1,0:T(8,128)(2,1)S(1)} collective-permute-done((bf16[512,512]{1,0:T(8,128)(2,1)S(1)}, bf16[512,512]{1,0:T(8,128)(2,1)S(1)}, u32[]{:S(2)}, u32[]{:S(2)}) %collective-permute-start.4) | collective-permute-done | bytes 524320 | tf_op jit(solution)/shard_map/ppermute | solution.py:237
  63.1 2.4 %collective-permute-start.8 = (bf16[512,512]{1,0:T(8,128)(2,1)S(1)}, bf16[512,512]{1,0:T(8,128)(2,1)S(1)}, u32[]{:S(2)}, u32[]{:S(2)}) collective-permute-start(bf16[512,512]{1,0:T(8,128)(2,1)S(1)} %collective-permute-done.2.refs_4_), channel_id=1, source_target_pairs={{0,1},{1,0},{2,3},{3,2},{256,257},{257,256},{258,259},{259,258},{4... | collective-permute-start | bytes 1572872 | tf_op jit(solution)/shard_map/ppermute | solution.py:237
  67.5 2.4 %collective-permute-start.6 = (bf16[256,512]{1,0:T(8,128)(2,1)S(1)}, bf16[256,512]{1,0:T(8,128)(2,1)S(1)}, u32[]{:S(2)}, u32[]{:S(2)}) collective-permute-start(bf16[256,512]{1,0:T(8,128)(2,1)S(1)} %collective-permute-done.3), channel_id=1, source_target_pairs={{0,1},{1,0},{2,3},{3,2},{256,257},{257,256},{258,259},{259,258},{4... | collective-permute-start | bytes 786440 | tf_op jit(solution)/shard_map/ppermute | solution.py:237
  75.3 3.7 %collective-permute-start.11 = (bf16[576,128]{1,0:T(8,128)(2,1)S(1)}, bf16[576,128]{1,0:T(8,128)(2,1)S(1)}, u32[]{:S(2)}, u32[]{:S(2)}) collective-permute-start(bf16[576,128]{1,0:T(8,128)(2,1)S(1)} %hidden.1.refs_0_), channel_id=1, source_target_pairs={{0,256},{1,257},{2,258},{3,259},{256,0},{257,1},{258,2},{259,3},{4... | collective-permute-start | bytes 442376 | tf_op jit(solution)/shard_map/ppermute | solution.py:237
  78.9 3.7 %collective-permute-start.13 = (bf16[576,128]{1,0:T(8,128)(2,1)S(1)}, bf16[576,128]{1,0:T(8,128)(2,1)S(1)}, u32[]{:S(2)}, u32[]{:S(2)}) collective-permute-start(bf16[576,128]{1,0:T(8,128)(2,1)S(1)} %hidden.1.refs_0_), channel_id=1, source_target_pairs={{0,258},{1,259},{2,256},{3,257},{256,2},{257,3},{258,0},{259,1},{4... | collective-permute-start | bytes 442376 | tf_op jit(solution)/shard_map/ppermute | solution.py:237
  85.0 2.5 %collective-permute-start.20 = (bf16[128,448]{1,0:T(8,128)(2,1)S(1)}, bf16[128,448]{1,0:T(8,128)(2,1)S(1)}, u32[]{:S(2)}, u32[]{:S(2)}) collective-permute-start(bf16[128,448]{1,0:T(8,128)(2,1)S(1)} %get-tuple-element.16), channel_id=1, source_target_pairs={{0,2},{1,3},{2,0},{3,1},{256,258},{257,259},{258,256},{259,257},{4... | collective-permute-start | bytes 344072 | tf_op jit(solution)/shard_map/ppermute | solution.py:237
  87.5 4.7 %collective-permute-start.21 = (bf16[128,448]{1,0:T(8,128)(2,1)S(1)}, bf16[128,448]{1,0:T(8,128)(2,1)S(1)}, u32[]{:S(2)}, u32[]{:S(2)}) collective-permute-start(bf16[128,448]{1,0:T(8,128)(2,1)S(1)} %get-tuple-element.17), channel_id=1, source_target_pairs={{0,3},{1,2},{2,1},{3,0},{256,259},{257,258},{258,257},{259,256},{4... | collective-permute-start | bytes 344072 | tf_op jit(solution)/shard_map/ppermute | solution.py:237
  94.2 3.5 %collective-permute-start.23 = (bf16[128,448]{1,0:T(8,128)(2,1)S(1)}, bf16[128,448]{1,0:T(8,128)(2,1)S(1)}, u32[]{:S(2)}, u32[]{:S(2)}) collective-permute-start(bf16[128,448]{1,0:T(8,128)(2,1)S(1)} %get-tuple-element.19), channel_id=1, source_target_pairs={{0,257},{1,256},{2,259},{3,258},{256,1},{257,0},{258,3},{259,2},{4... | collective-permute-start | bytes 344072 | tf_op jit(solution)/shard_map/ppermute | solution.py:237
  97.8 3.4 %collective-permute-start.12 = (bf16[288,128]{1,0:T(8,128)(2,1)S(1)}, bf16[288,128]{1,0:T(8,128)(2,1)S(1)}, u32[]{:S(2)}, u32[]{:S(2)}) collective-permute-start(bf16[288,128]{1,0:T(8,128)(2,1)S(1)} %slice.18), channel_id=1, source_target_pairs={{0,258},{1,259},{2,256},{3,257},{256,2},{257,3},{258,0},{259,1},{4... | collective-permute-start | bytes 221192 | tf_op jit(solution)/shard_map/ppermute | solution.py:237
  105.3 2.2 %collective-permute-start.17 = (bf16[576,128]{1,0:T(8,128)(2,1)S(1)}, bf16[576,128]{1,0:T(8,128)(2,1)S(1)}, u32[]{:S(2)}, u32[]{:S(2)}) collective-permute-start(bf16[576,128]{1,0:T(8,128)(2,1)S(1)} %collective-permute-done.11.refs_4_), channel_id=1, source_target_pairs={{0,1},{1,0},{2,3},{3,2},{256,257},{257,256},{258,259},{259,258},{4... | collective-permute-start | bytes 442376 | tf_op jit(solution)/shard_map/ppermute | solution.py:237
  109.6 2.2 %collective-permute-start.15 = (bf16[288,128]{1,0:T(8,128)(2,1)S(1)}, bf16[288,128]{1,0:T(8,128)(2,1)S(1)}, u32[]{:S(2)}, u32[]{:S(2)}) collective-permute-start(bf16[288,128]{1,0:T(8,128)(2,1)S(1)} %collective-permute-done.12), channel_id=1, source_target_pairs={{0,1},{1,0},{2,3},{3,2},{256,257},{257,256},{258,259},{259,258},{4... | collective-permute-start | bytes 221192 | tf_op jit(solution)/shard_map/ppermute | solution.py:237
  114.0 3.7 %collective-permute-start.24 = (bf16[128,448]{1,0:T(8,128)(2,1)S(1)}, bf16[128,448]{1,0:T(8,128)(2,1)S(1)}, u32[]{:S(2)}, u32[]{:S(2)}) collective-permute-start(bf16[128,448]{1,0:T(8,128)(2,1)S(1)} %get-tuple-element.20), channel_id=1, source_target_pairs={{0,258},{1,259},{2,256},{3,257},{256,2},{257,3},{258,0},{259,1},{4... | collective-permute-start | bytes 344072 | tf_op jit(solution)/shard_map/ppermute | solution.py:237
  117.7 3.0 %collective-permute-start.25 = (bf16[128,448]{1,0:T(8,128)(2,1)S(1)}, bf16[128,448]{1,0:T(8,128)(2,1)S(1)}, u32[]{:S(2)}, u32[]{:S(2)}) collective-permute-start(bf16[128,448]{1,0:T(8,128)(2,1)S(1)} %get-tuple-element.21), channel_id=1, source_target_pairs={{0,259},{1,258},{2,257},{3,256},{256,3},{257,2},{258,1},{259,0},{4... | collective-permute-start | bytes 344072 | tf_op jit(solution)/shard_map/ppermute | solution.py:237
  122.8 3.6 %collective-permute-done.25.refs_15_ = bf16[128,448]{1,0:T(8,128)(2,1)S(1)} collective-permute-done((bf16[128,448]{1,0:T(8,128)(2,1)S(1)}, bf16[128,448]{1,0:T(8,128)(2,1)S(1)}, u32[]{:S(2)}, u32[]{:S(2)}) %collective-permute-start.25) | collective-permute-done | bytes 114720 | tf_op jit(solution)/shard_map/ppermute | solution.py:237
  126.4 2.7 %down.1 = bf16[512,512]{1,0:T(8,128)(2,1)} custom-call(bf16[576,128]{1,0:T(8,128)(2,1)S(1)} %hidden.1.refs_0_, bf16[576,128]{1,0:T(8,128)(2,1)S(1)} %collective-permute-done.10.refs_1_, bf16[576,128]{1,0:T(8,128)(2,1)S(1)} %pad_maximum_fusion.2.refs_2_, bf16[576,128]{1,0:T(8,128)(2,1)S(1)} %pad_maximum_fusion.3.refs_3_, ...), custom_call_target="tpu_custom_call" | custom-call | flops 1000000000 | bytes 3000000 | tf_op jit(solution)/shard_map/down/pallas_call | solution.py:318
  129.1 5.2 %all-to-all-start.1 = ((bf16[64,8,512]{2,1,0:T(8,128)(2,1)}), bf16[64,8,512]{2,1,0:T(8,128)(2,1)S(1)}, u32[]{:S(2)}, u32[]{:S(2)}) async-start(bf16[64,8,512]{2,1,0:T(8,128)(2,1)} %bitcast.14), calls=%async_computation.1 | async-start | bytes 1048576 | tf_op jit(solution)/shard_map/all_to_all | solution.py:322
  140.2 5.8 %collective-permute-done.two_ref = f32[96,512]{1,0:T(8,128)S(1)} collective-permute-done((f32[96,512]{1,0:T(8,128)S(1)}, f32[96,512]{1,0:T(8,128)S(1)}, u32[]{:S(2)}, u32[]{:S(2)}) %collective-permute-start) | collective-permute-done | bytes 196640 | tf_op jit(solution)/shard_map/ppermute | solution.py:237
  146.8 7.4 %all-to-all-done.1 = bf16[64,8,512]{2,1,0:T(8,128)(2,1)S(1)} async-done(((bf16[64,8,512]{2,1,0:T(8,128)(2,1)}), bf16[64,8,512]{2,1,0:T(8,128)(2,1)S(1)}, u32[]{:S(2)}, u32[]{:S(2)}) %all-to-all-start.1) | async-done | bytes 524320 | tf_op jit(solution)/shard_map/all_to_all | solution.py:322
  (68 shorter events, 34.9 us)
Async XLA Ops:
  40.9 12.7 %collective-permute-start.2 = (bf16[512,512]{1,0:T(8,128)(2,1)S(1)}, bf16[512,512]{1,0:T(8,128)(2,1)S(1)}, u32[]{:S(2)}, u32[]{:S(2)}) collective-permute-start(bf16[512,512]{1,0:T(8,128)(2,1)S(1)} %bitcast.18), channel_id=1, source_target_pairs={{0,256},{1,257},{2,258},{3,259},{256,0},{257,1},{258,2},{259,3},{4... | collective-permute-start | bytes 1572872 | tf_op jit(solution)/shard_map/ppermute | solution.py:237
  43.7 15.3 %collective-permute-start.4 = (bf16[512,512]{1,0:T(8,128)(2,1)S(1)}, bf16[512,512]{1,0:T(8,128)(2,1)S(1)}, u32[]{:S(2)}, u32[]{:S(2)}) collective-permute-start(bf16[512,512]{1,0:T(8,128)(2,1)S(1)} %bitcast.19), channel_id=1, source_target_pairs={{0,258},{1,259},{2,256},{3,257},{256,2},{257,3},{258,0},{259,1},{4... | collective-permute-start | bytes 1572872 | tf_op jit(solution)/shard_map/ppermute | solution.py:237
  53.7 13.8 %collective-permute-start.3 = (bf16[256,512]{1,0:T(8,128)(2,1)S(1)}, bf16[256,512]{1,0:T(8,128)(2,1)S(1)}, u32[]{:S(2)}, u32[]{:S(2)}) collective-permute-start(bf16[256,512]{1,0:T(8,128)(2,1)S(1)} %slice.16), channel_id=1, source_target_pairs={{0,258},{1,259},{2,256},{3,257},{256,2},{257,3},{258,0},{259,1},{4... | collective-permute-start | bytes 786440 | tf_op jit(solution)/shard_map/ppermute | solution.py:237
  59.0 10.9 %collective-permute-start.5 = (bf16[256,512]{1,0:T(8,128)(2,1)S(1)}, bf16[256,512]{1,0:T(8,128)(2,1)S(1)}, u32[]{:S(2)}, u32[]{:S(2)}) collective-permute-start(bf16[256,512]{1,0:T(8,128)(2,1)S(1)} %slice.17), channel_id=1, source_target_pairs={{0,256},{1,257},{2,258},{3,259},{256,0},{257,1},{258,2},{259,3},{4... | collective-permute-start | bytes 786440 | tf_op jit(solution)/shard_map/ppermute | solution.py:237
  61.2 12.2 %collective-permute-start.1 = (bf16[512,512]{1,0:T(8,128)(2,1)S(1)}, bf16[512,512]{1,0:T(8,128)(2,1)S(1)}, u32[]{:S(2)}, u32[]{:S(2)}) collective-permute-start(bf16[512,512]{1,0:T(8,128)(2,1)S(1)} %bitcast.20), channel_id=1, source_target_pairs={{0,1},{1,0},{2,3},{3,2},{256,257},{257,256},{258,259},{259,258},{4... | collective-permute-start | bytes 1572872 | tf_op jit(solution)/shard_map/ppermute | solution.py:237
  63.1 10.3 %collective-permute-start.8 = (bf16[512,512]{1,0:T(8,128)(2,1)S(1)}, bf16[512,512]{1,0:T(8,128)(2,1)S(1)}, u32[]{:S(2)}, u32[]{:S(2)}) collective-permute-start(bf16[512,512]{1,0:T(8,128)(2,1)S(1)} %collective-permute-done.2.refs_4_), channel_id=1, source_target_pairs={{0,1},{1,0},{2,3},{3,2},{256,257},{257,256},{258,259},{259,258},{4... | collective-permute-start | bytes 1572872 | tf_op jit(solution)/shard_map/ppermute | solution.py:237
  65.5 7.9 %collective-permute-start.9 = (bf16[512,512]{1,0:T(8,128)(2,1)S(1)}, bf16[512,512]{1,0:T(8,128)(2,1)S(1)}, u32[]{:S(2)}, u32[]{:S(2)}) collective-permute-start(bf16[512,512]{1,0:T(8,128)(2,1)S(1)} %collective-permute-done.4.refs_6_), channel_id=1, source_target_pairs={{0,1},{1,0},{2,3},{3,2},{256,257},{257,256},{258,259},{259,258},{4... | collective-permute-start | bytes 1572872 | tf_op jit(solution)/shard_map/ppermute | solution.py:237
  75.3 17.0 %collective-permute-start.11 = (bf16[576,128]{1,0:T(8,128)(2,1)S(1)}, bf16[576,128]{1,0:T(8,128)(2,1)S(1)}, u32[]{:S(2)}, u32[]{:S(2)}) collective-permute-start(bf16[576,128]{1,0:T(8,128)(2,1)S(1)} %hidden.1.refs_0_), channel_id=1, source_target_pairs={{0,256},{1,257},{2,258},{3,259},{256,0},{257,1},{258,2},{259,3},{4... | collective-permute-start | bytes 442376 | tf_op jit(solution)/shard_map/ppermute | solution.py:237
  78.9 15.2 %collective-permute-start.13 = (bf16[576,128]{1,0:T(8,128)(2,1)S(1)}, bf16[576,128]{1,0:T(8,128)(2,1)S(1)}, u32[]{:S(2)}, u32[]{:S(2)}) collective-permute-start(bf16[576,128]{1,0:T(8,128)(2,1)S(1)} %hidden.1.refs_0_), channel_id=1, source_target_pairs={{0,258},{1,259},{2,256},{3,257},{256,2},{257,3},{258,0},{259,1},{4... | collective-permute-start | bytes 442376 | tf_op jit(solution)/shard_map/ppermute | solution.py:237
  83.1 14.6 %collective-permute-start.19 = (bf16[128,448]{1,0:T(8,128)(2,1)S(1)}, bf16[128,448]{1,0:T(8,128)(2,1)S(1)}, u32[]{:S(2)}, u32[]{:S(2)}) collective-permute-start(bf16[128,448]{1,0:T(8,128)(2,1)S(1)} %get-tuple-element.15), channel_id=1, source_target_pairs={{0,1},{1,0},{2,3},{3,2},{256,257},{257,256},{258,259},{259,258},{4... | collective-permute-start | bytes 344072 | tf_op jit(solution)/shard_map/ppermute | solution.py:237
  85.0 16.1 %collective-permute-start.20 = (bf16[128,448]{1,0:T(8,128)(2,1)S(1)}, bf16[128,448]{1,0:T(8,128)(2,1)S(1)}, u32[]{:S(2)}, u32[]{:S(2)}) collective-permute-start(bf16[128,448]{1,0:T(8,128)(2,1)S(1)} %get-tuple-element.16), channel_id=1, source_target_pairs={{0,2},{1,3},{2,0},{3,1},{256,258},{257,259},{258,256},{259,257},{4... | collective-permute-start | bytes 344072 | tf_op jit(solution)/shard_map/ppermute | solution.py:237
  87.5 15.6 %collective-permute-start.21 = (bf16[128,448]{1,0:T(8,128)(2,1)S(1)}, bf16[128,448]{1,0:T(8,128)(2,1)S(1)}, u32[]{:S(2)}, u32[]{:S(2)}) collective-permute-start(bf16[128,448]{1,0:T(8,128)(2,1)S(1)} %get-tuple-element.17), channel_id=1, source_target_pairs={{0,3},{1,2},{2,1},{3,0},{256,259},{257,258},{258,257},{259,256},{4... | collective-permute-start | bytes 344072 | tf_op jit(solution)/shard_map/ppermute | solution.py:237
  92.2 13.0 %collective-permute-start.22 = (bf16[128,448]{1,0:T(8,128)(2,1)S(1)}, bf16[128,448]{1,0:T(8,128)(2,1)S(1)}, u32[]{:S(2)}, u32[]{:S(2)}) collective-permute-start(bf16[128,448]{1,0:T(8,128)(2,1)S(1)} %get-tuple-element.18), channel_id=1, source_target_pairs={{0,256},{1,257},{2,258},{3,259},{256,0},{257,1},{258,2},{259,3},{4... | collective-permute-start | bytes 344072 | tf_op jit(solution)/shard_map/ppermute | solution.py:237
  94.2 13.3 %collective-permute-start.23 = (bf16[128,448]{1,0:T(8,128)(2,1)S(1)}, bf16[128,448]{1,0:T(8,128)(2,1)S(1)}, u32[]{:S(2)}, u32[]{:S(2)}) collective-permute-start(bf16[128,448]{1,0:T(8,128)(2,1)S(1)} %get-tuple-element.19), channel_id=1, source_target_pairs={{0,257},{1,256},{2,259},{3,258},{256,1},{257,0},{258,3},{259,2},{4... | collective-permute-start | bytes 344072 | tf_op jit(solution)/shard_map/ppermute | solution.py:237
  97.8 11.8 %collective-permute-start.12 = (bf16[288,128]{1,0:T(8,128)(2,1)S(1)}, bf16[288,128]{1,0:T(8,128)(2,1)S(1)}, u32[]{:S(2)}, u32[]{:S(2)}) collective-permute-start(bf16[288,128]{1,0:T(8,128)(2,1)S(1)} %slice.18), channel_id=1, source_target_pairs={{0,258},{1,259},{2,256},{3,257},{256,2},{257,3},{258,0},{259,1},{4... | collective-permute-start | bytes 221192 | tf_op jit(solution)/shard_map/ppermute | solution.py:237
  101.2 10.7 %collective-permute-start.14 = (bf16[288,128]{1,0:T(8,128)(2,1)S(1)}, bf16[288,128]{1,0:T(8,128)(2,1)S(1)}, u32[]{:S(2)}, u32[]{:S(2)}) collective-permute-start(bf16[288,128]{1,0:T(8,128)(2,1)S(1)} %slice.19), channel_id=1, source_target_pairs={{0,256},{1,257},{2,258},{3,259},{256,0},{257,1},{258,2},{259,3},{4... | collective-permute-start | bytes 221192 | tf_op jit(solution)/shard_map/ppermute | solution.py:237
  103.1 23.3 %collective-permute-start.10 = (bf16[576,128]{1,0:T(8,128)(2,1)S(1)}, bf16[576,128]{1,0:T(8,128)(2,1)S(1)}, u32[]{:S(2)}, u32[]{:S(2)}) collective-permute-start(bf16[576,128]{1,0:T(8,128)(2,1)S(1)} %hidden.1.refs_0_), channel_id=1, source_target_pairs={{0,1},{1,0},{2,3},{3,2},{256,257},{257,256},{258,259},{259,258},{4... | collective-permute-start | bytes 442376 | tf_op jit(solution)/shard_map/ppermute | solution.py:237
  105.3 21.1 %collective-permute-start.17 = (bf16[576,128]{1,0:T(8,128)(2,1)S(1)}, bf16[576,128]{1,0:T(8,128)(2,1)S(1)}, u32[]{:S(2)}, u32[]{:S(2)}) collective-permute-start(bf16[576,128]{1,0:T(8,128)(2,1)S(1)} %collective-permute-done.11.refs_4_), channel_id=1, source_target_pairs={{0,1},{1,0},{2,3},{3,2},{256,257},{257,256},{258,259},{259,258},{4... | collective-permute-start | bytes 442376 | tf_op jit(solution)/shard_map/ppermute | solution.py:237
  107.5 18.9 %collective-permute-start.18 = (bf16[576,128]{1,0:T(8,128)(2,1)S(1)}, bf16[576,128]{1,0:T(8,128)(2,1)S(1)}, u32[]{:S(2)}, u32[]{:S(2)}) collective-permute-start(bf16[576,128]{1,0:T(8,128)(2,1)S(1)} %collective-permute-done.13.refs_6_), channel_id=1, source_target_pairs={{0,1},{1,0},{2,3},{3,2},{256,257},{257,256},{258,259},{259,258},{4... | collective-permute-start | bytes 442376 | tf_op jit(solution)/shard_map/ppermute | solution.py:237
  111.8 5.8 %collective-permute-start.16 = (bf16[288,128]{1,0:T(8,128)(2,1)S(1)}, bf16[288,128]{1,0:T(8,128)(2,1)S(1)}, u32[]{:S(2)}, u32[]{:S(2)}) collective-permute-start(bf16[288,128]{1,0:T(8,128)(2,1)S(1)} %collective-permute-done.14), channel_id=1, source_target_pairs={{0,1},{1,0},{2,3},{3,2},{256,257},{257,256},{258,259},{259,258},{4... | collective-permute-start | bytes 221192 | tf_op jit(solution)/shard_map/ppermute | solution.py:237
  114.0 8.8 %collective-permute-start.24 = (bf16[128,448]{1,0:T(8,128)(2,1)S(1)}, bf16[128,448]{1,0:T(8,128)(2,1)S(1)}, u32[]{:S(2)}, u32[]{:S(2)}) collective-permute-start(bf16[128,448]{1,0:T(8,128)(2,1)S(1)} %get-tuple-element.20), channel_id=1, source_target_pairs={{0,258},{1,259},{2,256},{3,257},{256,2},{257,3},{258,0},{259,1},{4... | collective-permute-start | bytes 344072 | tf_op jit(solution)/shard_map/ppermute | solution.py:237
  117.7 8.7 %collective-permute-start.25 = (bf16[128,448]{1,0:T(8,128)(2,1)S(1)}, bf16[128,448]{1,0:T(8,128)(2,1)S(1)}, u32[]{:S(2)}, u32[]{:S(2)}) collective-permute-start(bf16[128,448]{1,0:T(8,128)(2,1)S(1)} %get-tuple-element.21), channel_id=1, source_target_pairs={{0,259},{1,258},{2,257},{3,256},{256,3},{257,2},{258,1},{259,0},{4... | collective-permute-start | bytes 344072 | tf_op jit(solution)/shard_map/ppermute | solution.py:237
  129.1 25.1 %all-to-all-start.1 = ((bf16[64,8,512]{2,1,0:T(8,128)(2,1)}), bf16[64,8,512]{2,1,0:T(8,128)(2,1)S(1)}, u32[]{:S(2)}, u32[]{:S(2)}) async-start(bf16[64,8,512]{2,1,0:T(8,128)(2,1)} %bitcast.14), calls=%async_computation.1 | async-start | bytes 1048576 | tf_op jit(solution)/shard_map/all_to_all | solution.py:322
  137.5 8.6 %collective-permute-start = (f32[96,512]{1,0:T(8,128)S(1)}, f32[96,512]{1,0:T(8,128)S(1)}, u32[]{:S(2)}, u32[]{:S(2)}) collective-permute-start(f32[96,512]{1,0:T(8,128)S(1)} %get-tuple-element.13), channel_id=1, source_target_pairs={{0,256},{1,257},{2,258},{3,259},{256,0},{257,1},{258,2},{259,3},{4... | collective-permute-start | bytes 589832 | tf_op jit(solution)/shard_map/ppermute | solution.py:237
  (11 other events, 77.3 us)

commit v2 on v1

--- a/solution.py
+++ b/solution.py
@@ -18,6 +18,7 @@
 
 SMEM = pl.BlockSpec(memory_space=pltpu.SMEM)
 VMEM = pl.BlockSpec(memory_space=pltpu.VMEM)
+ANY = pl.BlockSpec(memory_space=pl.ANY)
 
 
 def dot(a, b, dims=((1,), (0,))):
@@ -103,29 +104,40 @@
     return dot(values.astype(BF), repeat)
 
 
-def pack_body(where_ref, tokens_ref, routes_ref, out_ref):
+def pack_body(where_ref, tokens_ref, routes_ref, out_ref, tokens_here, routes_here, sems):
     chip, core = where_ref[0], where_ref[1]
     rows = out_ref.shape[0]
     experts = rows // ROWS
     steps, tokens = routes_ref.shape[0], routes_ref.shape[1]
     part = tokens_ref.shape[2] // 8
+    columns = pl.ds(pl.multiple_of(chip * 2 * part, 128), 2 * part)
+    fetch_routes = pltpu.make_async_copy(routes_ref, routes_here, sems.at[0])
+    fetch_tokens = pltpu.make_async_copy(tokens_ref.at[:, :, columns], tokens_here, sems.at[1])
+    fetch_routes.start()
+    fetch_tokens.start()
     place = iota((tokens, rows), 1) % ROWS
+    fetch_routes.wait()
+    slots = [spread(named_slots(routes_here[step], experts), experts) for step in range(steps)]
+    fetch_tokens.wait()
     main = jnp.zeros((rows, part), F32)
     for step in range(steps):
-        columns = tokens_ref[step, :, pl.ds(pl.multiple_of(chip * 2 * part, 128), 2 * part)]
-        own = jnp.where(core == 0, columns[:, :part], columns[:, part:])
-        slots = spread(named_slots(routes_ref[step], experts), experts)
+        both = tokens_here[step]
+        own = jnp.where(core == 0, both[:, :part], both[:, part:])
         wanted = (place - CAP * step).astype(F32)
-        chosen = ((slots == wanted) & (wanted >= 0)).astype(BF)
+        chosen = ((slots[step] == wanted) & (wanted >= 0)).astype(BF)
         main = main + dot(chosen, own, ((0,), (0,)))
         if step == steps - 1:
-            last = dot((slots == CAP - 1.0).astype(BF), own, ((0,), (0,)))
+            last = dot((slots[step] == CAP - 1.0).astype(BF), own, ((0,), (0,)))
     out_ref[:, :part] = main.astype(BF)
-    row = iota((rows, HALF), 0) % ROWS
-    tail = jnp.zeros((rows, HALF), F32)
+    out_ref[:, part:] = ninth_columns(last, part)
+
+
+def ninth_columns(last, part):
+    row = iota((last.shape[0], HALF), 0) % ROWS
+    tail = jnp.zeros((last.shape[0], HALF), F32)
     for i in range(part // HALF):
         tail = tail + jnp.where(row == i, last[:, i * HALF : (i + 1) * HALF], 0.0)
-    out_ref[:, part:] = tail.astype(BF)
+    return tail.astype(BF)
 
 
 def gates_body(routes_ref, gates_ref, out_ref):
@@ -156,66 +168,82 @@
                     ).astype(BF)
 
 
-def hidden_body(info, *refs):
-    pieces, (gate_ref, up_ref, out_ref) = refs[:8], refs[8:]
+def slices_body(where_ref, gate_ref, up_ref, down_ref, other_ref, *down_outs):
+    chip, core = where_ref[0], where_ref[1]
+    units = gate_ref.shape[1]
+    part = gate_ref.shape[0] // 8
+    for m in range(4):
+        offset = pl.multiple_of((2 * (chip ^ m) + 1 - core) * part, HALF)
+        rows = slice(m * part, (m + 1) * part)
+        other_ref[rows, :units] = gate_ref[pl.ds(offset, part), :]
+        other_ref[rows, units:] = up_ref[pl.ds(offset, part), :]
+        columns = pl.ds(pl.multiple_of((chip ^ m) * 2 * part, 128), 2 * part)
+        down_outs[m][...] = down_ref[:, columns]
+
+
+def partial_body(where_ref, *refs):
+    pieces, (gate_ref, up_ref, other_ref, keep_ref, send_ref) = refs[:4], refs[4:]
     rows = pieces[0].shape[0]
     experts = rows // ROWS
     part = gate_ref.shape[0] // 8
-    me = info[0]
-
-    def weights(k, start, size):
-        offset = pl.multiple_of((me ^ k) * part + start, HALF)
+    wide = keep_ref.shape[1]
+    chip, core = where_ref[0], where_ref[1]
+
+    def weights(m, start, size):
+        offset = pl.multiple_of((2 * (chip ^ m) + core) * part + start, HALF)
         return jnp.concatenate(
-            [gate_ref[pl.ds(offset, size), :], up_ref[pl.ds(offset, size), :]], axis=1
+            [
+                gate_ref[pl.ds(offset, size), :],
+                up_ref[pl.ds(offset, size), :],
+                other_ref[m * part + start : m * part + start + size, :],
+            ],
+            axis=1,
         )
 
-    def finish(pre):
-        wide = pre.shape[1] // 2
-        gate, up = pre[:, :wide], pre[:, wide:]
-        return (gate / (1.0 + jnp.exp(-gate)) * up).astype(BF)
-
-    pre = jnp.zeros((rows, 2 * out_ref.shape[1]), F32)
-    for k in range(8):
-        pre = pre + dot(pieces[k][:, :part], weights(k, 0, part))
-    out_ref[:rows, :] = finish(pre)
-    tail = jnp.concatenate([pieces[k][:, part:] for k in range(8)], axis=1)
-    count = part // HALF
-    source = iota((count * experts, rows), 0)
+    total = jnp.zeros((rows, 2 * wide), F32)
+    for m in range(4):
+        total = total + dot(pieces[m][:, :part], weights(m, 0, part))
+    keep_ref[:rows, :] = total[:, :wide]
+    send_ref[:rows, :] = total[:, wide:]
+    tail = jnp.concatenate([pieces[m][:, part:] for m in range(4)], axis=1)
+    blocks = part // HALF
+    source = iota((blocks * experts, rows), 0)
     wanted = (source % experts) * ROWS + source // experts
-    chosen = (iota((count * experts, rows), 1) == wanted).astype(BF)
+    chosen = (iota((blocks * experts, rows), 1) == wanted).astype(BF)
     ninth = dot(chosen, tail).astype(BF)
-    pre = jnp.zeros((experts, 2 * out_ref.shape[1]), F32)
-    for i in range(count):
-        part_weights = jnp.concatenate([weights(k, i * HALF, HALF) for k in range(8)], axis=0)
-        pre = pre + dot(ninth[i * experts : (i + 1) * experts], part_weights)
-    out_ref[rows:, :] = finish(pre)
-
-
-def down_body(*refs):
-    hidden, down, out_ref = refs[:8], refs[8:16], refs[16]
-    rows, part = out_ref.shape[0], down[0].shape[1]
+    total = jnp.zeros((experts, 2 * wide), F32)
+    for i in range(blocks):
+        block_weights = jnp.concatenate([weights(m, i * HALF, HALF) for m in range(4)], axis=0)
+        total = total + dot(ninth[i * experts : (i + 1) * experts], block_weights)
+    keep_ref[rows:, :] = total[:, :wide]
+    send_ref[rows:, :] = total[:, wide:]
+
+
+def hidden_body(one_ref, two_ref, out_ref):
+    units = out_ref.shape[1]
+    gate = one_ref[:, :units] + two_ref[:, :units]
+    up = one_ref[:, units:] + two_ref[:, units:]
+    out_ref[...] = (gate / (1.0 + jnp.exp(-gate)) * up).astype(BF)
+
+
+def down_body(where_ref, *refs):
+    hidden, down, (keep_ref, send_ref) = refs[:4], refs[4:8], refs[8:]
+    part = keep_ref.shape[1]
+    total = jnp.zeros((hidden[0].shape[0], 2 * part), F32)
+    for m in range(4):
+        total = total + dot(hidden[m][...], down[m][...])
+    first = where_ref[1] == 0
+    keep_ref[...] = jnp.where(first, total[:, :part], total[:, part:])
+    send_ref[...] = jnp.where(first, total[:, part:], total[:, :part]).astype(BF)
+
+
+def repack_body(one_ref, two_ref, out_ref):
+    rows, part = out_ref.shape[0], one_ref.shape[1]
     experts = rows // ROWS
-    total = jnp.zeros((hidden[0].shape[0], part), F32)
-    for k in range(8):
-        total = total + dot(hidden[k][...], down[k][...])
-    total = total.astype(BF)
+    total = (one_ref[...] + two_ref[...].astype(F32)).astype(BF)
     out_ref[:, :part] = total[:rows]
     repeat = (iota((rows, experts), 0) // ROWS == iota((rows, experts), 1)).astype(BF)
-    last = dot(repeat, total[rows:])
-    row = iota((rows, HALF), 0) % ROWS
-    tail = jnp.zeros((rows, HALF), F32)
-    for i in range(part // HALF):
-        tail = tail + jnp.where(row == i, last[:, i * HALF : (i + 1) * HALF], 0.0)
-    out_ref[:, part:] = tail.astype(BF)
-
-
-def slices_body(info, down_ref, *outs):
-    me = info[0]
-    part = outs[0].shape[1]
-    for k in range(8):
-        other = me ^ k
-        columns = down_ref[:, pl.ds(pl.multiple_of((other // 2) * 2 * part, 128), 2 * part)]
-        outs[k][...] = jnp.where(other % 2 == 0, columns[:, :part], columns[:, part:])
+    out_ref[:, part:] = ninth_columns(dot(repeat, total[rows:]), part)
 
 
 def combine_body(gates_ref, rows_ref, out_ref):
@@ -237,19 +265,12 @@
     return lax.ppermute(value, LINE, [(d, d ^ k) for d in range(8)])
 
 
-def gather_line(own):
-    middle = own.shape[0] // 2 // 16 * 16
-    pieces = [own] + [None] * 7
-    pieces[4] = swap(own, 4)
-    pieces[6] = swap(own, 6)
-    pieces[1] = swap(own, 1)
-    first = swap(pieces[4][:middle], 6)
-    second = swap(pieces[6][middle:], 4)
-    pieces[5] = swap(pieces[4], 1)
-    pieces[7] = swap(pieces[6], 1)
-    pieces[2] = jnp.concatenate([first, second], axis=0)
-    pieces[3] = jnp.concatenate([swap(first, 1), swap(second, 1)], axis=0)
-    return pieces
+def gather_rows(own):
+    middle = own.shape[0] // 2
+    one, three = swap(own, 2 * 2), swap(own, 3 * 2)
+    first = swap(one[:middle], 3 * 2)
+    second = swap(three[middle:], 2 * 2)
+    return one, three, first, second
 
 
 def local(
@@ -264,28 +285,56 @@
     up_proj,
     down_proj,
 ):
-    section = lax.axis_index("sec")
     me = lax.axis_index(LINE)
     experts = lax.axis_size("grp")
     rows = experts * ROWS
     steps, tokens, width = token_rows.shape
     part = width // 8
     units = gate_proj.shape[2]
-    here = me.astype(jnp.int32).reshape(1)
-
-    packed = call(
-        pack_body, jax.ShapeDtypeStruct((rows, part + HALF), BF), [SMEM, VMEM, VMEM],
-        10**8, 10**6, "pack",
-    )(jnp.stack([me // 2, me % 2]).astype(jnp.int32), token_rows, routes)
+    where = jnp.stack([me // 2, me % 2]).astype(jnp.int32)
+
+    packed = pl.pallas_call(
+        pack_body,
+        out_shape=jax.ShapeDtypeStruct((rows, part + HALF), BF),
+        in_specs=[SMEM, ANY, ANY],
+        out_specs=VMEM,
+        scratch_shapes=[
+            pltpu.VMEM((steps, tokens, 2 * part), BF),
+            pltpu.VMEM(routes.shape, jnp.int32),
+            pltpu.SemaphoreType.DMA((2,)),
+        ],
+        cost_estimate=pl.CostEstimate(flops=10**8, bytes_accessed=10**6, transcendentals=0),
+        name="pack",
+    )(where, token_rows, routes)
+    packed, later = lax.optimization_barrier((packed, where))
     arrived = lax.all_to_all(
         packed.reshape(experts, ROWS, part + HALF), "grp", split_axis=0, concat_axis=0, tiled=True
     ).reshape(rows, part + HALF)
 
-    down = call(
-        slices_body, [jax.ShapeDtypeStruct((units, part), BF)] * 8, [SMEM, VMEM],
-        10**6, 2 * 10**6, "slices",
-    )(here, down_proj.reshape(units, width))
-    down = [down[0]] + [swap(down[k], k) for k in range(1, 8)]
+    gate_proj, up_proj = gate_proj.reshape(width, units), up_proj.reshape(width, units)
+    other, *down = call(
+        slices_body,
+        [jax.ShapeDtypeStruct((width // 2, 2 * units), BF)]
+        + [jax.ShapeDtypeStruct((units, 2 * part), BF)] * 4,
+        [SMEM] + [VMEM] * 3, 10**6, 5 * 10**6, "slices",
+    )(later, gate_proj, up_proj, down_proj.reshape(units, width))
+    other = swap(other, 1)
+    down = [down[0]] + [swap(down[m], 2 * m) for m in range(1, 4)]
+
+    heads = queries.shape[2]
+    send, keep = call(
+        attend_body, [jax.ShapeDtypeStruct((steps * heads, KL // 2 + 256), F32)] * 2,
+        [SMEM, VMEM, VMEM, VMEM], 3 * 10**8, 2 * 10**6, "attend",
+    )(
+        jnp.stack([later[0] // 2, lengths[0]]),
+        queries.reshape(steps * heads, queries.shape[3]),
+        latent_cache.reshape(latent_cache.shape[1:]),
+        new_latent.reshape(steps, new_latent.shape[2]),
+    )
+    attention = call(
+        merge_body, jax.ShapeDtypeStruct((steps * heads, KL // 2), BF), [VMEM, VMEM],
+        10**6, 10**6, "merge",
+    )(keep, swap(send, 4))
 
     gates = call(
         gates_body,
@@ -293,32 +342,32 @@
         [VMEM, VMEM], 10**8, 10**6, "gates",
     )(routes, route_gates)
 
-    heads = queries.shape[2]
-    send, keep = call(
-        attend_body, [jax.ShapeDtypeStruct((steps * heads, KL // 2 + 256), F32)] * 2,
-        [SMEM, VMEM, VMEM, VMEM], 3 * 10**8, 2 * 10**6, "attend",
-    )(
-        jnp.stack([section.astype(jnp.int32), lengths[0]]),
-        queries.reshape(steps * heads, queries.shape[3]),
-        latent_cache.reshape(latent_cache.shape[1:]),
-        new_latent.reshape(steps, new_latent.shape[2]),
-    )
-    other = swap(send, 4)
-    attention = call(
-        merge_body, jax.ShapeDtypeStruct((steps * heads, KL // 2), BF), [VMEM, VMEM],
-        10**6, 10**6, "merge",
-    )(keep, other)
-
-    pieces = gather_line(arrived)
+    arrived, other, down, attention, gates = lax.optimization_barrier(
+        (arrived, other, down, attention, gates)
+    )
+    one, three, first, second = gather_rows(arrived)
+    two = jnp.concatenate([first, second], axis=0)
+    keep, send = call(
+        partial_body, [jax.ShapeDtypeStruct((rows + experts, 2 * units), F32)] * 2,
+        [SMEM] + [VMEM] * 7, 10**9, 6 * 10**6, "partial",
+    )(where, arrived, two, one, three, gate_proj, up_proj, other)
     hidden = call(
-        hidden_body, jax.ShapeDtypeStruct((rows + experts, units), BF), [SMEM] + [VMEM] * 10,
-        10**9, 6 * 10**6, "hidden",
-    )(here, *pieces, gate_proj.reshape(width, units), up_proj.reshape(width, units))
-    hidden = gather_line(hidden)
+        hidden_body, jax.ShapeDtypeStruct((rows + experts, units), BF), [VMEM] * 2,
+        10**7, 10**6, "hidden",
+    )(keep, swap(send, 1))
+    hidden = [hidden] + [swap(hidden, 2 * m) for m in range(1, 4)]
+    keep, send = call(
+        down_body,
+        [
+            jax.ShapeDtypeStruct((rows + experts, part), F32),
+            jax.ShapeDtypeStruct((rows + experts, part), BF),
+        ],
+        [SMEM] + [VMEM] * 8, 10**9, 3 * 10**6, "down",
+    )(where, *hidden, *down)
     outgoing = call(
-        down_body, jax.ShapeDtypeStruct((rows, part + HALF), BF), [VMEM] * 16,
-        10**9, 3 * 10**6, "down",
-    )(*hidden, *down)
+        repack_body, jax.ShapeDtypeStruct((rows, part + HALF), BF), [VMEM] * 2,
+        10**8, 2 * 10**6, "repack",
+    )(keep, swap(send, 1))
     returned = lax.all_to_all(
         outgoing.reshape(experts, ROWS, part + HALF), "grp", split_axis=0, concat_axis=0, tiled=True
     ).reshape(rows, part + HALF)

time: 157 us -> 147 us (0.936)
  starting transfers between devices: 72.9 us -> 56.4 us
  Pallas kernels: 11.3 us -> 17.6 us
  blocking collectives: 36.1 us -> 32.2 us
  local copies, waits for them, and re-layouts: 2.68 us -> 5.82 us
    ppermute x26 -> x14, starting transfers between devices: 67.6 us -> 39.5 us  [swap(): return lax.ppermute(value, LINE, [(d, d ^ k) for d in range(8)])]
    all_to_all x1, starting transfers between devices: 5.23 us -> 16.9 us  [local(): lax.all_to_all(packed.reshape(experts, ROWS, part + HALF), 'grp', split_a...]
    ppermute x26 -> x14, waiting for transfers between devices: 22.7 us -> 30.3 us  [swap(): return lax.ppermute(value, LINE, [(d, d ^ k) for d in range(8)])]
    all_to_all x1, waiting for transfers between devices: 7.42 us -> 0.01 us  [local(): lax.all_to_all(packed.reshape(experts, ROWS, part + HALF), 'grp', split_a...]
    pallas_call x4 -> x6, Pallas kernels: 7.28 us -> 12.8 us  [the longest x1 3.89 us: local(): pl.pallas_call(pack_body, out_shape=jax.ShapeDtypeStruct((rows, part + HA...]
    all_to_all x1, blocking collectives: 36.1 us -> 32.2 us  [local(): lax.all_to_all(outgoing.reshape(experts, ROWS, part + HALF), 'grp', split...]
    unnamed x19 -> x23, local copies, waits for them, and re-layouts: 2.63 us -> 5.25 us
  transfers between devices with their start and end apart: 27 -> 15, of which waited for: 7 -> 8; matrix products, arithmetic and copies ran while one was open for 1% -> 1% of each run, Pallas kernels for 2% -> 4%
where the time goes in v2:
time: 147 us; the launch traced here: 145 us
  starting transfers between devices  56.4 us (38%)
  blocking collectives  32.2 us (22%)
  waiting for transfers between devices  30.3 us (21%)
  Pallas kernels  17.6 us (12%)
  local copies, waits for them, and re-layouts  5.82 us (4%)
  between operations  1.77 us (1%)
    ppermute x14, starting transfers between devices, swap(): return lax.ppermute(value, LINE, [(d, d ^ k) for d in range(8)])  39.5 us
    all_to_all x1, blocking collectives, local(): lax.all_to_all(outgoing.reshape(experts, ROWS, part + HALF), 'grp', split...  32.2 us
    ppermute x14, waiting for transfers between devices, swap(): return lax.ppermute(value, LINE, [(d, d ^ k) for d in range(8)])  30.3 us
    all_to_all x1, starting transfers between devices, local(): lax.all_to_all(packed.reshape(experts, ROWS, part + HALF), 'grp', split_a...  16.9 us
    unnamed x23, local copies, waits for them, and re-layouts  5.25 us
    pallas_call x1, Pallas kernels, local(): pl.pallas_call(pack_body, out_shape=jax.ShapeDtypeStruct((rows, part + HA...  3.89 us
    pallas_call x1, Pallas kernels, local(): call(partial_body, [jax.ShapeDtypeStruct((rows + experts, 2 * units), F32...  3.47 us
  transfers between devices with their start and end apart: 15, of which 8 were waited for; matrix products, arithmetic and copies ran while one was open for 1% of the time, Pallas kernels for 4%

profile of v2, /device:TPU:6, one launch (start us, length us, event | category | flops | bytes accessed | tf_op | source)
XLA Modules:
  0.0 144.9 jit_solution(18263499774607250682)
XLA Ops:
  2.8 3.9 %pack.1 = bf16[512,512]{1,0:T(8,128)(2,1)} custom-call(s32[2]{0:T(128)} %pad_add_fusion.where_ref, bf16[3,12,3584]{2,1,0:T(8,128)(2,1)} %tokens_ref.1, s32[3,12,8]{2,1,0:T(8,128)} %copy.17.routes_ref), custom_call_target="tpu_custom_call" | custom-call | flops 100000000 | bytes 1000000 | tf_op jit(solution)/shard_map/pack/pallas_call | solution.py:296
  6.7 16.9 %all-to-all-start = ((bf16[64,8,512]{2,1,0:T(8,128)(2,1)}), bf16[64,8,512]{2,1,0:T(8,128)(2,1)}, u32[]{:S(2)}, u32[]{:S(2)}) async-start(bf16[64,8,512]{2,1,0:T(8,128)(2,1)} %bitcast.32), calls=%async_computation | async-start | bytes 1048576 | tf_op jit(solution)/shard_map/all_to_all | solution.py:310
  24.8 2.0 %slices.1 = (bf16[1792,256]{1,0:T(8,128)(2,1)}, bf16[128,896]{1,0:T(8,128)(2,1)S(1)}, bf16[128,896]{1,0:T(8,128)(2,1)}, bf16[128,896]{1,0:T(8,128)(2,1)}, bf16[128,896]{1,0:T(8,128)(2,1)}) custom-call(s32[2]{0:T(128)S(1)} %copy-done.5, bf16[3584,128]{1,0:T(8,128)(2,1)S(1)} %bitcast.19, bf16[3584,128]{1,0:T(8,128)(2,1)S(1)} %bitcast.21, ...), custom_call_target="tpu_custom_call" | custom-call | flops 1000000 | bytes 5000000 | tf_op jit(solution)/shard_map/slices/pallas_call | solution.py:315
  29.4 3.3 %collective-permute-start.1 = (bf16[128,896]{1,0:T(8,128)(2,1)}, bf16[128,896]{1,0:T(8,128)(2,1)}, u32[]{:S(2)}, u32[]{:S(2)}) collective-permute-start(bf16[128,896]{1,0:T(8,128)(2,1)} %get-tuple-element.27), channel_id=1, source_target_pairs={{0,2},{1,3},{2,0},{3,1},{256,258},{257,259},{258,256},{259,257},{4... | collective-permute-start | bytes 688136 | tf_op jit(solution)/shard_map/ppermute | solution.py:265
  32.7 1.9 %collective-permute-start.2 = (bf16[128,896]{1,0:T(8,128)(2,1)}, bf16[128,896]{1,0:T(8,128)(2,1)}, u32[]{:S(2)}, u32[]{:S(2)}) collective-permute-start(bf16[128,896]{1,0:T(8,128)(2,1)} %get-tuple-element.28), channel_id=1, source_target_pairs={{0,256},{1,257},{2,258},{3,259},{256,0},{257,1},{258,2},{259,3},{4... | collective-permute-start | bytes 688136 | tf_op jit(solution)/shard_map/ppermute | solution.py:265
  34.6 4.6 %collective-permute-start.3 = (bf16[128,896]{1,0:T(8,128)(2,1)}, bf16[128,896]{1,0:T(8,128)(2,1)}, u32[]{:S(2)}, u32[]{:S(2)}) collective-permute-start(bf16[128,896]{1,0:T(8,128)(2,1)} %get-tuple-element.29), channel_id=1, source_target_pairs={{0,258},{1,259},{2,256},{3,257},{256,2},{257,3},{258,0},{259,1},{4... | collective-permute-start | bytes 688136 | tf_op jit(solution)/shard_map/ppermute | solution.py:265
  41.9 2.3 %attend.1 = (f32[96,512]{1,0:T(8,128)}, f32[96,512]{1,0:T(8,128)S(1)}) custom-call(s32[2]{0:T(128)S(1)} %pad_add_fusion.1.info, bf16[96,576]{1,0:T(8,128)(2,1)S(1)} %bitcast.26, bf16[1024,576]{1,0:T(8,128)(2,1)S(1)} %bitcast.18, bf16[3,576]{1,0:T(4,128)(2,1)S(1)} %bitcast.31), custom_call_target="tpu_custom_call" | custom-call | flops 300000000 | bytes 2000000 | tf_op jit(solution)/shard_map/attend/pallas_call | solution.py:325
  44.2 2.7 %collective-permute-start.4 = (f32[96,512]{1,0:T(8,128)}, f32[96,512]{1,0:T(8,128)S(1)}, u32[]{:S(2)}, u32[]{:S(2)}) collective-permute-start(f32[96,512]{1,0:T(8,128)} %get-tuple-element.31), channel_id=1, source_target_pairs={{0,256},{1,257},{2,258},{3,259},{256,0},{257,1},{258,2},{259,3},{4... | collective-permute-start | bytes 589832 | tf_op jit(solution)/shard_map/ppermute | solution.py:265
  47.7 5.0 %collective-permute-done.4.two_ref = f32[96,512]{1,0:T(8,128)S(1)} collective-permute-done((f32[96,512]{1,0:T(8,128)}, f32[96,512]{1,0:T(8,128)S(1)}, u32[]{:S(2)}, u32[]{:S(2)}) %collective-permute-start.4) | collective-permute-done | bytes 196640 | tf_op jit(solution)/shard_map/ppermute | solution.py:265
  53.5 2.7 %collective-permute-start.7 = (bf16[512,512]{1,0:T(8,128)(2,1)}, bf16[512,512]{1,0:T(8,128)(2,1)S(1)}, u32[]{:S(2)}, u32[]{:S(2)}) collective-permute-start(bf16[512,512]{1,0:T(8,128)(2,1)} %bitcast.3.refs_0_), channel_id=1, source_target_pairs={{0,258},{1,259},{2,256},{3,257},{256,2},{257,3},{258,0},{259,1},{4... | collective-permute-start | bytes 1572872 | tf_op jit(solution)/shard_map/ppermute | solution.py:265
  56.3 2.4 %collective-permute-start.5 = (bf16[512,512]{1,0:T(8,128)(2,1)}, bf16[512,512]{1,0:T(8,128)(2,1)S(1)}, u32[]{:S(2)}, u32[]{:S(2)}) collective-permute-start(bf16[512,512]{1,0:T(8,128)(2,1)} %bitcast.3.refs_0_), channel_id=1, source_target_pairs={{0,256},{1,257},{2,258},{3,259},{256,0},{257,1},{258,2},{259,3},{4... | collective-permute-start | bytes 1572872 | tf_op jit(solution)/shard_map/ppermute | solution.py:265
  58.7 10.7 %collective-permute-done.7.refs_3_ = bf16[512,512]{1,0:T(8,128)(2,1)S(1)} collective-permute-done((bf16[512,512]{1,0:T(8,128)(2,1)}, bf16[512,512]{1,0:T(8,128)(2,1)S(1)}, u32[]{:S(2)}, u32[]{:S(2)}) %collective-permute-start.7) | collective-permute-done | bytes 524320 | tf_op jit(solution)/shard_map/ppermute | solution.py:265
  71.4 3.6 %collective-permute-start.6 = (bf16[256,512]{1,0:T(8,128)(2,1)S(1)}, bf16[256,512]{1,0:T(8,128)(2,1)S(1)}, u32[]{:S(2)}, u32[]{:S(2)}) collective-permute-start(bf16[256,512]{1,0:T(8,128)(2,1)S(1)} %slice.12), channel_id=1, source_target_pairs={{0,258},{1,259},{2,256},{3,257},{256,2},{257,3},{258,0},{259,1},{4... | collective-permute-start | bytes 786440 | tf_op jit(solution)/shard_map/ppermute | solution.py:265
  75.0 2.7 %collective-permute-done.8 = bf16[256,512]{1,0:T(8,128)(2,1)S(1)} collective-permute-done((bf16[256,512]{1,0:T(8,128)(2,1)S(1)}, bf16[256,512]{1,0:T(8,128)(2,1)S(1)}, u32[]{:S(2)}, u32[]{:S(2)}) %collective-permute-start.8) | collective-permute-done | bytes 262176 | tf_op jit(solution)/shard_map/ppermute | solution.py:265
  77.7 3.2 %collective-permute-done.6 = bf16[256,512]{1,0:T(8,128)(2,1)S(1)} collective-permute-done((bf16[256,512]{1,0:T(8,128)(2,1)S(1)}, bf16[256,512]{1,0:T(8,128)(2,1)S(1)}, u32[]{:S(2)}, u32[]{:S(2)}) %collective-permute-start.6) | collective-permute-done | bytes 262176 | tf_op jit(solution)/shard_map/ppermute | solution.py:265
  80.9 3.5 %partial.1 = (f32[576,256]{1,0:T(8,128)S(1)}, f32[576,256]{1,0:T(8,128)S(1)}) custom-call(s32[2]{0:T(128)S(1)} %copy-done.5, bf16[512,512]{1,0:T(8,128)(2,1)} %bitcast.3.refs_0_, bf16[512,512]{1,0:T(8,128)(2,1)S(1)} %pad_maximum_fusion.refs_1_, bf16[512,512]{1,0:T(8,128)(2,1)S(1)} %collective-permute-done.5.refs_2_, ...), custom_call_target="tpu_custom_call" | custom-call | flops 1000000000 | bytes 6000000 | tf_op jit(solution)/shard_map/partial/pallas_call | solution.py:350
  84.4 2.1 %collective-permute-start.9 = (f32[576,256]{1,0:T(8,128)S(1)}, f32[576,256]{1,0:T(8,128)S(1)}, u32[]{:S(2)}, u32[]{:S(2)}) collective-permute-start(f32[576,256]{1,0:T(8,128)S(1)} %get-tuple-element.37), channel_id=1, source_target_pairs={{0,1},{1,0},{2,3},{3,2},{256,257},{257,256},{258,259},{259,258},{4... | collective-permute-start | bytes 1769480 | tf_op jit(solution)/shard_map/ppermute | solution.py:265
  86.5 2.0 %collective-permute-done.9.two_ref = f32[576,256]{1,0:T(8,128)S(1)} collective-permute-done((f32[576,256]{1,0:T(8,128)S(1)}, f32[576,256]{1,0:T(8,128)S(1)}, u32[]{:S(2)}, u32[]{:S(2)}) %collective-permute-start.9) | collective-permute-done | bytes 589856 | tf_op jit(solution)/shard_map/ppermute | solution.py:265
  88.6 3.6 %collective-permute-start.12 = (bf16[576,128]{1,0:T(8,128)(2,1)S(1)}, bf16[576,128]{1,0:T(8,128)(2,1)S(1)}, u32[]{:S(2)}, u32[]{:S(2)}) collective-permute-start(bf16[576,128]{1,0:T(8,128)(2,1)S(1)} %hidden.1.refs_0_), channel_id=1, source_target_pairs={{0,258},{1,259},{2,256},{3,257},{256,2},{257,3},{258,0},{259,1},{4... | collective-permute-start | bytes 442376 | tf_op jit(solution)/shard_map/ppermute | solution.py:265
  94.1 4.9 %collective-permute-start.10 = (bf16[576,128]{1,0:T(8,128)(2,1)S(1)}, bf16[576,128]{1,0:T(8,128)(2,1)S(1)}, u32[]{:S(2)}, u32[]{:S(2)}) collective-permute-start(bf16[576,128]{1,0:T(8,128)(2,1)S(1)} %hidden.1.refs_0_), channel_id=1, source_target_pairs={{0,2},{1,3},{2,0},{3,1},{256,258},{257,259},{258,256},{259,257},{4... | collective-permute-start | bytes 442376 | tf_op jit(solution)/shard_map/ppermute | solution.py:265
  100.5 3.3 %collective-permute-done.10.refs_1_ = bf16[576,128]{1,0:T(8,128)(2,1)S(1)} collective-permute-done((bf16[576,128]{1,0:T(8,128)(2,1)S(1)}, bf16[576,128]{1,0:T(8,128)(2,1)S(1)}, u32[]{:S(2)}, u32[]{:S(2)}) %collective-permute-start.10) | collective-permute-done | bytes 147488 | tf_op jit(solution)/shard_map/ppermute | solution.py:265
  103.8 2.8 %down.1 = (f32[576,448]{1,0:T(8,128)S(1)}, bf16[576,448]{1,0:T(8,128)(2,1)S(1)}) custom-call(s32[2]{0:T(128)S(1)} %copy-done.5, bf16[576,128]{1,0:T(8,128)(2,1)S(1)} %hidden.1.refs_0_, bf16[576,128]{1,0:T(8,128)(2,1)S(1)} %collective-permute-done.10.refs_1_, bf16[576,128]{1,0:T(8,128)(2,1)S(1)} %collective-permute-done.11.refs_2_, ...), custom_call_target="tpu_custom_call" | custom-call | flops 1000000000 | bytes 3000000 | tf_op jit(solution)/shard_map/down/pallas_call | solution.py:359
  108.9 1.9 %collective-permute-done.13 = bf16[576,448]{0,1:T(8,128)(2,1)S(1)} collective-permute-done((bf16[576,448]{0,1:T(8,128)(2,1)S(1)}, bf16[576,448]{0,1:T(8,128)(2,1)S(1)}, u32[]{:S(2)}, u32[]{:S(2)}) %collective-permute-start.13) | collective-permute-done | bytes 516128 | tf_op jit(solution)/shard_map/ppermute | solution.py:265
  111.6 32.2 %all_to_all.10 = bf16[64,8,512]{2,1,0:T(8,128)(2,1)S(1)} all-to-all(bf16[64,8,512]{2,1,0:T(8,128)(2,1)S(1)} %bitcast.24), channel_id=1, replica_groups=mesh['sec'=2,'grp'=64,'tp'=4] {'grp'}, dimensions={0} | all-to-all | bytes 1048576 | tf_op jit(solution)/shard_map/all_to_all | solution.py:371
  (47 shorter events, 18.9 us)
Async XLA Ops:
  0.6 23.0 %copy-start.1 = (bf16[1,3584,128]{2,1,0:T(8,128)(2,1)S(1)}, bf16[1,3584,128]{2,1,0:T(8,128)(2,1)}, u32[]{:S(2)}) copy-start(bf16[1,3584,128]{2,1,0:T(8,128)(2,1)} %param.18) | copy-start | bytes 2752516
  0.6 23.0 %copy-start = (bf16[1,3584,128]{2,1,0:T(8,128)(2,1)S(1)}, bf16[1,3584,128]{2,1,0:T(8,128)(2,1)}, u32[]{:S(2)}) copy-start(bf16[1,3584,128]{2,1,0:T(8,128)(2,1)} %param.17) | copy-start | bytes 2752516
  2.8 20.8 %copy-start.5 = (s32[2]{0:T(128)S(1)}, s32[2]{0:T(128)}, u32[]{:S(2)}) copy-start(s32[2]{0:T(128)} %pad_add_fusion.where_ref) | copy-start | bytes 28
  6.7 46.8 %all-to-all-start = ((bf16[64,8,512]{2,1,0:T(8,128)(2,1)}), bf16[64,8,512]{2,1,0:T(8,128)(2,1)}, u32[]{:S(2)}, u32[]{:S(2)}) async-start(bf16[64,8,512]{2,1,0:T(8,128)(2,1)} %bitcast.32), calls=%async_computation | async-start | bytes 1048576 | tf_op jit(solution)/shard_map/all_to_all | solution.py:310
  23.6 1.2 copy-start.2
  27.5 26.1 %collective-permute-start = (bf16[1792,256]{1,0:T(8,128)(2,1)}, bf16[1792,256]{1,0:T(8,128)(2,1)}, u32[]{:S(2)}, u32[]{:S(2)}) collective-permute-start(bf16[1792,256]{1,0:T(8,128)(2,1)} %get-tuple-element.25), channel_id=1, source_target_pairs={{0,1},{1,0},{2,3},{3,2},{256,257},{257,256},{258,259},{259,258},{4... | collective-permute-start | bytes 2752520 | tf_op jit(solution)/shard_map/ppermute | solution.py:265
  29.4 24.1 %collective-permute-start.1 = (bf16[128,896]{1,0:T(8,128)(2,1)}, bf16[128,896]{1,0:T(8,128)(2,1)}, u32[]{:S(2)}, u32[]{:S(2)}) collective-permute-start(bf16[128,896]{1,0:T(8,128)(2,1)} %get-tuple-element.27), channel_id=1, source_target_pairs={{0,2},{1,3},{2,0},{3,1},{256,258},{257,259},{258,256},{259,257},{4... | collective-permute-start | bytes 688136 | tf_op jit(solution)/shard_map/ppermute | solution.py:265
  32.7 20.8 %collective-permute-start.2 = (bf16[128,896]{1,0:T(8,128)(2,1)}, bf16[128,896]{1,0:T(8,128)(2,1)}, u32[]{:S(2)}, u32[]{:S(2)}) collective-permute-start(bf16[128,896]{1,0:T(8,128)(2,1)} %get-tuple-element.28), channel_id=1, source_target_pairs={{0,256},{1,257},{2,258},{3,259},{256,0},{257,1},{258,2},{259,3},{4... | collective-permute-start | bytes 688136 | tf_op jit(solution)/shard_map/ppermute | solution.py:265
  34.6 18.9 %collective-permute-start.3 = (bf16[128,896]{1,0:T(8,128)(2,1)}, bf16[128,896]{1,0:T(8,128)(2,1)}, u32[]{:S(2)}, u32[]{:S(2)}) collective-permute-start(bf16[128,896]{1,0:T(8,128)(2,1)} %get-tuple-element.29), channel_id=1, source_target_pairs={{0,258},{1,259},{2,256},{3,257},{256,2},{257,3},{258,0},{259,1},{4... | collective-permute-start | bytes 688136 | tf_op jit(solution)/shard_map/ppermute | solution.py:265
  40.1 1.8 %copy-start.4 = (bf16[3,1,32,576]{3,2,1,0:T(8,128)(2,1)S(1)}, bf16[3,1,32,576]{3,2,1,0:T(8,128)(2,1)}, u32[]{:S(2)}) copy-start(bf16[3,1,32,576]{3,2,1,0:T(8,128)(2,1)} %param.12) | copy-start | bytes 331780
  40.1 1.8 %copy-start.6 = (bf16[3,1,576]{2,0,1:T(4,128)(2,1)S(1)}, bf16[3,1,576]{2,0,1:T(4,128)(2,1)}, u32[]{:S(2)}) copy-start(bf16[3,1,576]{2,0,1:T(4,128)(2,1)} %param.11) | copy-start | bytes 10372
  41.8 5.1 %copy-start.9 = (f32[3,12,8]{1,2,0:T(8,128)S(1)}, f32[3,12,8]{1,2,0:T(8,128)}, u32[]{:S(2)}) copy-start(f32[3,12,8]{1,2,0:T(8,128)} %param.16) | copy-start | bytes 3460
  41.8 5.2 %copy-start.3 = (s32[3,12,8]{2,1,0:T(8,128)S(1)}, s32[3,12,8]{2,1,0:T(8,128)}, u32[]{:S(2)}) copy-start(s32[3,12,8]{2,1,0:T(8,128)} %copy.17.routes_ref) | copy-start | bytes 3460
  44.2 8.6 %collective-permute-start.4 = (f32[96,512]{1,0:T(8,128)}, f32[96,512]{1,0:T(8,128)S(1)}, u32[]{:S(2)}, u32[]{:S(2)}) collective-permute-start(f32[96,512]{1,0:T(8,128)} %get-tuple-element.31), channel_id=1, source_target_pairs={{0,256},{1,257},{2,258},{3,259},{256,0},{257,1},{258,2},{259,3},{4... | collective-permute-start | bytes 589832 | tf_op jit(solution)/shard_map/ppermute | solution.py:265
  53.5 15.9 %collective-permute-start.7 = (bf16[512,512]{1,0:T(8,128)(2,1)}, bf16[512,512]{1,0:T(8,128)(2,1)S(1)}, u32[]{:S(2)}, u32[]{:S(2)}) collective-permute-start(bf16[512,512]{1,0:T(8,128)(2,1)} %bitcast.3.refs_0_), channel_id=1, source_target_pairs={{0,258},{1,259},{2,256},{3,257},{256,2},{257,3},{258,0},{259,1},{4... | collective-permute-start | bytes 1572872 | tf_op jit(solution)/shard_map/ppermute | solution.py:265
  56.3 15.1 %collective-permute-start.5 = (bf16[512,512]{1,0:T(8,128)(2,1)}, bf16[512,512]{1,0:T(8,128)(2,1)S(1)}, u32[]{:S(2)}, u32[]{:S(2)}) collective-permute-start(bf16[512,512]{1,0:T(8,128)(2,1)} %bitcast.3.refs_0_), channel_id=1, source_target_pairs={{0,256},{1,257},{2,258},{3,259},{256,0},{257,1},{258,2},{259,3},{4... | collective-permute-start | bytes 1572872 | tf_op jit(solution)/shard_map/ppermute | solution.py:265
  69.5 8.3 %collective-permute-start.8 = (bf16[256,512]{1,0:T(8,128)(2,1)S(1)}, bf16[256,512]{1,0:T(8,128)(2,1)S(1)}, u32[]{:S(2)}, u32[]{:S(2)}) collective-permute-start(bf16[256,512]{1,0:T(8,128)(2,1)S(1)} %slice.13), channel_id=1, source_target_pairs={{0,256},{1,257},{2,258},{3,259},{256,0},{257,1},{258,2},{259,3},{4... | collective-permute-start | bytes 786440 | tf_op jit(solution)/shard_map/ppermute | solution.py:265
  71.4 9.5 %collective-permute-start.6 = (bf16[256,512]{1,0:T(8,128)(2,1)S(1)}, bf16[256,512]{1,0:T(8,128)(2,1)S(1)}, u32[]{:S(2)}, u32[]{:S(2)}) collective-permute-start(bf16[256,512]{1,0:T(8,128)(2,1)S(1)} %slice.12), channel_id=1, source_target_pairs={{0,258},{1,259},{2,256},{3,257},{256,2},{257,3},{258,0},{259,1},{4... | collective-permute-start | bytes 786440 | tf_op jit(solution)/shard_map/ppermute | solution.py:265
  84.4 19.4 %copy-start.8 = (bf16[128,896]{1,0:T(8,128)(2,1)S(1)}, bf16[128,896]{1,0:T(8,128)(2,1)}, u32[]{:S(2)}) copy-start(bf16[128,896]{1,0:T(8,128)(2,1)} %copy-done.7) | copy-start | bytes 688132
  84.4 4.0 %collective-permute-start.9 = (f32[576,256]{1,0:T(8,128)S(1)}, f32[576,256]{1,0:T(8,128)S(1)}, u32[]{:S(2)}, u32[]{:S(2)}) collective-permute-start(f32[576,256]{1,0:T(8,128)S(1)} %get-tuple-element.37), channel_id=1, source_target_pairs={{0,1},{1,0},{2,3},{3,2},{256,257},{257,256},{258,259},{259,258},{4... | collective-permute-start | bytes 1769480 | tf_op jit(solution)/shard_map/ppermute | solution.py:265
  88.6 10.4 %collective-permute-start.12 = (bf16[576,128]{1,0:T(8,128)(2,1)S(1)}, bf16[576,128]{1,0:T(8,128)(2,1)S(1)}, u32[]{:S(2)}, u32[]{:S(2)}) collective-permute-start(bf16[576,128]{1,0:T(8,128)(2,1)S(1)} %hidden.1.refs_0_), channel_id=1, source_target_pairs={{0,258},{1,259},{2,256},{3,257},{256,2},{257,3},{258,0},{259,1},{4... | collective-permute-start | bytes 442376 | tf_op jit(solution)/shard_map/ppermute | solution.py:265
  92.2 8.3 %collective-permute-start.11 = (bf16[576,128]{1,0:T(8,128)(2,1)S(1)}, bf16[576,128]{1,0:T(8,128)(2,1)S(1)}, u32[]{:S(2)}, u32[]{:S(2)}) collective-permute-start(bf16[576,128]{1,0:T(8,128)(2,1)S(1)} %hidden.1.refs_0_), channel_id=1, source_target_pairs={{0,256},{1,257},{2,258},{3,259},{256,0},{257,1},{258,2},{259,3},{4... | collective-permute-start | bytes 442376 | tf_op jit(solution)/shard_map/ppermute | solution.py:265
  94.1 9.7 %collective-permute-start.10 = (bf16[576,128]{1,0:T(8,128)(2,1)S(1)}, bf16[576,128]{1,0:T(8,128)(2,1)S(1)}, u32[]{:S(2)}, u32[]{:S(2)}) collective-permute-start(bf16[576,128]{1,0:T(8,128)(2,1)S(1)} %hidden.1.refs_0_), channel_id=1, source_target_pairs={{0,2},{1,3},{2,0},{3,1},{256,258},{257,259},{258,256},{259,257},{4... | collective-permute-start | bytes 442376 | tf_op jit(solution)/shard_map/ppermute | solution.py:265
  107.0 3.9 %collective-permute-start.13 = (bf16[576,448]{0,1:T(8,128)(2,1)S(1)}, bf16[576,448]{0,1:T(8,128)(2,1)S(1)}, u32[]{:S(2)}, u32[]{:S(2)}) collective-permute-start(bf16[576,448]{0,1:T(8,128)(2,1)S(1)} %copy.21), channel_id=1, source_target_pairs={{0,1},{1,0},{2,3},{3,2},{256,257},{257,256},{258,259},{259,258},{4... | collective-permute-start | bytes 1548296 | tf_op jit(solution)/shard_map/ppermute | solution.py:265
  (1 other events, 0.7 us)

commit v3 on v2

--- a/solution.py
+++ b/solution.py
@@ -45,10 +45,10 @@
 def attend_body(info, q_ref, cache_ref, new_ref, send_ref, keep_ref):
     section, length = info[0], info[1]
     q = q_ref[...]
-    rows, local_length = q.shape[0], cache_ref.shape[0]
+    rows, local_length = q.shape[0], cache_ref.shape[1]
     steps = new_ref.shape[0]
     heads = rows // steps
-    scores = dot(q, cache_ref[...], ((1,), (1,))) * score_scale
+    scores = dot(q, cache_ref[...]) * score_scale
     usable = iota((rows, local_length), 1) + section * local_length < length
     scores = jnp.where(usable, scores, neg_big)
     top = jnp.max(scores, axis=1, keepdims=True)
@@ -61,7 +61,7 @@
     weights = jnp.where(usable, jnp.exp(scores - top), 0.0)
     new_weights = jnp.where(causal, jnp.exp(fresh - top), 0.0)
     total = jnp.sum(weights, axis=1, keepdims=True) + jnp.sum(new_weights, axis=1, keepdims=True)
-    out = dot(weights.astype(BF), cache_ref[:, :KL])
+    out = dot(weights.astype(BF), cache_ref[:KL, :], ((1,), (1,)))
     values = new_rows[:, :KL].astype(F32)
     for t in range(steps):
         out = out + new_weights[:, t : t + 1] * values[t : t + 1, :]
@@ -104,30 +104,31 @@
     return dot(values.astype(BF), repeat)
 
 
-def pack_body(where_ref, tokens_ref, routes_ref, out_ref, tokens_here, routes_here, sems):
+def pack_body(where_ref, tokens_ref, routes_ref, out_ref):
     chip, core = where_ref[0], where_ref[1]
     rows = out_ref.shape[0]
     experts = rows // ROWS
-    steps, tokens = routes_ref.shape[0], routes_ref.shape[1]
+    steps, picks, tokens = routes_ref.shape
     part = tokens_ref.shape[2] // 8
     columns = pl.ds(pl.multiple_of(chip * 2 * part, 128), 2 * part)
-    fetch_routes = pltpu.make_async_copy(routes_ref, routes_here, sems.at[0])
-    fetch_tokens = pltpu.make_async_copy(tokens_ref.at[:, :, columns], tokens_here, sems.at[1])
-    fetch_routes.start()
-    fetch_tokens.start()
-    place = iota((tokens, rows), 1) % ROWS
-    fetch_routes.wait()
-    slots = [spread(named_slots(routes_here[step], experts), experts) for step in range(steps)]
-    fetch_tokens.wait()
+    place = iota((rows, tokens), 0) % ROWS
+    repeat = (iota((rows, experts), 0) // ROWS == iota((rows, experts), 1)).astype(BF)
+    earlier = (iota((tokens, tokens), 0) < iota((tokens, tokens), 1)).astype(BF)
+    experts_of = iota((experts, tokens), 0)
     main = jnp.zeros((rows, part), F32)
     for step in range(steps):
-        both = tokens_here[step]
+        named = jnp.zeros((experts, tokens), F32)
+        for k in range(picks):
+            named = named + (routes_ref[step, k : k + 1, :] == experts_of).astype(F32)
+        before = dot(named.astype(BF), earlier)
+        slots = dot(repeat, jnp.where(named > 0.5, before, -1.0).astype(BF))
+        both = tokens_ref[step, :, columns]
         own = jnp.where(core == 0, both[:, :part], both[:, part:])
         wanted = (place - CAP * step).astype(F32)
-        chosen = ((slots[step] == wanted) & (wanted >= 0)).astype(BF)
-        main = main + dot(chosen, own, ((0,), (0,)))
+        chosen = ((slots == wanted) & (wanted >= 0)).astype(BF)
+        main = main + dot(chosen, own)
         if step == steps - 1:
-            last = dot((slots[step] == CAP - 1.0).astype(BF), own, ((0,), (0,)))
+            last = dot((slots == CAP - 1.0).astype(BF), own)
     out_ref[:, :part] = main.astype(BF)
     out_ref[:, part:] = ninth_columns(last, part)
 
@@ -182,8 +183,10 @@
 
 
 def partial_body(where_ref, *refs):
-    pieces, (gate_ref, up_ref, other_ref, keep_ref, send_ref) = refs[:4], refs[4:]
-    rows = pieces[0].shape[0]
+    own, (gate_ref, up_ref, other_ref, keep_ref, send_ref) = refs[0], refs[7:]
+    halves = [[own]] + [refs[m : m + 2] for m in (1, 3, 5)]
+    pieces = [jnp.concatenate([h[...] for h in m], axis=0) for m in halves]
+    rows = own.shape[0]
     experts = rows // ROWS
     part = gate_ref.shape[0] // 8
     wide = keep_ref.shape[1]
@@ -234,13 +237,14 @@
         total = total + dot(hidden[m][...], down[m][...])
     first = where_ref[1] == 0
     keep_ref[...] = jnp.where(first, total[:, :part], total[:, part:])
-    send_ref[...] = jnp.where(first, total[:, part:], total[:, :part]).astype(BF)
+    send_ref[:, :part] = jnp.where(first, total[:, part:], total[:, :part]).astype(BF)
+    send_ref[:, part:] = jnp.zeros((total.shape[0], HALF), BF)
 
 
 def repack_body(one_ref, two_ref, out_ref):
     rows, part = out_ref.shape[0], one_ref.shape[1]
     experts = rows // ROWS
-    total = (one_ref[...] + two_ref[...].astype(F32)).astype(BF)
+    total = (one_ref[...] + two_ref[:, :part].astype(F32)).astype(BF)
     out_ref[:, :part] = total[:rows]
     repeat = (iota((rows, experts), 0) // ROWS == iota((rows, experts), 1)).astype(BF)
     out_ref[:, part:] = ninth_columns(dot(repeat, total[rows:]), part)
@@ -267,10 +271,10 @@
 
 def gather_rows(own):
     middle = own.shape[0] // 2
-    one, three = swap(own, 2 * 2), swap(own, 3 * 2)
-    first = swap(one[:middle], 3 * 2)
-    second = swap(three[middle:], 2 * 2)
-    return one, three, first, second
+    upper, lower = own[:middle], own[middle:]
+    two_upper, three_lower = swap(upper, 4), swap(lower, 6)
+    two_lower, three_upper = swap(lower, 4), swap(upper, 6)
+    return swap(two_upper, 6), swap(three_lower, 4), two_upper, two_lower, three_upper, three_lower
 
 
 def local(
@@ -291,21 +295,13 @@
     steps, tokens, width = token_rows.shape
     part = width // 8
     units = gate_proj.shape[2]
+    section = lax.axis_index("sec").astype(jnp.int32)
     where = jnp.stack([me // 2, me % 2]).astype(jnp.int32)
 
-    packed = pl.pallas_call(
-        pack_body,
-        out_shape=jax.ShapeDtypeStruct((rows, part + HALF), BF),
-        in_specs=[SMEM, ANY, ANY],
-        out_specs=VMEM,
-        scratch_shapes=[
-            pltpu.VMEM((steps, tokens, 2 * part), BF),
-            pltpu.VMEM(routes.shape, jnp.int32),
-            pltpu.SemaphoreType.DMA((2,)),
-        ],
-        cost_estimate=pl.CostEstimate(flops=10**8, bytes_accessed=10**6, transcendentals=0),
-        name="pack",
-    )(where, token_rows, routes)
+    packed = call(
+        pack_body, jax.ShapeDtypeStruct((rows, part + HALF), BF), [SMEM, VMEM, VMEM],
+        10**8, 10**6, "pack",
+    )(where, token_rows, jnp.swapaxes(routes, 1, 2))
     packed, later = lax.optimization_barrier((packed, where))
     arrived = lax.all_to_all(
         packed.reshape(experts, ROWS, part + HALF), "grp", split_axis=0, concat_axis=0, tiled=True
@@ -321,46 +317,22 @@
     other = swap(other, 1)
     down = [down[0]] + [swap(down[m], 2 * m) for m in range(1, 4)]
 
-    heads = queries.shape[2]
-    send, keep = call(
-        attend_body, [jax.ShapeDtypeStruct((steps * heads, KL // 2 + 256), F32)] * 2,
-        [SMEM, VMEM, VMEM, VMEM], 3 * 10**8, 2 * 10**6, "attend",
-    )(
-        jnp.stack([later[0] // 2, lengths[0]]),
-        queries.reshape(steps * heads, queries.shape[3]),
-        latent_cache.reshape(latent_cache.shape[1:]),
-        new_latent.reshape(steps, new_latent.shape[2]),
-    )
-    attention = call(
-        merge_body, jax.ShapeDtypeStruct((steps * heads, KL // 2), BF), [VMEM, VMEM],
-        10**6, 10**6, "merge",
-    )(keep, swap(send, 4))
-
-    gates = call(
-        gates_body,
-        jax.ShapeDtypeStruct((2, 16 * (steps + part // HALF), rows), BF),
-        [VMEM, VMEM], 10**8, 10**6, "gates",
-    )(routes, route_gates)
-
-    arrived, other, down, attention, gates = lax.optimization_barrier(
-        (arrived, other, down, attention, gates)
-    )
-    one, three, first, second = gather_rows(arrived)
-    two = jnp.concatenate([first, second], axis=0)
+    arrived, other, down = lax.optimization_barrier((arrived, other, down))
     keep, send = call(
         partial_body, [jax.ShapeDtypeStruct((rows + experts, 2 * units), F32)] * 2,
-        [SMEM] + [VMEM] * 7, 10**9, 6 * 10**6, "partial",
-    )(where, arrived, two, one, three, gate_proj, up_proj, other)
+        [SMEM] + [VMEM] * 10, 10**9, 6 * 10**6, "partial",
+    )(where, arrived, *gather_rows(arrived), gate_proj, up_proj, other)
     hidden = call(
         hidden_body, jax.ShapeDtypeStruct((rows + experts, units), BF), [VMEM] * 2,
         10**7, 10**6, "hidden",
     )(keep, swap(send, 1))
-    hidden = [hidden] + [swap(hidden, 2 * m) for m in range(1, 4)]
+    two = swap(hidden, 4)
+    hidden = [hidden, swap(two, 6), two, swap(hidden, 6)]
     keep, send = call(
         down_body,
         [
             jax.ShapeDtypeStruct((rows + experts, part), F32),
-            jax.ShapeDtypeStruct((rows + experts, part), BF),
+            jax.ShapeDtypeStruct((rows + experts, part + HALF), BF),
         ],
         [SMEM] + [VMEM] * 8, 10**9, 3 * 10**6, "down",
     )(where, *hidden, *down)
@@ -368,9 +340,32 @@
         repack_body, jax.ShapeDtypeStruct((rows, part + HALF), BF), [VMEM] * 2,
         10**8, 2 * 10**6, "repack",
     )(keep, swap(send, 1))
+    outgoing, info, gates = lax.optimization_barrier(
+        (outgoing, jnp.stack([section, lengths[0]]), route_gates)
+    )
     returned = lax.all_to_all(
         outgoing.reshape(experts, ROWS, part + HALF), "grp", split_axis=0, concat_axis=0, tiled=True
     ).reshape(rows, part + HALF)
+
+    heads = queries.shape[2]
+    send, keep = call(
+        attend_body, [jax.ShapeDtypeStruct((steps * heads, KL // 2 + 256), F32)] * 2,
+        [SMEM, VMEM, VMEM, VMEM], 3 * 10**8, 2 * 10**6, "attend",
+    )(
+        info,
+        queries.reshape(steps * heads, queries.shape[3]),
+        latent_cache[0].T,
+        new_latent.reshape(steps, new_latent.shape[2]),
+    )
+    attention = call(
+        merge_body, jax.ShapeDtypeStruct((steps * heads, KL // 2), BF), [VMEM, VMEM],
+        10**6, 10**6, "merge",
+    )(keep, swap(send, 4))
+    gates = call(
+        gates_body,
+        jax.ShapeDtypeStruct((2, 16 * (steps + part // HALF), rows), BF),
+        [VMEM, VMEM], 10**8, 10**6, "gates",
+    )(routes, gates)
     moe = call(
         combine_body, jax.ShapeDtypeStruct((steps, tokens, part), BF), [VMEM, VMEM],
         10**8, 10**6, "combine",

time: 147 us -> 134 us (0.912)
  blocking collectives: 32.2 us -> 0 us
  starting transfers between devices: 56.4 us -> 74.8 us
  waiting for transfers between devices: 30.3 us -> 36 us
  Pallas kernels: 17.6 us -> 14 us
    all_to_all x1 -> x0, blocking collectives: 32.2 us -> none  [local(): lax.all_to_all(outgoing.reshape(experts, ROWS, part + HALF), 'grp', split...]
    all_to_all x0 -> x1, starting transfers between devices: none -> 12.8 us  [local(): lax.all_to_all(outgoing.reshape(experts, ROWS, part + HALF), 'grp', split...]
    all_to_all x0 -> x1, waiting for transfers between devices: none -> 9.08 us  [local(): lax.all_to_all(outgoing.reshape(experts, ROWS, part + HALF), 'grp', split...]
    ppermute x14 -> x16, starting transfers between devices: 39.5 us -> 45.4 us  [swap(): return lax.ppermute(value, LINE, [(d, d ^ k) for d in range(8)])]
    ppermute x14 -> x16, waiting for transfers between devices: 30.3 us -> 26.9 us  [swap(): return lax.ppermute(value, LINE, [(d, d ^ k) for d in range(8)])]
    unnamed x23 -> x33, local copies, waits for them, and re-layouts: 5.25 us -> 5.18 us
  transfers between devices with their start and end apart: 15 -> 18, of which waited for: 8 -> 11; matrix products, arithmetic and copies ran while one was open for 1% -> 0% of each run, Pallas kernels for 4% -> 3%
where the time goes in v3:
time: 134 us; the launch traced here: 132 us
  starting transfers between devices  74.8 us (56%)
  waiting for transfers between devices  36 us (27%)
  Pallas kernels  14 us (10%)
  local copies, waits for them, and re-layouts  5.31 us (4%)
  between operations  1.63 us (1%)
    ppermute x16, starting transfers between devices, swap(): return lax.ppermute(value, LINE, [(d, d ^ k) for d in range(8)])  45.4 us
    ppermute x16, waiting for transfers between devices, swap(): return lax.ppermute(value, LINE, [(d, d ^ k) for d in range(8)])  26.9 us
    all_to_all x1, starting transfers between devices, local(): lax.all_to_all(packed.reshape(experts, ROWS, part + HALF), 'grp', split_a...  16.6 us
    all_to_all x1, starting transfers between devices, local(): lax.all_to_all(outgoing.reshape(experts, ROWS, part + HALF), 'grp', split...  12.8 us
    all_to_all x1, waiting for transfers between devices, local(): lax.all_to_all(outgoing.reshape(experts, ROWS, part + HALF), 'grp', split...  9.08 us
    unnamed x33, local copies, waits for them, and re-layouts  5.18 us
    pallas_call x1, Pallas kernels, local(): call(pack_body, jax.ShapeDtypeStruct((rows, part + HALF), BF), [SMEM, VME...  2.96 us
  transfers between devices with their start and end apart: 18, of which 11 were waited for; matrix products, arithmetic and copies ran while one was open for 0% of the time, Pallas kernels for 3%

profile of v3, /device:TPU:6, one launch (start us, length us, event | category | flops | bytes accessed | tf_op | source)
XLA Modules:
  0.0 131.8 jit_solution(9439269838701562091)
XLA Ops:
  2.5 3.0 %pack.1 = bf16[512,512]{1,0:T(8,128)(2,1)} custom-call(s32[2]{0:T(128)S(1)} %pad_add_fusion.where_ref, bf16[3,12,3584]{2,1,0:T(8,128)(2,1)S(1)} %copy-done.4, s32[3,8,12]{2,1,0:T(8,128)S(1)} %bitcast.29), custom_call_target="tpu_custom_call" | custom-call | flops 100000000 | bytes 1000000 | tf_op jit(solution)/shard_map/pack/pallas_call | solution.py:301
  5.5 16.6 %all-to-all-start = ((bf16[64,8,512]{2,1,0:T(8,128)(2,1)}), bf16[64,8,512]{2,1,0:T(8,128)(2,1)S(1)}, u32[]{:S(2)}, u32[]{:S(2)}) async-start(bf16[64,8,512]{2,1,0:T(8,128)(2,1)} %bitcast.3), calls=%async_computation | async-start | bytes 1048576 | tf_op jit(solution)/shard_map/all_to_all | solution.py:306
  26.0 3.3 %collective-permute-start.1 = (bf16[128,896]{1,0:T(8,128)(2,1)S(1)}, bf16[128,896]{1,0:T(8,128)(2,1)S(1)}, u32[]{:S(2)}, u32[]{:S(2)}) collective-permute-start(bf16[128,896]{1,0:T(8,128)(2,1)S(1)} %get-tuple-element.28), channel_id=1, source_target_pairs={{0,2},{1,3},{2,0},{3,1},{256,258},{257,259},{258,256},{259,257},{4... | collective-permute-start | bytes 688136 | tf_op jit(solution)/shard_map/ppermute | solution.py:269
  31.3 4.6 %collective-permute-start.3 = (bf16[128,896]{1,0:T(8,128)(2,1)S(1)}, bf16[128,896]{1,0:T(8,128)(2,1)S(1)}, u32[]{:S(2)}, u32[]{:S(2)}) collective-permute-start(bf16[128,896]{1,0:T(8,128)(2,1)S(1)} %get-tuple-element.30), channel_id=1, source_target_pairs={{0,258},{1,259},{2,256},{3,257},{256,2},{257,3},{258,0},{259,1},{4... | collective-permute-start | bytes 688136 | tf_op jit(solution)/shard_map/ppermute | solution.py:269
  35.9 2.0 %collective-permute-done.1.refs_5_ = bf16[128,896]{1,0:T(8,128)(2,1)S(1)} collective-permute-done((bf16[128,896]{1,0:T(8,128)(2,1)S(1)}, bf16[128,896]{1,0:T(8,128)(2,1)S(1)}, u32[]{:S(2)}, u32[]{:S(2)}) %collective-permute-start.1) | collective-permute-done | bytes 229408 | tf_op jit(solution)/shard_map/ppermute | solution.py:269
  43.1 2.7 %collective-permute-start.4 = (bf16[256,512]{1,0:T(8,128)(2,1)S(1)}, bf16[256,512]{1,0:T(8,128)(2,1)S(1)}, u32[]{:S(2)}, u32[]{:S(2)}) collective-permute-start(bf16[256,512]{1,0:T(8,128)(2,1)S(1)} %get-tuple-element.49), channel_id=1, source_target_pairs={{0,256},{1,257},{2,258},{3,259},{256,0},{257,1},{258,2},{259,3},{4... | collective-permute-start | bytes 786440 | tf_op jit(solution)/shard_map/ppermute | solution.py:269
  45.8 3.8 %collective-permute-start.6 = (bf16[256,512]{1,0:T(8,128)(2,1)S(1)}, bf16[256,512]{1,0:T(8,128)(2,1)S(1)}, u32[]{:S(2)}, u32[]{:S(2)}) collective-permute-start(bf16[256,512]{1,0:T(8,128)(2,1)S(1)} %get-tuple-element.48), channel_id=1, source_target_pairs={{0,258},{1,259},{2,256},{3,257},{256,2},{257,3},{258,0},{259,1},{4... | collective-permute-start | bytes 786440 | tf_op jit(solution)/shard_map/ppermute | solution.py:269
  49.6 2.8 %collective-permute-start.8 = (bf16[256,512]{1,0:T(8,128)(2,1)S(1)}, bf16[256,512]{1,0:T(8,128)(2,1)S(1)}, u32[]{:S(2)}, u32[]{:S(2)}) collective-permute-start(bf16[256,512]{1,0:T(8,128)(2,1)S(1)} %get-tuple-element.48), channel_id=1, source_target_pairs={{0,256},{1,257},{2,258},{3,259},{256,0},{257,1},{258,2},{259,3},{4... | collective-permute-start | bytes 786440 | tf_op jit(solution)/shard_map/ppermute | solution.py:269
  52.4 3.1 %collective-permute-start.9 = (bf16[256,512]{1,0:T(8,128)(2,1)S(1)}, bf16[256,512]{1,0:T(8,128)(2,1)S(1)}, u32[]{:S(2)}, u32[]{:S(2)}) collective-permute-start(bf16[256,512]{1,0:T(8,128)(2,1)S(1)} %get-tuple-element.49), channel_id=1, source_target_pairs={{0,258},{1,259},{2,256},{3,257},{256,2},{257,3},{258,0},{259,1},{4... | collective-permute-start | bytes 786440 | tf_op jit(solution)/shard_map/ppermute | solution.py:269
  55.5 4.0 %collective-permute-start.5 = (bf16[256,512]{1,0:T(8,128)(2,1)S(1)}, bf16[256,512]{1,0:T(8,128)(2,1)S(1)}, u32[]{:S(2)}, u32[]{:S(2)}) collective-permute-start(bf16[256,512]{1,0:T(8,128)(2,1)S(1)} %collective-permute-done.4.refs_3_), channel_id=1, source_target_pairs={{0,258},{1,259},{2,256},{3,257},{256,2},{257,3},{258,0},{259,1},{4... | collective-permute-start | bytes 786440 | tf_op jit(solution)/shard_map/ppermute | solution.py:269
  61.4 3.0 %collective-permute-done.9.refs_5_ = bf16[256,512]{1,0:T(8,128)(2,1)S(1)} collective-permute-done((bf16[256,512]{1,0:T(8,128)(2,1)S(1)}, bf16[256,512]{1,0:T(8,128)(2,1)S(1)}, u32[]{:S(2)}, u32[]{:S(2)}) %collective-permute-start.9) | collective-permute-done | bytes 262176 | tf_op jit(solution)/shard_map/ppermute | solution.py:269
  64.4 3.3 %collective-permute-done.5.refs_1_ = bf16[256,512]{1,0:T(8,128)(2,1)S(1)} collective-permute-done((bf16[256,512]{1,0:T(8,128)(2,1)S(1)}, bf16[256,512]{1,0:T(8,128)(2,1)S(1)}, u32[]{:S(2)}, u32[]{:S(2)}) %collective-permute-start.5) | collective-permute-done | bytes 262176 | tf_op jit(solution)/shard_map/ppermute | solution.py:269
  67.7 2.7 %partial.1 = (f32[576,256]{1,0:T(8,128)S(1)}, f32[576,256]{1,0:T(8,128)S(1)}) custom-call(s32[2]{0:T(128)S(1)} %pad_add_fusion.where_ref, bf16[512,512]{1,0:T(8,128)(2,1)S(1)} %bitcast.20, bf16[256,512]{1,0:T(8,128)(2,1)S(1)} %collective-permute-done.5.refs_1_, bf16[256,512]{1,0:T(8,128)(2,1)S(1)} %collective-permute-done.7.refs_2_, ...), custom_call_target="tpu_custom_call" | custom-call | flops 1000000000 | bytes 6000000 | tf_op jit(solution)/shard_map/partial/pallas_call | solution.py:321
  70.4 2.1 %collective-permute-start.10 = (f32[576,256]{1,0:T(8,128)S(1)}, f32[576,256]{1,0:T(8,128)S(1)}, u32[]{:S(2)}, u32[]{:S(2)}) collective-permute-start(f32[576,256]{1,0:T(8,128)S(1)} %get-tuple-element.34), channel_id=1, source_target_pairs={{0,1},{1,0},{2,3},{3,2},{256,257},{257,256},{258,259},{259,258},{4... | collective-permute-start | bytes 1769480 | tf_op jit(solution)/shard_map/ppermute | solution.py:269
  72.5 2.0 %collective-permute-done.10.two_ref = f32[576,256]{1,0:T(8,128)S(1)} collective-permute-done((f32[576,256]{1,0:T(8,128)S(1)}, f32[576,256]{1,0:T(8,128)S(1)}, u32[]{:S(2)}, u32[]{:S(2)}) %collective-permute-start.10) | collective-permute-done | bytes 589856 | tf_op jit(solution)/shard_map/ppermute | solution.py:269
  74.6 2.3 %collective-permute-start.11 = (bf16[576,128]{1,0:T(8,128)(2,1)S(1)}, bf16[576,128]{1,0:T(8,128)(2,1)S(1)}, u32[]{:S(2)}, u32[]{:S(2)}) collective-permute-start(bf16[576,128]{1,0:T(8,128)(2,1)S(1)} %hidden.1.refs_0_), channel_id=1, source_target_pairs={{0,256},{1,257},{2,258},{3,259},{256,0},{257,1},{258,2},{259,3},{4... | collective-permute-start | bytes 442376 | tf_op jit(solution)/shard_map/ppermute | solution.py:269
  76.9 3.5 %collective-permute-start.13 = (bf16[576,128]{1,0:T(8,128)(2,1)S(1)}, bf16[576,128]{1,0:T(8,128)(2,1)S(1)}, u32[]{:S(2)}, u32[]{:S(2)}) collective-permute-start(bf16[576,128]{1,0:T(8,128)(2,1)S(1)} %hidden.1.refs_0_), channel_id=1, source_target_pairs={{0,258},{1,259},{2,256},{3,257},{256,2},{257,3},{258,0},{259,1},{4... | collective-permute-start | bytes 442376 | tf_op jit(solution)/shard_map/ppermute | solution.py:269
  80.3 2.0 %collective-permute-done.11.refs_2_ = bf16[576,128]{1,0:T(8,128)(2,1)S(1)} collective-permute-done((bf16[576,128]{1,0:T(8,128)(2,1)S(1)}, bf16[576,128]{1,0:T(8,128)(2,1)S(1)}, u32[]{:S(2)}, u32[]{:S(2)}) %collective-permute-start.11) | collective-permute-done | bytes 147488 | tf_op jit(solution)/shard_map/ppermute | solution.py:269
  82.4 3.8 %collective-permute-start.12 = (bf16[576,128]{1,0:T(8,128)(2,1)S(1)}, bf16[576,128]{1,0:T(8,128)(2,1)S(1)}, u32[]{:S(2)}, u32[]{:S(2)}) collective-permute-start(bf16[576,128]{1,0:T(8,128)(2,1)S(1)} %collective-permute-done.11.refs_2_), channel_id=1, source_target_pairs={{0,258},{1,259},{2,256},{3,257},{256,2},{257,3},{258,0},{259,1},{4... | collective-permute-start | bytes 442376 | tf_op jit(solution)/shard_map/ppermute | solution.py:269
  86.2 4.4 %collective-permute-done.12.refs_1_ = bf16[576,128]{1,0:T(8,128)(2,1)S(1)} collective-permute-done((bf16[576,128]{1,0:T(8,128)(2,1)S(1)}, bf16[576,128]{1,0:T(8,128)(2,1)S(1)}, u32[]{:S(2)}, u32[]{:S(2)}) %collective-permute-start.12) | collective-permute-done | bytes 147488 | tf_op jit(solution)/shard_map/ppermute | solution.py:269
  90.6 2.2 %down.1 = (f32[576,448]{1,0:T(8,128)S(1)}, bf16[576,512]{1,0:T(8,128)(2,1)S(1)}) custom-call(s32[2]{0:T(128)S(1)} %pad_add_fusion.where_ref, bf16[576,128]{1,0:T(8,128)(2,1)S(1)} %hidden.1.refs_0_, bf16[576,128]{1,0:T(8,128)(2,1)S(1)} %collective-permute-done.12.refs_1_, bf16[576,128]{1,0:T(8,128)(2,1)S(1)} %collective-permute-done.11.refs_2_, ...), custom_call_target="tpu_custom_call" | custom-call | flops 1000000000 | bytes 3000000 | tf_op jit(solution)/shard_map/down/pallas_call | solution.py:331
  98.1 12.8 %all-to-all-start.1 = ((bf16[64,8,512]{2,1,0:T(8,128)(2,1)}), bf16[64,8,512]{2,1,0:T(8,128)(2,1)S(1)}, u32[]{:S(2)}, u32[]{:S(2)}) async-start(bf16[64,8,512]{2,1,0:T(8,128)(2,1)} %bitcast.15), calls=%async_computation.1 | async-start | bytes 1048576 | tf_op jit(solution)/shard_map/all_to_all | solution.py:346
  115.2 5.7 %collective-permute-done.15.two_ref = f32[96,512]{1,0:T(8,128)S(1)} collective-permute-done((f32[96,512]{1,0:T(8,128)S(1)}, f32[96,512]{1,0:T(8,128)S(1)}, u32[]{:S(2)}, u32[]{:S(2)}) %collective-permute-start.15) | collective-permute-done | bytes 196640 | tf_op jit(solution)/shard_map/ppermute | solution.py:269
  121.7 9.1 %all-to-all-done.1 = bf16[64,8,512]{2,1,0:T(8,128)(2,1)S(1)} async-done(((bf16[64,8,512]{2,1,0:T(8,128)(2,1)}), bf16[64,8,512]{2,1,0:T(8,128)(2,1)S(1)}, u32[]{:S(2)}, u32[]{:S(2)}) %all-to-all-start.1) | async-done | bytes 524320 | tf_op jit(solution)/shard_map/all_to_all | solution.py:346
  (59 shorter events, 25.7 us)
Async XLA Ops:
  0.6 21.5 %copy-start = (bf16[1,3584,128]{2,1,0:T(8,128)(2,1)S(1)}, bf16[1,3584,128]{2,1,0:T(8,128)(2,1)}, u32[]{:S(2)}) copy-start(bf16[1,3584,128]{2,1,0:T(8,128)(2,1)} %param.17) | copy-start | bytes 2752516
  0.6 21.5 %copy-start.1 = (bf16[1,3584,128]{2,1,0:T(8,128)(2,1)S(1)}, bf16[1,3584,128]{2,1,0:T(8,128)(2,1)}, u32[]{:S(2)}) copy-start(bf16[1,3584,128]{2,1,0:T(8,128)(2,1)} %param.18) | copy-start | bytes 2752516
  5.5 37.6 %all-to-all-start = ((bf16[64,8,512]{2,1,0:T(8,128)(2,1)}), bf16[64,8,512]{2,1,0:T(8,128)(2,1)S(1)}, u32[]{:S(2)}, u32[]{:S(2)}) async-start(bf16[64,8,512]{2,1,0:T(8,128)(2,1)} %bitcast.3), calls=%async_computation | async-start | bytes 1048576 | tf_op jit(solution)/shard_map/all_to_all | solution.py:306
  24.1 19.0 %collective-permute-start = (bf16[1792,256]{1,0:T(8,128)(2,1)S(1)}, bf16[1792,256]{1,0:T(8,128)(2,1)S(1)}, u32[]{:S(2)}, u32[]{:S(2)}) collective-permute-start(bf16[1792,256]{1,0:T(8,128)(2,1)S(1)} %get-tuple-element.26), channel_id=1, source_target_pairs={{0,1},{1,0},{2,3},{3,2},{256,257},{257,256},{258,259},{259,258},{4... | collective-permute-start | bytes 2752520 | tf_op jit(solution)/shard_map/ppermute | solution.py:269
  26.0 11.8 %collective-permute-start.1 = (bf16[128,896]{1,0:T(8,128)(2,1)S(1)}, bf16[128,896]{1,0:T(8,128)(2,1)S(1)}, u32[]{:S(2)}, u32[]{:S(2)}) collective-permute-start(bf16[128,896]{1,0:T(8,128)(2,1)S(1)} %get-tuple-element.28), channel_id=1, source_target_pairs={{0,2},{1,3},{2,0},{3,1},{256,258},{257,259},{258,256},{259,257},{4... | collective-permute-start | bytes 688136 | tf_op jit(solution)/shard_map/ppermute | solution.py:269
  29.3 10.8 %collective-permute-start.2 = (bf16[128,896]{1,0:T(8,128)(2,1)S(1)}, bf16[128,896]{1,0:T(8,128)(2,1)S(1)}, u32[]{:S(2)}, u32[]{:S(2)}) collective-permute-start(bf16[128,896]{1,0:T(8,128)(2,1)S(1)} %get-tuple-element.29), channel_id=1, source_target_pairs={{0,256},{1,257},{2,258},{3,259},{256,0},{257,1},{258,2},{259,3},{4... | collective-permute-start | bytes 688136 | tf_op jit(solution)/shard_map/ppermute | solution.py:269
  31.3 11.1 %collective-permute-start.3 = (bf16[128,896]{1,0:T(8,128)(2,1)S(1)}, bf16[128,896]{1,0:T(8,128)(2,1)S(1)}, u32[]{:S(2)}, u32[]{:S(2)}) collective-permute-start(bf16[128,896]{1,0:T(8,128)(2,1)S(1)} %get-tuple-element.30), channel_id=1, source_target_pairs={{0,258},{1,259},{2,256},{3,257},{256,2},{257,3},{258,0},{259,1},{4... | collective-permute-start | bytes 688136 | tf_op jit(solution)/shard_map/ppermute | solution.py:269
  43.1 12.3 %collective-permute-start.4 = (bf16[256,512]{1,0:T(8,128)(2,1)S(1)}, bf16[256,512]{1,0:T(8,128)(2,1)S(1)}, u32[]{:S(2)}, u32[]{:S(2)}) collective-permute-start(bf16[256,512]{1,0:T(8,128)(2,1)S(1)} %get-tuple-element.49), channel_id=1, source_target_pairs={{0,256},{1,257},{2,258},{3,259},{256,0},{257,1},{258,2},{259,3},{4... | collective-permute-start | bytes 786440 | tf_op jit(solution)/shard_map/ppermute | solution.py:269
  45.8 13.7 %collective-permute-start.6 = (bf16[256,512]{1,0:T(8,128)(2,1)S(1)}, bf16[256,512]{1,0:T(8,128)(2,1)S(1)}, u32[]{:S(2)}, u32[]{:S(2)}) collective-permute-start(bf16[256,512]{1,0:T(8,128)(2,1)S(1)} %get-tuple-element.48), channel_id=1, source_target_pairs={{0,258},{1,259},{2,256},{3,257},{256,2},{257,3},{258,0},{259,1},{4... | collective-permute-start | bytes 786440 | tf_op jit(solution)/shard_map/ppermute | solution.py:269
  49.6 11.8 %collective-permute-start.8 = (bf16[256,512]{1,0:T(8,128)(2,1)S(1)}, bf16[256,512]{1,0:T(8,128)(2,1)S(1)}, u32[]{:S(2)}, u32[]{:S(2)}) collective-permute-start(bf16[256,512]{1,0:T(8,128)(2,1)S(1)} %get-tuple-element.48), channel_id=1, source_target_pairs={{0,256},{1,257},{2,258},{3,259},{256,0},{257,1},{258,2},{259,3},{4... | collective-permute-start | bytes 786440 | tf_op jit(solution)/shard_map/ppermute | solution.py:269
  52.4 12.1 %collective-permute-start.9 = (bf16[256,512]{1,0:T(8,128)(2,1)S(1)}, bf16[256,512]{1,0:T(8,128)(2,1)S(1)}, u32[]{:S(2)}, u32[]{:S(2)}) collective-permute-start(bf16[256,512]{1,0:T(8,128)(2,1)S(1)} %get-tuple-element.49), channel_id=1, source_target_pairs={{0,258},{1,259},{2,256},{3,257},{256,2},{257,3},{258,0},{259,1},{4... | collective-permute-start | bytes 786440 | tf_op jit(solution)/shard_map/ppermute | solution.py:269
  55.5 12.2 %collective-permute-start.5 = (bf16[256,512]{1,0:T(8,128)(2,1)S(1)}, bf16[256,512]{1,0:T(8,128)(2,1)S(1)}, u32[]{:S(2)}, u32[]{:S(2)}) collective-permute-start(bf16[256,512]{1,0:T(8,128)(2,1)S(1)} %collective-permute-done.4.refs_3_), channel_id=1, source_target_pairs={{0,258},{1,259},{2,256},{3,257},{256,2},{257,3},{258,0},{259,1},{4... | collective-permute-start | bytes 786440 | tf_op jit(solution)/shard_map/ppermute | solution.py:269
  59.5 8.3 %collective-permute-start.7 = (bf16[256,512]{1,0:T(8,128)(2,1)S(1)}, bf16[256,512]{1,0:T(8,128)(2,1)S(1)}, u32[]{:S(2)}, u32[]{:S(2)}) collective-permute-start(bf16[256,512]{1,0:T(8,128)(2,1)S(1)} %collective-permute-done.6.refs_6_), channel_id=1, source_target_pairs={{0,256},{1,257},{2,258},{3,259},{256,0},{257,1},{258,2},{259,3},{4... | collective-permute-start | bytes 786440 | tf_op jit(solution)/shard_map/ppermute | solution.py:269
  70.4 20.2 %copy-start.10 = (bf16[128,896]{1,0:T(8,128)(2,1)S(1)}, bf16[128,896]{1,0:T(8,128)(2,1)}, u32[]{:S(2)}) copy-start(bf16[128,896]{1,0:T(8,128)(2,1)} %copy-done.9) | copy-start | bytes 688132
  70.4 20.2 %copy-start.12 = (bf16[128,896]{1,0:T(8,128)(2,1)S(1)}, bf16[128,896]{1,0:T(8,128)(2,1)}, u32[]{:S(2)}) copy-start(bf16[128,896]{1,0:T(8,128)(2,1)} %copy-done.11) | copy-start | bytes 688132
  70.4 20.2 %copy-start.14 = (bf16[128,896]{1,0:T(8,128)(2,1)S(1)}, bf16[128,896]{1,0:T(8,128)(2,1)}, u32[]{:S(2)}) copy-start(bf16[128,896]{1,0:T(8,128)(2,1)} %copy-done.13) | copy-start | bytes 688132
  70.4 4.0 %collective-permute-start.10 = (f32[576,256]{1,0:T(8,128)S(1)}, f32[576,256]{1,0:T(8,128)S(1)}, u32[]{:S(2)}, u32[]{:S(2)}) collective-permute-start(f32[576,256]{1,0:T(8,128)S(1)} %get-tuple-element.34), channel_id=1, source_target_pairs={{0,1},{1,0},{2,3},{3,2},{256,257},{257,256},{258,259},{259,258},{4... | collective-permute-start | bytes 1769480 | tf_op jit(solution)/shard_map/ppermute | solution.py:269
  74.6 7.8 %collective-permute-start.11 = (bf16[576,128]{1,0:T(8,128)(2,1)S(1)}, bf16[576,128]{1,0:T(8,128)(2,1)S(1)}, u32[]{:S(2)}, u32[]{:S(2)}) collective-permute-start(bf16[576,128]{1,0:T(8,128)(2,1)S(1)} %hidden.1.refs_0_), channel_id=1, source_target_pairs={{0,256},{1,257},{2,258},{3,259},{256,0},{257,1},{258,2},{259,3},{4... | collective-permute-start | bytes 442376 | tf_op jit(solution)/shard_map/ppermute | solution.py:269
  76.9 9.3 %collective-permute-start.13 = (bf16[576,128]{1,0:T(8,128)(2,1)S(1)}, bf16[576,128]{1,0:T(8,128)(2,1)S(1)}, u32[]{:S(2)}, u32[]{:S(2)}) collective-permute-start(bf16[576,128]{1,0:T(8,128)(2,1)S(1)} %hidden.1.refs_0_), channel_id=1, source_target_pairs={{0,258},{1,259},{2,256},{3,257},{256,2},{257,3},{258,0},{259,1},{4... | collective-permute-start | bytes 442376 | tf_op jit(solution)/shard_map/ppermute | solution.py:269
  82.4 8.2 %collective-permute-start.12 = (bf16[576,128]{1,0:T(8,128)(2,1)S(1)}, bf16[576,128]{1,0:T(8,128)(2,1)S(1)}, u32[]{:S(2)}, u32[]{:S(2)}) collective-permute-start(bf16[576,128]{1,0:T(8,128)(2,1)S(1)} %collective-permute-done.11.refs_2_), channel_id=1, source_target_pairs={{0,258},{1,259},{2,256},{3,257},{256,2},{257,3},{258,0},{259,1},{4... | collective-permute-start | bytes 442376 | tf_op jit(solution)/shard_map/ppermute | solution.py:269
  92.8 3.9 %collective-permute-start.14 = (bf16[576,512]{1,0:T(8,128)(2,1)S(1)}, bf16[576,512]{1,0:T(8,128)(2,1)S(1)}, u32[]{:S(2)}, u32[]{:S(2)}) collective-permute-start(bf16[576,512]{1,0:T(8,128)(2,1)S(1)} %get-tuple-element.40), channel_id=1, source_target_pairs={{0,1},{1,0},{2,3},{3,2},{256,257},{257,256},{258,259},{259,258},{4... | collective-permute-start | bytes 1769480 | tf_op jit(solution)/shard_map/ppermute | solution.py:269
  98.1 16.4 %copy-start.15 = (f32[3,12,8]{1,2,0:T(8,128)S(1)}, f32[3,12,8]{1,2,0:T(8,128)}, u32[]{:S(2)}) copy-start(f32[3,12,8]{1,2,0:T(8,128)} %param.16) | copy-start | bytes 3460
  98.1 32.7 %all-to-all-start.1 = ((bf16[64,8,512]{2,1,0:T(8,128)(2,1)}), bf16[64,8,512]{2,1,0:T(8,128)(2,1)S(1)}, u32[]{:S(2)}, u32[]{:S(2)}) async-start(bf16[64,8,512]{2,1,0:T(8,128)(2,1)} %bitcast.15), calls=%async_computation.1 | async-start | bytes 1048576 | tf_op jit(solution)/shard_map/all_to_all | solution.py:346
  112.4 8.5 %collective-permute-start.15 = (f32[96,512]{1,0:T(8,128)S(1)}, f32[96,512]{1,0:T(8,128)S(1)}, u32[]{:S(2)}, u32[]{:S(2)}) collective-permute-start(f32[96,512]{1,0:T(8,128)S(1)} %get-tuple-element.43), channel_id=1, source_target_pairs={{0,256},{1,257},{2,258},{3,259},{256,0},{257,1},{258,2},{259,3},{4... | collective-permute-start | bytes 589832 | tf_op jit(solution)/shard_map/ppermute | solution.py:269
  (10 other events, 64.1 us)

commit v4 on v3

--- a/solution.py
+++ b/solution.py
@@ -18,7 +18,7 @@
 
 SMEM = pl.BlockSpec(memory_space=pltpu.SMEM)
 VMEM = pl.BlockSpec(memory_space=pltpu.VMEM)
-ANY = pl.BlockSpec(memory_space=pl.ANY)
+HBM = pl.BlockSpec(memory_space=pltpu.HBM)
 
 
 def dot(a, b, dims=((1,), (0,))):
@@ -42,8 +42,8 @@
     )
 
 
-def attend_body(info, q_ref, cache_ref, new_ref, send_ref, keep_ref):
-    section, length = info[0], info[1]
+def attend_body(length_ref, q_ref, cache_ref, new_ref, send_ref, keep_ref):
+    section, length = lax.axis_index("sec").astype(jnp.int32), length_ref[0]
     q = q_ref[...]
     rows, local_length = q.shape[0], cache_ref.shape[1]
     steps = new_ref.shape[0]
@@ -87,6 +87,29 @@
     out_ref[...] = (out / total).astype(BF)
 
 
+def place_here():
+    return lax.axis_index(LINE).astype(jnp.int32)
+
+
+def sources(d):
+    core = d % 2
+    return d, d ^ (4 + 2 * core), d ^ (5 + 2 * core), d ^ 2
+
+
+def permute(value, target):
+    return lax.ppermute(value, LINE, [(d, target(d)) for d in range(8)])
+
+
+def swap(value, k):
+    return permute(value, lambda d: d ^ k)
+
+
+def gather(own):
+    near = permute(own, lambda d: d ^ (4 + 2 * (d % 2)))
+    crossed = permute(own, lambda d: d ^ (7 - 2 * (d % 2)))
+    return own, near, crossed, permute(near, lambda d: d ^ (6 - 2 * (d % 2)))
+
+
 def named_slots(routes, experts):
     tokens, picks = routes.shape
     experts_of = iota((tokens, experts), 1)
@@ -104,31 +127,38 @@
     return dot(values.astype(BF), repeat)
 
 
-def pack_body(where_ref, tokens_ref, routes_ref, out_ref):
-    chip, core = where_ref[0], where_ref[1]
+def pack_body(tokens_ref, routes_ref, out_ref, tokens_here, routes_here, sems):
+    here = place_here()
     rows = out_ref.shape[0]
     experts = rows // ROWS
     steps, picks, tokens = routes_ref.shape
     part = tokens_ref.shape[2] // 8
-    columns = pl.ds(pl.multiple_of(chip * 2 * part, 128), 2 * part)
+    columns = pl.ds(pl.multiple_of((here // 2) * 2 * part, 128), 2 * part)
+    fetch_routes = pltpu.make_async_copy(routes_ref, routes_here, sems.at[0])
+    fetch_tokens = pltpu.make_async_copy(tokens_ref.at[:, :, columns], tokens_here, sems.at[1])
+    fetch_routes.start()
+    fetch_tokens.start()
     place = iota((rows, tokens), 0) % ROWS
     repeat = (iota((rows, experts), 0) // ROWS == iota((rows, experts), 1)).astype(BF)
     earlier = (iota((tokens, tokens), 0) < iota((tokens, tokens), 1)).astype(BF)
     experts_of = iota((experts, tokens), 0)
-    main = jnp.zeros((rows, part), F32)
+    fetch_routes.wait()
+    slots = []
     for step in range(steps):
         named = jnp.zeros((experts, tokens), F32)
         for k in range(picks):
-            named = named + (routes_ref[step, k : k + 1, :] == experts_of).astype(F32)
+            named = named + (routes_here[step, k : k + 1, :] == experts_of).astype(F32)
         before = dot(named.astype(BF), earlier)
-        slots = dot(repeat, jnp.where(named > 0.5, before, -1.0).astype(BF))
-        both = tokens_ref[step, :, columns]
-        own = jnp.where(core == 0, both[:, :part], both[:, part:])
+        slots.append(dot(repeat, jnp.where(named > 0.5, before, -1.0).astype(BF)))
+    fetch_tokens.wait()
+    main = jnp.zeros((rows, part), F32)
+    for step in range(steps):
+        both = tokens_here[step]
+        own = jnp.where(here % 2 == 0, both[:, :part], both[:, part:])
         wanted = (place - CAP * step).astype(F32)
-        chosen = ((slots == wanted) & (wanted >= 0)).astype(BF)
+        chosen = ((slots[step] == wanted) & (wanted >= 0)).astype(BF)
         main = main + dot(chosen, own)
-        if step == steps - 1:
-            last = dot((slots == CAP - 1.0).astype(BF), own)
+    last = dot((slots[-1] == CAP - 1.0).astype(BF), own)
     out_ref[:, :part] = main.astype(BF)
     out_ref[:, part:] = ninth_columns(last, part)
 
@@ -169,31 +199,31 @@
                     ).astype(BF)
 
 
-def slices_body(where_ref, gate_ref, up_ref, down_ref, other_ref, *down_outs):
-    chip, core = where_ref[0], where_ref[1]
+def slices_body(gate_ref, up_ref, down_ref, other_ref, *down_outs):
+    here = place_here()
     units = gate_ref.shape[1]
     part = gate_ref.shape[0] // 8
-    for m in range(4):
-        offset = pl.multiple_of((2 * (chip ^ m) + 1 - core) * part, HALF)
+    core = here % 2
+    for m, source in enumerate(sources(here ^ 1)):
+        offset = pl.multiple_of(source * part, HALF)
         rows = slice(m * part, (m + 1) * part)
         other_ref[rows, :units] = gate_ref[pl.ds(offset, part), :]
         other_ref[rows, units:] = up_ref[pl.ds(offset, part), :]
-        columns = pl.ds(pl.multiple_of((chip ^ m) * 2 * part, 128), 2 * part)
-        down_outs[m][...] = down_ref[:, columns]
-
-
-def partial_body(where_ref, *refs):
-    own, (gate_ref, up_ref, other_ref, keep_ref, send_ref) = refs[0], refs[7:]
-    halves = [[own]] + [refs[m : m + 2] for m in (1, 3, 5)]
-    pieces = [jnp.concatenate([h[...] for h in m], axis=0) for m in halves]
-    rows = own.shape[0]
+    targets = here, here ^ (4 + 2 * core), here ^ (7 - 2 * core), here ^ 2
+    for target, out in zip(targets, down_outs):
+        out[...] = down_ref[:, pl.ds(pl.multiple_of((target // 2) * 2 * part, 128), 2 * part)]
+
+
+def partial_body(*refs):
+    pieces, (gate_ref, up_ref, other_ref, keep_ref, send_ref) = refs[:4], refs[4:]
+    rows = pieces[0].shape[0]
     experts = rows // ROWS
     part = gate_ref.shape[0] // 8
     wide = keep_ref.shape[1]
-    chip, core = where_ref[0], where_ref[1]
+    blocks_of = sources(place_here())
 
     def weights(m, start, size):
-        offset = pl.multiple_of((2 * (chip ^ m) + core) * part + start, HALF)
+        offset = pl.multiple_of(blocks_of[m] * part + start, HALF)
         return jnp.concatenate(
             [
                 gate_ref[pl.ds(offset, size), :],
@@ -229,13 +259,13 @@
     out_ref[...] = (gate / (1.0 + jnp.exp(-gate)) * up).astype(BF)
 
 
-def down_body(where_ref, *refs):
+def down_body(*refs):
     hidden, down, (keep_ref, send_ref) = refs[:4], refs[4:8], refs[8:]
     part = keep_ref.shape[1]
     total = jnp.zeros((hidden[0].shape[0], 2 * part), F32)
     for m in range(4):
         total = total + dot(hidden[m][...], down[m][...])
-    first = where_ref[1] == 0
+    first = place_here() % 2 == 0
     keep_ref[...] = jnp.where(first, total[:, :part], total[:, part:])
     send_ref[:, :part] = jnp.where(first, total[:, part:], total[:, :part]).astype(BF)
     send_ref[:, part:] = jnp.zeros((total.shape[0], HALF), BF)
@@ -265,18 +295,6 @@
         out_ref[step] = out.astype(BF)
 
 
-def swap(value, k):
-    return lax.ppermute(value, LINE, [(d, d ^ k) for d in range(8)])
-
-
-def gather_rows(own):
-    middle = own.shape[0] // 2
-    upper, lower = own[:middle], own[middle:]
-    two_upper, three_lower = swap(upper, 4), swap(lower, 6)
-    two_lower, three_upper = swap(lower, 4), swap(upper, 6)
-    return swap(two_upper, 6), swap(three_lower, 4), two_upper, two_lower, three_upper, three_lower
-
-
 def local(
     latent_cache,
     new_latent,
@@ -289,20 +307,25 @@
     up_proj,
     down_proj,
 ):
-    me = lax.axis_index(LINE)
     experts = lax.axis_size("grp")
     rows = experts * ROWS
     steps, tokens, width = token_rows.shape
     part = width // 8
     units = gate_proj.shape[2]
-    section = lax.axis_index("sec").astype(jnp.int32)
-    where = jnp.stack([me // 2, me % 2]).astype(jnp.int32)
-
-    packed = call(
-        pack_body, jax.ShapeDtypeStruct((rows, part + HALF), BF), [SMEM, VMEM, VMEM],
-        10**8, 10**6, "pack",
-    )(where, token_rows, jnp.swapaxes(routes, 1, 2))
-    packed, later = lax.optimization_barrier((packed, where))
+    packed = pl.pallas_call(
+        pack_body,
+        out_shape=jax.ShapeDtypeStruct((rows, part + HALF), BF),
+        in_specs=[HBM, HBM],
+        out_specs=VMEM,
+        scratch_shapes=[
+            pltpu.VMEM((steps, tokens, 2 * part), BF),
+            pltpu.VMEM((steps, routes.shape[2], tokens), jnp.int32),
+            pltpu.SemaphoreType.DMA((2,)),
+        ],
+        cost_estimate=pl.CostEstimate(flops=10**8, bytes_accessed=10**6, transcendentals=0),
+        name="pack",
+    )(token_rows, jnp.swapaxes(routes, 1, 2))
+    packed, down_proj = lax.optimization_barrier((packed, down_proj))
     arrived = lax.all_to_all(
         packed.reshape(experts, ROWS, part + HALF), "grp", split_axis=0, concat_axis=0, tiled=True
     ).reshape(rows, part + HALF)
@@ -312,37 +335,38 @@
         slices_body,
         [jax.ShapeDtypeStruct((width // 2, 2 * units), BF)]
         + [jax.ShapeDtypeStruct((units, 2 * part), BF)] * 4,
-        [SMEM] + [VMEM] * 3, 10**6, 5 * 10**6, "slices",
-    )(later, gate_proj, up_proj, down_proj.reshape(units, width))
+        [VMEM] * 3, 10**6, 5 * 10**6, "slices",
+    )(gate_proj, up_proj, down_proj.reshape(units, width))
     other = swap(other, 1)
-    down = [down[0]] + [swap(down[m], 2 * m) for m in range(1, 4)]
+    down = [
+        down[0],
+        permute(down[1], lambda d: d ^ (4 + 2 * (d % 2))),
+        permute(down[2], lambda d: d ^ (7 - 2 * (d % 2))),
+        swap(down[3], 2),
+    ]
 
     arrived, other, down = lax.optimization_barrier((arrived, other, down))
     keep, send = call(
         partial_body, [jax.ShapeDtypeStruct((rows + experts, 2 * units), F32)] * 2,
-        [SMEM] + [VMEM] * 10, 10**9, 6 * 10**6, "partial",
-    )(where, arrived, *gather_rows(arrived), gate_proj, up_proj, other)
+        [VMEM] * 7, 10**9, 6 * 10**6, "partial",
+    )(*gather(arrived), gate_proj, up_proj, other)
     hidden = call(
         hidden_body, jax.ShapeDtypeStruct((rows + experts, units), BF), [VMEM] * 2,
         10**7, 10**6, "hidden",
     )(keep, swap(send, 1))
-    two = swap(hidden, 4)
-    hidden = [hidden, swap(two, 6), two, swap(hidden, 6)]
     keep, send = call(
         down_body,
         [
             jax.ShapeDtypeStruct((rows + experts, part), F32),
             jax.ShapeDtypeStruct((rows + experts, part + HALF), BF),
         ],
-        [SMEM] + [VMEM] * 8, 10**9, 3 * 10**6, "down",
-    )(where, *hidden, *down)
+        [VMEM] * 8, 10**9, 3 * 10**6, "down",
+    )(*gather(hidden), *down)
     outgoing = call(
         repack_body, jax.ShapeDtypeStruct((rows, part + HALF), BF), [VMEM] * 2,
         10**8, 2 * 10**6, "repack",
     )(keep, swap(send, 1))
-    outgoing, info, gates = lax.optimization_barrier(
-        (outgoing, jnp.stack([section, lengths[0]]), route_gates)
-    )
+    outgoing, lengths, gates = lax.optimization_barrier((outgoing, lengths, route_gates))
     returned = lax.all_to_all(
         outgoing.reshape(experts, ROWS, part + HALF), "grp", split_axis=0, concat_axis=0, tiled=True
     ).reshape(rows, part + HALF)
@@ -352,7 +376,7 @@
         attend_body, [jax.ShapeDtypeStruct((steps * heads, KL // 2 + 256), F32)] * 2,
         [SMEM, VMEM, VMEM, VMEM], 3 * 10**8, 2 * 10**6, "attend",
     )(
-        info,
+        lengths,
         queries.reshape(steps * heads, queries.shape[3]),
         latent_cache[0].T,
         new_latent.reshape(steps, new_latent.shape[2]),

time: 134 us -> 132 us (0.985)
  waiting for transfers between devices: 36 us -> 47.4 us
  starting transfers between devices: 74.8 us -> 66.1 us
  Pallas kernels: 14 us -> 12 us
  local copies, waits for them, and re-layouts: 5.31 us -> 3.48 us
    ppermute x16 -> x13, waiting for transfers between devices: 26.9 us -> 39.2 us  [permute(): return lax.ppermute(value, LINE, [(d, target(d)) for d in range(8)])]
    ppermute x16 -> x13, starting transfers between devices: 45.4 us -> 36.6 us  [permute(): return lax.ppermute(value, LINE, [(d, target(d)) for d in range(8)])]
    unnamed x33 -> x29, local copies, waits for them, and re-layouts: 5.18 us -> 3.38 us
  transfers between devices with their start and end apart: 18 -> 15, of which waited for: 11 -> 10; matrix products, arithmetic and copies ran while one was open for 0% -> 0% of each run, Pallas kernels for 3% -> 2%
where the time goes in v4:
time: 132 us; the launch traced here: 131 us
  starting transfers between devices  66.1 us (50%)
  waiting for transfers between devices  47.4 us (36%)
  Pallas kernels  12 us (9%)
  local copies, waits for them, and re-layouts  3.48 us (3%)
  between operations  1.58 us (1%)
    ppermute x13, waiting for transfers between devices, permute(): return lax.ppermute(value, LINE, [(d, target(d)) for d in range(8)])  39.2 us
    ppermute x13, starting transfers between devices, permute(): return lax.ppermute(value, LINE, [(d, target(d)) for d in range(8)])  36.6 us
    all_to_all x1, starting transfers between devices, local(): lax.all_to_all(packed.reshape(experts, ROWS, part + HALF), 'grp', split_a...  16.6 us
    all_to_all x1, starting transfers between devices, local(): lax.all_to_all(outgoing.reshape(experts, ROWS, part + HALF), 'grp', split...  12.8 us
    all_to_all x1, waiting for transfers between devices, local(): lax.all_to_all(outgoing.reshape(experts, ROWS, part + HALF), 'grp', split...  8.19 us
    unnamed x29, local copies, waits for them, and re-layouts  3.38 us
    pallas_call x1, Pallas kernels, local(): pl.pallas_call(pack_body, out_shape=jax.ShapeDtypeStruct((rows, part + HA...  3.18 us
  transfers between devices with their start and end apart: 15, of which 10 were waited for; matrix products, arithmetic and copies ran while one was open for 0% of the time, Pallas kernels for 2%

profile of v4, /device:TPU:6, one launch (start us, length us, event | category | flops | bytes accessed | tf_op | source)
XLA Modules:
  0.0 130.5 jit_solution(4139602832737204625)
XLA Ops:
  0.7 3.2 %pack.1 = bf16[512,512]{1,0:T(8,128)(2,1)} custom-call(bf16[3,12,3584]{2,1,0:T(8,128)(2,1)} %tokens_ref.1, s32[3,8,12]{2,1,0:T(8,128)} %bitcast.29), custom_call_target="tpu_custom_call" | custom-call | flops 100000000 | bytes 1000000 | tf_op jit(solution)/shard_map/pack/pallas_call | solution.py:315
  3.8 16.6 %all-to-all-start = ((bf16[64,8,512]{2,1,0:T(8,128)(2,1)}), bf16[64,8,512]{2,1,0:T(8,128)(2,1)S(1)}, u32[]{:S(2)}, u32[]{:S(2)}) async-start(bf16[64,8,512]{2,1,0:T(8,128)(2,1)} %bitcast.28), calls=%async_computation | async-start | bytes 1048576 | tf_op jit(solution)/shard_map/all_to_all | solution.py:329
  21.9 1.9 %collective-permute-start = (bf16[1792,256]{1,0:T(8,128)(2,1)S(1)}, bf16[1792,256]{1,0:T(8,128)(2,1)S(1)}, u32[]{:S(2)}, u32[]{:S(2)}) collective-permute-start(bf16[1792,256]{1,0:T(8,128)(2,1)S(1)} %get-tuple-element.26), channel_id=1, source_target_pairs={{0,1},{1,0},{2,3},{3,2},{256,257},{257,256},{258,259},{259,258},{4... | collective-permute-start | bytes 2752520 | tf_op jit(solution)/shard_map/ppermute | solution.py:100
  23.8 2.7 %collective-permute-start.1 = (bf16[128,896]{1,0:T(8,128)(2,1)S(1)}, bf16[128,896]{1,0:T(8,128)(2,1)S(1)}, u32[]{:S(2)}, u32[]{:S(2)}) collective-permute-start(bf16[128,896]{1,0:T(8,128)(2,1)S(1)} %get-tuple-element.28), channel_id=1, source_target_pairs={{0,256},{1,259},{2,258},{3,257},{256,0},{257,3},{258,2},{259,1},{4... | collective-permute-start | bytes 688136 | tf_op jit(solution)/shard_map/ppermute | solution.py:100
  26.6 4.1 %collective-permute-start.2 = (bf16[128,896]{1,0:T(8,128)(2,1)S(1)}, bf16[128,896]{1,0:T(8,128)(2,1)S(1)}, u32[]{:S(2)}, u32[]{:S(2)}) collective-permute-start(bf16[128,896]{1,0:T(8,128)(2,1)S(1)} %get-tuple-element.29), channel_id=1, source_target_pairs={{0,259},{1,256},{2,257},{3,258},{256,3},{257,0},{258,1},{259,2},{4... | collective-permute-start | bytes 688136 | tf_op jit(solution)/shard_map/ppermute | solution.py:100
  30.7 2.1 %collective-permute-start.3 = (bf16[128,896]{1,0:T(8,128)(2,1)S(1)}, bf16[128,896]{1,0:T(8,128)(2,1)S(1)}, u32[]{:S(2)}, u32[]{:S(2)}) collective-permute-start(bf16[128,896]{1,0:T(8,128)(2,1)S(1)} %get-tuple-element.30), channel_id=1, source_target_pairs={{0,2},{1,3},{2,0},{3,1},{256,258},{257,259},{258,256},{259,257},{4... | collective-permute-start | bytes 688136 | tf_op jit(solution)/shard_map/ppermute | solution.py:100
  33.5 5.7 %collective-permute-done.2.refs_6_ = bf16[128,896]{1,0:T(8,128)(2,1)S(1)} collective-permute-done((bf16[128,896]{1,0:T(8,128)(2,1)S(1)}, bf16[128,896]{1,0:T(8,128)(2,1)S(1)}, u32[]{:S(2)}, u32[]{:S(2)}) %collective-permute-start.2) | collective-permute-done | bytes 229408 | tf_op jit(solution)/shard_map/ppermute | solution.py:100
  41.4 2.7 %collective-permute-start.4 = (bf16[512,512]{1,0:T(8,128)(2,1)S(1)}, bf16[512,512]{1,0:T(8,128)(2,1)S(1)}, u32[]{:S(2)}, u32[]{:S(2)}) collective-permute-start(bf16[512,512]{1,0:T(8,128)(2,1)S(1)} %bitcast.20), channel_id=1, source_target_pairs={{0,256},{1,259},{2,258},{3,257},{256,0},{257,3},{258,2},{259,1},{4... | collective-permute-start | bytes 1572872 | tf_op jit(solution)/shard_map/ppermute | solution.py:100
  44.1 3.4 %collective-permute-start.5 = (bf16[512,512]{1,0:T(8,128)(2,1)S(1)}, bf16[512,512]{1,0:T(8,128)(2,1)S(1)}, u32[]{:S(2)}, u32[]{:S(2)}) collective-permute-start(bf16[512,512]{1,0:T(8,128)(2,1)S(1)} %bitcast.21), channel_id=1, source_target_pairs={{0,259},{1,256},{2,257},{3,258},{256,3},{257,0},{258,1},{259,2},{4... | collective-permute-start | bytes 1572872 | tf_op jit(solution)/shard_map/ppermute | solution.py:100
  47.5 8.3 %collective-permute-done.4.refs_1_ = bf16[512,512]{1,0:T(8,128)(2,1)S(1)} collective-permute-done((bf16[512,512]{1,0:T(8,128)(2,1)S(1)}, bf16[512,512]{1,0:T(8,128)(2,1)S(1)}, u32[]{:S(2)}, u32[]{:S(2)}) %collective-permute-start.4) | collective-permute-done | bytes 524320 | tf_op jit(solution)/shard_map/ppermute | solution.py:100
  55.8 3.6 %collective-permute-start.6 = (bf16[512,512]{1,0:T(8,128)(2,1)S(1)}, bf16[512,512]{1,0:T(8,128)(2,1)S(1)}, u32[]{:S(2)}, u32[]{:S(2)}) collective-permute-start(bf16[512,512]{1,0:T(8,128)(2,1)S(1)} %collective-permute-done.4.refs_1_), channel_id=1, source_target_pairs={{0,258},{1,257},{2,256},{3,259},{256,2},{257,1},{258,0},{259,3},{4... | collective-permute-start | bytes 1572872 | tf_op jit(solution)/shard_map/ppermute | solution.py:100
  59.5 8.6 %collective-permute-done.6.refs_3_ = bf16[512,512]{1,0:T(8,128)(2,1)S(1)} collective-permute-done((bf16[512,512]{1,0:T(8,128)(2,1)S(1)}, bf16[512,512]{1,0:T(8,128)(2,1)S(1)}, u32[]{:S(2)}, u32[]{:S(2)}) %collective-permute-start.6) | collective-permute-done | bytes 524320 | tf_op jit(solution)/shard_map/ppermute | solution.py:100
  68.1 2.1 %partial.1 = (f32[576,256]{1,0:T(8,128)S(1)}, f32[576,256]{1,0:T(8,128)S(1)}) custom-call(bf16[512,512]{1,0:T(8,128)(2,1)S(1)} %bitcast.22, bf16[512,512]{1,0:T(8,128)(2,1)S(1)} %collective-permute-done.4.refs_1_, bf16[512,512]{1,0:T(8,128)(2,1)S(1)} %collective-permute-done.5.refs_2_, bf16[512,512]{1,0:T(8,128)(2,1)S(1)} %collective-permute-done.6.refs_3_, ...), custom_call_target="tpu_custom_call" | custom-call | flops 1000000000 | bytes 6000000 | tf_op jit(solution)/shard_map/partial/pallas_call | solution.py:349
  70.3 2.1 %collective-permute-start.7 = (f32[576,256]{1,0:T(8,128)S(1)}, f32[576,256]{1,0:T(8,128)S(1)}, u32[]{:S(2)}, u32[]{:S(2)}) collective-permute-start(f32[576,256]{1,0:T(8,128)S(1)} %get-tuple-element.34), channel_id=1, source_target_pairs={{0,1},{1,0},{2,3},{3,2},{256,257},{257,256},{258,259},{259,258},{4... | collective-permute-start | bytes 1769480 | tf_op jit(solution)/shard_map/ppermute | solution.py:100
  72.3 2.0 %collective-permute-done.7.two_ref = f32[576,256]{1,0:T(8,128)S(1)} collective-permute-done((f32[576,256]{1,0:T(8,128)S(1)}, f32[576,256]{1,0:T(8,128)S(1)}, u32[]{:S(2)}, u32[]{:S(2)}) %collective-permute-start.7) | collective-permute-done | bytes 589856 | tf_op jit(solution)/shard_map/ppermute | solution.py:100
  74.4 1.9 %collective-permute-start.8 = (bf16[576,128]{1,0:T(8,128)(2,1)S(1)}, bf16[576,128]{1,0:T(8,128)(2,1)S(1)}, u32[]{:S(2)}, u32[]{:S(2)}) collective-permute-start(bf16[576,128]{1,0:T(8,128)(2,1)S(1)} %hidden.1.refs_0_), channel_id=1, source_target_pairs={{0,256},{1,259},{2,258},{3,257},{256,0},{257,3},{258,2},{259,1},{4... | collective-permute-start | bytes 442376 | tf_op jit(solution)/shard_map/ppermute | solution.py:100
  76.3 4.6 %collective-permute-start.9 = (bf16[576,128]{1,0:T(8,128)(2,1)S(1)}, bf16[576,128]{1,0:T(8,128)(2,1)S(1)}, u32[]{:S(2)}, u32[]{:S(2)}) collective-permute-start(bf16[576,128]{1,0:T(8,128)(2,1)S(1)} %hidden.1.refs_0_), channel_id=1, source_target_pairs={{0,259},{1,256},{2,257},{3,258},{256,3},{257,0},{258,1},{259,2},{4... | collective-permute-start | bytes 442376 | tf_op jit(solution)/shard_map/ppermute | solution.py:100
  81.6 3.6 %collective-permute-start.10 = (bf16[576,128]{1,0:T(8,128)(2,1)S(1)}, bf16[576,128]{1,0:T(8,128)(2,1)S(1)}, u32[]{:S(2)}, u32[]{:S(2)}) collective-permute-start(bf16[576,128]{1,0:T(8,128)(2,1)S(1)} %collective-permute-done.8.refs_1_), channel_id=1, source_target_pairs={{0,258},{1,257},{2,256},{3,259},{256,2},{257,1},{258,0},{259,3},{4... | collective-permute-start | bytes 442376 | tf_op jit(solution)/shard_map/ppermute | solution.py:100
  85.3 4.6 %collective-permute-done.10.refs_3_ = bf16[576,128]{1,0:T(8,128)(2,1)S(1)} collective-permute-done((bf16[576,128]{1,0:T(8,128)(2,1)S(1)}, bf16[576,128]{1,0:T(8,128)(2,1)S(1)}, u32[]{:S(2)}, u32[]{:S(2)}) %collective-permute-start.10) | collective-permute-done | bytes 147488 | tf_op jit(solution)/shard_map/ppermute | solution.py:100
  91.5 1.9 %collective-permute-start.11 = (bf16[576,512]{1,0:T(8,128)(2,1)S(1)}, bf16[576,512]{1,0:T(8,128)(2,1)S(1)}, u32[]{:S(2)}, u32[]{:S(2)}) collective-permute-start(bf16[576,512]{1,0:T(8,128)(2,1)S(1)} %get-tuple-element.40), channel_id=1, source_target_pairs={{0,1},{1,0},{2,3},{3,2},{256,257},{257,256},{258,259},{259,258},{4... | collective-permute-start | bytes 1769480 | tf_op jit(solution)/shard_map/ppermute | solution.py:100
  93.4 2.0 %collective-permute-done.11.two_ref = bf16[576,512]{1,0:T(8,128)(2,1)S(1)} collective-permute-done((bf16[576,512]{1,0:T(8,128)(2,1)S(1)}, bf16[576,512]{1,0:T(8,128)(2,1)S(1)}, u32[]{:S(2)}, u32[]{:S(2)}) %collective-permute-start.11) | collective-permute-done | bytes 589856 | tf_op jit(solution)/shard_map/ppermute | solution.py:100
  96.8 12.8 %all-to-all-start.1 = ((bf16[64,8,512]{2,1,0:T(8,128)(2,1)}), bf16[64,8,512]{2,1,0:T(8,128)(2,1)S(1)}, u32[]{:S(2)}, u32[]{:S(2)}) async-start(bf16[64,8,512]{2,1,0:T(8,128)(2,1)} %bitcast.12), calls=%async_computation.1 | async-start | bytes 1048576 | tf_op jit(solution)/shard_map/all_to_all | solution.py:370
  113.2 6.5 %collective-permute-done.12.two_ref = f32[96,512]{1,0:T(8,128)S(1)} collective-permute-done((f32[96,512]{1,0:T(8,128)S(1)}, f32[96,512]{1,0:T(8,128)S(1)}, u32[]{:S(2)}, u32[]{:S(2)}) %collective-permute-start.12) | collective-permute-done | bytes 196640 | tf_op jit(solution)/shard_map/ppermute | solution.py:100
  121.3 8.2 %all-to-all-done.1 = bf16[64,8,512]{2,1,0:T(8,128)(2,1)S(1)} async-done(((bf16[64,8,512]{2,1,0:T(8,128)(2,1)}), bf16[64,8,512]{2,1,0:T(8,128)(2,1)S(1)}, u32[]{:S(2)}, u32[]{:S(2)}) %all-to-all-start.1) | async-done | bytes 524320 | tf_op jit(solution)/shard_map/all_to_all | solution.py:370
  (46 shorter events, 13.6 us)
Async XLA Ops:
  0.6 19.8 %copy-start = (bf16[1,3584,128]{2,1,0:T(8,128)(2,1)S(1)}, bf16[1,3584,128]{2,1,0:T(8,128)(2,1)}, u32[]{:S(2)}) copy-start(bf16[1,3584,128]{2,1,0:T(8,128)(2,1)} %param.17) | copy-start | bytes 2752516
  0.6 19.8 %copy-start.1 = (bf16[1,3584,128]{2,1,0:T(8,128)(2,1)S(1)}, bf16[1,3584,128]{2,1,0:T(8,128)(2,1)}, u32[]{:S(2)}) copy-start(bf16[1,3584,128]{2,1,0:T(8,128)(2,1)} %param.18) | copy-start | bytes 2752516
  3.8 37.6 %all-to-all-start = ((bf16[64,8,512]{2,1,0:T(8,128)(2,1)}), bf16[64,8,512]{2,1,0:T(8,128)(2,1)S(1)}, u32[]{:S(2)}, u32[]{:S(2)}) async-start(bf16[64,8,512]{2,1,0:T(8,128)(2,1)} %bitcast.28), calls=%async_computation | async-start | bytes 1048576 | tf_op jit(solution)/shard_map/all_to_all | solution.py:329
  21.9 19.5 %collective-permute-start = (bf16[1792,256]{1,0:T(8,128)(2,1)S(1)}, bf16[1792,256]{1,0:T(8,128)(2,1)S(1)}, u32[]{:S(2)}, u32[]{:S(2)}) collective-permute-start(bf16[1792,256]{1,0:T(8,128)(2,1)S(1)} %get-tuple-element.26), channel_id=1, source_target_pairs={{0,1},{1,0},{2,3},{3,2},{256,257},{257,256},{258,259},{259,258},{4... | collective-permute-start | bytes 2752520 | tf_op jit(solution)/shard_map/ppermute | solution.py:100
  23.8 9.0 %collective-permute-start.1 = (bf16[128,896]{1,0:T(8,128)(2,1)S(1)}, bf16[128,896]{1,0:T(8,128)(2,1)S(1)}, u32[]{:S(2)}, u32[]{:S(2)}) collective-permute-start(bf16[128,896]{1,0:T(8,128)(2,1)S(1)} %get-tuple-element.28), channel_id=1, source_target_pairs={{0,256},{1,259},{2,258},{3,257},{256,0},{257,3},{258,2},{259,1},{4... | collective-permute-start | bytes 688136 | tf_op jit(solution)/shard_map/ppermute | solution.py:100
  26.6 12.6 %collective-permute-start.2 = (bf16[128,896]{1,0:T(8,128)(2,1)S(1)}, bf16[128,896]{1,0:T(8,128)(2,1)S(1)}, u32[]{:S(2)}, u32[]{:S(2)}) collective-permute-start(bf16[128,896]{1,0:T(8,128)(2,1)S(1)} %get-tuple-element.29), channel_id=1, source_target_pairs={{0,259},{1,256},{2,257},{3,258},{256,3},{257,0},{258,1},{259,2},{4... | collective-permute-start | bytes 688136 | tf_op jit(solution)/shard_map/ppermute | solution.py:100
  30.7 10.0 %collective-permute-start.3 = (bf16[128,896]{1,0:T(8,128)(2,1)S(1)}, bf16[128,896]{1,0:T(8,128)(2,1)S(1)}, u32[]{:S(2)}, u32[]{:S(2)}) collective-permute-start(bf16[128,896]{1,0:T(8,128)(2,1)S(1)} %get-tuple-element.30), channel_id=1, source_target_pairs={{0,2},{1,3},{2,0},{3,1},{256,258},{257,259},{258,256},{259,257},{4... | collective-permute-start | bytes 688136 | tf_op jit(solution)/shard_map/ppermute | solution.py:100
  41.4 14.4 %collective-permute-start.4 = (bf16[512,512]{1,0:T(8,128)(2,1)S(1)}, bf16[512,512]{1,0:T(8,128)(2,1)S(1)}, u32[]{:S(2)}, u32[]{:S(2)}) collective-permute-start(bf16[512,512]{1,0:T(8,128)(2,1)S(1)} %bitcast.20), channel_id=1, source_target_pairs={{0,256},{1,259},{2,258},{3,257},{256,0},{257,3},{258,2},{259,1},{4... | collective-permute-start | bytes 1572872 | tf_op jit(solution)/shard_map/ppermute | solution.py:100
  44.1 15.3 %collective-permute-start.5 = (bf16[512,512]{1,0:T(8,128)(2,1)S(1)}, bf16[512,512]{1,0:T(8,128)(2,1)S(1)}, u32[]{:S(2)}, u32[]{:S(2)}) collective-permute-start(bf16[512,512]{1,0:T(8,128)(2,1)S(1)} %bitcast.21), channel_id=1, source_target_pairs={{0,259},{1,256},{2,257},{3,258},{256,3},{257,0},{258,1},{259,2},{4... | collective-permute-start | bytes 1572872 | tf_op jit(solution)/shard_map/ppermute | solution.py:100
  55.8 12.3 %collective-permute-start.6 = (bf16[512,512]{1,0:T(8,128)(2,1)S(1)}, bf16[512,512]{1,0:T(8,128)(2,1)S(1)}, u32[]{:S(2)}, u32[]{:S(2)}) collective-permute-start(bf16[512,512]{1,0:T(8,128)(2,1)S(1)} %collective-permute-done.4.refs_1_), channel_id=1, source_target_pairs={{0,258},{1,257},{2,256},{3,259},{256,2},{257,1},{258,0},{259,3},{4... | collective-permute-start | bytes 1572872 | tf_op jit(solution)/shard_map/ppermute | solution.py:100
  70.2 19.6 %copy-start.7 = (bf16[128,896]{1,0:T(8,128)(2,1)S(1)}, bf16[128,896]{1,0:T(8,128)(2,1)}, u32[]{:S(2)}) copy-start(bf16[128,896]{1,0:T(8,128)(2,1)} %copy-done.6) | copy-start | bytes 688132
  70.2 19.6 %copy-start.9 = (bf16[128,896]{1,0:T(8,128)(2,1)S(1)}, bf16[128,896]{1,0:T(8,128)(2,1)}, u32[]{:S(2)}) copy-start(bf16[128,896]{1,0:T(8,128)(2,1)} %copy-done.8) | copy-start | bytes 688132
  70.3 19.6 %copy-start.11 = (bf16[128,896]{1,0:T(8,128)(2,1)S(1)}, bf16[128,896]{1,0:T(8,128)(2,1)}, u32[]{:S(2)}) copy-start(bf16[128,896]{1,0:T(8,128)(2,1)} %copy-done.10) | copy-start | bytes 688132
  70.3 4.0 %collective-permute-start.7 = (f32[576,256]{1,0:T(8,128)S(1)}, f32[576,256]{1,0:T(8,128)S(1)}, u32[]{:S(2)}, u32[]{:S(2)}) collective-permute-start(f32[576,256]{1,0:T(8,128)S(1)} %get-tuple-element.34), channel_id=1, source_target_pairs={{0,1},{1,0},{2,3},{3,2},{256,257},{257,256},{258,259},{259,258},{4... | collective-permute-start | bytes 1769480 | tf_op jit(solution)/shard_map/ppermute | solution.py:100
  74.4 7.2 %collective-permute-start.8 = (bf16[576,128]{1,0:T(8,128)(2,1)S(1)}, bf16[576,128]{1,0:T(8,128)(2,1)S(1)}, u32[]{:S(2)}, u32[]{:S(2)}) collective-permute-start(bf16[576,128]{1,0:T(8,128)(2,1)S(1)} %hidden.1.refs_0_), channel_id=1, source_target_pairs={{0,256},{1,259},{2,258},{3,257},{256,0},{257,3},{258,2},{259,1},{4... | collective-permute-start | bytes 442376 | tf_op jit(solution)/shard_map/ppermute | solution.py:100
  76.3 8.9 %collective-permute-start.9 = (bf16[576,128]{1,0:T(8,128)(2,1)S(1)}, bf16[576,128]{1,0:T(8,128)(2,1)S(1)}, u32[]{:S(2)}, u32[]{:S(2)}) collective-permute-start(bf16[576,128]{1,0:T(8,128)(2,1)S(1)} %hidden.1.refs_0_), channel_id=1, source_target_pairs={{0,259},{1,256},{2,257},{3,258},{256,3},{257,0},{258,1},{259,2},{4... | collective-permute-start | bytes 442376 | tf_op jit(solution)/shard_map/ppermute | solution.py:100
  81.6 8.2 %collective-permute-start.10 = (bf16[576,128]{1,0:T(8,128)(2,1)S(1)}, bf16[576,128]{1,0:T(8,128)(2,1)S(1)}, u32[]{:S(2)}, u32[]{:S(2)}) collective-permute-start(bf16[576,128]{1,0:T(8,128)(2,1)S(1)} %collective-permute-done.8.refs_1_), channel_id=1, source_target_pairs={{0,258},{1,257},{2,256},{3,259},{256,2},{257,1},{258,0},{259,3},{4... | collective-permute-start | bytes 442376 | tf_op jit(solution)/shard_map/ppermute | solution.py:100
  91.5 3.9 %collective-permute-start.11 = (bf16[576,512]{1,0:T(8,128)(2,1)S(1)}, bf16[576,512]{1,0:T(8,128)(2,1)S(1)}, u32[]{:S(2)}, u32[]{:S(2)}) collective-permute-start(bf16[576,512]{1,0:T(8,128)(2,1)S(1)} %get-tuple-element.40), channel_id=1, source_target_pairs={{0,1},{1,0},{2,3},{3,2},{256,257},{257,256},{258,259},{259,258},{4... | collective-permute-start | bytes 1769480 | tf_op jit(solution)/shard_map/ppermute | solution.py:100
  95.4 14.9 %copy-start.4 = (bf16[3,1,32,576]{3,2,1,0:T(8,128)(2,1)S(1)}, bf16[3,1,32,576]{3,2,1,0:T(8,128)(2,1)}, u32[]{:S(2)}) copy-start(bf16[3,1,32,576]{3,2,1,0:T(8,128)(2,1)} %param.12) | copy-start | bytes 331780
  95.4 14.9 %copy-start.5 = (bf16[3,1,576]{2,0,1:T(4,128)(2,1)S(1)}, bf16[3,1,576]{2,0,1:T(4,128)(2,1)}, u32[]{:S(2)}) copy-start(bf16[3,1,576]{2,0,1:T(4,128)(2,1)} %param.11) | copy-start | bytes 10372
  96.8 16.4 %copy-start.12 = (s32[3,12,8]{1,2,0:T(8,128)S(1)}, s32[3,12,8]{1,2,0:T(8,128)}, u32[]{:S(2)}) copy-start(s32[3,12,8]{1,2,0:T(8,128)} %param.15) | copy-start | bytes 3460
  96.8 23.7 %copy-start.13 = (f32[3,12,8]{1,2,0:T(8,128)S(1)}, f32[3,12,8]{1,2,0:T(8,128)}, u32[]{:S(2)}) copy-start(f32[3,12,8]{1,2,0:T(8,128)} %param.16) | copy-start | bytes 3460
  96.8 32.7 %all-to-all-start.1 = ((bf16[64,8,512]{2,1,0:T(8,128)(2,1)}), bf16[64,8,512]{2,1,0:T(8,128)(2,1)S(1)}, u32[]{:S(2)}, u32[]{:S(2)}) async-start(bf16[64,8,512]{2,1,0:T(8,128)(2,1)} %bitcast.12), calls=%async_computation.1 | async-start | bytes 1048576 | tf_op jit(solution)/shard_map/all_to_all | solution.py:370
  111.2 8.6 %collective-permute-start.12 = (f32[96,512]{1,0:T(8,128)S(1)}, f32[96,512]{1,0:T(8,128)S(1)}, u32[]{:S(2)}, u32[]{:S(2)}) collective-permute-start(f32[96,512]{1,0:T(8,128)S(1)} %get-tuple-element.43), channel_id=1, source_target_pairs={{0,256},{1,257},{2,258},{3,259},{256,0},{257,1},{258,2},{259,3},{4... | collective-permute-start | bytes 589832 | tf_op jit(solution)/shard_map/ppermute | solution.py:100
  (5 other events, 18.1 us)

commit v5 on v4

--- a/solution.py
+++ b/solution.py
@@ -36,13 +36,13 @@
         out_shape=out_shape,
         in_specs=in_specs,
         out_specs=VMEM if single else [VMEM] * len(out_shape),
-        compiler_params=pltpu.CompilerParams(vmem_limit_bytes=40 * 1024 * 1024),
+        compiler_params=pltpu.CompilerParams(vmem_limit_bytes=20 * 1024 * 1024),
         cost_estimate=pl.CostEstimate(flops=flops, bytes_accessed=moved, transcendentals=0),
         name=name,
     )
 
 
-def attend_body(length_ref, q_ref, cache_ref, new_ref, send_ref, keep_ref):
+def attend_body(_, length_ref, q_ref, cache_ref, new_ref, send_ref, keep_ref):
     section, length = lax.axis_index("sec").astype(jnp.int32), length_ref[0]
     q = q_ref[...]
     rows, local_length = q.shape[0], cache_ref.shape[1]
@@ -104,10 +104,16 @@
     return permute(value, lambda d: d ^ k)
 
 
-def gather(own):
-    near = permute(own, lambda d: d ^ (4 + 2 * (d % 2)))
-    crossed = permute(own, lambda d: d ^ (7 - 2 * (d % 2)))
-    return own, near, crossed, permute(near, lambda d: d ^ (6 - 2 * (d % 2)))
+def to_near(value):
+    return permute(value, lambda d: d ^ (4 + 2 * (d % 2)))
+
+
+def to_crossed(value):
+    return permute(value, lambda d: d ^ (7 - 2 * (d % 2)))
+
+
+def onward(value):
+    return permute(value, lambda d: d ^ (6 - 2 * (d % 2)))
 
 
 def named_slots(routes, experts):
@@ -171,7 +177,7 @@
     return tail.astype(BF)
 
 
-def gates_body(routes_ref, gates_ref, out_ref):
+def gates_body(_, routes_ref, gates_ref, out_ref):
     steps, tokens, picks = routes_ref.shape
     rows = out_ref.shape[2]
     experts = rows // ROWS
@@ -199,19 +205,24 @@
                     ).astype(BF)
 
 
-def slices_body(gate_ref, up_ref, down_ref, other_ref, *down_outs):
+def slices_body(_, gate_ref, up_ref, down_ref, other_ref, own_ref, near_ref, crossed_ref):
     here = place_here()
     units = gate_ref.shape[1]
     part = gate_ref.shape[0] // 8
     core = here % 2
+
+    def columns(target):
+        return down_ref[:, pl.ds(pl.multiple_of((target // 2) * 2 * part, 128), 2 * part)]
+
     for m, source in enumerate(sources(here ^ 1)):
         offset = pl.multiple_of(source * part, HALF)
         rows = slice(m * part, (m + 1) * part)
         other_ref[rows, :units] = gate_ref[pl.ds(offset, part), :]
         other_ref[rows, units:] = up_ref[pl.ds(offset, part), :]
-    targets = here, here ^ (4 + 2 * core), here ^ (7 - 2 * core), here ^ 2
-    for target, out in zip(targets, down_outs):
-        out[...] = down_ref[:, pl.ds(pl.multiple_of((target // 2) * 2 * part, 128), 2 * part)]
+    own_ref[...] = columns(here)
+    near_ref[:units, :] = columns(here ^ (4 + 2 * core))
+    near_ref[units:, :] = columns(here ^ 2)
+    crossed_ref[...] = columns(here ^ (7 - 2 * core))
 
 
 def partial_body(*refs):
@@ -233,38 +244,41 @@
             axis=1,
         )
 
-    total = jnp.zeros((rows, 2 * wide), F32)
+    total = jnp.zeros((rows, wide), F32)
     for m in range(4):
         total = total + dot(pieces[m][:, :part], weights(m, 0, part))
-    keep_ref[:rows, :] = total[:, :wide]
-    send_ref[:rows, :] = total[:, wide:]
+    keep_ref[:rows, :] = total
+    send_ref[:rows, :] = total.astype(BF)
     tail = jnp.concatenate([pieces[m][:, part:] for m in range(4)], axis=1)
     blocks = part // HALF
     source = iota((blocks * experts, rows), 0)
     wanted = (source % experts) * ROWS + source // experts
     chosen = (iota((blocks * experts, rows), 1) == wanted).astype(BF)
     ninth = dot(chosen, tail).astype(BF)
-    total = jnp.zeros((experts, 2 * wide), F32)
+    total = jnp.zeros((experts, wide), F32)
     for i in range(blocks):
         block_weights = jnp.concatenate([weights(m, i * HALF, HALF) for m in range(4)], axis=0)
         total = total + dot(ninth[i * experts : (i + 1) * experts], block_weights)
-    keep_ref[rows:, :] = total[:, :wide]
-    send_ref[rows:, :] = total[:, wide:]
-
-
-def hidden_body(one_ref, two_ref, out_ref):
-    units = out_ref.shape[1]
-    gate = one_ref[:, :units] + two_ref[:, :units]
-    up = one_ref[:, units:] + two_ref[:, units:]
-    out_ref[...] = (gate / (1.0 + jnp.exp(-gate)) * up).astype(BF)
-
-
-def down_body(*refs):
-    hidden, down, (keep_ref, send_ref) = refs[:4], refs[4:8], refs[8:]
-    part = keep_ref.shape[1]
-    total = jnp.zeros((hidden[0].shape[0], 2 * part), F32)
-    for m in range(4):
-        total = total + dot(hidden[m][...], down[m][...])
+    keep_ref[rows:, :] = total
+    send_ref[rows:, :] = total.astype(BF)
+
+
+def hidden_body(mine_ref, other_ref, out_ref):
+    units = out_ref.shape[1] // 2
+    for half in range(2):
+        mine, other = 2 * half * units, 2 * (1 - half) * units
+        gate = mine_ref[:, mine : mine + units] + other_ref[:, other : other + units].astype(F32)
+        mine, other = mine + units, other + units
+        up = mine_ref[:, mine : mine + units] + other_ref[:, other : other + units].astype(F32)
+        out_ref[:, half * units : (half + 1) * units] = (
+            gate / (1.0 + jnp.exp(-gate)) * up
+        ).astype(BF)
+
+
+def down_body(chip_ref, near_ref, far_ref, own_w, near_w, crossed_w, far_w, keep_ref, send_ref):
+    part, units = keep_ref.shape[1], own_w.shape[0]
+    total = dot(chip_ref[:, :units], own_w[...]) + dot(near_ref[:, :units], near_w[:units, :])
+    total = total + dot(near_ref[:, units:], crossed_w[...]) + dot(far_ref[...], far_w[...])
     first = place_here() % 2 == 0
     keep_ref[...] = jnp.where(first, total[:, :part], total[:, part:])
     send_ref[:, :part] = jnp.where(first, total[:, part:], total[:, :part]).astype(BF)
@@ -325,48 +339,55 @@
         cost_estimate=pl.CostEstimate(flops=10**8, bytes_accessed=10**6, transcendentals=0),
         name="pack",
     )(token_rows, jnp.swapaxes(routes, 1, 2))
-    packed, down_proj = lax.optimization_barrier((packed, down_proj))
     arrived = lax.all_to_all(
         packed.reshape(experts, ROWS, part + HALF), "grp", split_axis=0, concat_axis=0, tiled=True
     ).reshape(rows, part + HALF)
 
     gate_proj, up_proj = gate_proj.reshape(width, units), up_proj.reshape(width, units)
-    other, *down = call(
+    other, own_down, near_down, crossed_down = call(
         slices_body,
-        [jax.ShapeDtypeStruct((width // 2, 2 * units), BF)]
-        + [jax.ShapeDtypeStruct((units, 2 * part), BF)] * 4,
-        [VMEM] * 3, 10**6, 5 * 10**6, "slices",
-    )(gate_proj, up_proj, down_proj.reshape(units, width))
+        [
+            jax.ShapeDtypeStruct((width // 2, 2 * units), BF),
+            jax.ShapeDtypeStruct((units, 2 * part), BF),
+            jax.ShapeDtypeStruct((2 * units, 2 * part), BF),
+            jax.ShapeDtypeStruct((units, 2 * part), BF),
+        ],
+        [HBM] + [VMEM] * 3, 10**6, 5 * 10**6, "slices",
+    )(packed, gate_proj, up_proj, down_proj.reshape(units, width))
     other = swap(other, 1)
-    down = [
-        down[0],
-        permute(down[1], lambda d: d ^ (4 + 2 * (d % 2))),
-        permute(down[2], lambda d: d ^ (7 - 2 * (d % 2))),
-        swap(down[3], 2),
-    ]
-
-    arrived, other, down = lax.optimization_barrier((arrived, other, down))
+    near_down, crossed_down = to_near(near_down), to_crossed(crossed_down)
+    arrived, near_down, crossed_down = lax.optimization_barrier(
+        (arrived, near_down, crossed_down)
+    )
+    far_down = onward(near_down[units:])
+
+    near = to_near(arrived)
+    crossed = to_crossed(arrived)
     keep, send = call(
-        partial_body, [jax.ShapeDtypeStruct((rows + experts, 2 * units), F32)] * 2,
+        partial_body,
+        [
+            jax.ShapeDtypeStruct((rows + experts, 4 * units), F32),
+            jax.ShapeDtypeStruct((rows + experts, 4 * units), BF),
+        ],
         [VMEM] * 7, 10**9, 6 * 10**6, "partial",
-    )(*gather(arrived), gate_proj, up_proj, other)
+    )(arrived, near, crossed, onward(near), gate_proj, up_proj, other)
     hidden = call(
-        hidden_body, jax.ShapeDtypeStruct((rows + experts, units), BF), [VMEM] * 2,
+        hidden_body, jax.ShapeDtypeStruct((rows + experts, 2 * units), BF), [VMEM] * 2,
         10**7, 10**6, "hidden",
     )(keep, swap(send, 1))
+    near = to_near(hidden)
     keep, send = call(
         down_body,
         [
             jax.ShapeDtypeStruct((rows + experts, part), F32),
             jax.ShapeDtypeStruct((rows + experts, part + HALF), BF),
         ],
-        [VMEM] * 8, 10**9, 3 * 10**6, "down",
-    )(*gather(hidden), *down)
+        [VMEM] * 7, 10**9, 3 * 10**6, "down",
+    )(hidden, near, onward(near[:, :units]), own_down, near_down, crossed_down, far_down)
     outgoing = call(
         repack_body, jax.ShapeDtypeStruct((rows, part + HALF), BF), [VMEM] * 2,
         10**8, 2 * 10**6, "repack",
     )(keep, swap(send, 1))
-    outgoing, lengths, gates = lax.optimization_barrier((outgoing, lengths, route_gates))
     returned = lax.all_to_all(
         outgoing.reshape(experts, ROWS, part + HALF), "grp", split_axis=0, concat_axis=0, tiled=True
     ).reshape(rows, part + HALF)
@@ -374,8 +395,9 @@
     heads = queries.shape[2]
     send, keep = call(
         attend_body, [jax.ShapeDtypeStruct((steps * heads, KL // 2 + 256), F32)] * 2,
-        [SMEM, VMEM, VMEM, VMEM], 3 * 10**8, 2 * 10**6, "attend",
+        [HBM, SMEM, VMEM, VMEM, VMEM], 3 * 10**8, 2 * 10**6, "attend",
     )(
+        outgoing,
         lengths,
         queries.reshape(steps * heads, queries.shape[3]),
         latent_cache[0].T,
@@ -388,8 +410,8 @@
     gates = call(
         gates_body,
         jax.ShapeDtypeStruct((2, 16 * (steps + part // HALF), rows), BF),
-        [VMEM, VMEM], 10**8, 10**6, "gates",
-    )(routes, gates)
+        [HBM, VMEM, VMEM], 10**8, 10**6, "gates",
+    )(outgoing, routes, route_gates)
     moe = call(
         combine_body, jax.ShapeDtypeStruct((steps, tokens, part), BF), [VMEM, VMEM],
         10**8, 10**6, "combine",

time: 132 us -> 129 us (0.977)
  starting transfers between devices: 66.1 us -> 55 us
  waiting for transfers between devices: 47.4 us -> 55.2 us
    ppermute x13 -> x12, starting transfers between devices: 36.6 us -> 28.2 us  [permute(): return lax.ppermute(value, LINE, [(d, target(d)) for d in range(8)])]
    ppermute x13 -> x12, waiting for transfers between devices: 39.2 us -> 43.6 us  [permute(): return lax.ppermute(value, LINE, [(d, target(d)) for d in range(8)])]
    all_to_all x1, starting transfers between devices: 12.8 us -> 10.1 us  [local(): lax.all_to_all(outgoing.reshape(experts, ROWS, part + HALF), 'grp', split...]
    all_to_all x1, waiting for transfers between devices: 0.01 us -> 2.63 us  [local(): lax.all_to_all(packed.reshape(experts, ROWS, part + HALF), 'grp', split_a...]
    unnamed x29 -> x28, local copies, waits for them, and re-layouts: 3.38 us -> 4.2 us
  transfers between devices with their start and end apart: 15 -> 14, of which waited for: 10 -> 12; matrix products, arithmetic and copies ran while one was open for 0% -> 0% of each run, Pallas kernels for 2% -> 2%
where the time goes in v5:
time: 129 us; the launch traced here: 128 us
  waiting for transfers between devices  55.2 us (43%)
  starting transfers between devices  55 us (43%)
  Pallas kernels  12.1 us (9%)
  local copies, waits for them, and re-layouts  4.23 us (3%)
  between operations  1.58 us (1%)
    ppermute x12, waiting for transfers between devices, permute(): return lax.ppermute(value, LINE, [(d, target(d)) for d in range(8)])  43.6 us
    ppermute x12, starting transfers between devices, permute(): return lax.ppermute(value, LINE, [(d, target(d)) for d in range(8)])  28.2 us
    all_to_all x1, starting transfers between devices, local(): lax.all_to_all(packed.reshape(experts, ROWS, part + HALF), 'grp', split_a...  16.7 us
    all_to_all x1, starting transfers between devices, local(): lax.all_to_all(outgoing.reshape(experts, ROWS, part + HALF), 'grp', split...  10.1 us
    all_to_all x1, waiting for transfers between devices, local(): lax.all_to_all(outgoing.reshape(experts, ROWS, part + HALF), 'grp', split...  8.93 us
    unnamed x28, local copies, waits for them, and re-layouts  4.2 us
    pallas_call x1, Pallas kernels, local(): pl.pallas_call(pack_body, out_shape=jax.ShapeDtypeStruct((rows, part + HA...  3.13 us
    all_to_all x1, waiting for transfers between devices, local(): lax.all_to_all(packed.reshape(experts, ROWS, part + HALF), 'grp', split_a...  2.63 us
  transfers between devices with their start and end apart: 14, of which 12 were waited for; matrix products, arithmetic and copies ran while one was open for 0% of the time, Pallas kernels for 2%

profile of v5, /device:TPU:6, one launch (start us, length us, event | category | flops | bytes accessed | tf_op | source)
XLA Modules:
  0.0 128.1 jit_solution(15059760443507565531)
XLA Ops:
  0.6 3.1 %pack.1._ = bf16[512,512]{1,0:T(8,128)(2,1)} custom-call(bf16[3,12,3584]{2,1,0:T(8,128)(2,1)} %tokens_ref.1, s32[3,8,12]{2,1,0:T(8,128)} %bitcast.29), custom_call_target="tpu_custom_call" | custom-call | flops 100000000 | bytes 1000000 | tf_op jit(solution)/shard_map/pack/pallas_call | solution.py:329
  3.8 16.7 %all-to-all-start = ((bf16[64,8,512]{2,1,0:T(8,128)(2,1)}), bf16[64,8,512]{2,1,0:T(8,128)(2,1)S(1)}, u32[]{:S(2)}, u32[]{:S(2)}) async-start(bf16[64,8,512]{2,1,0:T(8,128)(2,1)} %bitcast.16), calls=%async_computation | async-start | bytes 1048576 | tf_op jit(solution)/shard_map/all_to_all | solution.py:342
  24.8 2.7 %collective-permute-start = (bf16[256,896]{1,0:T(8,128)(2,1)S(1)}, bf16[256,896]{1,0:T(8,128)(2,1)S(1)}, u32[]{:S(2)}, u32[]{:S(2)}) collective-permute-start(bf16[256,896]{1,0:T(8,128)(2,1)S(1)} %get-tuple-element.15), channel_id=1, source_target_pairs={{0,256},{1,259},{2,258},{3,257},{256,0},{257,3},{258,2},{259,1},{4... | collective-permute-start | bytes 1376264 | tf_op jit(solution)/shard_map/ppermute | solution.py:100
  27.5 3.2 %collective-permute-start.1 = (bf16[128,896]{1,0:T(8,128)(2,1)S(1)}, bf16[128,896]{1,0:T(8,128)(2,1)S(1)}, u32[]{:S(2)}, u32[]{:S(2)}) collective-permute-start(bf16[128,896]{1,0:T(8,128)(2,1)S(1)} %get-tuple-element.16), channel_id=1, source_target_pairs={{0,259},{1,256},{2,257},{3,258},{256,3},{257,0},{258,1},{259,2},{4... | collective-permute-start | bytes 688136 | tf_op jit(solution)/shard_map/ppermute | solution.py:100
  30.7 6.7 %collective-permute-done.1.crossed_w = bf16[128,896]{1,0:T(8,128)(2,1)S(1)} collective-permute-done((bf16[128,896]{1,0:T(8,128)(2,1)S(1)}, bf16[128,896]{1,0:T(8,128)(2,1)S(1)}, u32[]{:S(2)}, u32[]{:S(2)}) %collective-permute-start.1) | collective-permute-done | bytes 229408 | tf_op jit(solution)/shard_map/ppermute | solution.py:100
  37.6 2.6 %all-to-all-done = bf16[64,8,512]{2,1,0:T(8,128)(2,1)S(1)} async-done(((bf16[64,8,512]{2,1,0:T(8,128)(2,1)}), bf16[64,8,512]{2,1,0:T(8,128)(2,1)S(1)}, u32[]{:S(2)}, u32[]{:S(2)}) %all-to-all-start) | async-done | bytes 524320 | tf_op jit(solution)/shard_map/all_to_all | solution.py:342
  40.2 2.7 %collective-permute-start.2 = (bf16[512,512]{1,0:T(8,128)(2,1)S(1)}, bf16[512,512]{1,0:T(8,128)(2,1)S(1)}, u32[]{:S(2)}, u32[]{:S(2)}) collective-permute-start(bf16[512,512]{1,0:T(8,128)(2,1)S(1)} %bitcast.21), channel_id=1, source_target_pairs={{0,256},{1,259},{2,258},{3,257},{256,0},{257,3},{258,2},{259,1},{4... | collective-permute-start | bytes 1572872 | tf_op jit(solution)/shard_map/ppermute | solution.py:100
  44.9 3.2 %collective-permute-start.3 = (bf16[512,512]{1,0:T(8,128)(2,1)S(1)}, bf16[512,512]{1,0:T(8,128)(2,1)S(1)}, u32[]{:S(2)}, u32[]{:S(2)}) collective-permute-start(bf16[512,512]{1,0:T(8,128)(2,1)S(1)} %bitcast.22), channel_id=1, source_target_pairs={{0,259},{1,256},{2,257},{3,258},{256,3},{257,0},{258,1},{259,2},{4... | collective-permute-start | bytes 1572872 | tf_op jit(solution)/shard_map/ppermute | solution.py:100
  48.1 4.7 %collective-permute-done.2.refs_1_ = bf16[512,512]{1,0:T(8,128)(2,1)S(1)} collective-permute-done((bf16[512,512]{1,0:T(8,128)(2,1)S(1)}, bf16[512,512]{1,0:T(8,128)(2,1)S(1)}, u32[]{:S(2)}, u32[]{:S(2)}) %collective-permute-start.2) | collective-permute-done | bytes 524320 | tf_op jit(solution)/shard_map/ppermute | solution.py:100
  54.7 2.2 %collective-permute-done.3.refs_2_ = bf16[512,512]{1,0:T(8,128)(2,1)S(1)} collective-permute-done((bf16[512,512]{1,0:T(8,128)(2,1)S(1)}, bf16[512,512]{1,0:T(8,128)(2,1)S(1)}, u32[]{:S(2)}, u32[]{:S(2)}) %collective-permute-start.3) | collective-permute-done | bytes 524320 | tf_op jit(solution)/shard_map/ppermute | solution.py:100
  56.9 8.1 %collective-permute-done.4.refs_3_ = bf16[512,512]{1,0:T(8,128)(2,1)S(1)} collective-permute-done((bf16[512,512]{1,0:T(8,128)(2,1)S(1)}, bf16[512,512]{1,0:T(8,128)(2,1)S(1)}, u32[]{:S(2)}, u32[]{:S(2)}) %collective-permute-start.4) | collective-permute-done | bytes 524320 | tf_op jit(solution)/shard_map/ppermute | solution.py:100
  65.0 2.1 %partial.1 = (f32[576,512]{1,0:T(8,128)S(1)}, bf16[576,512]{1,0:T(8,128)(2,1)S(1)}) custom-call(bf16[512,512]{1,0:T(8,128)(2,1)S(1)} %bitcast.23, bf16[512,512]{1,0:T(8,128)(2,1)S(1)} %collective-permute-done.2.refs_1_, bf16[512,512]{1,0:T(8,128)(2,1)S(1)} %collective-permute-done.3.refs_2_, bf16[512,512]{1,0:T(8,128)(2,1)S(1)} %collective-permute-done.4.refs_3_, ...), custom_call_target="tpu_custom_call" | custom-call | flops 1000000000 | bytes 6000000 | tf_op jit(solution)/shard_map/partial/pallas_call | solution.py:366
  67.1 1.9 %collective-permute-start.6 = (bf16[576,512]{1,0:T(8,128)(2,1)S(1)}, bf16[576,512]{1,0:T(8,128)(2,1)S(1)}, u32[]{:S(2)}, u32[]{:S(2)}) collective-permute-start(bf16[576,512]{1,0:T(8,128)(2,1)S(1)} %get-tuple-element.20), channel_id=1, source_target_pairs={{0,1},{1,0},{2,3},{3,2},{256,257},{257,256},{258,259},{259,258},{4... | collective-permute-start | bytes 1769480 | tf_op jit(solution)/shard_map/ppermute | solution.py:100
  69.1 2.0 %collective-permute-done.6.other_ref = bf16[576,512]{1,0:T(8,128)(2,1)S(1)} collective-permute-done((bf16[576,512]{1,0:T(8,128)(2,1)S(1)}, bf16[576,512]{1,0:T(8,128)(2,1)S(1)}, u32[]{:S(2)}, u32[]{:S(2)}) %collective-permute-start.6) | collective-permute-done | bytes 589856 | tf_op jit(solution)/shard_map/ppermute | solution.py:100
  71.3 1.9 %collective-permute-start.7 = (bf16[576,256]{1,0:T(8,128)(2,1)S(1)}, bf16[576,256]{1,0:T(8,128)(2,1)S(1)}, u32[]{:S(2)}, u32[]{:S(2)}) collective-permute-start(bf16[576,256]{1,0:T(8,128)(2,1)S(1)} %hidden.1.chip_ref), channel_id=1, source_target_pairs={{0,256},{1,259},{2,258},{3,257},{256,0},{257,3},{258,2},{259,1},{4... | collective-permute-start | bytes 884744 | tf_op jit(solution)/shard_map/ppermute | solution.py:100
  73.2 3.0 %collective-permute-start.9 = (bf16[128,896]{1,0:T(8,128)(2,1)S(1)}, bf16[128,896]{1,0:T(8,128)(2,1)S(1)}, u32[]{:S(2)}, u32[]{:S(2)}) collective-permute-start(bf16[128,896]{1,0:T(8,128)(2,1)S(1)} %slice.7), channel_id=1, source_target_pairs={{0,258},{1,257},{2,256},{3,259},{256,2},{257,1},{258,0},{259,3},{4... | collective-permute-start | bytes 688136 | tf_op jit(solution)/shard_map/ppermute | solution.py:100
  76.2 5.7 %collective-permute-done.7.near_ref = bf16[576,256]{1,0:T(8,128)(2,1)S(1)} collective-permute-done((bf16[576,256]{1,0:T(8,128)(2,1)S(1)}, bf16[576,256]{1,0:T(8,128)(2,1)S(1)}, u32[]{:S(2)}, u32[]{:S(2)}) %collective-permute-start.7) | collective-permute-done | bytes 294944 | tf_op jit(solution)/shard_map/ppermute | solution.py:100
  81.9 1.9 %collective-permute-start.8 = (bf16[576,128]{1,0:T(8,128)(2,1)S(1)}, bf16[576,128]{1,0:T(8,128)(2,1)S(1)}, u32[]{:S(2)}, u32[]{:S(2)}) collective-permute-start(bf16[576,128]{1,0:T(8,128)(2,1)S(1)} %slice.8), channel_id=1, source_target_pairs={{0,258},{1,257},{2,256},{3,259},{256,2},{257,1},{258,0},{259,3},{4... | collective-permute-start | bytes 442376 | tf_op jit(solution)/shard_map/ppermute | solution.py:100
  83.9 6.3 %collective-permute-done.8.far_ref = bf16[576,128]{1,0:T(8,128)(2,1)S(1)} collective-permute-done((bf16[576,128]{1,0:T(8,128)(2,1)S(1)}, bf16[576,128]{1,0:T(8,128)(2,1)S(1)}, u32[]{:S(2)}, u32[]{:S(2)}) %collective-permute-start.8) | collective-permute-done | bytes 147488 | tf_op jit(solution)/shard_map/ppermute | solution.py:100
  91.8 1.9 %collective-permute-start.10 = (bf16[576,512]{1,0:T(8,128)(2,1)S(1)}, bf16[576,512]{1,0:T(8,128)(2,1)S(1)}, u32[]{:S(2)}, u32[]{:S(2)}) collective-permute-start(bf16[576,512]{1,0:T(8,128)(2,1)S(1)} %get-tuple-element.25), channel_id=1, source_target_pairs={{0,1},{1,0},{2,3},{3,2},{256,257},{257,256},{258,259},{259,258},{4... | collective-permute-start | bytes 1769480 | tf_op jit(solution)/shard_map/ppermute | solution.py:100
  93.8 2.0 %collective-permute-done.10.two_ref = bf16[576,512]{1,0:T(8,128)(2,1)S(1)} collective-permute-done((bf16[576,512]{1,0:T(8,128)(2,1)S(1)}, bf16[576,512]{1,0:T(8,128)(2,1)S(1)}, u32[]{:S(2)}, u32[]{:S(2)}) %collective-permute-start.10) | collective-permute-done | bytes 589856 | tf_op jit(solution)/shard_map/ppermute | solution.py:100
  97.1 10.1 %all-to-all-start.1 = ((bf16[64,8,512]{2,1,0:T(8,128)(2,1)}), bf16[64,8,512]{2,1,0:T(8,128)(2,1)S(1)}, u32[]{:S(2)}, u32[]{:S(2)}) async-start(bf16[64,8,512]{2,1,0:T(8,128)(2,1)} %bitcast.12), calls=%async_computation.1 | async-start | bytes 1048576 | tf_op jit(solution)/shard_map/all_to_all | solution.py:391
  111.6 5.7 %collective-permute-done.11.two_ref = f32[96,512]{1,0:T(8,128)S(1)} collective-permute-done((f32[96,512]{1,0:T(8,128)S(1)}, f32[96,512]{1,0:T(8,128)S(1)}, u32[]{:S(2)}, u32[]{:S(2)}) %collective-permute-start.11) | collective-permute-done | bytes 196640 | tf_op jit(solution)/shard_map/ppermute | solution.py:100
  118.1 8.9 %all-to-all-done.1 = bf16[64,8,512]{2,1,0:T(8,128)(2,1)S(1)} async-done(((bf16[64,8,512]{2,1,0:T(8,128)(2,1)}), bf16[64,8,512]{2,1,0:T(8,128)(2,1)S(1)}, u32[]{:S(2)}, u32[]{:S(2)}) %all-to-all-start.1) | async-done | bytes 524320 | tf_op jit(solution)/shard_map/all_to_all | solution.py:391
  (44 shorter events, 17.1 us)
Async XLA Ops:
  0.6 19.9 %copy-start.1 = (bf16[1,3584,128]{2,1,0:T(8,128)(2,1)S(1)}, bf16[1,3584,128]{2,1,0:T(8,128)(2,1)}, u32[]{:S(2)}) copy-start(bf16[1,3584,128]{2,1,0:T(8,128)(2,1)} %param.17) | copy-start | bytes 2752516
  3.8 16.8 %copy-start = (bf16[512,512]{1,0:T(8,128)(2,1)S(1)}, bf16[512,512]{1,0:T(8,128)(2,1)}, u32[]{:S(2)}) copy-start(bf16[512,512]{1,0:T(8,128)(2,1)} %pack.1._) | copy-start | bytes 1572868
  3.8 36.4 %all-to-all-start = ((bf16[64,8,512]{2,1,0:T(8,128)(2,1)}), bf16[64,8,512]{2,1,0:T(8,128)(2,1)S(1)}, u32[]{:S(2)}, u32[]{:S(2)}) async-start(bf16[64,8,512]{2,1,0:T(8,128)(2,1)} %bitcast.16), calls=%async_computation | async-start | bytes 1048576 | tf_op jit(solution)/shard_map/all_to_all | solution.py:342
  20.5 1.2 copy-start.2
  22.9 42.1 %copy-start.3 = (bf16[1,3584,128]{2,1,0:T(8,128)(2,1)S(1)}, bf16[1,3584,128]{2,1,0:T(8,128)(2,1)}, u32[]{:S(2)}) copy-start(bf16[1,3584,128]{2,1,0:T(8,128)(2,1)} %param.18) | copy-start | bytes 2752516
  24.8 12.8 %collective-permute-start = (bf16[256,896]{1,0:T(8,128)(2,1)S(1)}, bf16[256,896]{1,0:T(8,128)(2,1)S(1)}, u32[]{:S(2)}, u32[]{:S(2)}) collective-permute-start(bf16[256,896]{1,0:T(8,128)(2,1)S(1)} %get-tuple-element.15), channel_id=1, source_target_pairs={{0,256},{1,259},{2,258},{3,257},{256,0},{257,3},{258,2},{259,1},{4... | collective-permute-start | bytes 1376264 | tf_op jit(solution)/shard_map/ppermute | solution.py:100
  27.5 9.9 %collective-permute-start.1 = (bf16[128,896]{1,0:T(8,128)(2,1)S(1)}, bf16[128,896]{1,0:T(8,128)(2,1)S(1)}, u32[]{:S(2)}, u32[]{:S(2)}) collective-permute-start(bf16[128,896]{1,0:T(8,128)(2,1)S(1)} %get-tuple-element.16), channel_id=1, source_target_pairs={{0,259},{1,256},{2,257},{3,258},{256,3},{257,0},{258,1},{259,2},{4... | collective-permute-start | bytes 688136 | tf_op jit(solution)/shard_map/ppermute | solution.py:100
  40.2 12.5 %collective-permute-start.2 = (bf16[512,512]{1,0:T(8,128)(2,1)S(1)}, bf16[512,512]{1,0:T(8,128)(2,1)S(1)}, u32[]{:S(2)}, u32[]{:S(2)}) collective-permute-start(bf16[512,512]{1,0:T(8,128)(2,1)S(1)} %bitcast.21), channel_id=1, source_target_pairs={{0,256},{1,259},{2,258},{3,257},{256,0},{257,3},{258,2},{259,1},{4... | collective-permute-start | bytes 1572872 | tf_op jit(solution)/shard_map/ppermute | solution.py:100
  43.0 11.7 %collective-permute-start.5 = (bf16[1792,256]{1,0:T(8,128)(2,1)}, bf16[1792,256]{1,0:T(8,128)(2,1)S(1)}, u32[]{:S(2)}, u32[]{:S(2)}) collective-permute-start(bf16[1792,256]{1,0:T(8,128)(2,1)} %copy-done.8), channel_id=1, source_target_pairs={{0,1},{1,0},{2,3},{3,2},{256,257},{257,256},{258,259},{259,258},{4... | collective-permute-start | bytes 2752520 | tf_op jit(solution)/shard_map/ppermute | solution.py:100
  44.9 12.0 %collective-permute-start.3 = (bf16[512,512]{1,0:T(8,128)(2,1)S(1)}, bf16[512,512]{1,0:T(8,128)(2,1)S(1)}, u32[]{:S(2)}, u32[]{:S(2)}) collective-permute-start(bf16[512,512]{1,0:T(8,128)(2,1)S(1)} %bitcast.22), channel_id=1, source_target_pairs={{0,259},{1,256},{2,257},{3,258},{256,3},{257,0},{258,1},{259,2},{4... | collective-permute-start | bytes 1572872 | tf_op jit(solution)/shard_map/ppermute | solution.py:100
  52.7 12.3 %collective-permute-start.4 = (bf16[512,512]{1,0:T(8,128)(2,1)S(1)}, bf16[512,512]{1,0:T(8,128)(2,1)S(1)}, u32[]{:S(2)}, u32[]{:S(2)}) collective-permute-start(bf16[512,512]{1,0:T(8,128)(2,1)S(1)} %collective-permute-done.2.refs_1_), channel_id=1, source_target_pairs={{0,258},{1,257},{2,256},{3,259},{256,2},{257,1},{258,0},{259,3},{4... | collective-permute-start | bytes 1572872 | tf_op jit(solution)/shard_map/ppermute | solution.py:100
  67.1 3.9 %collective-permute-start.6 = (bf16[576,512]{1,0:T(8,128)(2,1)S(1)}, bf16[576,512]{1,0:T(8,128)(2,1)S(1)}, u32[]{:S(2)}, u32[]{:S(2)}) collective-permute-start(bf16[576,512]{1,0:T(8,128)(2,1)S(1)} %get-tuple-element.20), channel_id=1, source_target_pairs={{0,1},{1,0},{2,3},{3,2},{256,257},{257,256},{258,259},{259,258},{4... | collective-permute-start | bytes 1769480 | tf_op jit(solution)/shard_map/ppermute | solution.py:100
  71.0 19.1 %copy-start.10 = (bf16[128,896]{1,0:T(8,128)(2,1)S(1)}, bf16[128,896]{1,0:T(8,128)(2,1)}, u32[]{:S(2)}) copy-start(bf16[128,896]{1,0:T(8,128)(2,1)} %copy-done.9) | copy-start | bytes 688132
  71.3 10.6 %collective-permute-start.7 = (bf16[576,256]{1,0:T(8,128)(2,1)S(1)}, bf16[576,256]{1,0:T(8,128)(2,1)S(1)}, u32[]{:S(2)}, u32[]{:S(2)}) collective-permute-start(bf16[576,256]{1,0:T(8,128)(2,1)S(1)} %hidden.1.chip_ref), channel_id=1, source_target_pairs={{0,256},{1,259},{2,258},{3,257},{256,0},{257,3},{258,2},{259,1},{4... | collective-permute-start | bytes 884744 | tf_op jit(solution)/shard_map/ppermute | solution.py:100
  73.2 10.6 %collective-permute-start.9 = (bf16[128,896]{1,0:T(8,128)(2,1)S(1)}, bf16[128,896]{1,0:T(8,128)(2,1)S(1)}, u32[]{:S(2)}, u32[]{:S(2)}) collective-permute-start(bf16[128,896]{1,0:T(8,128)(2,1)S(1)} %slice.7), channel_id=1, source_target_pairs={{0,258},{1,257},{2,256},{3,259},{256,2},{257,1},{258,0},{259,3},{4... | collective-permute-start | bytes 688136 | tf_op jit(solution)/shard_map/ppermute | solution.py:100
  81.9 8.2 %collective-permute-start.8 = (bf16[576,128]{1,0:T(8,128)(2,1)S(1)}, bf16[576,128]{1,0:T(8,128)(2,1)S(1)}, u32[]{:S(2)}, u32[]{:S(2)}) collective-permute-start(bf16[576,128]{1,0:T(8,128)(2,1)S(1)} %slice.8), channel_id=1, source_target_pairs={{0,258},{1,257},{2,256},{3,259},{256,2},{257,1},{258,0},{259,3},{4... | collective-permute-start | bytes 442376 | tf_op jit(solution)/shard_map/ppermute | solution.py:100
  91.8 3.9 %collective-permute-start.10 = (bf16[576,512]{1,0:T(8,128)(2,1)S(1)}, bf16[576,512]{1,0:T(8,128)(2,1)S(1)}, u32[]{:S(2)}, u32[]{:S(2)}) collective-permute-start(bf16[576,512]{1,0:T(8,128)(2,1)S(1)} %get-tuple-element.25), channel_id=1, source_target_pairs={{0,1},{1,0},{2,3},{3,2},{256,257},{257,256},{258,259},{259,258},{4... | collective-permute-start | bytes 1769480 | tf_op jit(solution)/shard_map/ppermute | solution.py:100
  95.7 12.1 %copy-start.4 = (bf16[1,1024,576]{1,2,0:T(8,128)(2,1)S(1)}, bf16[1,1024,576]{1,2,0:T(8,128)(2,1)}, u32[]{:S(2)}) copy-start(bf16[1,1024,576]{1,2,0:T(8,128)(2,1)} %param.10) | copy-start | bytes 3538948
  95.7 12.1 %copy-start.6 = (bf16[3,1,32,576]{3,2,1,0:T(8,128)(2,1)S(1)}, bf16[3,1,32,576]{3,2,1,0:T(8,128)(2,1)}, u32[]{:S(2)}) copy-start(bf16[3,1,32,576]{3,2,1,0:T(8,128)(2,1)} %param.12) | copy-start | bytes 331780
  95.7 12.2 %copy-start.7 = (bf16[3,1,576]{2,0,1:T(4,128)(2,1)S(1)}, bf16[3,1,576]{2,0,1:T(4,128)(2,1)}, u32[]{:S(2)}) copy-start(bf16[3,1,576]{2,0,1:T(4,128)(2,1)} %param.11) | copy-start | bytes 10372
  97.1 29.9 %all-to-all-start.1 = ((bf16[64,8,512]{2,1,0:T(8,128)(2,1)}), bf16[64,8,512]{2,1,0:T(8,128)(2,1)S(1)}, u32[]{:S(2)}, u32[]{:S(2)}) async-start(bf16[64,8,512]{2,1,0:T(8,128)(2,1)} %bitcast.12), calls=%async_computation.1 | async-start | bytes 1048576 | tf_op jit(solution)/shard_map/all_to_all | solution.py:391
  107.2 3.6 %copy-start.11 = (s32[3,12,8]{1,2,0:T(8,128)S(1)}, s32[3,12,8]{1,2,0:T(8,128)}, u32[]{:S(2)}) copy-start(s32[3,12,8]{1,2,0:T(8,128)} %param.15) | copy-start | bytes 3460
  107.2 3.7 %copy-start.12 = (f32[3,12,8]{1,2,0:T(8,128)S(1)}, f32[3,12,8]{1,2,0:T(8,128)}, u32[]{:S(2)}) copy-start(f32[3,12,8]{1,2,0:T(8,128)} %param.16) | copy-start | bytes 3460
  108.8 8.5 %collective-permute-start.11 = (f32[96,512]{1,0:T(8,128)S(1)}, f32[96,512]{1,0:T(8,128)S(1)}, u32[]{:S(2)}, u32[]{:S(2)}) collective-permute-start(f32[96,512]{1,0:T(8,128)S(1)} %get-tuple-element.27), channel_id=1, source_target_pairs={{0,256},{1,257},{2,258},{3,259},{256,0},{257,1},{258,2},{259,3},{4... | collective-permute-start | bytes 589832 | tf_op jit(solution)/shard_map/ppermute | solution.py:100
  (3 other events, 2.8 us)

commit v6 on v4

--- a/solution.py
+++ b/solution.py
@@ -36,13 +36,13 @@
         out_shape=out_shape,
         in_specs=in_specs,
         out_specs=VMEM if single else [VMEM] * len(out_shape),
-        compiler_params=pltpu.CompilerParams(vmem_limit_bytes=40 * 1024 * 1024),
+        compiler_params=pltpu.CompilerParams(vmem_limit_bytes=20 * 1024 * 1024),
         cost_estimate=pl.CostEstimate(flops=flops, bytes_accessed=moved, transcendentals=0),
         name=name,
     )
 
 
-def attend_body(length_ref, q_ref, cache_ref, new_ref, send_ref, keep_ref):
+def attend_body(_, length_ref, q_ref, cache_ref, new_ref, send_ref, keep_ref):
     section, length = lax.axis_index("sec").astype(jnp.int32), length_ref[0]
     q = q_ref[...]
     rows, local_length = q.shape[0], cache_ref.shape[1]
@@ -104,10 +104,21 @@
     return permute(value, lambda d: d ^ k)
 
 
+def to_near(value):
+    return permute(value, lambda d: d ^ (4 + 2 * (d % 2)))
+
+
+def to_crossed(value):
+    return permute(value, lambda d: d ^ (7 - 2 * (d % 2)))
+
+
+def onward(value):
+    return permute(value, lambda d: d ^ (6 - 2 * (d % 2)))
+
+
 def gather(own):
-    near = permute(own, lambda d: d ^ (4 + 2 * (d % 2)))
-    crossed = permute(own, lambda d: d ^ (7 - 2 * (d % 2)))
-    return own, near, crossed, permute(near, lambda d: d ^ (6 - 2 * (d % 2)))
+    near = to_near(own)
+    return own, near, to_crossed(own), onward(near)
 
 
 def named_slots(routes, experts):
@@ -127,7 +138,7 @@
     return dot(values.astype(BF), repeat)
 
 
-def pack_body(tokens_ref, routes_ref, out_ref, tokens_here, routes_here, sems):
+def pack_body(tokens_ref, routes_ref, out_ref, mark_ref, tokens_here, routes_here, sems):
     here = place_here()
     rows = out_ref.shape[0]
     experts = rows // ROWS
@@ -161,6 +172,7 @@
     last = dot((slots[-1] == CAP - 1.0).astype(BF), own)
     out_ref[:, :part] = main.astype(BF)
     out_ref[:, part:] = ninth_columns(last, part)
+    mark_ref[...] = jnp.zeros(mark_ref.shape, F32)
 
 
 def ninth_columns(last, part):
@@ -171,7 +183,7 @@
     return tail.astype(BF)
 
 
-def gates_body(routes_ref, gates_ref, out_ref):
+def gates_body(_, routes_ref, gates_ref, out_ref):
     steps, tokens, picks = routes_ref.shape
     rows = out_ref.shape[2]
     experts = rows // ROWS
@@ -199,23 +211,31 @@
                     ).astype(BF)
 
 
-def slices_body(gate_ref, up_ref, down_ref, other_ref, *down_outs):
+def down_slices_body(_, down_ref, near_ref, crossed_ref):
     here = place_here()
+    core = here % 2
+    units, wide = crossed_ref.shape
+
+    def columns(target):
+        return down_ref[:, pl.ds(pl.multiple_of((target // 2) * wide, 128), wide)]
+
+    near_ref[:units, :] = columns(here ^ (4 + 2 * core))
+    near_ref[units:, :] = columns(here ^ 2)
+    crossed_ref[...] = columns(here ^ (7 - 2 * core))
+
+
+def other_slices_body(_, gate_ref, up_ref, other_ref):
     units = gate_ref.shape[1]
     part = gate_ref.shape[0] // 8
-    core = here % 2
-    for m, source in enumerate(sources(here ^ 1)):
+    for m, source in enumerate(sources(place_here() ^ 1)):
         offset = pl.multiple_of(source * part, HALF)
         rows = slice(m * part, (m + 1) * part)
         other_ref[rows, :units] = gate_ref[pl.ds(offset, part), :]
         other_ref[rows, units:] = up_ref[pl.ds(offset, part), :]
-    targets = here, here ^ (4 + 2 * core), here ^ (7 - 2 * core), here ^ 2
-    for target, out in zip(targets, down_outs):
-        out[...] = down_ref[:, pl.ds(pl.multiple_of((target // 2) * 2 * part, 128), 2 * part)]
 
 
 def partial_body(*refs):
-    pieces, (gate_ref, up_ref, other_ref, keep_ref, send_ref) = refs[:4], refs[4:]
+    pieces, (gate_ref, up_ref, other_ref, keep_ref, send_ref) = refs[:4], refs[5:]
     rows = pieces[0].shape[0]
     experts = rows // ROWS
     part = gate_ref.shape[0] // 8
@@ -259,12 +279,11 @@
     out_ref[...] = (gate / (1.0 + jnp.exp(-gate)) * up).astype(BF)
 
 
-def down_body(*refs):
-    hidden, down, (keep_ref, send_ref) = refs[:4], refs[4:8], refs[8:]
-    part = keep_ref.shape[1]
-    total = jnp.zeros((hidden[0].shape[0], 2 * part), F32)
-    for m in range(4):
-        total = total + dot(hidden[m][...], down[m][...])
+def down_body(own_h, near_h, crossed_h, far_h, down_ref, near_w, crossed_w, far_w, keep_ref, send_ref):
+    part, units = keep_ref.shape[1], down_ref.shape[0]
+    here = pl.ds(pl.multiple_of((place_here() // 2) * 2 * part, 128), 2 * part)
+    total = dot(own_h[...], down_ref[:, here]) + dot(near_h[...], near_w[:units, :])
+    total = total + dot(crossed_h[...], crossed_w[...]) + dot(far_h[...], far_w[...])
     first = place_here() % 2 == 0
     keep_ref[...] = jnp.where(first, total[:, :part], total[:, part:])
     send_ref[:, :part] = jnp.where(first, total[:, part:], total[:, :part]).astype(BF)
@@ -312,11 +331,14 @@
     steps, tokens, width = token_rows.shape
     part = width // 8
     units = gate_proj.shape[2]
-    packed = pl.pallas_call(
+    packed, mark = pl.pallas_call(
         pack_body,
-        out_shape=jax.ShapeDtypeStruct((rows, part + HALF), BF),
+        out_shape=[
+            jax.ShapeDtypeStruct((rows, part + HALF), BF),
+            jax.ShapeDtypeStruct((8, 128), F32),
+        ],
         in_specs=[HBM, HBM],
-        out_specs=VMEM,
+        out_specs=[VMEM, VMEM],
         scratch_shapes=[
             pltpu.VMEM((steps, tokens, 2 * part), BF),
             pltpu.VMEM((steps, routes.shape[2], tokens), jnp.int32),
@@ -325,31 +347,35 @@
         cost_estimate=pl.CostEstimate(flops=10**8, bytes_accessed=10**6, transcendentals=0),
         name="pack",
     )(token_rows, jnp.swapaxes(routes, 1, 2))
-    packed, down_proj = lax.optimization_barrier((packed, down_proj))
     arrived = lax.all_to_all(
         packed.reshape(experts, ROWS, part + HALF), "grp", split_axis=0, concat_axis=0, tiled=True
     ).reshape(rows, part + HALF)
 
     gate_proj, up_proj = gate_proj.reshape(width, units), up_proj.reshape(width, units)
-    other, *down = call(
-        slices_body,
-        [jax.ShapeDtypeStruct((width // 2, 2 * units), BF)]
-        + [jax.ShapeDtypeStruct((units, 2 * part), BF)] * 4,
-        [VMEM] * 3, 10**6, 5 * 10**6, "slices",
-    )(gate_proj, up_proj, down_proj.reshape(units, width))
+    down_proj = down_proj.reshape(units, width)
+    near_down, crossed_down = call(
+        down_slices_body,
+        [
+            jax.ShapeDtypeStruct((2 * units, 2 * part), BF),
+            jax.ShapeDtypeStruct((units, 2 * part), BF),
+        ],
+        [VMEM, VMEM], 10**6, 2 * 10**6, "down_slices",
+    )(mark, down_proj)
+    near_down, crossed_down = to_near(near_down), to_crossed(crossed_down)
+    arrived, near_down, crossed_down = lax.optimization_barrier(
+        (arrived, near_down, crossed_down)
+    )
+    other = call(
+        other_slices_body, jax.ShapeDtypeStruct((width // 2, 2 * units), BF),
+        [VMEM] * 3, 10**6, 4 * 10**6, "other_slices",
+    )(arrived, gate_proj, up_proj)
     other = swap(other, 1)
-    down = [
-        down[0],
-        permute(down[1], lambda d: d ^ (4 + 2 * (d % 2))),
-        permute(down[2], lambda d: d ^ (7 - 2 * (d % 2))),
-        swap(down[3], 2),
-    ]
-
-    arrived, other, down = lax.optimization_barrier((arrived, other, down))
+    far_down = onward(near_down[units:])
+
     keep, send = call(
         partial_body, [jax.ShapeDtypeStruct((rows + experts, 2 * units), F32)] * 2,
-        [VMEM] * 7, 10**9, 6 * 10**6, "partial",
-    )(*gather(arrived), gate_proj, up_proj, other)
+        [VMEM] * 4 + [HBM] + [VMEM] * 3, 10**9, 6 * 10**6, "partial",
+    )(*gather(arrived), far_down, gate_proj, up_proj, other)
     hidden = call(
         hidden_body, jax.ShapeDtypeStruct((rows + experts, units), BF), [VMEM] * 2,
         10**7, 10**6, "hidden",
@@ -361,12 +387,11 @@
             jax.ShapeDtypeStruct((rows + experts, part + HALF), BF),
         ],
         [VMEM] * 8, 10**9, 3 * 10**6, "down",
-    )(*gather(hidden), *down)
+    )(*gather(hidden), down_proj, near_down, crossed_down, far_down)
     outgoing = call(
         repack_body, jax.ShapeDtypeStruct((rows, part + HALF), BF), [VMEM] * 2,
         10**8, 2 * 10**6, "repack",
     )(keep, swap(send, 1))
-    outgoing, lengths, gates = lax.optimization_barrier((outgoing, lengths, route_gates))
     returned = lax.all_to_all(
         outgoing.reshape(experts, ROWS, part + HALF), "grp", split_axis=0, concat_axis=0, tiled=True
     ).reshape(rows, part + HALF)
@@ -374,8 +399,9 @@
     heads = queries.shape[2]
     send, keep = call(
         attend_body, [jax.ShapeDtypeStruct((steps * heads, KL // 2 + 256), F32)] * 2,
-        [SMEM, VMEM, VMEM, VMEM], 3 * 10**8, 2 * 10**6, "attend",
+        [HBM, SMEM, VMEM, VMEM, VMEM], 3 * 10**8, 2 * 10**6, "attend",
     )(
+        outgoing,
         lengths,
         queries.reshape(steps * heads, queries.shape[3]),
         latent_cache[0].T,
@@ -388,8 +414,8 @@
     gates = call(
         gates_body,
         jax.ShapeDtypeStruct((2, 16 * (steps + part // HALF), rows), BF),
-        [VMEM, VMEM], 10**8, 10**6, "gates",
-    )(routes, gates)
+        [HBM, VMEM, VMEM], 10**8, 10**6, "gates",
+    )(outgoing, routes, route_gates)
     moe = call(
         combine_body, jax.ShapeDtypeStruct((steps, tokens, part), BF), [VMEM, VMEM],
         10**8, 10**6, "combine",

time: 132 us -> 125 us (0.947)
  starting transfers between devices: 66.1 us -> 59.4 us
  waiting for transfers between devices: 47.4 us -> 49.4 us
  local copies, waits for them, and re-layouts: 3.48 us -> 2.1 us
    all_to_all x1, starting transfers between devices: 12.8 us -> 7.74 us  [local(): lax.all_to_all(outgoing.reshape(experts, ROWS, part + HALF), 'grp', split...]
    all_to_all x1, waiting for transfers between devices: 0.01 us -> 4.95 us  [local(): lax.all_to_all(packed.reshape(experts, ROWS, part + HALF), 'grp', split_a...]
    ppermute x13, waiting for transfers between devices: 39.2 us -> 35.5 us  [permute(): return lax.ppermute(value, LINE, [(d, target(d)) for d in range(8)])]
    ppermute x13, starting transfers between devices: 36.6 us -> 35.1 us  [permute(): return lax.ppermute(value, LINE, [(d, target(d)) for d in range(8)])]
    unnamed x29 -> x22, local copies, waits for them, and re-layouts: 3.38 us -> 2.08 us
    pallas_call x2 -> x3, Pallas kernels: 3.41 us -> 3.43 us  [the longest x1 3.2 us: local(): pl.pallas_call(pack_body, out_shape=[jax.ShapeDtypeStruct((rows, part + H...]
  transfers between devices with their start and end apart: 15 -> 15, of which waited for: 10 -> 12; matrix products, arithmetic and copies ran while one was open for 0% -> 0% of each run, Pallas kernels for 2% -> 2%
where the time goes in v6:
time: 125 us
  starting transfers between devices  59.4 us (48%)
  waiting for transfers between devices  49.4 us (40%)
  Pallas kernels  12 us (10%)
  local copies, waits for them, and re-layouts  2.1 us (2%)
  between operations  1.57 us (1%)
    ppermute x13, waiting for transfers between devices, permute(): return lax.ppermute(value, LINE, [(d, target(d)) for d in range(8)])  35.5 us
    ppermute x13, starting transfers between devices, permute(): return lax.ppermute(value, LINE, [(d, target(d)) for d in range(8)])  35.1 us
    all_to_all x1, starting transfers between devices, local(): lax.all_to_all(packed.reshape(experts, ROWS, part + HALF), 'grp', split_a...  16.6 us
    all_to_all x1, waiting for transfers between devices, local(): lax.all_to_all(outgoing.reshape(experts, ROWS, part + HALF), 'grp', split...  8.93 us
    all_to_all x1, starting transfers between devices, local(): lax.all_to_all(outgoing.reshape(experts, ROWS, part + HALF), 'grp', split...  7.74 us
    all_to_all x1, waiting for transfers between devices, local(): lax.all_to_all(packed.reshape(experts, ROWS, part + HALF), 'grp', split_a...  4.95 us
    pallas_call x1, Pallas kernels, local(): pl.pallas_call(pack_body, out_shape=[jax.ShapeDtypeStruct((rows, part + H...  3.2 us
  transfers between devices with their start and end apart: 15, of which 12 were waited for; matrix products, arithmetic and copies ran while one was open for 0% of the time, Pallas kernels for 2%

profile of v6, /device:TPU:6, one launch (start us, length us, event | category | flops | bytes accessed | tf_op | source)
XLA Modules:
  0.0 124.5 jit_solution(15001946591428745054)
XLA Ops:
  0.7 3.2 %pack.1 = (bf16[512,512]{1,0:T(8,128)(2,1)}, f32[8,128]{1,0:T(8,128)}) custom-call(bf16[3,12,3584]{2,1,0:T(8,128)(2,1)} %tokens_ref.1, s32[3,8,12]{2,1,0:T(8,128)} %bitcast.32), custom_call_target="tpu_custom_call" | custom-call | flops 100000000 | bytes 1000000 | tf_op jit(solution)/shard_map/pack/pallas_call | solution.py:334
  3.9 16.6 %all-to-all-start = ((bf16[64,8,512]{2,1,0:T(8,128)(2,1)}), bf16[64,8,512]{2,1,0:T(8,128)(2,1)S(1)}, u32[]{:S(2)}, u32[]{:S(2)}) async-start(bf16[64,8,512]{2,1,0:T(8,128)(2,1)} %bitcast.30), calls=%async_computation | async-start | bytes 1048576 | tf_op jit(solution)/shard_map/all_to_all | solution.py:350
  22.4 2.7 %collective-permute-start = (bf16[256,896]{1,0:T(8,128)(2,1)S(1)}, bf16[256,896]{1,0:T(8,128)(2,1)S(1)}, u32[]{:S(2)}, u32[]{:S(2)}) collective-permute-start(bf16[256,896]{1,0:T(8,128)(2,1)S(1)} %get-tuple-element.17), channel_id=1, source_target_pairs={{0,256},{1,259},{2,258},{3,257},{256,0},{257,3},{258,2},{259,1},{4... | collective-permute-start | bytes 1376264 | tf_op jit(solution)/shard_map/ppermute | solution.py:100
  25.1 3.2 %collective-permute-start.1 = (bf16[128,896]{1,0:T(8,128)(2,1)S(1)}, bf16[128,896]{1,0:T(8,128)(2,1)S(1)}, u32[]{:S(2)}, u32[]{:S(2)}) collective-permute-start(bf16[128,896]{1,0:T(8,128)(2,1)S(1)} %get-tuple-element.18), channel_id=1, source_target_pairs={{0,259},{1,256},{2,257},{3,258},{256,3},{257,0},{258,1},{259,2},{4... | collective-permute-start | bytes 688136 | tf_op jit(solution)/shard_map/ppermute | solution.py:100
  28.3 6.7 %collective-permute-done.1.crossed_w = bf16[128,896]{1,0:T(8,128)(2,1)S(1)} collective-permute-done((bf16[128,896]{1,0:T(8,128)(2,1)S(1)}, bf16[128,896]{1,0:T(8,128)(2,1)S(1)}, u32[]{:S(2)}, u32[]{:S(2)}) %collective-permute-start.1) | collective-permute-done | bytes 229408 | tf_op jit(solution)/shard_map/ppermute | solution.py:100
  35.2 5.0 %all-to-all-done = bf16[64,8,512]{2,1,0:T(8,128)(2,1)S(1)} async-done(((bf16[64,8,512]{2,1,0:T(8,128)(2,1)}), bf16[64,8,512]{2,1,0:T(8,128)(2,1)S(1)}, u32[]{:S(2)}, u32[]{:S(2)}) %all-to-all-start) | async-done | bytes 524320 | tf_op jit(solution)/shard_map/all_to_all | solution.py:350
  40.2 2.7 %collective-permute-start.2 = (bf16[512,512]{1,0:T(8,128)(2,1)S(1)}, bf16[512,512]{1,0:T(8,128)(2,1)S(1)}, u32[]{:S(2)}, u32[]{:S(2)}) collective-permute-start(bf16[512,512]{1,0:T(8,128)(2,1)S(1)} %bitcast.16), channel_id=1, source_target_pairs={{0,256},{1,259},{2,258},{3,257},{256,0},{257,3},{258,2},{259,1},{4... | collective-permute-start | bytes 1572872 | tf_op jit(solution)/shard_map/ppermute | solution.py:100
  43.1 1.9 %collective-permute-start.6 = (bf16[1792,256]{1,0:T(8,128)(2,1)S(1)}, bf16[1792,256]{1,0:T(8,128)(2,1)S(1)}, u32[]{:S(2)}, u32[]{:S(2)}) collective-permute-start(bf16[1792,256]{1,0:T(8,128)(2,1)S(1)} %other_slices.1), channel_id=1, source_target_pairs={{0,1},{1,0},{2,3},{3,2},{256,257},{257,256},{258,259},{259,258},{4... | collective-permute-start | bytes 2752520 | tf_op jit(solution)/shard_map/ppermute | solution.py:100
  45.0 3.2 %collective-permute-start.3 = (bf16[512,512]{1,0:T(8,128)(2,1)S(1)}, bf16[512,512]{1,0:T(8,128)(2,1)S(1)}, u32[]{:S(2)}, u32[]{:S(2)}) collective-permute-start(bf16[512,512]{1,0:T(8,128)(2,1)S(1)} %bitcast.18), channel_id=1, source_target_pairs={{0,259},{1,256},{2,257},{3,258},{256,3},{257,0},{258,1},{259,2},{4... | collective-permute-start | bytes 1572872 | tf_op jit(solution)/shard_map/ppermute | solution.py:100
  48.2 4.3 %collective-permute-done.2.refs_1_ = bf16[512,512]{1,0:T(8,128)(2,1)S(1)} collective-permute-done((bf16[512,512]{1,0:T(8,128)(2,1)S(1)}, bf16[512,512]{1,0:T(8,128)(2,1)S(1)}, u32[]{:S(2)}, u32[]{:S(2)}) %collective-permute-start.2) | collective-permute-done | bytes 524320 | tf_op jit(solution)/shard_map/ppermute | solution.py:100
  54.4 5.1 %collective-permute-start.5 = (bf16[128,896]{1,0:T(8,128)(2,1)S(1)}, bf16[128,896]{1,0:T(8,128)(2,1)S(1)}, u32[]{:S(2)}, u32[]{:S(2)}) collective-permute-start(bf16[128,896]{1,0:T(8,128)(2,1)S(1)} %slice.3), channel_id=1, source_target_pairs={{0,258},{1,257},{2,256},{3,259},{256,2},{257,1},{258,0},{259,3},{4... | collective-permute-start | bytes 688136 | tf_op jit(solution)/shard_map/ppermute | solution.py:100
  59.6 7.6 %collective-permute-done.5.refs_4_.far_w = bf16[128,896]{1,0:T(8,128)(2,1)S(1)} collective-permute-done((bf16[128,896]{1,0:T(8,128)(2,1)S(1)}, bf16[128,896]{1,0:T(8,128)(2,1)S(1)}, u32[]{:S(2)}, u32[]{:S(2)}) %collective-permute-start.5) | collective-permute-done | bytes 229408 | tf_op jit(solution)/shard_map/ppermute | solution.py:100
  67.2 2.1 %partial.1 = (f32[576,256]{1,0:T(8,128)S(1)}, f32[576,256]{1,0:T(8,128)S(1)}) custom-call(bf16[512,512]{1,0:T(8,128)(2,1)S(1)} %bitcast.19, bf16[512,512]{1,0:T(8,128)(2,1)S(1)} %collective-permute-done.2.refs_1_, bf16[512,512]{1,0:T(8,128)(2,1)S(1)} %collective-permute-done.3.refs_2_, bf16[512,512]{1,0:T(8,128)(2,1)S(1)} %collective-permute-done.4.refs_3_, ...), custom_call_target="tpu_custom_call" | custom-call | flops 1000000000 | bytes 6000000 | tf_op jit(solution)/shard_map/partial/pallas_call | solution.py:375
  69.4 2.1 %collective-permute-start.7 = (f32[576,256]{1,0:T(8,128)S(1)}, f32[576,256]{1,0:T(8,128)S(1)}, u32[]{:S(2)}, u32[]{:S(2)}) collective-permute-start(f32[576,256]{1,0:T(8,128)S(1)} %get-tuple-element.22), channel_id=1, source_target_pairs={{0,1},{1,0},{2,3},{3,2},{256,257},{257,256},{258,259},{259,258},{4... | collective-permute-start | bytes 1769480 | tf_op jit(solution)/shard_map/ppermute | solution.py:100
  71.4 2.0 %collective-permute-done.7.two_ref = f32[576,256]{1,0:T(8,128)S(1)} collective-permute-done((f32[576,256]{1,0:T(8,128)S(1)}, f32[576,256]{1,0:T(8,128)S(1)}, u32[]{:S(2)}, u32[]{:S(2)}) %collective-permute-start.7) | collective-permute-done | bytes 589856 | tf_op jit(solution)/shard_map/ppermute | solution.py:100
  73.5 1.9 %collective-permute-start.8 = (bf16[576,128]{1,0:T(8,128)(2,1)S(1)}, bf16[576,128]{1,0:T(8,128)(2,1)S(1)}, u32[]{:S(2)}, u32[]{:S(2)}) collective-permute-start(bf16[576,128]{1,0:T(8,128)(2,1)S(1)} %hidden.1.own_h), channel_id=1, source_target_pairs={{0,256},{1,259},{2,258},{3,257},{256,0},{257,3},{258,2},{259,1},{4... | collective-permute-start | bytes 442376 | tf_op jit(solution)/shard_map/ppermute | solution.py:100
  75.4 4.6 %collective-permute-start.9 = (bf16[576,128]{1,0:T(8,128)(2,1)S(1)}, bf16[576,128]{1,0:T(8,128)(2,1)S(1)}, u32[]{:S(2)}, u32[]{:S(2)}) collective-permute-start(bf16[576,128]{1,0:T(8,128)(2,1)S(1)} %hidden.1.own_h), channel_id=1, source_target_pairs={{0,259},{1,256},{2,257},{3,258},{256,3},{257,0},{258,1},{259,2},{4... | collective-permute-start | bytes 442376 | tf_op jit(solution)/shard_map/ppermute | solution.py:100
  82.7 6.3 %collective-permute-done.10.far_h = bf16[576,128]{1,0:T(8,128)(2,1)S(1)} collective-permute-done((bf16[576,128]{1,0:T(8,128)(2,1)S(1)}, bf16[576,128]{1,0:T(8,128)(2,1)S(1)}, u32[]{:S(2)}, u32[]{:S(2)}) %collective-permute-start.10) | collective-permute-done | bytes 147488 | tf_op jit(solution)/shard_map/ppermute | solution.py:100
  90.6 1.9 %collective-permute-start.11 = (bf16[576,512]{1,0:T(8,128)(2,1)S(1)}, bf16[576,512]{1,0:T(8,128)(2,1)S(1)}, u32[]{:S(2)}, u32[]{:S(2)}) collective-permute-start(bf16[576,512]{1,0:T(8,128)(2,1)S(1)} %get-tuple-element.25), channel_id=1, source_target_pairs={{0,1},{1,0},{2,3},{3,2},{256,257},{257,256},{258,259},{259,258},{4... | collective-permute-start | bytes 1769480 | tf_op jit(solution)/shard_map/ppermute | solution.py:100
  92.5 2.0 %collective-permute-done.11.two_ref = bf16[576,512]{1,0:T(8,128)(2,1)S(1)} collective-permute-done((bf16[576,512]{1,0:T(8,128)(2,1)S(1)}, bf16[576,512]{1,0:T(8,128)(2,1)S(1)}, u32[]{:S(2)}, u32[]{:S(2)}) %collective-permute-start.11) | collective-permute-done | bytes 589856 | tf_op jit(solution)/shard_map/ppermute | solution.py:100
  95.9 7.7 %all-to-all-start.1 = ((bf16[64,8,512]{2,1,0:T(8,128)(2,1)}), bf16[64,8,512]{2,1,0:T(8,128)(2,1)S(1)}, u32[]{:S(2)}, u32[]{:S(2)}) async-start(bf16[64,8,512]{2,1,0:T(8,128)(2,1)} %bitcast.12), calls=%async_computation.1 | async-start | bytes 1048576 | tf_op jit(solution)/shard_map/all_to_all | solution.py:395
  105.3 1.9 %collective-permute-start.12 = (f32[96,512]{1,0:T(8,128)S(1)}, f32[96,512]{1,0:T(8,128)S(1)}, u32[]{:S(2)}, u32[]{:S(2)}) collective-permute-start(f32[96,512]{1,0:T(8,128)S(1)} %get-tuple-element.27), channel_id=1, source_target_pairs={{0,256},{1,257},{2,258},{3,259},{256,0},{257,1},{258,2},{259,3},{4... | collective-permute-start | bytes 589832 | tf_op jit(solution)/shard_map/ppermute | solution.py:100
  108.1 5.7 %collective-permute-done.12.two_ref = f32[96,512]{1,0:T(8,128)S(1)} collective-permute-done((f32[96,512]{1,0:T(8,128)S(1)}, f32[96,512]{1,0:T(8,128)S(1)}, u32[]{:S(2)}, u32[]{:S(2)}) %collective-permute-start.12) | collective-permute-done | bytes 196640 | tf_op jit(solution)/shard_map/ppermute | solution.py:100
  114.6 8.9 %all-to-all-done.1 = bf16[64,8,512]{2,1,0:T(8,128)(2,1)S(1)} async-done(((bf16[64,8,512]{2,1,0:T(8,128)(2,1)}), bf16[64,8,512]{2,1,0:T(8,128)(2,1)S(1)}, u32[]{:S(2)}, u32[]{:S(2)}) %all-to-all-start.1) | async-done | bytes 524320 | tf_op jit(solution)/shard_map/all_to_all | solution.py:395
  (40 shorter events, 13.6 us)
Async XLA Ops:
  0.6 42.3 %copy-start = (bf16[1,3584,128]{2,1,0:T(8,128)(2,1)S(1)}, bf16[1,3584,128]{2,1,0:T(8,128)(2,1)}, u32[]{:S(2)}) copy-start(bf16[1,3584,128]{2,1,0:T(8,128)(2,1)} %param.17) | copy-start | bytes 2752516
  0.6 42.3 %copy-start.1 = (bf16[1,3584,128]{2,1,0:T(8,128)(2,1)S(1)}, bf16[1,3584,128]{2,1,0:T(8,128)(2,1)}, u32[]{:S(2)}) copy-start(bf16[1,3584,128]{2,1,0:T(8,128)(2,1)} %param.18) | copy-start | bytes 2752516
  3.9 36.3 %all-to-all-start = ((bf16[64,8,512]{2,1,0:T(8,128)(2,1)}), bf16[64,8,512]{2,1,0:T(8,128)(2,1)S(1)}, u32[]{:S(2)}, u32[]{:S(2)}) async-start(bf16[64,8,512]{2,1,0:T(8,128)(2,1)} %bitcast.30), calls=%async_computation | async-start | bytes 1048576 | tf_op jit(solution)/shard_map/all_to_all | solution.py:350
  20.5 1.2 copy-start.3
  22.4 12.8 %collective-permute-start = (bf16[256,896]{1,0:T(8,128)(2,1)S(1)}, bf16[256,896]{1,0:T(8,128)(2,1)S(1)}, u32[]{:S(2)}, u32[]{:S(2)}) collective-permute-start(bf16[256,896]{1,0:T(8,128)(2,1)S(1)} %get-tuple-element.17), channel_id=1, source_target_pairs={{0,256},{1,259},{2,258},{3,257},{256,0},{257,3},{258,2},{259,1},{4... | collective-permute-start | bytes 1376264 | tf_op jit(solution)/shard_map/ppermute | solution.py:100
  25.1 9.9 %collective-permute-start.1 = (bf16[128,896]{1,0:T(8,128)(2,1)S(1)}, bf16[128,896]{1,0:T(8,128)(2,1)S(1)}, u32[]{:S(2)}, u32[]{:S(2)}) collective-permute-start(bf16[128,896]{1,0:T(8,128)(2,1)S(1)} %get-tuple-element.18), channel_id=1, source_target_pairs={{0,259},{1,256},{2,257},{3,258},{256,3},{257,0},{258,1},{259,2},{4... | collective-permute-start | bytes 688136 | tf_op jit(solution)/shard_map/ppermute | solution.py:100
  40.2 12.3 %collective-permute-start.2 = (bf16[512,512]{1,0:T(8,128)(2,1)S(1)}, bf16[512,512]{1,0:T(8,128)(2,1)S(1)}, u32[]{:S(2)}, u32[]{:S(2)}) collective-permute-start(bf16[512,512]{1,0:T(8,128)(2,1)S(1)} %bitcast.16), channel_id=1, source_target_pairs={{0,256},{1,259},{2,258},{3,257},{256,0},{257,3},{258,2},{259,1},{4... | collective-permute-start | bytes 1572872 | tf_op jit(solution)/shard_map/ppermute | solution.py:100
  43.1 24.1 %collective-permute-start.6 = (bf16[1792,256]{1,0:T(8,128)(2,1)S(1)}, bf16[1792,256]{1,0:T(8,128)(2,1)S(1)}, u32[]{:S(2)}, u32[]{:S(2)}) collective-permute-start(bf16[1792,256]{1,0:T(8,128)(2,1)S(1)} %other_slices.1), channel_id=1, source_target_pairs={{0,1},{1,0},{2,3},{3,2},{256,257},{257,256},{258,259},{259,258},{4... | collective-permute-start | bytes 2752520 | tf_op jit(solution)/shard_map/ppermute | solution.py:100
  45.0 22.2 %collective-permute-start.3 = (bf16[512,512]{1,0:T(8,128)(2,1)S(1)}, bf16[512,512]{1,0:T(8,128)(2,1)S(1)}, u32[]{:S(2)}, u32[]{:S(2)}) collective-permute-start(bf16[512,512]{1,0:T(8,128)(2,1)S(1)} %bitcast.18), channel_id=1, source_target_pairs={{0,259},{1,256},{2,257},{3,258},{256,3},{257,0},{258,1},{259,2},{4... | collective-permute-start | bytes 1572872 | tf_op jit(solution)/shard_map/ppermute | solution.py:100
  52.5 14.7 %collective-permute-start.4 = (bf16[512,512]{1,0:T(8,128)(2,1)S(1)}, bf16[512,512]{1,0:T(8,128)(2,1)S(1)}, u32[]{:S(2)}, u32[]{:S(2)}) collective-permute-start(bf16[512,512]{1,0:T(8,128)(2,1)S(1)} %collective-permute-done.2.refs_1_), channel_id=1, source_target_pairs={{0,258},{1,257},{2,256},{3,259},{256,2},{257,1},{258,0},{259,3},{4... | collective-permute-start | bytes 1572872 | tf_op jit(solution)/shard_map/ppermute | solution.py:100
  54.4 12.8 %collective-permute-start.5 = (bf16[128,896]{1,0:T(8,128)(2,1)S(1)}, bf16[128,896]{1,0:T(8,128)(2,1)S(1)}, u32[]{:S(2)}, u32[]{:S(2)}) collective-permute-start(bf16[128,896]{1,0:T(8,128)(2,1)S(1)} %slice.3), channel_id=1, source_target_pairs={{0,258},{1,257},{2,256},{3,259},{256,2},{257,1},{258,0},{259,3},{4... | collective-permute-start | bytes 688136 | tf_op jit(solution)/shard_map/ppermute | solution.py:100
  69.4 19.6 %copy-start.4 = (bf16[1,128,3584]{2,1,0:T(8,128)(2,1)S(1)}, bf16[1,128,3584]{2,1,0:T(8,128)(2,1)}, u32[]{:S(2)}) copy-start(bf16[1,128,3584]{2,1,0:T(8,128)(2,1)} %param.19) | copy-start | bytes 2752516
  69.4 4.0 %collective-permute-start.7 = (f32[576,256]{1,0:T(8,128)S(1)}, f32[576,256]{1,0:T(8,128)S(1)}, u32[]{:S(2)}, u32[]{:S(2)}) collective-permute-start(f32[576,256]{1,0:T(8,128)S(1)} %get-tuple-element.22), channel_id=1, source_target_pairs={{0,1},{1,0},{2,3},{3,2},{256,257},{257,256},{258,259},{259,258},{4... | collective-permute-start | bytes 1769480 | tf_op jit(solution)/shard_map/ppermute | solution.py:100
  73.5 7.2 %collective-permute-start.8 = (bf16[576,128]{1,0:T(8,128)(2,1)S(1)}, bf16[576,128]{1,0:T(8,128)(2,1)S(1)}, u32[]{:S(2)}, u32[]{:S(2)}) collective-permute-start(bf16[576,128]{1,0:T(8,128)(2,1)S(1)} %hidden.1.own_h), channel_id=1, source_target_pairs={{0,256},{1,259},{2,258},{3,257},{256,0},{257,3},{258,2},{259,1},{4... | collective-permute-start | bytes 442376 | tf_op jit(solution)/shard_map/ppermute | solution.py:100
  75.4 7.3 %collective-permute-start.9 = (bf16[576,128]{1,0:T(8,128)(2,1)S(1)}, bf16[576,128]{1,0:T(8,128)(2,1)S(1)}, u32[]{:S(2)}, u32[]{:S(2)}) collective-permute-start(bf16[576,128]{1,0:T(8,128)(2,1)S(1)} %hidden.1.own_h), channel_id=1, source_target_pairs={{0,259},{1,256},{2,257},{3,258},{256,3},{257,0},{258,1},{259,2},{4... | collective-permute-start | bytes 442376 | tf_op jit(solution)/shard_map/ppermute | solution.py:100
  80.7 8.2 %collective-permute-start.10 = (bf16[576,128]{1,0:T(8,128)(2,1)S(1)}, bf16[576,128]{1,0:T(8,128)(2,1)S(1)}, u32[]{:S(2)}, u32[]{:S(2)}) collective-permute-start(bf16[576,128]{1,0:T(8,128)(2,1)S(1)} %collective-permute-done.8.near_h), channel_id=1, source_target_pairs={{0,258},{1,257},{2,256},{3,259},{256,2},{257,1},{258,0},{259,3},{4... | collective-permute-start | bytes 442376 | tf_op jit(solution)/shard_map/ppermute | solution.py:100
  90.6 3.9 %collective-permute-start.11 = (bf16[576,512]{1,0:T(8,128)(2,1)S(1)}, bf16[576,512]{1,0:T(8,128)(2,1)S(1)}, u32[]{:S(2)}, u32[]{:S(2)}) collective-permute-start(bf16[576,512]{1,0:T(8,128)(2,1)S(1)} %get-tuple-element.25), channel_id=1, source_target_pairs={{0,1},{1,0},{2,3},{3,2},{256,257},{257,256},{258,259},{259,258},{4... | collective-permute-start | bytes 1769480 | tf_op jit(solution)/shard_map/ppermute | solution.py:100
  94.5 9.8 %copy-start.2 = (bf16[1,1024,576]{1,2,0:T(8,128)(2,1)S(1)}, bf16[1,1024,576]{1,2,0:T(8,128)(2,1)}, u32[]{:S(2)}) copy-start(bf16[1,1024,576]{1,2,0:T(8,128)(2,1)} %param.10) | copy-start | bytes 3538948
  94.5 9.8 %copy-start.5 = (bf16[3,1,32,576]{3,2,1,0:T(8,128)(2,1)S(1)}, bf16[3,1,32,576]{3,2,1,0:T(8,128)(2,1)}, u32[]{:S(2)}) copy-start(bf16[3,1,32,576]{3,2,1,0:T(8,128)(2,1)} %param.12) | copy-start | bytes 331780
  94.5 9.8 %copy-start.6 = (bf16[3,1,576]{2,0,1:T(4,128)(2,1)S(1)}, bf16[3,1,576]{2,0,1:T(4,128)(2,1)}, u32[]{:S(2)}) copy-start(bf16[3,1,576]{2,0,1:T(4,128)(2,1)} %param.11) | copy-start | bytes 10372
  95.9 27.6 %all-to-all-start.1 = ((bf16[64,8,512]{2,1,0:T(8,128)(2,1)}), bf16[64,8,512]{2,1,0:T(8,128)(2,1)S(1)}, u32[]{:S(2)}, u32[]{:S(2)}) async-start(bf16[64,8,512]{2,1,0:T(8,128)(2,1)} %bitcast.12), calls=%async_computation.1 | async-start | bytes 1048576 | tf_op jit(solution)/shard_map/all_to_all | solution.py:395
  103.6 3.6 %copy-start.8 = (s32[3,12,8]{1,2,0:T(8,128)S(1)}, s32[3,12,8]{1,2,0:T(8,128)}, u32[]{:S(2)}) copy-start(s32[3,12,8]{1,2,0:T(8,128)} %param.15) | copy-start | bytes 3460
  103.6 3.7 %copy-start.9 = (f32[3,12,8]{1,2,0:T(8,128)S(1)}, f32[3,12,8]{1,2,0:T(8,128)}, u32[]{:S(2)}) copy-start(f32[3,12,8]{1,2,0:T(8,128)} %param.16) | copy-start | bytes 3460
  105.3 8.5 %collective-permute-start.12 = (f32[96,512]{1,0:T(8,128)S(1)}, f32[96,512]{1,0:T(8,128)S(1)}, u32[]{:S(2)}, u32[]{:S(2)}) collective-permute-start(f32[96,512]{1,0:T(8,128)S(1)} %get-tuple-element.27), channel_id=1, source_target_pairs={{0,256},{1,257},{2,258},{3,259},{256,0},{257,1},{258,2},{259,3},{4... | collective-permute-start | bytes 589832 | tf_op jit(solution)/shard_map/ppermute | solution.py:100
  (1 other events, 0.7 us)

commit v7 on v6

--- a/solution.py
+++ b/solution.py
@@ -138,7 +138,10 @@
     return dot(values.astype(BF), repeat)
 
 
-def pack_body(tokens_ref, routes_ref, out_ref, mark_ref, tokens_here, routes_here, sems):
+def pack_body(
+    tokens_ref, routes_ref, down_ref, out_ref, near_ref, crossed_ref,
+    tokens_here, routes_here, down_here, sems,
+):
     here = place_here()
     rows = out_ref.shape[0]
     experts = rows // ROWS
@@ -147,8 +150,10 @@
     columns = pl.ds(pl.multiple_of((here // 2) * 2 * part, 128), 2 * part)
     fetch_routes = pltpu.make_async_copy(routes_ref, routes_here, sems.at[0])
     fetch_tokens = pltpu.make_async_copy(tokens_ref.at[:, :, columns], tokens_here, sems.at[1])
+    fetch_down = pltpu.make_async_copy(down_ref, down_here, sems.at[2])
     fetch_routes.start()
     fetch_tokens.start()
+    fetch_down.start()
     place = iota((rows, tokens), 0) % ROWS
     repeat = (iota((rows, experts), 0) // ROWS == iota((rows, experts), 1)).astype(BF)
     earlier = (iota((tokens, tokens), 0) < iota((tokens, tokens), 1)).astype(BF)
@@ -172,7 +177,16 @@
     last = dot((slots[-1] == CAP - 1.0).astype(BF), own)
     out_ref[:, :part] = main.astype(BF)
     out_ref[:, part:] = ninth_columns(last, part)
-    mark_ref[...] = jnp.zeros(mark_ref.shape, F32)
+    fetch_down.wait()
+    core = here % 2
+    units, wide = crossed_ref.shape
+
+    def columns(target):
+        return down_here[:, pl.ds(pl.multiple_of((target // 2) * wide, 128), wide)]
+
+    near_ref[:units, :] = columns(here ^ (4 + 2 * core))
+    near_ref[units:, :] = columns(here ^ 2)
+    crossed_ref[...] = columns(here ^ (7 - 2 * core))
 
 
 def ninth_columns(last, part):
@@ -211,19 +225,6 @@
                     ).astype(BF)
 
 
-def down_slices_body(_, down_ref, near_ref, crossed_ref):
-    here = place_here()
-    core = here % 2
-    units, wide = crossed_ref.shape
-
-    def columns(target):
-        return down_ref[:, pl.ds(pl.multiple_of((target // 2) * wide, 128), wide)]
-
-    near_ref[:units, :] = columns(here ^ (4 + 2 * core))
-    near_ref[units:, :] = columns(here ^ 2)
-    crossed_ref[...] = columns(here ^ (7 - 2 * core))
-
-
 def other_slices_body(_, gate_ref, up_ref, other_ref):
     units = gate_ref.shape[1]
     part = gate_ref.shape[0] // 8
@@ -331,46 +332,41 @@
     steps, tokens, width = token_rows.shape
     part = width // 8
     units = gate_proj.shape[2]
-    packed, mark = pl.pallas_call(
+    down_proj = down_proj.reshape(units, width)
+    packed, near_down, crossed_down = pl.pallas_call(
         pack_body,
         out_shape=[
             jax.ShapeDtypeStruct((rows, part + HALF), BF),
-            jax.ShapeDtypeStruct((8, 128), F32),
+            jax.ShapeDtypeStruct((2 * units, 2 * part), BF),
+            jax.ShapeDtypeStruct((units, 2 * part), BF),
         ],
-        in_specs=[HBM, HBM],
-        out_specs=[VMEM, VMEM],
+        in_specs=[HBM] * 3,
+        out_specs=[VMEM] * 3,
         scratch_shapes=[
             pltpu.VMEM((steps, tokens, 2 * part), BF),
             pltpu.VMEM((steps, routes.shape[2], tokens), jnp.int32),
-            pltpu.SemaphoreType.DMA((2,)),
+            pltpu.VMEM((units, width), BF),
+            pltpu.SemaphoreType.DMA((3,)),
         ],
+        compiler_params=pltpu.CompilerParams(vmem_limit_bytes=20 * 1024 * 1024),
         cost_estimate=pl.CostEstimate(flops=10**8, bytes_accessed=10**6, transcendentals=0),
         name="pack",
-    )(token_rows, jnp.swapaxes(routes, 1, 2))
+    )(token_rows, jnp.swapaxes(routes, 1, 2), down_proj)
     arrived = lax.all_to_all(
         packed.reshape(experts, ROWS, part + HALF), "grp", split_axis=0, concat_axis=0, tiled=True
     ).reshape(rows, part + HALF)
 
     gate_proj, up_proj = gate_proj.reshape(width, units), up_proj.reshape(width, units)
-    down_proj = down_proj.reshape(units, width)
-    near_down, crossed_down = call(
-        down_slices_body,
-        [
-            jax.ShapeDtypeStruct((2 * units, 2 * part), BF),
-            jax.ShapeDtypeStruct((units, 2 * part), BF),
-        ],
-        [VMEM, VMEM], 10**6, 2 * 10**6, "down_slices",
-    )(mark, down_proj)
     near_down, crossed_down = to_near(near_down), to_crossed(crossed_down)
-    arrived, near_down, crossed_down = lax.optimization_barrier(
-        (arrived, near_down, crossed_down)
+    far_down = onward(near_down[units:])
+    arrived, near_down, crossed_down, far_down = lax.optimization_barrier(
+        (arrived, near_down, crossed_down, far_down)
     )
     other = call(
         other_slices_body, jax.ShapeDtypeStruct((width // 2, 2 * units), BF),
         [VMEM] * 3, 10**6, 4 * 10**6, "other_slices",
     )(arrived, gate_proj, up_proj)
     other = swap(other, 1)
-    far_down = onward(near_down[units:])
 
     keep, send = call(
         partial_body, [jax.ShapeDtypeStruct((rows + experts, 2 * units), F32)] * 2,

time: 125 us -> 133 us (1.064)
  waiting for transfers between devices: 49.4 us -> 55.3 us
  local copies, waits for them, and re-layouts: 2.1 us -> 3.8 us
    ppermute x13, waiting for transfers between devices: 35.5 us -> 46.3 us  [permute(): return lax.ppermute(value, LINE, [(d, target(d)) for d in range(8)])]
    all_to_all x1, starting transfers between devices: 7.74 us -> 12.7 us  [local(): lax.all_to_all(outgoing.reshape(experts, ROWS, part + HALF), 'grp', split...]
    all_to_all x1, waiting for transfers between devices: 4.95 us -> 0.01 us  [local(): lax.all_to_all(packed.reshape(experts, ROWS, part + HALF), 'grp', split_a...]
    ppermute x13, starting transfers between devices: 35.1 us -> 30.7 us  [permute(): return lax.ppermute(value, LINE, [(d, target(d)) for d in range(8)])]
    unnamed x22 -> x28, local copies, waits for them, and re-layouts: 2.08 us -> 3.78 us
where the time goes in v7:
time: 133 us; the launch traced here: 132 us
  starting transfers between devices  60 us (45%)
  waiting for transfers between devices  55.3 us (42%)
  Pallas kernels  11.6 us (9%)
  local copies, waits for them, and re-layouts  3.8 us (3%)
  between operations  1.57 us (1%)
    ppermute x13, waiting for transfers between devices, permute(): return lax.ppermute(value, LINE, [(d, target(d)) for d in range(8)])  46.3 us
    ppermute x13, starting transfers between devices, permute(): return lax.ppermute(value, LINE, [(d, target(d)) for d in range(8)])  30.7 us
    all_to_all x1, starting transfers between devices, local(): lax.all_to_all(packed.reshape(experts, ROWS, part + HALF), 'grp', split_a...  16.6 us
    all_to_all x1, starting transfers between devices, local(): lax.all_to_all(outgoing.reshape(experts, ROWS, part + HALF), 'grp', split...  12.7 us
    all_to_all x1, waiting for transfers between devices, local(): lax.all_to_all(outgoing.reshape(experts, ROWS, part + HALF), 'grp', split...  8.94 us
    unnamed x28, local copies, waits for them, and re-layouts  3.78 us
    pallas_call x1, Pallas kernels, local(): pl.pallas_call(pack_body, out_shape=[jax.ShapeDtypeStruct((rows, part + H...  2.81 us
  transfers between devices with their start and end apart: 15, of which 12 were waited for; matrix products, arithmetic and copies ran while one was open for 0% of the time, Pallas kernels for 2%

profile of v7, /device:TPU:6, one launch (start us, length us, event | category | flops | bytes accessed | tf_op | source)
XLA Modules:
  0.0 132.2 jit_solution(17471838883833242430)
XLA Ops:
  3.5 2.8 %pack.1 = (bf16[512,512]{1,0:T(8,128)(2,1)}, bf16[256,896]{1,0:T(8,128)(2,1)S(1)}, bf16[128,896]{1,0:T(8,128)(2,1)}) custom-call(bf16[3,12,3584]{2,1,0:T(8,128)(2,1)S(1)} %copy-done.5, s32[3,8,12]{2,1,0:T(8,128)S(1)} %bitcast.29, bf16[128,3584]{1,0:T(8,128)(2,1)S(1)} %bitcast.26), custom_call_target="tpu_custom_call" | custom-call | flops 100000000 | bytes 1000000 | tf_op jit(solution)/shard_map/pack/pallas_call | solution.py:336
  6.3 16.6 %all-to-all-start = ((bf16[64,8,512]{2,1,0:T(8,128)(2,1)}), bf16[64,8,512]{2,1,0:T(8,128)(2,1)S(1)}, u32[]{:S(2)}, u32[]{:S(2)}) async-start(bf16[64,8,512]{2,1,0:T(8,128)(2,1)} %bitcast.2), calls=%async_computation | async-start | bytes 1048576 | tf_op jit(solution)/shard_map/all_to_all | solution.py:355
  22.9 2.7 %collective-permute-start = (bf16[256,896]{1,0:T(8,128)(2,1)S(1)}, bf16[256,896]{1,0:T(8,128)(2,1)S(1)}, u32[]{:S(2)}, u32[]{:S(2)}) collective-permute-start(bf16[256,896]{1,0:T(8,128)(2,1)S(1)} %get-tuple-element.16), channel_id=1, source_target_pairs={{0,256},{1,259},{2,258},{3,257},{256,0},{257,3},{258,2},{259,1},{4... | collective-permute-start | bytes 1376264 | tf_op jit(solution)/shard_map/ppermute | solution.py:100
  25.7 3.2 %collective-permute-start.1 = (bf16[128,896]{1,0:T(8,128)(2,1)}, bf16[128,896]{1,0:T(8,128)(2,1)S(1)}, u32[]{:S(2)}, u32[]{:S(2)}) collective-permute-start(bf16[128,896]{1,0:T(8,128)(2,1)} %get-tuple-element.17), channel_id=1, source_target_pairs={{0,259},{1,256},{2,257},{3,258},{256,3},{257,0},{258,1},{259,2},{4... | collective-permute-start | bytes 688136 | tf_op jit(solution)/shard_map/ppermute | solution.py:100
  28.9 6.9 %collective-permute-done.near_w = bf16[256,896]{1,0:T(8,128)(2,1)S(1)} collective-permute-done((bf16[256,896]{1,0:T(8,128)(2,1)S(1)}, bf16[256,896]{1,0:T(8,128)(2,1)S(1)}, u32[]{:S(2)}, u32[]{:S(2)}) %collective-permute-start) | collective-permute-done | bytes 458784 | tf_op jit(solution)/shard_map/ppermute | solution.py:100
  35.8 1.9 %collective-permute-start.2 = (bf16[128,896]{1,0:T(8,128)(2,1)S(1)}, bf16[128,896]{1,0:T(8,128)(2,1)S(1)}, u32[]{:S(2)}, u32[]{:S(2)}) collective-permute-start(bf16[128,896]{1,0:T(8,128)(2,1)S(1)} %slice.4), channel_id=1, source_target_pairs={{0,258},{1,257},{2,256},{3,259},{256,2},{257,1},{258,0},{259,3},{4... | collective-permute-start | bytes 688136 | tf_op jit(solution)/shard_map/ppermute | solution.py:100
  38.4 6.5 %collective-permute-done.2.refs_4_.far_w = bf16[128,896]{1,0:T(8,128)(2,1)S(1)} collective-permute-done((bf16[128,896]{1,0:T(8,128)(2,1)S(1)}, bf16[128,896]{1,0:T(8,128)(2,1)S(1)}, u32[]{:S(2)}, u32[]{:S(2)}) %collective-permute-start.2) | collective-permute-done | bytes 229408 | tf_op jit(solution)/shard_map/ppermute | solution.py:100
  47.0 1.9 %collective-permute-start.6 = (bf16[1792,256]{1,0:T(8,128)(2,1)S(1)}, bf16[1792,256]{1,0:T(8,128)(2,1)S(1)}, u32[]{:S(2)}, u32[]{:S(2)}) collective-permute-start(bf16[1792,256]{1,0:T(8,128)(2,1)S(1)} %other_slices.1), channel_id=1, source_target_pairs={{0,1},{1,0},{2,3},{3,2},{256,257},{257,256},{258,259},{259,258},{4... | collective-permute-start | bytes 2752520 | tf_op jit(solution)/shard_map/ppermute | solution.py:100
  49.0 2.8 %collective-permute-start.4 = (bf16[512,512]{1,0:T(8,128)(2,1)S(1)}, bf16[512,512]{1,0:T(8,128)(2,1)S(1)}, u32[]{:S(2)}, u32[]{:S(2)}) collective-permute-start(bf16[512,512]{1,0:T(8,128)(2,1)S(1)} %bitcast.18), channel_id=1, source_target_pairs={{0,259},{1,256},{2,257},{3,258},{256,3},{257,0},{258,1},{259,2},{4... | collective-permute-start | bytes 1572872 | tf_op jit(solution)/shard_map/ppermute | solution.py:100
  51.7 5.9 %collective-permute-done.3.refs_1_ = bf16[512,512]{1,0:T(8,128)(2,1)S(1)} collective-permute-done((bf16[512,512]{1,0:T(8,128)(2,1)S(1)}, bf16[512,512]{1,0:T(8,128)(2,1)S(1)}, u32[]{:S(2)}, u32[]{:S(2)}) %collective-permute-start.3) | collective-permute-done | bytes 524320 | tf_op jit(solution)/shard_map/ppermute | solution.py:100
  59.6 2.0 %collective-permute-done.4.refs_2_ = bf16[512,512]{1,0:T(8,128)(2,1)S(1)} collective-permute-done((bf16[512,512]{1,0:T(8,128)(2,1)S(1)}, bf16[512,512]{1,0:T(8,128)(2,1)S(1)}, u32[]{:S(2)}, u32[]{:S(2)}) %collective-permute-start.4) | collective-permute-done | bytes 524320 | tf_op jit(solution)/shard_map/ppermute | solution.py:100
  61.6 8.3 %collective-permute-done.5.refs_3_ = bf16[512,512]{1,0:T(8,128)(2,1)S(1)} collective-permute-done((bf16[512,512]{1,0:T(8,128)(2,1)S(1)}, bf16[512,512]{1,0:T(8,128)(2,1)S(1)}, u32[]{:S(2)}, u32[]{:S(2)}) %collective-permute-start.5) | collective-permute-done | bytes 524320 | tf_op jit(solution)/shard_map/ppermute | solution.py:100
  69.9 2.1 %partial.1 = (f32[576,256]{1,0:T(8,128)S(1)}, f32[576,256]{1,0:T(8,128)S(1)}) custom-call(bf16[512,512]{1,0:T(8,128)(2,1)S(1)} %bitcast.19, bf16[512,512]{1,0:T(8,128)(2,1)S(1)} %collective-permute-done.3.refs_1_, bf16[512,512]{1,0:T(8,128)(2,1)S(1)} %collective-permute-done.4.refs_2_, bf16[512,512]{1,0:T(8,128)(2,1)S(1)} %collective-permute-done.5.refs_3_, ...), custom_call_target="tpu_custom_call" | custom-call | flops 1000000000 | bytes 6000000 | tf_op jit(solution)/shard_map/partial/pallas_call | solution.py:371
  72.1 2.1 %collective-permute-start.7 = (f32[576,256]{1,0:T(8,128)S(1)}, f32[576,256]{1,0:T(8,128)S(1)}, u32[]{:S(2)}, u32[]{:S(2)}) collective-permute-start(f32[576,256]{1,0:T(8,128)S(1)} %get-tuple-element.21), channel_id=1, source_target_pairs={{0,1},{1,0},{2,3},{3,2},{256,257},{257,256},{258,259},{259,258},{4... | collective-permute-start | bytes 1769480 | tf_op jit(solution)/shard_map/ppermute | solution.py:100
  74.1 2.0 %collective-permute-done.7.two_ref = f32[576,256]{1,0:T(8,128)S(1)} collective-permute-done((f32[576,256]{1,0:T(8,128)S(1)}, f32[576,256]{1,0:T(8,128)S(1)}, u32[]{:S(2)}, u32[]{:S(2)}) %collective-permute-start.7) | collective-permute-done | bytes 589856 | tf_op jit(solution)/shard_map/ppermute | solution.py:100
  76.2 1.9 %collective-permute-start.8 = (bf16[576,128]{1,0:T(8,128)(2,1)S(1)}, bf16[576,128]{1,0:T(8,128)(2,1)S(1)}, u32[]{:S(2)}, u32[]{:S(2)}) collective-permute-start(bf16[576,128]{1,0:T(8,128)(2,1)S(1)} %hidden.1.own_h), channel_id=1, source_target_pairs={{0,256},{1,259},{2,258},{3,257},{256,0},{257,3},{258,2},{259,1},{4... | collective-permute-start | bytes 442376 | tf_op jit(solution)/shard_map/ppermute | solution.py:100
  78.1 4.6 %collective-permute-start.9 = (bf16[576,128]{1,0:T(8,128)(2,1)S(1)}, bf16[576,128]{1,0:T(8,128)(2,1)S(1)}, u32[]{:S(2)}, u32[]{:S(2)}) collective-permute-start(bf16[576,128]{1,0:T(8,128)(2,1)S(1)} %hidden.1.own_h), channel_id=1, source_target_pairs={{0,259},{1,256},{2,257},{3,258},{256,3},{257,0},{258,1},{259,2},{4... | collective-permute-start | bytes 442376 | tf_op jit(solution)/shard_map/ppermute | solution.py:100
  85.4 6.3 %collective-permute-done.10.far_h = bf16[576,128]{1,0:T(8,128)(2,1)S(1)} collective-permute-done((bf16[576,128]{1,0:T(8,128)(2,1)S(1)}, bf16[576,128]{1,0:T(8,128)(2,1)S(1)}, u32[]{:S(2)}, u32[]{:S(2)}) %collective-permute-start.10) | collective-permute-done | bytes 147488 | tf_op jit(solution)/shard_map/ppermute | solution.py:100
  93.3 1.9 %collective-permute-start.11 = (bf16[576,512]{1,0:T(8,128)(2,1)S(1)}, bf16[576,512]{1,0:T(8,128)(2,1)S(1)}, u32[]{:S(2)}, u32[]{:S(2)}) collective-permute-start(bf16[576,512]{1,0:T(8,128)(2,1)S(1)} %get-tuple-element.25), channel_id=1, source_target_pairs={{0,1},{1,0},{2,3},{3,2},{256,257},{257,256},{258,259},{259,258},{4... | collective-permute-start | bytes 1769480 | tf_op jit(solution)/shard_map/ppermute | solution.py:100
  95.2 2.0 %collective-permute-done.11.two_ref = bf16[576,512]{1,0:T(8,128)(2,1)S(1)} collective-permute-done((bf16[576,512]{1,0:T(8,128)(2,1)S(1)}, bf16[576,512]{1,0:T(8,128)(2,1)S(1)}, u32[]{:S(2)}, u32[]{:S(2)}) %collective-permute-start.11) | collective-permute-done | bytes 589856 | tf_op jit(solution)/shard_map/ppermute | solution.py:100
  98.5 12.7 %all-to-all-start.1 = ((bf16[64,8,512]{2,1,0:T(8,128)(2,1)}), bf16[64,8,512]{2,1,0:T(8,128)(2,1)S(1)}, u32[]{:S(2)}, u32[]{:S(2)}) async-start(bf16[64,8,512]{2,1,0:T(8,128)(2,1)} %bitcast.12), calls=%async_computation.1 | async-start | bytes 1048576 | tf_op jit(solution)/shard_map/all_to_all | solution.py:391
  112.9 1.9 %collective-permute-start.12 = (f32[96,512]{1,0:T(8,128)S(1)}, f32[96,512]{1,0:T(8,128)S(1)}, u32[]{:S(2)}, u32[]{:S(2)}) collective-permute-start(f32[96,512]{1,0:T(8,128)S(1)} %get-tuple-element.27), channel_id=1, source_target_pairs={{0,256},{1,257},{2,258},{3,259},{256,0},{257,1},{258,2},{259,3},{4... | collective-permute-start | bytes 589832 | tf_op jit(solution)/shard_map/ppermute | solution.py:100
  115.7 5.7 %collective-permute-done.12.two_ref = f32[96,512]{1,0:T(8,128)S(1)} collective-permute-done((f32[96,512]{1,0:T(8,128)S(1)}, f32[96,512]{1,0:T(8,128)S(1)}, u32[]{:S(2)}, u32[]{:S(2)}) %collective-permute-start.12) | collective-permute-done | bytes 196640 | tf_op jit(solution)/shard_map/ppermute | solution.py:100
  122.2 8.9 %all-to-all-done.1 = bf16[64,8,512]{2,1,0:T(8,128)(2,1)S(1)} async-done(((bf16[64,8,512]{2,1,0:T(8,128)(2,1)}), bf16[64,8,512]{2,1,0:T(8,128)(2,1)S(1)}, u32[]{:S(2)}, u32[]{:S(2)}) %all-to-all-start.1) | async-done | bytes 524320 | tf_op jit(solution)/shard_map/all_to_all | solution.py:391
  (45 shorter events, 16.9 us)
Async XLA Ops:
  3.5 43.3 %copy-start = (bf16[1,3584,128]{2,1,0:T(8,128)(2,1)S(1)}, bf16[1,3584,128]{2,1,0:T(8,128)(2,1)}, u32[]{:S(2)}) copy-start(bf16[1,3584,128]{2,1,0:T(8,128)(2,1)} %param.17) | copy-start | bytes 2752516
  3.5 43.3 %copy-start.1 = (bf16[1,3584,128]{2,1,0:T(8,128)(2,1)S(1)}, bf16[1,3584,128]{2,1,0:T(8,128)(2,1)}, u32[]{:S(2)}) copy-start(bf16[1,3584,128]{2,1,0:T(8,128)(2,1)} %param.18) | copy-start | bytes 2752516
  6.3 38.6 %all-to-all-start = ((bf16[64,8,512]{2,1,0:T(8,128)(2,1)}), bf16[64,8,512]{2,1,0:T(8,128)(2,1)S(1)}, u32[]{:S(2)}, u32[]{:S(2)}) async-start(bf16[64,8,512]{2,1,0:T(8,128)(2,1)} %bitcast.2), calls=%async_computation | async-start | bytes 1048576 | tf_op jit(solution)/shard_map/all_to_all | solution.py:355
  22.9 12.8 %collective-permute-start = (bf16[256,896]{1,0:T(8,128)(2,1)S(1)}, bf16[256,896]{1,0:T(8,128)(2,1)S(1)}, u32[]{:S(2)}, u32[]{:S(2)}) collective-permute-start(bf16[256,896]{1,0:T(8,128)(2,1)S(1)} %get-tuple-element.16), channel_id=1, source_target_pairs={{0,256},{1,259},{2,258},{3,257},{256,0},{257,3},{258,2},{259,1},{4... | collective-permute-start | bytes 1376264 | tf_op jit(solution)/shard_map/ppermute | solution.py:100
  25.7 12.0 %collective-permute-start.1 = (bf16[128,896]{1,0:T(8,128)(2,1)}, bf16[128,896]{1,0:T(8,128)(2,1)S(1)}, u32[]{:S(2)}, u32[]{:S(2)}) collective-permute-start(bf16[128,896]{1,0:T(8,128)(2,1)} %get-tuple-element.17), channel_id=1, source_target_pairs={{0,259},{1,256},{2,257},{3,258},{256,3},{257,0},{258,1},{259,2},{4... | collective-permute-start | bytes 688136 | tf_op jit(solution)/shard_map/ppermute | solution.py:100
  35.8 9.1 %collective-permute-start.2 = (bf16[128,896]{1,0:T(8,128)(2,1)S(1)}, bf16[128,896]{1,0:T(8,128)(2,1)S(1)}, u32[]{:S(2)}, u32[]{:S(2)}) collective-permute-start(bf16[128,896]{1,0:T(8,128)(2,1)S(1)} %slice.4), channel_id=1, source_target_pairs={{0,258},{1,257},{2,256},{3,259},{256,2},{257,1},{258,0},{259,3},{4... | collective-permute-start | bytes 688136 | tf_op jit(solution)/shard_map/ppermute | solution.py:100
  44.9 12.7 %collective-permute-start.3 = (bf16[512,512]{1,0:T(8,128)(2,1)S(1)}, bf16[512,512]{1,0:T(8,128)(2,1)S(1)}, u32[]{:S(2)}, u32[]{:S(2)}) collective-permute-start(bf16[512,512]{1,0:T(8,128)(2,1)S(1)} %bitcast.16), channel_id=1, source_target_pairs={{0,256},{1,259},{2,258},{3,257},{256,0},{257,3},{258,2},{259,1},{4... | collective-permute-start | bytes 1572872 | tf_op jit(solution)/shard_map/ppermute | solution.py:100
  47.0 14.6 %collective-permute-start.6 = (bf16[1792,256]{1,0:T(8,128)(2,1)S(1)}, bf16[1792,256]{1,0:T(8,128)(2,1)S(1)}, u32[]{:S(2)}, u32[]{:S(2)}) collective-permute-start(bf16[1792,256]{1,0:T(8,128)(2,1)S(1)} %other_slices.1), channel_id=1, source_target_pairs={{0,1},{1,0},{2,3},{3,2},{256,257},{257,256},{258,259},{259,258},{4... | collective-permute-start | bytes 2752520 | tf_op jit(solution)/shard_map/ppermute | solution.py:100
  49.0 12.6 %collective-permute-start.4 = (bf16[512,512]{1,0:T(8,128)(2,1)S(1)}, bf16[512,512]{1,0:T(8,128)(2,1)S(1)}, u32[]{:S(2)}, u32[]{:S(2)}) collective-permute-start(bf16[512,512]{1,0:T(8,128)(2,1)S(1)} %bitcast.18), channel_id=1, source_target_pairs={{0,259},{1,256},{2,257},{3,258},{256,3},{257,0},{258,1},{259,2},{4... | collective-permute-start | bytes 1572872 | tf_op jit(solution)/shard_map/ppermute | solution.py:100
  57.6 12.3 %collective-permute-start.5 = (bf16[512,512]{1,0:T(8,128)(2,1)S(1)}, bf16[512,512]{1,0:T(8,128)(2,1)S(1)}, u32[]{:S(2)}, u32[]{:S(2)}) collective-permute-start(bf16[512,512]{1,0:T(8,128)(2,1)S(1)} %collective-permute-done.3.refs_1_), channel_id=1, source_target_pairs={{0,258},{1,257},{2,256},{3,259},{256,2},{257,1},{258,0},{259,3},{4... | collective-permute-start | bytes 1572872 | tf_op jit(solution)/shard_map/ppermute | solution.py:100
  72.0 19.6 %copy-start.4 = (bf16[1,128,3584]{2,1,0:T(8,128)(2,1)S(1)}, bf16[1,128,3584]{2,1,0:T(8,128)(2,1)}, u32[]{:S(2)}) copy-start(bf16[1,128,3584]{2,1,0:T(8,128)(2,1)} %param.19) | copy-start | bytes 2752516
  72.1 19.6 %copy-start.11 = (bf16[128,896]{1,0:T(8,128)(2,1)S(1)}, bf16[128,896]{1,0:T(8,128)(2,1)}, u32[]{:S(2)}) copy-start(bf16[128,896]{1,0:T(8,128)(2,1)} %copy-done.10) | copy-start | bytes 688132
  72.1 4.0 %collective-permute-start.7 = (f32[576,256]{1,0:T(8,128)S(1)}, f32[576,256]{1,0:T(8,128)S(1)}, u32[]{:S(2)}, u32[]{:S(2)}) collective-permute-start(f32[576,256]{1,0:T(8,128)S(1)} %get-tuple-element.21), channel_id=1, source_target_pairs={{0,1},{1,0},{2,3},{3,2},{256,257},{257,256},{258,259},{259,258},{4... | collective-permute-start | bytes 1769480 | tf_op jit(solution)/shard_map/ppermute | solution.py:100
  76.2 7.2 %collective-permute-start.8 = (bf16[576,128]{1,0:T(8,128)(2,1)S(1)}, bf16[576,128]{1,0:T(8,128)(2,1)S(1)}, u32[]{:S(2)}, u32[]{:S(2)}) collective-permute-start(bf16[576,128]{1,0:T(8,128)(2,1)S(1)} %hidden.1.own_h), channel_id=1, source_target_pairs={{0,256},{1,259},{2,258},{3,257},{256,0},{257,3},{258,2},{259,1},{4... | collective-permute-start | bytes 442376 | tf_op jit(solution)/shard_map/ppermute | solution.py:100
  78.1 7.3 %collective-permute-start.9 = (bf16[576,128]{1,0:T(8,128)(2,1)S(1)}, bf16[576,128]{1,0:T(8,128)(2,1)S(1)}, u32[]{:S(2)}, u32[]{:S(2)}) collective-permute-start(bf16[576,128]{1,0:T(8,128)(2,1)S(1)} %hidden.1.own_h), channel_id=1, source_target_pairs={{0,259},{1,256},{2,257},{3,258},{256,3},{257,0},{258,1},{259,2},{4... | collective-permute-start | bytes 442376 | tf_op jit(solution)/shard_map/ppermute | solution.py:100
  83.4 8.2 %collective-permute-start.10 = (bf16[576,128]{1,0:T(8,128)(2,1)S(1)}, bf16[576,128]{1,0:T(8,128)(2,1)S(1)}, u32[]{:S(2)}, u32[]{:S(2)}) collective-permute-start(bf16[576,128]{1,0:T(8,128)(2,1)S(1)} %collective-permute-done.8.near_h), channel_id=1, source_target_pairs={{0,258},{1,257},{2,256},{3,259},{256,2},{257,1},{258,0},{259,3},{4... | collective-permute-start | bytes 442376 | tf_op jit(solution)/shard_map/ppermute | solution.py:100
  93.3 3.9 %collective-permute-start.11 = (bf16[576,512]{1,0:T(8,128)(2,1)S(1)}, bf16[576,512]{1,0:T(8,128)(2,1)S(1)}, u32[]{:S(2)}, u32[]{:S(2)}) collective-permute-start(bf16[576,512]{1,0:T(8,128)(2,1)S(1)} %get-tuple-element.25), channel_id=1, source_target_pairs={{0,1},{1,0},{2,3},{3,2},{256,257},{257,256},{258,259},{259,258},{4... | collective-permute-start | bytes 1769480 | tf_op jit(solution)/shard_map/ppermute | solution.py:100
  97.2 14.8 %copy-start.2 = (bf16[1,1024,576]{1,2,0:T(8,128)(2,1)S(1)}, bf16[1,1024,576]{1,2,0:T(8,128)(2,1)}, u32[]{:S(2)}) copy-start(bf16[1,1024,576]{1,2,0:T(8,128)(2,1)} %param.10) | copy-start | bytes 3538948
  97.2 14.8 %copy-start.6 = (bf16[3,1,32,576]{3,2,1,0:T(8,128)(2,1)S(1)}, bf16[3,1,32,576]{3,2,1,0:T(8,128)(2,1)}, u32[]{:S(2)}) copy-start(bf16[3,1,32,576]{3,2,1,0:T(8,128)(2,1)} %param.12) | copy-start | bytes 331780
  97.2 14.8 %copy-start.9 = (bf16[3,1,576]{2,0,1:T(4,128)(2,1)S(1)}, bf16[3,1,576]{2,0,1:T(4,128)(2,1)}, u32[]{:S(2)}) copy-start(bf16[3,1,576]{2,0,1:T(4,128)(2,1)} %param.11) | copy-start | bytes 10372
  98.5 32.6 %all-to-all-start.1 = ((bf16[64,8,512]{2,1,0:T(8,128)(2,1)}), bf16[64,8,512]{2,1,0:T(8,128)(2,1)S(1)}, u32[]{:S(2)}, u32[]{:S(2)}) async-start(bf16[64,8,512]{2,1,0:T(8,128)(2,1)} %bitcast.12), calls=%async_computation.1 | async-start | bytes 1048576 | tf_op jit(solution)/shard_map/all_to_all | solution.py:391
  111.3 3.6 %copy-start.8 = (s32[3,12,8]{1,2,0:T(8,128)S(1)}, s32[3,12,8]{1,2,0:T(8,128)}, u32[]{:S(2)}) copy-start(s32[3,12,8]{1,2,0:T(8,128)} %param.15) | copy-start | bytes 3460
  111.3 3.7 %copy-start.12 = (f32[3,12,8]{1,2,0:T(8,128)S(1)}, f32[3,12,8]{1,2,0:T(8,128)}, u32[]{:S(2)}) copy-start(f32[3,12,8]{1,2,0:T(8,128)} %param.16) | copy-start | bytes 3460
  112.9 8.5 %collective-permute-start.12 = (f32[96,512]{1,0:T(8,128)S(1)}, f32[96,512]{1,0:T(8,128)S(1)}, u32[]{:S(2)}, u32[]{:S(2)}) collective-permute-start(f32[96,512]{1,0:T(8,128)S(1)} %get-tuple-element.27), channel_id=1, source_target_pairs={{0,256},{1,257},{2,258},{3,259},{256,0},{257,1},{258,2},{259,3},{4... | collective-permute-start | bytes 589832 | tf_op jit(solution)/shard_map/ppermute | solution.py:100
  (4 other events, 3.6 us)

commit v8 on v7

--- a/solution.py
+++ b/solution.py
@@ -348,7 +348,6 @@
             pltpu.VMEM((units, width), BF),
             pltpu.SemaphoreType.DMA((3,)),
         ],
-        compiler_params=pltpu.CompilerParams(vmem_limit_bytes=20 * 1024 * 1024),
         cost_estimate=pl.CostEstimate(flops=10**8, bytes_accessed=10**6, transcendentals=0),
         name="pack",
     )(token_rows, jnp.swapaxes(routes, 1, 2), down_proj)
@@ -358,10 +357,10 @@
 
     gate_proj, up_proj = gate_proj.reshape(width, units), up_proj.reshape(width, units)
     near_down, crossed_down = to_near(near_down), to_crossed(crossed_down)
+    arrived, near_down, crossed_down = lax.optimization_barrier(
+        (arrived, near_down, crossed_down)
+    )
     far_down = onward(near_down[units:])
-    arrived, near_down, crossed_down, far_down = lax.optimization_barrier(
-        (arrived, near_down, crossed_down, far_down)
-    )
     other = call(
         other_slices_body, jax.ShapeDtypeStruct((width // 2, 2 * units), BF),
         [VMEM] * 3, 10**6, 4 * 10**6, "other_slices",

time: 133 us -> 124 us (0.932)
  waiting for transfers between devices: 55.3 us -> 51.3 us
  local copies, waits for them, and re-layouts: 3.8 us -> 0.24 us
  starting transfers between devices: 60 us -> 57.7 us
    ppermute x13, waiting for transfers between devices: 46.3 us -> 35.7 us  [permute(): return lax.ppermute(value, LINE, [(d, target(d)) for d in range(8)])]
    all_to_all x1, starting transfers between devices: 12.7 us -> 6.01 us  [local(): lax.all_to_all(outgoing.reshape(experts, ROWS, part + HALF), 'grp', split...]
    all_to_all x1, waiting for transfers between devices: 0.01 us -> 6.67 us  [local(): lax.all_to_all(packed.reshape(experts, ROWS, part + HALF), 'grp', split_a...]
    ppermute x13, starting transfers between devices: 30.7 us -> 35.1 us  [permute(): return lax.ppermute(value, LINE, [(d, target(d)) for d in range(8)])]
    unnamed x28 -> x18, local copies, waits for them, and re-layouts: 3.78 us -> 0.22 us
where the time goes in v8:
time: 124 us; the launch traced here: 123 us
  starting transfers between devices  57.7 us (47%)
  waiting for transfers between devices  51.3 us (41%)
  Pallas kernels  12.3 us (10%)
  between operations  1.56 us (1%)
    ppermute x13, waiting for transfers between devices, permute(): return lax.ppermute(value, LINE, [(d, target(d)) for d in range(8)])  35.7 us
    ppermute x13, starting transfers between devices, permute(): return lax.ppermute(value, LINE, [(d, target(d)) for d in range(8)])  35.1 us
    all_to_all x1, starting transfers between devices, local(): lax.all_to_all(packed.reshape(experts, ROWS, part + HALF), 'grp', split_a...  16.6 us
    all_to_all x1, waiting for transfers between devices, local(): lax.all_to_all(outgoing.reshape(experts, ROWS, part + HALF), 'grp', split...  8.94 us
    all_to_all x1, waiting for transfers between devices, local(): lax.all_to_all(packed.reshape(experts, ROWS, part + HALF), 'grp', split_a...  6.67 us
    all_to_all x1, starting transfers between devices, local(): lax.all_to_all(outgoing.reshape(experts, ROWS, part + HALF), 'grp', split...  6.01 us
    pallas_call x1, Pallas kernels, local(): pl.pallas_call(pack_body, out_shape=[jax.ShapeDtypeStruct((rows, part + H...  3.51 us
  transfers between devices with their start and end apart: 15, of which 12 were waited for; matrix products, arithmetic and copies ran while one was open for 0% of the time, Pallas kernels for 2%

profile of v8, /device:TPU:6, one launch (start us, length us, event | category | flops | bytes accessed | tf_op | source)
XLA Modules:
  0.0 123.1 jit_solution(5186564112463604426)
XLA Ops:
  0.7 3.5 %pack.1 = (bf16[512,512]{1,0:T(8,128)(2,1)}, bf16[256,896]{1,0:T(8,128)(2,1)}, bf16[128,896]{1,0:T(8,128)(2,1)}) custom-call(bf16[3,12,3584]{2,1,0:T(8,128)(2,1)} %tokens_ref.1, s32[3,8,12]{2,1,0:T(8,128)} %bitcast.31, bf16[128,3584]{1,0:T(8,128)(2,1)} %bitcast.26), custom_call_target="tpu_custom_call" | custom-call | flops 100000000 | bytes 1000000 | tf_op jit(solution)/shard_map/pack/pallas_call | solution.py:336
  4.2 16.6 %all-to-all-start = ((bf16[64,8,512]{2,1,0:T(8,128)(2,1)}), bf16[64,8,512]{2,1,0:T(8,128)(2,1)S(1)}, u32[]{:S(2)}, u32[]{:S(2)}) async-start(bf16[64,8,512]{2,1,0:T(8,128)(2,1)} %bitcast.30), calls=%async_computation | async-start | bytes 1048576 | tf_op jit(solution)/shard_map/all_to_all | solution.py:354
  20.8 2.7 %collective-permute-start = (bf16[256,896]{1,0:T(8,128)(2,1)}, bf16[256,896]{1,0:T(8,128)(2,1)S(1)}, u32[]{:S(2)}, u32[]{:S(2)}) collective-permute-start(bf16[256,896]{1,0:T(8,128)(2,1)} %get-tuple-element.15), channel_id=1, source_target_pairs={{0,256},{1,259},{2,258},{3,257},{256,0},{257,3},{258,2},{259,1},{4... | collective-permute-start | bytes 1376264 | tf_op jit(solution)/shard_map/ppermute | solution.py:100
  23.5 3.2 %collective-permute-start.1 = (bf16[128,896]{1,0:T(8,128)(2,1)}, bf16[128,896]{1,0:T(8,128)(2,1)S(1)}, u32[]{:S(2)}, u32[]{:S(2)}) collective-permute-start(bf16[128,896]{1,0:T(8,128)(2,1)} %get-tuple-element.16), channel_id=1, source_target_pairs={{0,259},{1,256},{2,257},{3,258},{256,3},{257,0},{258,1},{259,2},{4... | collective-permute-start | bytes 688136 | tf_op jit(solution)/shard_map/ppermute | solution.py:100
  26.7 6.9 %collective-permute-done.1.crossed_w = bf16[128,896]{1,0:T(8,128)(2,1)S(1)} collective-permute-done((bf16[128,896]{1,0:T(8,128)(2,1)}, bf16[128,896]{1,0:T(8,128)(2,1)S(1)}, u32[]{:S(2)}, u32[]{:S(2)}) %collective-permute-start.1) | collective-permute-done | bytes 229408 | tf_op jit(solution)/shard_map/ppermute | solution.py:100
  33.8 6.7 %all-to-all-done = bf16[64,8,512]{2,1,0:T(8,128)(2,1)S(1)} async-done(((bf16[64,8,512]{2,1,0:T(8,128)(2,1)}), bf16[64,8,512]{2,1,0:T(8,128)(2,1)S(1)}, u32[]{:S(2)}, u32[]{:S(2)}) %all-to-all-start) | async-done | bytes 524320 | tf_op jit(solution)/shard_map/all_to_all | solution.py:354
  40.5 2.7 %collective-permute-start.2 = (bf16[512,512]{1,0:T(8,128)(2,1)S(1)}, bf16[512,512]{1,0:T(8,128)(2,1)S(1)}, u32[]{:S(2)}, u32[]{:S(2)}) collective-permute-start(bf16[512,512]{1,0:T(8,128)(2,1)S(1)} %bitcast.16), channel_id=1, source_target_pairs={{0,256},{1,259},{2,258},{3,257},{256,0},{257,3},{258,2},{259,1},{4... | collective-permute-start | bytes 1572872 | tf_op jit(solution)/shard_map/ppermute | solution.py:100
  43.4 1.9 %collective-permute-start.6 = (bf16[1792,256]{1,0:T(8,128)(2,1)S(1)}, bf16[1792,256]{1,0:T(8,128)(2,1)S(1)}, u32[]{:S(2)}, u32[]{:S(2)}) collective-permute-start(bf16[1792,256]{1,0:T(8,128)(2,1)S(1)} %other_slices.1), channel_id=1, source_target_pairs={{0,1},{1,0},{2,3},{3,2},{256,257},{257,256},{258,259},{259,258},{4... | collective-permute-start | bytes 2752520 | tf_op jit(solution)/shard_map/ppermute | solution.py:100
  45.3 3.2 %collective-permute-start.3 = (bf16[512,512]{1,0:T(8,128)(2,1)S(1)}, bf16[512,512]{1,0:T(8,128)(2,1)S(1)}, u32[]{:S(2)}, u32[]{:S(2)}) collective-permute-start(bf16[512,512]{1,0:T(8,128)(2,1)S(1)} %bitcast.18), channel_id=1, source_target_pairs={{0,259},{1,256},{2,257},{3,258},{256,3},{257,0},{258,1},{259,2},{4... | collective-permute-start | bytes 1572872 | tf_op jit(solution)/shard_map/ppermute | solution.py:100
  48.5 4.3 %collective-permute-done.2.refs_1_ = bf16[512,512]{1,0:T(8,128)(2,1)S(1)} collective-permute-done((bf16[512,512]{1,0:T(8,128)(2,1)S(1)}, bf16[512,512]{1,0:T(8,128)(2,1)S(1)}, u32[]{:S(2)}, u32[]{:S(2)}) %collective-permute-start.2) | collective-permute-done | bytes 524320 | tf_op jit(solution)/shard_map/ppermute | solution.py:100
  54.8 5.1 %collective-permute-start.5 = (bf16[128,896]{1,0:T(8,128)(2,1)S(1)}, bf16[128,896]{1,0:T(8,128)(2,1)S(1)}, u32[]{:S(2)}, u32[]{:S(2)}) collective-permute-start(bf16[128,896]{1,0:T(8,128)(2,1)S(1)} %slice.3), channel_id=1, source_target_pairs={{0,258},{1,257},{2,256},{3,259},{256,2},{257,1},{258,0},{259,3},{4... | collective-permute-start | bytes 688136 | tf_op jit(solution)/shard_map/ppermute | solution.py:100
  59.9 7.6 %collective-permute-done.5.refs_4_.far_w = bf16[128,896]{1,0:T(8,128)(2,1)S(1)} collective-permute-done((bf16[128,896]{1,0:T(8,128)(2,1)S(1)}, bf16[128,896]{1,0:T(8,128)(2,1)S(1)}, u32[]{:S(2)}, u32[]{:S(2)}) %collective-permute-start.5) | collective-permute-done | bytes 229408 | tf_op jit(solution)/shard_map/ppermute | solution.py:100
  67.6 2.1 %partial.1 = (f32[576,256]{1,0:T(8,128)S(1)}, f32[576,256]{1,0:T(8,128)S(1)}) custom-call(bf16[512,512]{1,0:T(8,128)(2,1)S(1)} %bitcast.19, bf16[512,512]{1,0:T(8,128)(2,1)S(1)} %collective-permute-done.2.refs_1_, bf16[512,512]{1,0:T(8,128)(2,1)S(1)} %collective-permute-done.3.refs_2_, bf16[512,512]{1,0:T(8,128)(2,1)S(1)} %collective-permute-done.4.refs_3_, ...), custom_call_target="tpu_custom_call" | custom-call | flops 1000000000 | bytes 6000000 | tf_op jit(solution)/shard_map/partial/pallas_call | solution.py:370
  69.7 2.1 %collective-permute-start.7 = (f32[576,256]{1,0:T(8,128)S(1)}, f32[576,256]{1,0:T(8,128)S(1)}, u32[]{:S(2)}, u32[]{:S(2)}) collective-permute-start(f32[576,256]{1,0:T(8,128)S(1)} %get-tuple-element.20), channel_id=1, source_target_pairs={{0,1},{1,0},{2,3},{3,2},{256,257},{257,256},{258,259},{259,258},{4... | collective-permute-start | bytes 1769480 | tf_op jit(solution)/shard_map/ppermute | solution.py:100
  71.7 2.0 %collective-permute-done.7.two_ref = f32[576,256]{1,0:T(8,128)S(1)} collective-permute-done((f32[576,256]{1,0:T(8,128)S(1)}, f32[576,256]{1,0:T(8,128)S(1)}, u32[]{:S(2)}, u32[]{:S(2)}) %collective-permute-start.7) | collective-permute-done | bytes 589856 | tf_op jit(solution)/shard_map/ppermute | solution.py:100
  73.8 1.9 %collective-permute-start.8 = (bf16[576,128]{1,0:T(8,128)(2,1)S(1)}, bf16[576,128]{1,0:T(8,128)(2,1)S(1)}, u32[]{:S(2)}, u32[]{:S(2)}) collective-permute-start(bf16[576,128]{1,0:T(8,128)(2,1)S(1)} %hidden.1.own_h), channel_id=1, source_target_pairs={{0,256},{1,259},{2,258},{3,257},{256,0},{257,3},{258,2},{259,1},{4... | collective-permute-start | bytes 442376 | tf_op jit(solution)/shard_map/ppermute | solution.py:100
  75.8 4.6 %collective-permute-start.9 = (bf16[576,128]{1,0:T(8,128)(2,1)S(1)}, bf16[576,128]{1,0:T(8,128)(2,1)S(1)}, u32[]{:S(2)}, u32[]{:S(2)}) collective-permute-start(bf16[576,128]{1,0:T(8,128)(2,1)S(1)} %hidden.1.own_h), channel_id=1, source_target_pairs={{0,259},{1,256},{2,257},{3,258},{256,3},{257,0},{258,1},{259,2},{4... | collective-permute-start | bytes 442376 | tf_op jit(solution)/shard_map/ppermute | solution.py:100
  83.0 6.3 %collective-permute-done.10.far_h = bf16[576,128]{1,0:T(8,128)(2,1)S(1)} collective-permute-done((bf16[576,128]{1,0:T(8,128)(2,1)S(1)}, bf16[576,128]{1,0:T(8,128)(2,1)S(1)}, u32[]{:S(2)}, u32[]{:S(2)}) %collective-permute-start.10) | collective-permute-done | bytes 147488 | tf_op jit(solution)/shard_map/ppermute | solution.py:100
  90.9 1.9 %collective-permute-start.11 = (bf16[576,512]{1,0:T(8,128)(2,1)S(1)}, bf16[576,512]{1,0:T(8,128)(2,1)S(1)}, u32[]{:S(2)}, u32[]{:S(2)}) collective-permute-start(bf16[576,512]{1,0:T(8,128)(2,1)S(1)} %get-tuple-element.23), channel_id=1, source_target_pairs={{0,1},{1,0},{2,3},{3,2},{256,257},{257,256},{258,259},{259,258},{4... | collective-permute-start | bytes 1769480 | tf_op jit(solution)/shard_map/ppermute | solution.py:100
  92.8 2.0 %collective-permute-done.11.two_ref = bf16[576,512]{1,0:T(8,128)(2,1)S(1)} collective-permute-done((bf16[576,512]{1,0:T(8,128)(2,1)S(1)}, bf16[576,512]{1,0:T(8,128)(2,1)S(1)}, u32[]{:S(2)}, u32[]{:S(2)}) %collective-permute-start.11) | collective-permute-done | bytes 589856 | tf_op jit(solution)/shard_map/ppermute | solution.py:100
  96.2 6.0 %all-to-all-start.1 = ((bf16[64,8,512]{2,1,0:T(8,128)(2,1)}), bf16[64,8,512]{2,1,0:T(8,128)(2,1)S(1)}, u32[]{:S(2)}, u32[]{:S(2)}) async-start(bf16[64,8,512]{2,1,0:T(8,128)(2,1)} %bitcast.12), calls=%async_computation.1 | async-start | bytes 1048576 | tf_op jit(solution)/shard_map/all_to_all | solution.py:390
  103.9 1.9 %collective-permute-start.12 = (f32[96,512]{1,0:T(8,128)S(1)}, f32[96,512]{1,0:T(8,128)S(1)}, u32[]{:S(2)}, u32[]{:S(2)}) collective-permute-start(f32[96,512]{1,0:T(8,128)S(1)} %get-tuple-element.25), channel_id=1, source_target_pairs={{0,256},{1,257},{2,258},{3,259},{256,0},{257,1},{258,2},{259,3},{4... | collective-permute-start | bytes 589832 | tf_op jit(solution)/shard_map/ppermute | solution.py:100
  106.7 5.7 %collective-permute-done.12.two_ref = f32[96,512]{1,0:T(8,128)S(1)} collective-permute-done((f32[96,512]{1,0:T(8,128)S(1)}, f32[96,512]{1,0:T(8,128)S(1)}, u32[]{:S(2)}, u32[]{:S(2)}) %collective-permute-start.12) | collective-permute-done | bytes 196640 | tf_op jit(solution)/shard_map/ppermute | solution.py:100
  113.1 8.9 %all-to-all-done.1 = bf16[64,8,512]{2,1,0:T(8,128)(2,1)S(1)} async-done(((bf16[64,8,512]{2,1,0:T(8,128)(2,1)}), bf16[64,8,512]{2,1,0:T(8,128)(2,1)S(1)}, u32[]{:S(2)}, u32[]{:S(2)}) %all-to-all-start.1) | async-done | bytes 524320 | tf_op jit(solution)/shard_map/all_to_all | solution.py:390
  (35 shorter events, 11.7 us)
Async XLA Ops:
  0.6 42.6 %copy-start = (bf16[1,3584,128]{2,1,0:T(8,128)(2,1)S(1)}, bf16[1,3584,128]{2,1,0:T(8,128)(2,1)}, u32[]{:S(2)}) copy-start(bf16[1,3584,128]{2,1,0:T(8,128)(2,1)} %param.17) | copy-start | bytes 2752516
  0.6 42.6 %copy-start.1 = (bf16[1,3584,128]{2,1,0:T(8,128)(2,1)S(1)}, bf16[1,3584,128]{2,1,0:T(8,128)(2,1)}, u32[]{:S(2)}) copy-start(bf16[1,3584,128]{2,1,0:T(8,128)(2,1)} %param.18) | copy-start | bytes 2752516
  4.2 36.3 %all-to-all-start = ((bf16[64,8,512]{2,1,0:T(8,128)(2,1)}), bf16[64,8,512]{2,1,0:T(8,128)(2,1)S(1)}, u32[]{:S(2)}, u32[]{:S(2)}) async-start(bf16[64,8,512]{2,1,0:T(8,128)(2,1)} %bitcast.30), calls=%async_computation | async-start | bytes 1048576 | tf_op jit(solution)/shard_map/all_to_all | solution.py:354
  20.8 13.0 %collective-permute-start = (bf16[256,896]{1,0:T(8,128)(2,1)}, bf16[256,896]{1,0:T(8,128)(2,1)S(1)}, u32[]{:S(2)}, u32[]{:S(2)}) collective-permute-start(bf16[256,896]{1,0:T(8,128)(2,1)} %get-tuple-element.15), channel_id=1, source_target_pairs={{0,256},{1,259},{2,258},{3,257},{256,0},{257,3},{258,2},{259,1},{4... | collective-permute-start | bytes 1376264 | tf_op jit(solution)/shard_map/ppermute | solution.py:100
  23.5 10.1 %collective-permute-start.1 = (bf16[128,896]{1,0:T(8,128)(2,1)}, bf16[128,896]{1,0:T(8,128)(2,1)S(1)}, u32[]{:S(2)}, u32[]{:S(2)}) collective-permute-start(bf16[128,896]{1,0:T(8,128)(2,1)} %get-tuple-element.16), channel_id=1, source_target_pairs={{0,259},{1,256},{2,257},{3,258},{256,3},{257,0},{258,1},{259,2},{4... | collective-permute-start | bytes 688136 | tf_op jit(solution)/shard_map/ppermute | solution.py:100
  40.5 12.3 %collective-permute-start.2 = (bf16[512,512]{1,0:T(8,128)(2,1)S(1)}, bf16[512,512]{1,0:T(8,128)(2,1)S(1)}, u32[]{:S(2)}, u32[]{:S(2)}) collective-permute-start(bf16[512,512]{1,0:T(8,128)(2,1)S(1)} %bitcast.16), channel_id=1, source_target_pairs={{0,256},{1,259},{2,258},{3,257},{256,0},{257,3},{258,2},{259,1},{4... | collective-permute-start | bytes 1572872 | tf_op jit(solution)/shard_map/ppermute | solution.py:100
  43.4 24.1 %collective-permute-start.6 = (bf16[1792,256]{1,0:T(8,128)(2,1)S(1)}, bf16[1792,256]{1,0:T(8,128)(2,1)S(1)}, u32[]{:S(2)}, u32[]{:S(2)}) collective-permute-start(bf16[1792,256]{1,0:T(8,128)(2,1)S(1)} %other_slices.1), channel_id=1, source_target_pairs={{0,1},{1,0},{2,3},{3,2},{256,257},{257,256},{258,259},{259,258},{4... | collective-permute-start | bytes 2752520 | tf_op jit(solution)/shard_map/ppermute | solution.py:100
  45.3 22.2 %collective-permute-start.3 = (bf16[512,512]{1,0:T(8,128)(2,1)S(1)}, bf16[512,512]{1,0:T(8,128)(2,1)S(1)}, u32[]{:S(2)}, u32[]{:S(2)}) collective-permute-start(bf16[512,512]{1,0:T(8,128)(2,1)S(1)} %bitcast.18), channel_id=1, source_target_pairs={{0,259},{1,256},{2,257},{3,258},{256,3},{257,0},{258,1},{259,2},{4... | collective-permute-start | bytes 1572872 | tf_op jit(solution)/shard_map/ppermute | solution.py:100
  52.8 14.7 %collective-permute-start.4 = (bf16[512,512]{1,0:T(8,128)(2,1)S(1)}, bf16[512,512]{1,0:T(8,128)(2,1)S(1)}, u32[]{:S(2)}, u32[]{:S(2)}) collective-permute-start(bf16[512,512]{1,0:T(8,128)(2,1)S(1)} %collective-permute-done.2.refs_1_), channel_id=1, source_target_pairs={{0,258},{1,257},{2,256},{3,259},{256,2},{257,1},{258,0},{259,3},{4... | collective-permute-start | bytes 1572872 | tf_op jit(solution)/shard_map/ppermute | solution.py:100
  54.8 12.8 %collective-permute-start.5 = (bf16[128,896]{1,0:T(8,128)(2,1)S(1)}, bf16[128,896]{1,0:T(8,128)(2,1)S(1)}, u32[]{:S(2)}, u32[]{:S(2)}) collective-permute-start(bf16[128,896]{1,0:T(8,128)(2,1)S(1)} %slice.3), channel_id=1, source_target_pairs={{0,258},{1,257},{2,256},{3,259},{256,2},{257,1},{258,0},{259,3},{4... | collective-permute-start | bytes 688136 | tf_op jit(solution)/shard_map/ppermute | solution.py:100
  69.7 19.6 %copy-start.3 = (bf16[1,128,3584]{2,1,0:T(8,128)(2,1)S(1)}, bf16[1,128,3584]{2,1,0:T(8,128)(2,1)}, u32[]{:S(2)}) copy-start(bf16[1,128,3584]{2,1,0:T(8,128)(2,1)} %param.19) | copy-start | bytes 2752516
  69.7 4.0 %collective-permute-start.7 = (f32[576,256]{1,0:T(8,128)S(1)}, f32[576,256]{1,0:T(8,128)S(1)}, u32[]{:S(2)}, u32[]{:S(2)}) collective-permute-start(f32[576,256]{1,0:T(8,128)S(1)} %get-tuple-element.20), channel_id=1, source_target_pairs={{0,1},{1,0},{2,3},{3,2},{256,257},{257,256},{258,259},{259,258},{4... | collective-permute-start | bytes 1769480 | tf_op jit(solution)/shard_map/ppermute | solution.py:100
  73.8 7.2 %collective-permute-start.8 = (bf16[576,128]{1,0:T(8,128)(2,1)S(1)}, bf16[576,128]{1,0:T(8,128)(2,1)S(1)}, u32[]{:S(2)}, u32[]{:S(2)}) collective-permute-start(bf16[576,128]{1,0:T(8,128)(2,1)S(1)} %hidden.1.own_h), channel_id=1, source_target_pairs={{0,256},{1,259},{2,258},{3,257},{256,0},{257,3},{258,2},{259,1},{4... | collective-permute-start | bytes 442376 | tf_op jit(solution)/shard_map/ppermute | solution.py:100
  75.8 7.3 %collective-permute-start.9 = (bf16[576,128]{1,0:T(8,128)(2,1)S(1)}, bf16[576,128]{1,0:T(8,128)(2,1)S(1)}, u32[]{:S(2)}, u32[]{:S(2)}) collective-permute-start(bf16[576,128]{1,0:T(8,128)(2,1)S(1)} %hidden.1.own_h), channel_id=1, source_target_pairs={{0,259},{1,256},{2,257},{3,258},{256,3},{257,0},{258,1},{259,2},{4... | collective-permute-start | bytes 442376 | tf_op jit(solution)/shard_map/ppermute | solution.py:100
  81.0 8.2 %collective-permute-start.10 = (bf16[576,128]{1,0:T(8,128)(2,1)S(1)}, bf16[576,128]{1,0:T(8,128)(2,1)S(1)}, u32[]{:S(2)}, u32[]{:S(2)}) collective-permute-start(bf16[576,128]{1,0:T(8,128)(2,1)S(1)} %collective-permute-done.8.near_h), channel_id=1, source_target_pairs={{0,258},{1,257},{2,256},{3,259},{256,2},{257,1},{258,0},{259,3},{4... | collective-permute-start | bytes 442376 | tf_op jit(solution)/shard_map/ppermute | solution.py:100
  90.9 3.9 %collective-permute-start.11 = (bf16[576,512]{1,0:T(8,128)(2,1)S(1)}, bf16[576,512]{1,0:T(8,128)(2,1)S(1)}, u32[]{:S(2)}, u32[]{:S(2)}) collective-permute-start(bf16[576,512]{1,0:T(8,128)(2,1)S(1)} %get-tuple-element.23), channel_id=1, source_target_pairs={{0,1},{1,0},{2,3},{3,2},{256,257},{257,256},{258,259},{259,258},{4... | collective-permute-start | bytes 1769480 | tf_op jit(solution)/shard_map/ppermute | solution.py:100
  94.8 8.1 %copy-start.2 = (bf16[1,1024,576]{1,2,0:T(8,128)(2,1)S(1)}, bf16[1,1024,576]{1,2,0:T(8,128)(2,1)}, u32[]{:S(2)}) copy-start(bf16[1,1024,576]{1,2,0:T(8,128)(2,1)} %param.10) | copy-start | bytes 3538948
  94.8 8.1 %copy-start.4 = (bf16[3,1,32,576]{3,2,1,0:T(8,128)(2,1)S(1)}, bf16[3,1,32,576]{3,2,1,0:T(8,128)(2,1)}, u32[]{:S(2)}) copy-start(bf16[3,1,32,576]{3,2,1,0:T(8,128)(2,1)} %param.12) | copy-start | bytes 331780
  94.8 8.1 %copy-start.5 = (bf16[3,1,576]{2,0,1:T(4,128)(2,1)S(1)}, bf16[3,1,576]{2,0,1:T(4,128)(2,1)}, u32[]{:S(2)}) copy-start(bf16[3,1,576]{2,0,1:T(4,128)(2,1)} %param.11) | copy-start | bytes 10372
  96.2 25.9 %all-to-all-start.1 = ((bf16[64,8,512]{2,1,0:T(8,128)(2,1)}), bf16[64,8,512]{2,1,0:T(8,128)(2,1)S(1)}, u32[]{:S(2)}, u32[]{:S(2)}) async-start(bf16[64,8,512]{2,1,0:T(8,128)(2,1)} %bitcast.12), calls=%async_computation.1 | async-start | bytes 1048576 | tf_op jit(solution)/shard_map/all_to_all | solution.py:390
  102.2 3.6 %copy-start.6 = (s32[3,12,8]{1,2,0:T(8,128)S(1)}, s32[3,12,8]{1,2,0:T(8,128)}, u32[]{:S(2)}) copy-start(s32[3,12,8]{1,2,0:T(8,128)} %param.15) | copy-start | bytes 3460
  102.2 3.7 %copy-start.7 = (f32[3,12,8]{1,2,0:T(8,128)S(1)}, f32[3,12,8]{1,2,0:T(8,128)}, u32[]{:S(2)}) copy-start(f32[3,12,8]{1,2,0:T(8,128)} %param.16) | copy-start | bytes 3460
  103.9 8.5 %collective-permute-start.12 = (f32[96,512]{1,0:T(8,128)S(1)}, f32[96,512]{1,0:T(8,128)S(1)}, u32[]{:S(2)}, u32[]{:S(2)}) collective-permute-start(f32[96,512]{1,0:T(8,128)S(1)} %get-tuple-element.25), channel_id=1, source_target_pairs={{0,256},{1,257},{2,258},{3,259},{256,0},{257,1},{258,2},{259,3},{4... | collective-permute-start | bytes 589832 | tf_op jit(solution)/shard_map/ppermute | solution.py:100

commit v9 on v8

--- a/solution.py
+++ b/solution.py
@@ -235,42 +235,49 @@
         other_ref[rows, units:] = up_ref[pl.ds(offset, part), :]
 
 
-def partial_body(*refs):
-    pieces, (gate_ref, up_ref, other_ref, keep_ref, send_ref) = refs[:4], refs[5:]
-    rows = pieces[0].shape[0]
+def partial_sums(pieces, weights, out_ref):
+    rows, wide = pieces[0].shape[0], out_ref.shape[1]
     experts = rows // ROWS
-    part = gate_ref.shape[0] // 8
-    wide = keep_ref.shape[1]
-    blocks_of = sources(place_here())
-
-    def weights(m, start, size):
-        offset = pl.multiple_of(blocks_of[m] * part + start, HALF)
-        return jnp.concatenate(
-            [
-                gate_ref[pl.ds(offset, size), :],
-                up_ref[pl.ds(offset, size), :],
-                other_ref[m * part + start : m * part + start + size, :],
-            ],
-            axis=1,
-        )
-
-    total = jnp.zeros((rows, 2 * wide), F32)
+    part = pieces[0].shape[1] - HALF
+    total = jnp.zeros((rows, wide), F32)
     for m in range(4):
         total = total + dot(pieces[m][:, :part], weights(m, 0, part))
-    keep_ref[:rows, :] = total[:, :wide]
-    send_ref[:rows, :] = total[:, wide:]
+    out_ref[:rows, :] = total
     tail = jnp.concatenate([pieces[m][:, part:] for m in range(4)], axis=1)
     blocks = part // HALF
     source = iota((blocks * experts, rows), 0)
     wanted = (source % experts) * ROWS + source // experts
     chosen = (iota((blocks * experts, rows), 1) == wanted).astype(BF)
     ninth = dot(chosen, tail).astype(BF)
-    total = jnp.zeros((experts, 2 * wide), F32)
+    total = jnp.zeros((experts, wide), F32)
     for i in range(blocks):
         block_weights = jnp.concatenate([weights(m, i * HALF, HALF) for m in range(4)], axis=0)
         total = total + dot(ninth[i * experts : (i + 1) * experts], block_weights)
-    keep_ref[rows:, :] = total[:, :wide]
-    send_ref[rows:, :] = total[:, wide:]
+    out_ref[rows:, :] = total
+
+
+def partial_send_body(*refs):
+    pieces, (other_ref, out_ref) = refs[:4], refs[5:]
+    part = pieces[0].shape[1] - HALF
+
+    def weights(m, start, size):
+        return other_ref[m * part + start : m * part + start + size, :]
+
+    partial_sums(pieces, weights, out_ref)
+
+
+def partial_keep_body(*refs):
+    pieces, (gate_ref, up_ref, out_ref) = refs[:4], refs[4:]
+    part = pieces[0].shape[1] - HALF
+    blocks_of = sources(place_here())
+
+    def weights(m, start, size):
+        offset = pl.multiple_of(blocks_of[m] * part + start, HALF)
+        return jnp.concatenate(
+            [gate_ref[pl.ds(offset, size), :], up_ref[pl.ds(offset, size), :]], axis=1
+        )
+
+    partial_sums(pieces, weights, out_ref)
 
 
 def hidden_body(one_ref, two_ref, out_ref):
@@ -280,15 +287,32 @@
     out_ref[...] = (gate / (1.0 + jnp.exp(-gate)) * up).astype(BF)
 
 
-def down_body(own_h, near_h, crossed_h, far_h, down_ref, near_w, crossed_w, far_w, keep_ref, send_ref):
-    part, units = keep_ref.shape[1], down_ref.shape[0]
+def down_sums(core, hidden, down_ref, near_w, crossed_w, far_w, part):
+    own_h, near_h, crossed_h, far_h = hidden
+    units = down_ref.shape[0]
+
+    def half(both):
+        return jnp.where(core == 0, both[:, :part], both[:, part:])
+
     here = pl.ds(pl.multiple_of((place_here() // 2) * 2 * part, 128), 2 * part)
-    total = dot(own_h[...], down_ref[:, here]) + dot(near_h[...], near_w[:units, :])
-    total = total + dot(crossed_h[...], crossed_w[...]) + dot(far_h[...], far_w[...])
-    first = place_here() % 2 == 0
-    keep_ref[...] = jnp.where(first, total[:, :part], total[:, part:])
-    send_ref[:, :part] = jnp.where(first, total[:, part:], total[:, :part]).astype(BF)
-    send_ref[:, part:] = jnp.zeros((total.shape[0], HALF), BF)
+    total = dot(own_h[...], half(down_ref[:, here])) + dot(near_h[...], half(near_w[:units, :]))
+    return total + dot(crossed_h[...], half(crossed_w[...])) + dot(far_h[...], half(far_w[...]))
+
+
+def down_send_body(*refs):
+    hidden, (down_ref, near_w, crossed_w, far_w, out_ref) = refs[:4], refs[4:]
+    part = near_w.shape[1] // 2
+    core = 1 - place_here() % 2
+    total = down_sums(core, hidden, down_ref, near_w, crossed_w, far_w, part)
+    out_ref[:, :part] = total.astype(BF)
+    out_ref[:, part:] = jnp.zeros((total.shape[0], HALF), BF)
+
+
+def down_keep_body(*refs):
+    hidden, (down_ref, near_w, crossed_w, far_w, out_ref) = refs[:4], refs[4:]
+    part = near_w.shape[1] // 2
+    core = place_here() % 2
+    out_ref[...] = down_sums(core, hidden, down_ref, near_w, crossed_w, far_w, part)
 
 
 def repack_body(one_ref, two_ref, out_ref):
@@ -367,22 +391,27 @@
     )(arrived, gate_proj, up_proj)
     other = swap(other, 1)
 
-    keep, send = call(
-        partial_body, [jax.ShapeDtypeStruct((rows + experts, 2 * units), F32)] * 2,
-        [VMEM] * 4 + [HBM] + [VMEM] * 3, 10**9, 6 * 10**6, "partial",
-    )(*gather(arrived), far_down, gate_proj, up_proj, other)
+    pieces = gather(arrived)
+    sums = jax.ShapeDtypeStruct((rows + experts, 2 * units), F32)
+    send = call(
+        partial_send_body, sums, [VMEM] * 4 + [HBM, VMEM], 10**9, 4 * 10**6, "partial_send",
+    )(*pieces, far_down, other)
+    keep = call(
+        partial_keep_body, sums, [VMEM] * 6, 10**9, 4 * 10**6, "partial_keep",
+    )(*pieces, gate_proj, up_proj)
     hidden = call(
         hidden_body, jax.ShapeDtypeStruct((rows + experts, units), BF), [VMEM] * 2,
         10**7, 10**6, "hidden",
     )(keep, swap(send, 1))
-    keep, send = call(
-        down_body,
-        [
-            jax.ShapeDtypeStruct((rows + experts, part), F32),
-            jax.ShapeDtypeStruct((rows + experts, part + HALF), BF),
-        ],
-        [VMEM] * 8, 10**9, 3 * 10**6, "down",
-    )(*gather(hidden), down_proj, near_down, crossed_down, far_down)
+    operands = *gather(hidden), down_proj, near_down, crossed_down, far_down
+    send = call(
+        down_send_body, jax.ShapeDtypeStruct((rows + experts, part + HALF), BF), [VMEM] * 8,
+        10**9, 2 * 10**6, "down_send",
+    )(*operands)
+    keep = call(
+        down_keep_body, jax.ShapeDtypeStruct((rows + experts, part), F32), [VMEM] * 8,
+        10**9, 2 * 10**6, "down_keep",
+    )(*operands)
     outgoing = call(
         repack_body, jax.ShapeDtypeStruct((rows, part + HALF), BF), [VMEM] * 2,
         10**8, 2 * 10**6, "repack",

time: 124 us -> 122 us (0.984)
  waiting for transfers between devices: 51.3 us -> 49.4 us
    ppermute x13, waiting for transfers between devices: 35.7 us -> 33.8 us  [permute(): return lax.ppermute(value, LINE, [(d, target(d)) for d in range(8)])]
    pallas_call x2 -> x4, Pallas kernels: 3.75 us -> 3.72 us  [the longest x1 0.99 us: local(): call(partial_keep_body, sums, [VMEM] * 6, 10 ** 9, 4 * 10 ** 6, 'partial_...]
  transfers between devices with their start and end apart: 15 -> 15, of which waited for: 12 -> 12; matrix products, arithmetic and copies ran while one was open for 0% -> 0% of each run, Pallas kernels for 2% -> 4%
where the time goes in v9:
time: 122 us; the launch traced here: 121 us
  starting transfers between devices  57.6 us (47%)
  waiting for transfers between devices  49.4 us (40%)
  Pallas kernels  12.2 us (10%)
  between operations  1.59 us (1%)
    ppermute x13, starting transfers between devices, permute(): return lax.ppermute(value, LINE, [(d, target(d)) for d in range(8)])  34.9 us
    ppermute x13, waiting for transfers between devices, permute(): return lax.ppermute(value, LINE, [(d, target(d)) for d in range(8)])  33.8 us
    all_to_all x1, starting transfers between devices, local(): lax.all_to_all(packed.reshape(experts, ROWS, part + HALF), 'grp', split_a...  16.6 us
    all_to_all x1, waiting for transfers between devices, local(): lax.all_to_all(outgoing.reshape(experts, ROWS, part + HALF), 'grp', split...  8.91 us
    all_to_all x1, waiting for transfers between devices, local(): lax.all_to_all(packed.reshape(experts, ROWS, part + HALF), 'grp', split_a...  6.67 us
    all_to_all x1, starting transfers between devices, local(): lax.all_to_all(outgoing.reshape(experts, ROWS, part + HALF), 'grp', split...  6.01 us
    pallas_call x1, Pallas kernels, local(): pl.pallas_call(pack_body, out_shape=[jax.ShapeDtypeStruct((rows, part + H...  3.5 us
  transfers between devices with their start and end apart: 15, of which 12 were waited for; matrix products, arithmetic and copies ran while one was open for 0% of the time, Pallas kernels for 4%

profile of v9, /device:TPU:6, one launch (start us, length us, event | category | flops | bytes accessed | tf_op | source)
XLA Modules:
  0.0 121.0 jit_solution(12922038813356718921)
XLA Ops:
  0.7 3.5 %pack.1 = (bf16[512,512]{1,0:T(8,128)(2,1)}, bf16[256,896]{1,0:T(8,128)(2,1)}, bf16[128,896]{1,0:T(8,128)(2,1)}) custom-call(bf16[3,12,3584]{2,1,0:T(8,128)(2,1)} %tokens_ref.1, s32[3,8,12]{2,1,0:T(8,128)} %bitcast.33, bf16[128,3584]{1,0:T(8,128)(2,1)} %bitcast.27), custom_call_target="tpu_custom_call" | custom-call | flops 100000000 | bytes 1000000 | tf_op jit(solution)/shard_map/pack/pallas_call | solution.py:360
  4.2 16.6 %all-to-all-start = ((bf16[64,8,512]{2,1,0:T(8,128)(2,1)}), bf16[64,8,512]{2,1,0:T(8,128)(2,1)S(1)}, u32[]{:S(2)}, u32[]{:S(2)}) async-start(bf16[64,8,512]{2,1,0:T(8,128)(2,1)} %bitcast.32), calls=%async_computation | async-start | bytes 1048576 | tf_op jit(solution)/shard_map/all_to_all | solution.py:378
  20.8 2.7 %collective-permute-start = (bf16[256,896]{1,0:T(8,128)(2,1)}, bf16[256,896]{1,0:T(8,128)(2,1)S(1)}, u32[]{:S(2)}, u32[]{:S(2)}) collective-permute-start(bf16[256,896]{1,0:T(8,128)(2,1)} %get-tuple-element.11), channel_id=1, source_target_pairs={{0,256},{1,259},{2,258},{3,257},{256,0},{257,3},{258,2},{259,1},{4... | collective-permute-start | bytes 1376264 | tf_op jit(solution)/shard_map/ppermute | solution.py:100
  23.5 3.2 %collective-permute-start.1 = (bf16[128,896]{1,0:T(8,128)(2,1)}, bf16[128,896]{1,0:T(8,128)(2,1)S(1)}, u32[]{:S(2)}, u32[]{:S(2)}) collective-permute-start(bf16[128,896]{1,0:T(8,128)(2,1)} %get-tuple-element.12), channel_id=1, source_target_pairs={{0,259},{1,256},{2,257},{3,258},{256,3},{257,0},{258,1},{259,2},{4... | collective-permute-start | bytes 688136 | tf_op jit(solution)/shard_map/ppermute | solution.py:100
  26.7 6.9 %collective-permute-done.1.refs_6_ = bf16[128,896]{1,0:T(8,128)(2,1)S(1)} collective-permute-done((bf16[128,896]{1,0:T(8,128)(2,1)}, bf16[128,896]{1,0:T(8,128)(2,1)S(1)}, u32[]{:S(2)}, u32[]{:S(2)}) %collective-permute-start.1) | collective-permute-done | bytes 229408 | tf_op jit(solution)/shard_map/ppermute | solution.py:100
  33.8 6.7 %all-to-all-done = bf16[64,8,512]{2,1,0:T(8,128)(2,1)S(1)} async-done(((bf16[64,8,512]{2,1,0:T(8,128)(2,1)}), bf16[64,8,512]{2,1,0:T(8,128)(2,1)S(1)}, u32[]{:S(2)}, u32[]{:S(2)}) %all-to-all-start) | async-done | bytes 524320 | tf_op jit(solution)/shard_map/all_to_all | solution.py:378
  40.5 2.7 %collective-permute-start.2 = (bf16[512,512]{1,0:T(8,128)(2,1)S(1)}, bf16[512,512]{1,0:T(8,128)(2,1)S(1)}, u32[]{:S(2)}, u32[]{:S(2)}) collective-permute-start(bf16[512,512]{1,0:T(8,128)(2,1)S(1)} %bitcast.16), channel_id=1, source_target_pairs={{0,256},{1,259},{2,258},{3,257},{256,0},{257,3},{258,2},{259,1},{4... | collective-permute-start | bytes 1572872 | tf_op jit(solution)/shard_map/ppermute | solution.py:100
  43.4 1.9 %collective-permute-start.6 = (bf16[1792,256]{1,0:T(8,128)(2,1)S(1)}, bf16[1792,256]{1,0:T(8,128)(2,1)S(1)}, u32[]{:S(2)}, u32[]{:S(2)}) collective-permute-start(bf16[1792,256]{1,0:T(8,128)(2,1)S(1)} %other_slices.1), channel_id=1, source_target_pairs={{0,1},{1,0},{2,3},{3,2},{256,257},{257,256},{258,259},{259,258},{4... | collective-permute-start | bytes 2752520 | tf_op jit(solution)/shard_map/ppermute | solution.py:100
  45.3 3.2 %collective-permute-start.3 = (bf16[512,512]{1,0:T(8,128)(2,1)S(1)}, bf16[512,512]{1,0:T(8,128)(2,1)S(1)}, u32[]{:S(2)}, u32[]{:S(2)}) collective-permute-start(bf16[512,512]{1,0:T(8,128)(2,1)S(1)} %bitcast.18), channel_id=1, source_target_pairs={{0,259},{1,256},{2,257},{3,258},{256,3},{257,0},{258,1},{259,2},{4... | collective-permute-start | bytes 1572872 | tf_op jit(solution)/shard_map/ppermute | solution.py:100
  48.5 4.3 %collective-permute-done.2.refs_1_ = bf16[512,512]{1,0:T(8,128)(2,1)S(1)} collective-permute-done((bf16[512,512]{1,0:T(8,128)(2,1)S(1)}, bf16[512,512]{1,0:T(8,128)(2,1)S(1)}, u32[]{:S(2)}, u32[]{:S(2)}) %collective-permute-start.2) | collective-permute-done | bytes 524320 | tf_op jit(solution)/shard_map/ppermute | solution.py:100
  52.8 1.9 %collective-permute-start.4 = (bf16[512,512]{1,0:T(8,128)(2,1)S(1)}, bf16[512,512]{1,0:T(8,128)(2,1)S(1)}, u32[]{:S(2)}, u32[]{:S(2)}) collective-permute-start(bf16[512,512]{1,0:T(8,128)(2,1)S(1)} %collective-permute-done.2.refs_1_), channel_id=1, source_target_pairs={{0,258},{1,257},{2,256},{3,259},{256,2},{257,1},{258,0},{259,3},{4... | collective-permute-start | bytes 1572872 | tf_op jit(solution)/shard_map/ppermute | solution.py:100
  54.7 5.1 %collective-permute-start.5 = (bf16[128,896]{1,0:T(8,128)(2,1)S(1)}, bf16[128,896]{1,0:T(8,128)(2,1)S(1)}, u32[]{:S(2)}, u32[]{:S(2)}) collective-permute-start(bf16[128,896]{1,0:T(8,128)(2,1)S(1)} %slice.3), channel_id=1, source_target_pairs={{0,258},{1,257},{2,256},{3,259},{256,2},{257,1},{258,0},{259,3},{4... | collective-permute-start | bytes 688136 | tf_op jit(solution)/shard_map/ppermute | solution.py:100
  59.9 7.6 %collective-permute-done.5.refs_4_.refs_7_ = bf16[128,896]{1,0:T(8,128)(2,1)S(1)} collective-permute-done((bf16[128,896]{1,0:T(8,128)(2,1)S(1)}, bf16[128,896]{1,0:T(8,128)(2,1)S(1)}, u32[]{:S(2)}, u32[]{:S(2)}) %collective-permute-start.5) | collective-permute-done | bytes 229408 | tf_op jit(solution)/shard_map/ppermute | solution.py:100
  68.5 1.9 %collective-permute-start.7 = (f32[576,256]{1,0:T(8,128)S(1)}, f32[576,256]{1,0:T(8,128)S(1)}, u32[]{:S(2)}, u32[]{:S(2)}) collective-permute-start(f32[576,256]{1,0:T(8,128)S(1)} %partial_send.1), channel_id=1, source_target_pairs={{0,1},{1,0},{2,3},{3,2},{256,257},{257,256},{258,259},{259,258},{4... | collective-permute-start | bytes 1769480 | tf_op jit(solution)/shard_map/ppermute | solution.py:100
  72.5 1.9 %collective-permute-start.8 = (bf16[576,128]{1,0:T(8,128)(2,1)S(1)}, bf16[576,128]{1,0:T(8,128)(2,1)S(1)}, u32[]{:S(2)}, u32[]{:S(2)}) collective-permute-start(bf16[576,128]{1,0:T(8,128)(2,1)S(1)} %hidden.1.refs_0_), channel_id=1, source_target_pairs={{0,256},{1,259},{2,258},{3,257},{256,0},{257,3},{258,2},{259,1},{4... | collective-permute-start | bytes 442376 | tf_op jit(solution)/shard_map/ppermute | solution.py:100
  74.5 4.6 %collective-permute-start.9 = (bf16[576,128]{1,0:T(8,128)(2,1)S(1)}, bf16[576,128]{1,0:T(8,128)(2,1)S(1)}, u32[]{:S(2)}, u32[]{:S(2)}) collective-permute-start(bf16[576,128]{1,0:T(8,128)(2,1)S(1)} %hidden.1.refs_0_), channel_id=1, source_target_pairs={{0,259},{1,256},{2,257},{3,258},{256,3},{257,0},{258,1},{259,2},{4... | collective-permute-start | bytes 442376 | tf_op jit(solution)/shard_map/ppermute | solution.py:100
  79.8 1.9 %collective-permute-start.10 = (bf16[576,128]{1,0:T(8,128)(2,1)S(1)}, bf16[576,128]{1,0:T(8,128)(2,1)S(1)}, u32[]{:S(2)}, u32[]{:S(2)}) collective-permute-start(bf16[576,128]{1,0:T(8,128)(2,1)S(1)} %collective-permute-done.8.refs_1_), channel_id=1, source_target_pairs={{0,258},{1,257},{2,256},{3,259},{256,2},{257,1},{258,0},{259,3},{4... | collective-permute-start | bytes 442376 | tf_op jit(solution)/shard_map/ppermute | solution.py:100
  81.7 6.3 %collective-permute-done.10.refs_3_ = bf16[576,128]{1,0:T(8,128)(2,1)S(1)} collective-permute-done((bf16[576,128]{1,0:T(8,128)(2,1)S(1)}, bf16[576,128]{1,0:T(8,128)(2,1)S(1)}, u32[]{:S(2)}, u32[]{:S(2)}) %collective-permute-start.10) | collective-permute-done | bytes 147488 | tf_op jit(solution)/shard_map/ppermute | solution.py:100
  88.9 1.9 %collective-permute-start.11 = (bf16[576,512]{1,0:T(8,128)(2,1)S(1)}, bf16[576,512]{1,0:T(8,128)(2,1)S(1)}, u32[]{:S(2)}, u32[]{:S(2)}) collective-permute-start(bf16[576,512]{1,0:T(8,128)(2,1)S(1)} %down_send.1), channel_id=1, source_target_pairs={{0,1},{1,0},{2,3},{3,2},{256,257},{257,256},{258,259},{259,258},{4... | collective-permute-start | bytes 1769480 | tf_op jit(solution)/shard_map/ppermute | solution.py:100
  92.8 1.4 %repack.1._ = bf16[512,512]{1,0:T(8,128)(2,1)} custom-call(f32[576,448]{1,0:T(8,128)S(1)} %down_keep.1.one_ref, bf16[576,512]{1,0:T(8,128)(2,1)S(1)} %collective-permute-done.11.two_ref), custom_call_target="tpu_custom_call" | custom-call | flops 100000000 | bytes 2000000 | tf_op jit(solution)/shard_map/repack/pallas_call | solution.py:415
  94.1 6.0 %all-to-all-start.1 = ((bf16[64,8,512]{2,1,0:T(8,128)(2,1)}), bf16[64,8,512]{2,1,0:T(8,128)(2,1)S(1)}, u32[]{:S(2)}, u32[]{:S(2)}) async-start(bf16[64,8,512]{2,1,0:T(8,128)(2,1)} %bitcast.12), calls=%async_computation.1 | async-start | bytes 1048576 | tf_op jit(solution)/shard_map/all_to_all | solution.py:419
  101.8 1.9 %collective-permute-start.12 = (f32[96,512]{1,0:T(8,128)S(1)}, f32[96,512]{1,0:T(8,128)S(1)}, u32[]{:S(2)}, u32[]{:S(2)}) collective-permute-start(f32[96,512]{1,0:T(8,128)S(1)} %get-tuple-element.17), channel_id=1, source_target_pairs={{0,256},{1,257},{2,258},{3,259},{256,0},{257,1},{258,2},{259,3},{4... | collective-permute-start | bytes 589832 | tf_op jit(solution)/shard_map/ppermute | solution.py:100
  104.6 5.7 %collective-permute-done.12.two_ref = f32[96,512]{1,0:T(8,128)S(1)} collective-permute-done((f32[96,512]{1,0:T(8,128)S(1)}, f32[96,512]{1,0:T(8,128)S(1)}, u32[]{:S(2)}, u32[]{:S(2)}) %collective-permute-start.12) | collective-permute-done | bytes 196640 | tf_op jit(solution)/shard_map/ppermute | solution.py:100
  111.1 8.9 %all-to-all-done.1 = bf16[64,8,512]{2,1,0:T(8,128)(2,1)S(1)} async-done(((bf16[64,8,512]{2,1,0:T(8,128)(2,1)}), bf16[64,8,512]{2,1,0:T(8,128)(2,1)S(1)}, u32[]{:S(2)}, u32[]{:S(2)}) %all-to-all-start.1) | async-done | bytes 524320 | tf_op jit(solution)/shard_map/all_to_all | solution.py:419
  (37 shorter events, 10.6 us)
Async XLA Ops:
  0.6 42.6 %copy-start = (bf16[1,3584,128]{2,1,0:T(8,128)(2,1)S(1)}, bf16[1,3584,128]{2,1,0:T(8,128)(2,1)}, u32[]{:S(2)}) copy-start(bf16[1,3584,128]{2,1,0:T(8,128)(2,1)} %param.17) | copy-start | bytes 2752516
  0.6 42.6 %copy-start.1 = (bf16[1,3584,128]{2,1,0:T(8,128)(2,1)S(1)}, bf16[1,3584,128]{2,1,0:T(8,128)(2,1)}, u32[]{:S(2)}) copy-start(bf16[1,3584,128]{2,1,0:T(8,128)(2,1)} %param.18) | copy-start | bytes 2752516
  4.2 36.3 %all-to-all-start = ((bf16[64,8,512]{2,1,0:T(8,128)(2,1)}), bf16[64,8,512]{2,1,0:T(8,128)(2,1)S(1)}, u32[]{:S(2)}, u32[]{:S(2)}) async-start(bf16[64,8,512]{2,1,0:T(8,128)(2,1)} %bitcast.32), calls=%async_computation | async-start | bytes 1048576 | tf_op jit(solution)/shard_map/all_to_all | solution.py:378
  20.8 13.0 %collective-permute-start = (bf16[256,896]{1,0:T(8,128)(2,1)}, bf16[256,896]{1,0:T(8,128)(2,1)S(1)}, u32[]{:S(2)}, u32[]{:S(2)}) collective-permute-start(bf16[256,896]{1,0:T(8,128)(2,1)} %get-tuple-element.11), channel_id=1, source_target_pairs={{0,256},{1,259},{2,258},{3,257},{256,0},{257,3},{258,2},{259,1},{4... | collective-permute-start | bytes 1376264 | tf_op jit(solution)/shard_map/ppermute | solution.py:100
  23.5 10.1 %collective-permute-start.1 = (bf16[128,896]{1,0:T(8,128)(2,1)}, bf16[128,896]{1,0:T(8,128)(2,1)S(1)}, u32[]{:S(2)}, u32[]{:S(2)}) collective-permute-start(bf16[128,896]{1,0:T(8,128)(2,1)} %get-tuple-element.12), channel_id=1, source_target_pairs={{0,259},{1,256},{2,257},{3,258},{256,3},{257,0},{258,1},{259,2},{4... | collective-permute-start | bytes 688136 | tf_op jit(solution)/shard_map/ppermute | solution.py:100
  40.5 12.3 %collective-permute-start.2 = (bf16[512,512]{1,0:T(8,128)(2,1)S(1)}, bf16[512,512]{1,0:T(8,128)(2,1)S(1)}, u32[]{:S(2)}, u32[]{:S(2)}) collective-permute-start(bf16[512,512]{1,0:T(8,128)(2,1)S(1)} %bitcast.16), channel_id=1, source_target_pairs={{0,256},{1,259},{2,258},{3,257},{256,0},{257,3},{258,2},{259,1},{4... | collective-permute-start | bytes 1572872 | tf_op jit(solution)/shard_map/ppermute | solution.py:100
  43.4 24.1 %collective-permute-start.6 = (bf16[1792,256]{1,0:T(8,128)(2,1)S(1)}, bf16[1792,256]{1,0:T(8,128)(2,1)S(1)}, u32[]{:S(2)}, u32[]{:S(2)}) collective-permute-start(bf16[1792,256]{1,0:T(8,128)(2,1)S(1)} %other_slices.1), channel_id=1, source_target_pairs={{0,1},{1,0},{2,3},{3,2},{256,257},{257,256},{258,259},{259,258},{4... | collective-permute-start | bytes 2752520 | tf_op jit(solution)/shard_map/ppermute | solution.py:100
  45.3 22.2 %collective-permute-start.3 = (bf16[512,512]{1,0:T(8,128)(2,1)S(1)}, bf16[512,512]{1,0:T(8,128)(2,1)S(1)}, u32[]{:S(2)}, u32[]{:S(2)}) collective-permute-start(bf16[512,512]{1,0:T(8,128)(2,1)S(1)} %bitcast.18), channel_id=1, source_target_pairs={{0,259},{1,256},{2,257},{3,258},{256,3},{257,0},{258,1},{259,2},{4... | collective-permute-start | bytes 1572872 | tf_op jit(solution)/shard_map/ppermute | solution.py:100
  52.8 14.7 %collective-permute-start.4 = (bf16[512,512]{1,0:T(8,128)(2,1)S(1)}, bf16[512,512]{1,0:T(8,128)(2,1)S(1)}, u32[]{:S(2)}, u32[]{:S(2)}) collective-permute-start(bf16[512,512]{1,0:T(8,128)(2,1)S(1)} %collective-permute-done.2.refs_1_), channel_id=1, source_target_pairs={{0,258},{1,257},{2,256},{3,259},{256,2},{257,1},{258,0},{259,3},{4... | collective-permute-start | bytes 1572872 | tf_op jit(solution)/shard_map/ppermute | solution.py:100
  54.7 12.8 %collective-permute-start.5 = (bf16[128,896]{1,0:T(8,128)(2,1)S(1)}, bf16[128,896]{1,0:T(8,128)(2,1)S(1)}, u32[]{:S(2)}, u32[]{:S(2)}) collective-permute-start(bf16[128,896]{1,0:T(8,128)(2,1)S(1)} %slice.3), channel_id=1, source_target_pairs={{0,258},{1,257},{2,256},{3,259},{256,2},{257,1},{258,0},{259,3},{4... | collective-permute-start | bytes 688136 | tf_op jit(solution)/shard_map/ppermute | solution.py:100
  68.5 3.9 %collective-permute-start.7 = (f32[576,256]{1,0:T(8,128)S(1)}, f32[576,256]{1,0:T(8,128)S(1)}, u32[]{:S(2)}, u32[]{:S(2)}) collective-permute-start(f32[576,256]{1,0:T(8,128)S(1)} %partial_send.1), channel_id=1, source_target_pairs={{0,1},{1,0},{2,3},{3,2},{256,257},{257,256},{258,259},{259,258},{4... | collective-permute-start | bytes 1769480 | tf_op jit(solution)/shard_map/ppermute | solution.py:100
  71.5 16.5 %copy-start.3 = (bf16[1,128,3584]{2,1,0:T(8,128)(2,1)S(1)}, bf16[1,128,3584]{2,1,0:T(8,128)(2,1)}, u32[]{:S(2)}) copy-start(bf16[1,128,3584]{2,1,0:T(8,128)(2,1)} %param.19) | copy-start | bytes 2752516
  72.5 7.2 %collective-permute-start.8 = (bf16[576,128]{1,0:T(8,128)(2,1)S(1)}, bf16[576,128]{1,0:T(8,128)(2,1)S(1)}, u32[]{:S(2)}, u32[]{:S(2)}) collective-permute-start(bf16[576,128]{1,0:T(8,128)(2,1)S(1)} %hidden.1.refs_0_), channel_id=1, source_target_pairs={{0,256},{1,259},{2,258},{3,257},{256,0},{257,3},{258,2},{259,1},{4... | collective-permute-start | bytes 442376 | tf_op jit(solution)/shard_map/ppermute | solution.py:100
  74.5 7.3 %collective-permute-start.9 = (bf16[576,128]{1,0:T(8,128)(2,1)S(1)}, bf16[576,128]{1,0:T(8,128)(2,1)S(1)}, u32[]{:S(2)}, u32[]{:S(2)}) collective-permute-start(bf16[576,128]{1,0:T(8,128)(2,1)S(1)} %hidden.1.refs_0_), channel_id=1, source_target_pairs={{0,259},{1,256},{2,257},{3,258},{256,3},{257,0},{258,1},{259,2},{4... | collective-permute-start | bytes 442376 | tf_op jit(solution)/shard_map/ppermute | solution.py:100
  79.8 8.2 %collective-permute-start.10 = (bf16[576,128]{1,0:T(8,128)(2,1)S(1)}, bf16[576,128]{1,0:T(8,128)(2,1)S(1)}, u32[]{:S(2)}, u32[]{:S(2)}) collective-permute-start(bf16[576,128]{1,0:T(8,128)(2,1)S(1)} %collective-permute-done.8.refs_1_), channel_id=1, source_target_pairs={{0,258},{1,257},{2,256},{3,259},{256,2},{257,1},{258,0},{259,3},{4... | collective-permute-start | bytes 442376 | tf_op jit(solution)/shard_map/ppermute | solution.py:100
  88.9 3.9 %collective-permute-start.11 = (bf16[576,512]{1,0:T(8,128)(2,1)S(1)}, bf16[576,512]{1,0:T(8,128)(2,1)S(1)}, u32[]{:S(2)}, u32[]{:S(2)}) collective-permute-start(bf16[576,512]{1,0:T(8,128)(2,1)S(1)} %down_send.1), channel_id=1, source_target_pairs={{0,1},{1,0},{2,3},{3,2},{256,257},{257,256},{258,259},{259,258},{4... | collective-permute-start | bytes 1769480 | tf_op jit(solution)/shard_map/ppermute | solution.py:100
  91.7 9.2 %copy-start.2 = (bf16[1,1024,576]{1,2,0:T(8,128)(2,1)S(1)}, bf16[1,1024,576]{1,2,0:T(8,128)(2,1)}, u32[]{:S(2)}) copy-start(bf16[1,1024,576]{1,2,0:T(8,128)(2,1)} %param.10) | copy-start | bytes 3538948
  91.7 9.2 %copy-start.4 = (bf16[3,1,32,576]{3,2,1,0:T(8,128)(2,1)S(1)}, bf16[3,1,32,576]{3,2,1,0:T(8,128)(2,1)}, u32[]{:S(2)}) copy-start(bf16[3,1,32,576]{3,2,1,0:T(8,128)(2,1)} %param.12) | copy-start | bytes 331780
  91.7 9.1 %copy-start.5 = (bf16[3,1,576]{2,0,1:T(4,128)(2,1)S(1)}, bf16[3,1,576]{2,0,1:T(4,128)(2,1)}, u32[]{:S(2)}) copy-start(bf16[3,1,576]{2,0,1:T(4,128)(2,1)} %param.11) | copy-start | bytes 10372
  94.1 25.9 %all-to-all-start.1 = ((bf16[64,8,512]{2,1,0:T(8,128)(2,1)}), bf16[64,8,512]{2,1,0:T(8,128)(2,1)S(1)}, u32[]{:S(2)}, u32[]{:S(2)}) async-start(bf16[64,8,512]{2,1,0:T(8,128)(2,1)} %bitcast.12), calls=%async_computation.1 | async-start | bytes 1048576 | tf_op jit(solution)/shard_map/all_to_all | solution.py:419
  100.1 3.6 %copy-start.6 = (s32[3,12,8]{1,2,0:T(8,128)S(1)}, s32[3,12,8]{1,2,0:T(8,128)}, u32[]{:S(2)}) copy-start(s32[3,12,8]{1,2,0:T(8,128)} %param.15) | copy-start | bytes 3460
  100.1 3.7 %copy-start.7 = (f32[3,12,8]{1,2,0:T(8,128)S(1)}, f32[3,12,8]{1,2,0:T(8,128)}, u32[]{:S(2)}) copy-start(f32[3,12,8]{1,2,0:T(8,128)} %param.16) | copy-start | bytes 3460
  101.8 8.5 %collective-permute-start.12 = (f32[96,512]{1,0:T(8,128)S(1)}, f32[96,512]{1,0:T(8,128)S(1)}, u32[]{:S(2)}, u32[]{:S(2)}) collective-permute-start(f32[96,512]{1,0:T(8,128)S(1)} %get-tuple-element.17), channel_id=1, source_target_pairs={{0,256},{1,257},{2,258},{3,259},{256,0},{257,1},{258,2},{259,3},{4... | collective-permute-start | bytes 589832 | tf_op jit(solution)/shard_map/ppermute | solution.py:100

commit v10 on v9

--- a/solution.py
+++ b/solution.py
@@ -242,7 +242,7 @@
     total = jnp.zeros((rows, wide), F32)
     for m in range(4):
         total = total + dot(pieces[m][:, :part], weights(m, 0, part))
-    out_ref[:rows, :] = total
+    out_ref[:rows, :] = total.astype(out_ref.dtype)
     tail = jnp.concatenate([pieces[m][:, part:] for m in range(4)], axis=1)
     blocks = part // HALF
     source = iota((blocks * experts, rows), 0)
@@ -253,7 +253,7 @@
     for i in range(blocks):
         block_weights = jnp.concatenate([weights(m, i * HALF, HALF) for m in range(4)], axis=0)
         total = total + dot(ninth[i * experts : (i + 1) * experts], block_weights)
-    out_ref[rows:, :] = total
+    out_ref[rows:, :] = total.astype(out_ref.dtype)
 
 
 def partial_send_body(*refs):
@@ -282,8 +282,8 @@
 
 def hidden_body(one_ref, two_ref, out_ref):
     units = out_ref.shape[1]
-    gate = one_ref[:, :units] + two_ref[:, :units]
-    up = one_ref[:, units:] + two_ref[:, units:]
+    gate = one_ref[:, :units] + two_ref[:, :units].astype(F32)
+    up = one_ref[:, units:] + two_ref[:, units:].astype(F32)
     out_ref[...] = (gate / (1.0 + jnp.exp(-gate)) * up).astype(BF)
 
 
@@ -394,7 +394,7 @@
     pieces = gather(arrived)
     sums = jax.ShapeDtypeStruct((rows + experts, 2 * units), F32)
     send = call(
-        partial_send_body, sums, [VMEM] * 4 + [HBM, VMEM], 10**9, 4 * 10**6, "partial_send",
+        partial_send_body, jax.ShapeDtypeStruct(sums.shape, BF), [VMEM] * 4 + [HBM, VMEM], 10**9, 4 * 10**6, "partial_send",
     )(*pieces, far_down, other)
     keep = call(
         partial_keep_body, sums, [VMEM] * 6, 10**9, 4 * 10**6, "partial_keep",

time: 122 us -> 121 us (level)
  no operation moved by 1% of the time
where the time goes in v10:
time: 121 us
  starting transfers between devices  57.7 us (48%)
  waiting for transfers between devices  49 us (40%)
  Pallas kernels  12.3 us (10%)
  between operations  1.59 us (1%)
    ppermute x13, starting transfers between devices, permute(): return lax.ppermute(value, LINE, [(d, target(d)) for d in range(8)])  35.1 us
    ppermute x13, waiting for transfers between devices, permute(): return lax.ppermute(value, LINE, [(d, target(d)) for d in range(8)])  33.4 us
    all_to_all x1, starting transfers between devices, local(): lax.all_to_all(packed.reshape(experts, ROWS, part + HALF), 'grp', split_a...  16.6 us
    all_to_all x1, waiting for transfers between devices, local(): lax.all_to_all(outgoing.reshape(experts, ROWS, part + HALF), 'grp', split...  8.94 us
    all_to_all x1, waiting for transfers between devices, local(): lax.all_to_all(packed.reshape(experts, ROWS, part + HALF), 'grp', split_a...  6.67 us
    all_to_all x1, starting transfers between devices, local(): lax.all_to_all(outgoing.reshape(experts, ROWS, part + HALF), 'grp', split...  6.02 us
    pallas_call x1, Pallas kernels, local(): pl.pallas_call(pack_body, out_shape=[jax.ShapeDtypeStruct((rows, part + H...  3.5 us
  transfers between devices with their start and end apart: 15, of which 12 were waited for; matrix products, arithmetic and copies ran while one was open for 0% of the time, Pallas kernels for 4%

profile of v10, /device:TPU:6, one launch (start us, length us, event | category | flops | bytes accessed | tf_op | source)
XLA Modules:
  0.0 120.8 jit_solution(1938466596702533873)
XLA Ops:
  0.7 3.5 %pack.1 = (bf16[512,512]{1,0:T(8,128)(2,1)}, bf16[256,896]{1,0:T(8,128)(2,1)}, bf16[128,896]{1,0:T(8,128)(2,1)}) custom-call(bf16[3,12,3584]{2,1,0:T(8,128)(2,1)} %tokens_ref.1, s32[3,8,12]{2,1,0:T(8,128)} %bitcast.33, bf16[128,3584]{1,0:T(8,128)(2,1)} %bitcast.27), custom_call_target="tpu_custom_call" | custom-call | flops 100000000 | bytes 1000000 | tf_op jit(solution)/shard_map/pack/pallas_call | solution.py:360
  4.2 16.6 %all-to-all-start = ((bf16[64,8,512]{2,1,0:T(8,128)(2,1)}), bf16[64,8,512]{2,1,0:T(8,128)(2,1)S(1)}, u32[]{:S(2)}, u32[]{:S(2)}) async-start(bf16[64,8,512]{2,1,0:T(8,128)(2,1)} %bitcast.32), calls=%async_computation | async-start | bytes 1048576 | tf_op jit(solution)/shard_map/all_to_all | solution.py:378
  20.8 2.7 %collective-permute-start = (bf16[256,896]{1,0:T(8,128)(2,1)}, bf16[256,896]{1,0:T(8,128)(2,1)S(1)}, u32[]{:S(2)}, u32[]{:S(2)}) collective-permute-start(bf16[256,896]{1,0:T(8,128)(2,1)} %get-tuple-element.11), channel_id=1, source_target_pairs={{0,256},{1,259},{2,258},{3,257},{256,0},{257,3},{258,2},{259,1},{4... | collective-permute-start | bytes 1376264 | tf_op jit(solution)/shard_map/ppermute | solution.py:100
  23.5 3.2 %collective-permute-start.1 = (bf16[128,896]{1,0:T(8,128)(2,1)}, bf16[128,896]{1,0:T(8,128)(2,1)S(1)}, u32[]{:S(2)}, u32[]{:S(2)}) collective-permute-start(bf16[128,896]{1,0:T(8,128)(2,1)} %get-tuple-element.12), channel_id=1, source_target_pairs={{0,259},{1,256},{2,257},{3,258},{256,3},{257,0},{258,1},{259,2},{4... | collective-permute-start | bytes 688136 | tf_op jit(solution)/shard_map/ppermute | solution.py:100
  26.7 6.9 %collective-permute-done.1.refs_6_ = bf16[128,896]{1,0:T(8,128)(2,1)S(1)} collective-permute-done((bf16[128,896]{1,0:T(8,128)(2,1)}, bf16[128,896]{1,0:T(8,128)(2,1)S(1)}, u32[]{:S(2)}, u32[]{:S(2)}) %collective-permute-start.1) | collective-permute-done | bytes 229408 | tf_op jit(solution)/shard_map/ppermute | solution.py:100
  33.8 6.7 %all-to-all-done = bf16[64,8,512]{2,1,0:T(8,128)(2,1)S(1)} async-done(((bf16[64,8,512]{2,1,0:T(8,128)(2,1)}), bf16[64,8,512]{2,1,0:T(8,128)(2,1)S(1)}, u32[]{:S(2)}, u32[]{:S(2)}) %all-to-all-start) | async-done | bytes 524320 | tf_op jit(solution)/shard_map/all_to_all | solution.py:378
  40.5 2.7 %collective-permute-start.2 = (bf16[512,512]{1,0:T(8,128)(2,1)S(1)}, bf16[512,512]{1,0:T(8,128)(2,1)S(1)}, u32[]{:S(2)}, u32[]{:S(2)}) collective-permute-start(bf16[512,512]{1,0:T(8,128)(2,1)S(1)} %bitcast.16), channel_id=1, source_target_pairs={{0,256},{1,259},{2,258},{3,257},{256,0},{257,3},{258,2},{259,1},{4... | collective-permute-start | bytes 1572872 | tf_op jit(solution)/shard_map/ppermute | solution.py:100
  43.4 1.9 %collective-permute-start.6 = (bf16[1792,256]{1,0:T(8,128)(2,1)S(1)}, bf16[1792,256]{1,0:T(8,128)(2,1)S(1)}, u32[]{:S(2)}, u32[]{:S(2)}) collective-permute-start(bf16[1792,256]{1,0:T(8,128)(2,1)S(1)} %other_slices.1), channel_id=1, source_target_pairs={{0,1},{1,0},{2,3},{3,2},{256,257},{257,256},{258,259},{259,258},{4... | collective-permute-start | bytes 2752520 | tf_op jit(solution)/shard_map/ppermute | solution.py:100
  45.3 3.2 %collective-permute-start.3 = (bf16[512,512]{1,0:T(8,128)(2,1)S(1)}, bf16[512,512]{1,0:T(8,128)(2,1)S(1)}, u32[]{:S(2)}, u32[]{:S(2)}) collective-permute-start(bf16[512,512]{1,0:T(8,128)(2,1)S(1)} %bitcast.18), channel_id=1, source_target_pairs={{0,259},{1,256},{2,257},{3,258},{256,3},{257,0},{258,1},{259,2},{4... | collective-permute-start | bytes 1572872 | tf_op jit(solution)/shard_map/ppermute | solution.py:100
  48.5 4.3 %collective-permute-done.2.refs_1_ = bf16[512,512]{1,0:T(8,128)(2,1)S(1)} collective-permute-done((bf16[512,512]{1,0:T(8,128)(2,1)S(1)}, bf16[512,512]{1,0:T(8,128)(2,1)S(1)}, u32[]{:S(2)}, u32[]{:S(2)}) %collective-permute-start.2) | collective-permute-done | bytes 524320 | tf_op jit(solution)/shard_map/ppermute | solution.py:100
  52.8 1.9 %collective-permute-start.4 = (bf16[512,512]{1,0:T(8,128)(2,1)S(1)}, bf16[512,512]{1,0:T(8,128)(2,1)S(1)}, u32[]{:S(2)}, u32[]{:S(2)}) collective-permute-start(bf16[512,512]{1,0:T(8,128)(2,1)S(1)} %collective-permute-done.2.refs_1_), channel_id=1, source_target_pairs={{0,258},{1,257},{2,256},{3,259},{256,2},{257,1},{258,0},{259,3},{4... | collective-permute-start | bytes 1572872 | tf_op jit(solution)/shard_map/ppermute | solution.py:100
  54.7 5.1 %collective-permute-start.5 = (bf16[128,896]{1,0:T(8,128)(2,1)S(1)}, bf16[128,896]{1,0:T(8,128)(2,1)S(1)}, u32[]{:S(2)}, u32[]{:S(2)}) collective-permute-start(bf16[128,896]{1,0:T(8,128)(2,1)S(1)} %slice.3), channel_id=1, source_target_pairs={{0,258},{1,257},{2,256},{3,259},{256,2},{257,1},{258,0},{259,3},{4... | collective-permute-start | bytes 688136 | tf_op jit(solution)/shard_map/ppermute | solution.py:100
  59.9 7.6 %collective-permute-done.5.refs_4_.refs_7_ = bf16[128,896]{1,0:T(8,128)(2,1)S(1)} collective-permute-done((bf16[128,896]{1,0:T(8,128)(2,1)S(1)}, bf16[128,896]{1,0:T(8,128)(2,1)S(1)}, u32[]{:S(2)}, u32[]{:S(2)}) %collective-permute-start.5) | collective-permute-done | bytes 229408 | tf_op jit(solution)/shard_map/ppermute | solution.py:100
  68.5 2.1 %collective-permute-start.7 = (bf16[576,256]{1,0:T(8,128)(2,1)S(1)}, bf16[576,256]{1,0:T(8,128)(2,1)S(1)}, u32[]{:S(2)}, u32[]{:S(2)}) collective-permute-start(bf16[576,256]{1,0:T(8,128)(2,1)S(1)} %partial_send.1), channel_id=1, source_target_pairs={{0,1},{1,0},{2,3},{3,2},{256,257},{257,256},{258,259},{259,258},{4... | collective-permute-start | bytes 884744 | tf_op jit(solution)/shard_map/ppermute | solution.py:100
  72.3 1.9 %collective-permute-start.8 = (bf16[576,128]{1,0:T(8,128)(2,1)S(1)}, bf16[576,128]{1,0:T(8,128)(2,1)S(1)}, u32[]{:S(2)}, u32[]{:S(2)}) collective-permute-start(bf16[576,128]{1,0:T(8,128)(2,1)S(1)} %hidden.1.refs_0_), channel_id=1, source_target_pairs={{0,256},{1,259},{2,258},{3,257},{256,0},{257,3},{258,2},{259,1},{4... | collective-permute-start | bytes 442376 | tf_op jit(solution)/shard_map/ppermute | solution.py:100
  74.2 4.6 %collective-permute-start.9 = (bf16[576,128]{1,0:T(8,128)(2,1)S(1)}, bf16[576,128]{1,0:T(8,128)(2,1)S(1)}, u32[]{:S(2)}, u32[]{:S(2)}) collective-permute-start(bf16[576,128]{1,0:T(8,128)(2,1)S(1)} %hidden.1.refs_0_), channel_id=1, source_target_pairs={{0,259},{1,256},{2,257},{3,258},{256,3},{257,0},{258,1},{259,2},{4... | collective-permute-start | bytes 442376 | tf_op jit(solution)/shard_map/ppermute | solution.py:100
  79.5 1.9 %collective-permute-start.10 = (bf16[576,128]{1,0:T(8,128)(2,1)S(1)}, bf16[576,128]{1,0:T(8,128)(2,1)S(1)}, u32[]{:S(2)}, u32[]{:S(2)}) collective-permute-start(bf16[576,128]{1,0:T(8,128)(2,1)S(1)} %collective-permute-done.8.refs_1_), channel_id=1, source_target_pairs={{0,258},{1,257},{2,256},{3,259},{256,2},{257,1},{258,0},{259,3},{4... | collective-permute-start | bytes 442376 | tf_op jit(solution)/shard_map/ppermute | solution.py:100
  81.5 6.3 %collective-permute-done.10.refs_3_ = bf16[576,128]{1,0:T(8,128)(2,1)S(1)} collective-permute-done((bf16[576,128]{1,0:T(8,128)(2,1)S(1)}, bf16[576,128]{1,0:T(8,128)(2,1)S(1)}, u32[]{:S(2)}, u32[]{:S(2)}) %collective-permute-start.10) | collective-permute-done | bytes 147488 | tf_op jit(solution)/shard_map/ppermute | solution.py:100
  88.6 1.9 %collective-permute-start.11 = (bf16[576,512]{1,0:T(8,128)(2,1)S(1)}, bf16[576,512]{1,0:T(8,128)(2,1)S(1)}, u32[]{:S(2)}, u32[]{:S(2)}) collective-permute-start(bf16[576,512]{1,0:T(8,128)(2,1)S(1)} %down_send.1), channel_id=1, source_target_pairs={{0,1},{1,0},{2,3},{3,2},{256,257},{257,256},{258,259},{259,258},{4... | collective-permute-start | bytes 1769480 | tf_op jit(solution)/shard_map/ppermute | solution.py:100
  92.5 1.4 %repack.1._ = bf16[512,512]{1,0:T(8,128)(2,1)} custom-call(f32[576,448]{1,0:T(8,128)S(1)} %down_keep.1.one_ref, bf16[576,512]{1,0:T(8,128)(2,1)S(1)} %collective-permute-done.11.two_ref), custom_call_target="tpu_custom_call" | custom-call | flops 100000000 | bytes 2000000 | tf_op jit(solution)/shard_map/repack/pallas_call | solution.py:415
  93.9 6.0 %all-to-all-start.1 = ((bf16[64,8,512]{2,1,0:T(8,128)(2,1)}), bf16[64,8,512]{2,1,0:T(8,128)(2,1)S(1)}, u32[]{:S(2)}, u32[]{:S(2)}) async-start(bf16[64,8,512]{2,1,0:T(8,128)(2,1)} %bitcast.12), calls=%async_computation.1 | async-start | bytes 1048576 | tf_op jit(solution)/shard_map/all_to_all | solution.py:419
  101.5 1.9 %collective-permute-start.12 = (f32[96,512]{1,0:T(8,128)S(1)}, f32[96,512]{1,0:T(8,128)S(1)}, u32[]{:S(2)}, u32[]{:S(2)}) collective-permute-start(f32[96,512]{1,0:T(8,128)S(1)} %get-tuple-element.17), channel_id=1, source_target_pairs={{0,256},{1,257},{2,258},{3,259},{256,0},{257,1},{258,2},{259,3},{4... | collective-permute-start | bytes 589832 | tf_op jit(solution)/shard_map/ppermute | solution.py:100
  104.3 5.7 %collective-permute-done.12.two_ref = f32[96,512]{1,0:T(8,128)S(1)} collective-permute-done((f32[96,512]{1,0:T(8,128)S(1)}, f32[96,512]{1,0:T(8,128)S(1)}, u32[]{:S(2)}, u32[]{:S(2)}) %collective-permute-start.12) | collective-permute-done | bytes 196640 | tf_op jit(solution)/shard_map/ppermute | solution.py:100
  110.8 8.9 %all-to-all-done.1 = bf16[64,8,512]{2,1,0:T(8,128)(2,1)S(1)} async-done(((bf16[64,8,512]{2,1,0:T(8,128)(2,1)}), bf16[64,8,512]{2,1,0:T(8,128)(2,1)S(1)}, u32[]{:S(2)}, u32[]{:S(2)}) %all-to-all-start.1) | async-done | bytes 524320 | tf_op jit(solution)/shard_map/all_to_all | solution.py:419
  (37 shorter events, 10.2 us)
Async XLA Ops:
  0.6 42.6 %copy-start = (bf16[1,3584,128]{2,1,0:T(8,128)(2,1)S(1)}, bf16[1,3584,128]{2,1,0:T(8,128)(2,1)}, u32[]{:S(2)}) copy-start(bf16[1,3584,128]{2,1,0:T(8,128)(2,1)} %param.17) | copy-start | bytes 2752516
  0.6 42.6 %copy-start.1 = (bf16[1,3584,128]{2,1,0:T(8,128)(2,1)S(1)}, bf16[1,3584,128]{2,1,0:T(8,128)(2,1)}, u32[]{:S(2)}) copy-start(bf16[1,3584,128]{2,1,0:T(8,128)(2,1)} %param.18) | copy-start | bytes 2752516
  4.2 36.3 %all-to-all-start = ((bf16[64,8,512]{2,1,0:T(8,128)(2,1)}), bf16[64,8,512]{2,1,0:T(8,128)(2,1)S(1)}, u32[]{:S(2)}, u32[]{:S(2)}) async-start(bf16[64,8,512]{2,1,0:T(8,128)(2,1)} %bitcast.32), calls=%async_computation | async-start | bytes 1048576 | tf_op jit(solution)/shard_map/all_to_all | solution.py:378
  20.8 13.0 %collective-permute-start = (bf16[256,896]{1,0:T(8,128)(2,1)}, bf16[256,896]{1,0:T(8,128)(2,1)S(1)}, u32[]{:S(2)}, u32[]{:S(2)}) collective-permute-start(bf16[256,896]{1,0:T(8,128)(2,1)} %get-tuple-element.11), channel_id=1, source_target_pairs={{0,256},{1,259},{2,258},{3,257},{256,0},{257,3},{258,2},{259,1},{4... | collective-permute-start | bytes 1376264 | tf_op jit(solution)/shard_map/ppermute | solution.py:100
  23.5 10.1 %collective-permute-start.1 = (bf16[128,896]{1,0:T(8,128)(2,1)}, bf16[128,896]{1,0:T(8,128)(2,1)S(1)}, u32[]{:S(2)}, u32[]{:S(2)}) collective-permute-start(bf16[128,896]{1,0:T(8,128)(2,1)} %get-tuple-element.12), channel_id=1, source_target_pairs={{0,259},{1,256},{2,257},{3,258},{256,3},{257,0},{258,1},{259,2},{4... | collective-permute-start | bytes 688136 | tf_op jit(solution)/shard_map/ppermute | solution.py:100
  40.5 12.3 %collective-permute-start.2 = (bf16[512,512]{1,0:T(8,128)(2,1)S(1)}, bf16[512,512]{1,0:T(8,128)(2,1)S(1)}, u32[]{:S(2)}, u32[]{:S(2)}) collective-permute-start(bf16[512,512]{1,0:T(8,128)(2,1)S(1)} %bitcast.16), channel_id=1, source_target_pairs={{0,256},{1,259},{2,258},{3,257},{256,0},{257,3},{258,2},{259,1},{4... | collective-permute-start | bytes 1572872 | tf_op jit(solution)/shard_map/ppermute | solution.py:100
  43.4 24.1 %collective-permute-start.6 = (bf16[1792,256]{1,0:T(8,128)(2,1)S(1)}, bf16[1792,256]{1,0:T(8,128)(2,1)S(1)}, u32[]{:S(2)}, u32[]{:S(2)}) collective-permute-start(bf16[1792,256]{1,0:T(8,128)(2,1)S(1)} %other_slices.1), channel_id=1, source_target_pairs={{0,1},{1,0},{2,3},{3,2},{256,257},{257,256},{258,259},{259,258},{4... | collective-permute-start | bytes 2752520 | tf_op jit(solution)/shard_map/ppermute | solution.py:100
  45.3 22.2 %collective-permute-start.3 = (bf16[512,512]{1,0:T(8,128)(2,1)S(1)}, bf16[512,512]{1,0:T(8,128)(2,1)S(1)}, u32[]{:S(2)}, u32[]{:S(2)}) collective-permute-start(bf16[512,512]{1,0:T(8,128)(2,1)S(1)} %bitcast.18), channel_id=1, source_target_pairs={{0,259},{1,256},{2,257},{3,258},{256,3},{257,0},{258,1},{259,2},{4... | collective-permute-start | bytes 1572872 | tf_op jit(solution)/shard_map/ppermute | solution.py:100
  52.8 14.7 %collective-permute-start.4 = (bf16[512,512]{1,0:T(8,128)(2,1)S(1)}, bf16[512,512]{1,0:T(8,128)(2,1)S(1)}, u32[]{:S(2)}, u32[]{:S(2)}) collective-permute-start(bf16[512,512]{1,0:T(8,128)(2,1)S(1)} %collective-permute-done.2.refs_1_), channel_id=1, source_target_pairs={{0,258},{1,257},{2,256},{3,259},{256,2},{257,1},{258,0},{259,3},{4... | collective-permute-start | bytes 1572872 | tf_op jit(solution)/shard_map/ppermute | solution.py:100
  54.7 12.8 %collective-permute-start.5 = (bf16[128,896]{1,0:T(8,128)(2,1)S(1)}, bf16[128,896]{1,0:T(8,128)(2,1)S(1)}, u32[]{:S(2)}, u32[]{:S(2)}) collective-permute-start(bf16[128,896]{1,0:T(8,128)(2,1)S(1)} %slice.3), channel_id=1, source_target_pairs={{0,258},{1,257},{2,256},{3,259},{256,2},{257,1},{258,0},{259,3},{4... | collective-permute-start | bytes 688136 | tf_op jit(solution)/shard_map/ppermute | solution.py:100
  68.5 19.2 %copy-start.3 = (bf16[1,128,3584]{2,1,0:T(8,128)(2,1)S(1)}, bf16[1,128,3584]{2,1,0:T(8,128)(2,1)}, u32[]{:S(2)}) copy-start(bf16[1,128,3584]{2,1,0:T(8,128)(2,1)} %param.19) | copy-start | bytes 2752516
  68.5 3.6 %collective-permute-start.7 = (bf16[576,256]{1,0:T(8,128)(2,1)S(1)}, bf16[576,256]{1,0:T(8,128)(2,1)S(1)}, u32[]{:S(2)}, u32[]{:S(2)}) collective-permute-start(bf16[576,256]{1,0:T(8,128)(2,1)S(1)} %partial_send.1), channel_id=1, source_target_pairs={{0,1},{1,0},{2,3},{3,2},{256,257},{257,256},{258,259},{259,258},{4... | collective-permute-start | bytes 884744 | tf_op jit(solution)/shard_map/ppermute | solution.py:100
  72.3 7.2 %collective-permute-start.8 = (bf16[576,128]{1,0:T(8,128)(2,1)S(1)}, bf16[576,128]{1,0:T(8,128)(2,1)S(1)}, u32[]{:S(2)}, u32[]{:S(2)}) collective-permute-start(bf16[576,128]{1,0:T(8,128)(2,1)S(1)} %hidden.1.refs_0_), channel_id=1, source_target_pairs={{0,256},{1,259},{2,258},{3,257},{256,0},{257,3},{258,2},{259,1},{4... | collective-permute-start | bytes 442376 | tf_op jit(solution)/shard_map/ppermute | solution.py:100
  74.2 7.3 %collective-permute-start.9 = (bf16[576,128]{1,0:T(8,128)(2,1)S(1)}, bf16[576,128]{1,0:T(8,128)(2,1)S(1)}, u32[]{:S(2)}, u32[]{:S(2)}) collective-permute-start(bf16[576,128]{1,0:T(8,128)(2,1)S(1)} %hidden.1.refs_0_), channel_id=1, source_target_pairs={{0,259},{1,256},{2,257},{3,258},{256,3},{257,0},{258,1},{259,2},{4... | collective-permute-start | bytes 442376 | tf_op jit(solution)/shard_map/ppermute | solution.py:100
  79.5 8.2 %collective-permute-start.10 = (bf16[576,128]{1,0:T(8,128)(2,1)S(1)}, bf16[576,128]{1,0:T(8,128)(2,1)S(1)}, u32[]{:S(2)}, u32[]{:S(2)}) collective-permute-start(bf16[576,128]{1,0:T(8,128)(2,1)S(1)} %collective-permute-done.8.refs_1_), channel_id=1, source_target_pairs={{0,258},{1,257},{2,256},{3,259},{256,2},{257,1},{258,0},{259,3},{4... | collective-permute-start | bytes 442376 | tf_op jit(solution)/shard_map/ppermute | solution.py:100
  88.6 3.9 %collective-permute-start.11 = (bf16[576,512]{1,0:T(8,128)(2,1)S(1)}, bf16[576,512]{1,0:T(8,128)(2,1)S(1)}, u32[]{:S(2)}, u32[]{:S(2)}) collective-permute-start(bf16[576,512]{1,0:T(8,128)(2,1)S(1)} %down_send.1), channel_id=1, source_target_pairs={{0,1},{1,0},{2,3},{3,2},{256,257},{257,256},{258,259},{259,258},{4... | collective-permute-start | bytes 1769480 | tf_op jit(solution)/shard_map/ppermute | solution.py:100
  91.4 9.2 %copy-start.2 = (bf16[1,1024,576]{1,2,0:T(8,128)(2,1)S(1)}, bf16[1,1024,576]{1,2,0:T(8,128)(2,1)}, u32[]{:S(2)}) copy-start(bf16[1,1024,576]{1,2,0:T(8,128)(2,1)} %param.10) | copy-start | bytes 3538948
  91.4 9.2 %copy-start.4 = (bf16[3,1,32,576]{3,2,1,0:T(8,128)(2,1)S(1)}, bf16[3,1,32,576]{3,2,1,0:T(8,128)(2,1)}, u32[]{:S(2)}) copy-start(bf16[3,1,32,576]{3,2,1,0:T(8,128)(2,1)} %param.12) | copy-start | bytes 331780
  91.4 9.2 %copy-start.5 = (bf16[3,1,576]{2,0,1:T(4,128)(2,1)S(1)}, bf16[3,1,576]{2,0,1:T(4,128)(2,1)}, u32[]{:S(2)}) copy-start(bf16[3,1,576]{2,0,1:T(4,128)(2,1)} %param.11) | copy-start | bytes 10372
  93.9 25.9 %all-to-all-start.1 = ((bf16[64,8,512]{2,1,0:T(8,128)(2,1)}), bf16[64,8,512]{2,1,0:T(8,128)(2,1)S(1)}, u32[]{:S(2)}, u32[]{:S(2)}) async-start(bf16[64,8,512]{2,1,0:T(8,128)(2,1)} %bitcast.12), calls=%async_computation.1 | async-start | bytes 1048576 | tf_op jit(solution)/shard_map/all_to_all | solution.py:419
  99.9 3.6 %copy-start.6 = (s32[3,12,8]{1,2,0:T(8,128)S(1)}, s32[3,12,8]{1,2,0:T(8,128)}, u32[]{:S(2)}) copy-start(s32[3,12,8]{1,2,0:T(8,128)} %param.15) | copy-start | bytes 3460
  99.9 3.7 %copy-start.7 = (f32[3,12,8]{1,2,0:T(8,128)S(1)}, f32[3,12,8]{1,2,0:T(8,128)}, u32[]{:S(2)}) copy-start(f32[3,12,8]{1,2,0:T(8,128)} %param.16) | copy-start | bytes 3460
  101.5 8.5 %collective-permute-start.12 = (f32[96,512]{1,0:T(8,128)S(1)}, f32[96,512]{1,0:T(8,128)S(1)}, u32[]{:S(2)}, u32[]{:S(2)}) collective-permute-start(f32[96,512]{1,0:T(8,128)S(1)} %get-tuple-element.17), channel_id=1, source_target_pairs={{0,256},{1,257},{2,258},{3,259},{256,0},{257,1},{258,2},{259,3},{4... | collective-permute-start | bytes 589832 | tf_op jit(solution)/shard_map/ppermute | solution.py:100
